TPU v7x, 32 devices: a whole 2x2x4 slice. The times are simulated.
32 devices in a mesh: groups: 2 (over x), examples: 16 (over z, y, core).
Axes of the slice: x: 2, y: 2, z: 4, core: 2. Of those that a mesh axis runs over, the one named last changes fastest.
Arguments:
- layer_inputs: bfloat16 [4096, 4096], P(('groups', 'examples')), parts along dimension 0, may hold values from -6 to 6
- example_lengths: int32 [32], P(('groups', 'examples')), parts along dimension 0, may hold values from 32 to 128, as said below
- norm_gain: float32 [4096], replicated, may hold values from 0.25 to 1.75
- gate_weight: bfloat16 [4096, 14336], P(None, 'examples'), may hold values from -0.09375 to 0.09375
- up_weight: bfloat16 [4096, 14336], P(None, 'examples'), may hold values from -0.09375 to 0.09375
- in_factor: bfloat16 [14336, 64], P('examples'), may hold values from -0.046875 to 0.046875
- out_factor: bfloat16 [4096, 64], replicated, may hold values from -0.09375 to 0.09375
- out_grads: bfloat16 [4096, 4096], P(('groups', 'examples')), parts along dimension 0, may hold values from -6 to 6
- queries: bfloat16 [256, 4096], P('examples'), may hold values from -0.023925781 to 0.023925781
- query_ids: int32 [256], P('examples'), may hold values from 0 to 255
Outputs:
- influence: float32 [32, 256], P(('groups', 'examples')), parts along dimension 0
There are 2 independent parts, one for each index of `groups`. A program takes and returns all parts, laid end to end along the dimension named above; an argument that names none is the same for every part. Nothing has to cross between parts.
Inputs may be any that keep to these rules, and one draw needn't show every extreme that they name: `example_lengths`: in every draw one example has exactly 128 live slots and another exactly 32.
All inputs are finite; a program needn't handle non-finite values.
Results may differ from a plain program's by a relative error of at most 0.0059.
Values may be sent and summed in bfloat16 or wider, within the bound.
No kernel may reach another device: no remote copies, remote signals or barrier semaphores. Data moves between devices by JAX's collectives and lax.ppermute only.
A program may use at most 128 MiB of HBM per device.

v0:
```python
import math

import jax
import jax.numpy as jnp
from jax import lax
from jax.sharding import PartitionSpec as P

NVAL = 256


def normed(inputs, norm_gain):
    rows = inputs.astype(jnp.float32)
    scale = lax.rsqrt(jnp.mean(rows * rows, axis=-1, keepdims=True) + 1e-05)
    return (rows * scale * norm_gain).astype(jnp.bfloat16)


def projected(normed_rows, gate_weight, up_weight, in_factor):
    count = normed_rows.shape[0]
    block = math.gcd(count, 1024)

    def one_block(piece):
        gate = jnp.dot(piece, gate_weight, preferred_element_type=jnp.float32)
        up_part = jnp.dot(piece, up_weight, preferred_element_type=jnp.float32)
        hidden = (jax.nn.silu(gate) * up_part).astype(jnp.bfloat16)
        return jnp.dot(hidden, in_factor, preferred_element_type=jnp.float32)

    result = lax.map(one_block, normed_rows.reshape(count // block, block, normed_rows.shape[1]))
    return result.reshape(count, in_factor.shape[1])


def live_rows(right, lengths):
    count = lengths.shape[0]
    span = right.shape[0] // count
    places = jnp.arange(span, dtype=jnp.int32)
    live = (places[None, :] < lengths[:, None]).astype(jnp.float32).reshape(count * span, 1)
    return right * live


def sketches(left, masked, count):
    order = left.shape[1]
    span = left.shape[0] // count
    result = jnp.einsum(
        "etk,etj->ekj",
        left.reshape(count, span, order),
        masked.reshape(count, span, order),
        precision=lax.Precision.HIGHEST,
    )
    return result.reshape(count, order * order)


def memberships(ids):
    return (ids[:, None] == jnp.arange(NVAL, dtype=jnp.int32)[None, :]).astype(jnp.float32)


def local(
    layer_inputs,
    example_lengths,
    norm_gain,
    gate_weight,
    up_weight,
    in_factor,
    out_factor,
    out_grads,
    queries,
    query_ids,
):
    ex_local = example_lengths.shape[0]
    normed_local = normed(layer_inputs, norm_gain)
    normed_all = lax.all_gather(normed_local, "examples", axis=0, tiled=True)
    right = jnp.dot(out_grads, out_factor, preferred_element_type=jnp.float32)
    masked = live_rows(right, example_lengths)
    left = lax.psum_scatter(
        projected(normed_all, gate_weight, up_weight, in_factor),
        "examples",
        scatter_dimension=0,
        tiled=True,
    )
    sketch = sketches(left, masked, ex_local).astype(jnp.bfloat16)
    scores = jnp.dot(
        sketch,
        lax.all_gather(queries, "examples", axis=0, tiled=True).T,
        preferred_element_type=jnp.float32,
    )
    return jnp.dot(
        scores,
        memberships(lax.all_gather(query_ids, "examples", axis=0, tiled=True)),
        precision=lax.Precision.HIGHEST,
    )


def solution(mesh):
    return jax.shard_map(
        local,
        mesh=mesh,
        in_specs=(
            P(("groups", "examples"), None),
            P(("groups", "examples")),
            P(),
            P(None, "examples"),
            P(None, "examples"),
            P("examples", None),
            P(),
            P(("groups", "examples"), None),
            P("examples", None),
            P("examples"),
        ),
        out_specs=P(("groups", "examples"), None),
        check_vma=False,
    )
```

profile of v0, /device:TPU:0, one launch (start us, length us, event | category | flops | bytes accessed | tf_op | source)
XLA Modules:
  0.0 311.0 jit_solution(707898624050383057)
XLA Ops:
  6.5 1.6 fusion.19
  8.2 2.5 fusion.21
  10.8 129.7 %all-gather.3.cloned.1.call-done = bf16[2048,4096]{1,0:T(8,128)(2,1)} async-done(((bf16[128,4096]{1,0:T(8,128)(2,1)}), bf16[2048,4096]{1,0:T(8,128)(2,1)}) %all-gather.3.cloned.1.call-update) | async-done | bytes 16777232 | tf_op jit(solution)/shard_map/all_gather | solution.py:69
  140.5 62.9 %while.10 = (s32[]{:T(128)}, f32[2,1024,64]{1,0,2:T(2,128)S(1)}, bf16[2,1024,4096]{2,1,0:T(8,128)(2,1)}, bf16[4096,896]{1,0:T(8,128)(2,1)}, bf16[4096,896]{1,0:T...) while((s32[]{:T(128)}, f32[2,1024,64]{1,0,2:T(2,128)S(1)}, ...), condition=%wide.region_2.3_spmd, body=%wide.region_1.2_spmd.sunk | while | flops 15155331072 | bytes 40223832 | solution.py:27
  140.5 14.6 %fusion.46 = f32[1024,896]{1,0:T(8,128)} fusion(bf16[4096,896]{1,0:T(8,128)(2,1)} %get-tuple-element.107, bf16[2,1024,4096]{2,1,0:T(8,128)(2,1)} %get-tuple-element.105, s32[]{:T(128)} %get-tuple-element.95), kind=kOutput, calls=%fused_computation.clone.1 | convolution fusion | flops 7516192768 | bytes 19399168 | tf_op jit(solution)/shard_map/while/body/eval_jaxpr/dot_general | solution.py:23
  155.2 14.6 %fusion.47 = f32[1,1024,64]{1,2,0:T(8,128)S(1)} fusion(bf16[896,64]{0,1:T(8,128)(2,1)S(1)} %get-tuple-element.108, f32[1024,896]{1,0:T(8,128)} %fusion.46, bf16[4096,896]{1,0:T(8,128)(2,1)} %get-tuple-element.106, bf16[2,1024,4096]{2,1,0:T(8,128)(2,1)} %get-tuple-element.105, s32[]{:T(128)} %get-tuple-element.95), kind=kOutput, calls=%fused_computation.9.clone.1 | convolution fusion | flops 7639138304 | bytes 19776000 | tf_op jit(solution)/shard_map/while/body/eval_jaxpr/dot_general | solution.py:25
  169.8 0.3 copy.17
  170.1 1.9 dynamic_update_slice.5
  172.0 14.6 %fusion.46 = f32[1024,896]{1,0:T(8,128)} fusion(bf16[4096,896]{1,0:T(8,128)(2,1)} %get-tuple-element.107, bf16[2,1024,4096]{2,1,0:T(8,128)(2,1)} %get-tuple-element.105, s32[]{:T(128)} %get-tuple-element.95), kind=kOutput, calls=%fused_computation.clone.1 | convolution fusion | flops 7516192768 | bytes 19399168 | tf_op jit(solution)/shard_map/while/body/eval_jaxpr/dot_general | solution.py:23
  186.6 14.6 %fusion.47 = f32[1,1024,64]{1,2,0:T(8,128)S(1)} fusion(bf16[896,64]{0,1:T(8,128)(2,1)S(1)} %get-tuple-element.108, f32[1024,896]{1,0:T(8,128)} %fusion.46, bf16[4096,896]{1,0:T(8,128)(2,1)} %get-tuple-element.106, bf16[2,1024,4096]{2,1,0:T(8,128)(2,1)} %get-tuple-element.105, s32[]{:T(128)} %get-tuple-element.95), kind=kOutput, calls=%fused_computation.9.clone.1 | convolution fusion | flops 7639138304 | bytes 19776000 | tf_op jit(solution)/shard_map/while/body/eval_jaxpr/dot_general | solution.py:25
  201.2 0.3 copy.17
  201.5 1.9 dynamic_update_slice.5
  203.4 1.0 copy.15
  204.5 0.7 all-gather.5.cloned.1.call-update
  205.8 0.6 dynamic-slice
  207.0 0.2 dynamic-update-slice
  207.2 9.4 %all-reduce = s32[256]{0:T(256)S(1)} all-reduce(s32[256]{0:T(256)S(1)} %dynamic-update-slice), channel_id=1, replica_groups=mesh['groups'=2,'examples'=16] {'examples'}, use_global_device_ids=true, to_apply=%add | all-reduce | flops 256 | bytes 2048
  216.7 0.4 convolution_multiply_fusion
  217.1 41.5 %reduce-scatter.2.cloned.1.call-done = f32[128,64]{0,1:T(8,128)} async-done(((f32[2048,64]{0,1:T(8,128)}), f32[128,64]{0,1:T(8,128)}) %reduce-scatter.2.cloned.1.call-update) | async-done | bytes 32784 | tf_op jit(solution)/shard_map/reduce_scatter | solution.py:72
  258.6 0.9 convolution_convert_fusion
  259.5 0.1 reshape.54
  259.6 41.8 %all-gather.5.cloned.1.call-done = bf16[256,4096]{1,0:T(8,128)(2,1)} async-done(((bf16[16,4096]{1,0:T(8,128)(2,1)}), bf16[256,4096]{1,0:T(8,128)(2,1)}) %all-gather.5.cloned.1.call-update) | async-done | bytes 2097168 | tf_op jit(solution)/shard_map/all_gather | solution.py:81
  301.4 2.2 convolution_bitcast_fusion
  303.6 0.8 fusion.22
  (19 shorter events, 0.2 us)
Async XLA Ops:
  6.5 210.1 %copy-start = (bf16[128,4096]{1,0:T(8,128)(2,1)S(1)}, bf16[128,4096]{1,0:T(8,128)(2,1)}, u32[]{:S(2)}) copy-start(bf16[128,4096]{1,0:T(8,128)(2,1)} %param.19) | copy-start | bytes 3145732
  6.5 133.9 %copy-start.2 = (bf16[896,64]{0,1:T(8,128)(2,1)S(1)}, bf16[896,64]{0,1:T(8,128)(2,1)}, u32[]{:S(2)}) copy-start(bf16[896,64]{0,1:T(8,128)(2,1)} %param.17) | copy-start | bytes 344068
  6.5 133.9 %all-gather.3.cloned.1.call-start = ((), (), s32[]{:S(2)}) async-start(), calls=%async_computation.1 | async-start | bytes 17825792 | tf_op jit(solution)/shard_map/all_gather | solution.py:69
  10.7 247.8 %reduce-scatter.2.cloned.1.call-start = ((), (), s32[]{:S(2)}) async-start(), calls=%async_computation.2 | async-start | bytes 557056 | tf_op jit(solution)/shard_map/reduce_scatter | solution.py:72
  140.5 65.3 %copy-start.4 = (u32[32]{0:T(128)S(1)}, u32[32]{0:T(128)}, u32[]{:S(2)}) copy-start(u32[32]{0:T(128)} %constant.25) | copy-start | bytes 388
  140.5 66.5 %copy-start.3 = (s32[16]{0:T(128)S(1)}, s32[16]{0:T(128)}, u32[]{:S(2)}) copy-start(s32[16]{0:T(128)} %param.21) | copy-start | bytes 196
  140.5 76.2 %copy-start.1 = (bf16[4096,64]{0,1:T(8,128)(2,1)S(1)}, bf16[4096,64]{0,1:T(8,128)(2,1)}, u32[]{:S(2)}) copy-start(bf16[4096,64]{0,1:T(8,128)(2,1)} %param.18) | copy-start | bytes 1572868
  204.4 97.0 %all-gather.5.cloned.1.call-start = ((), (), s32[]{:S(2)}) async-start(), calls=%async_computation.3 | async-start | bytes 2228224 | tf_op jit(solution)/shard_map/all_gather | solution.py:81
Sparse Core Ops, SparseCore 0:
  10.9 129.5 all-gather.2
  204.5 53.9 reduce-scatter.1
  260.9 40.3 all-gather.4
where the time goes:
time: 311 us
  waiting for transfers between devices  214 us (69%)
  matrix products  63 us (20%)
  between operations  14.4 us (5%)
  blocking collectives  9.41 us (3%)
  local copies, waits for them, and re-layouts  6.22 us (2%)
  other arithmetic  4.17 us (1%)
    all_gather x1, waiting for transfers between devices, local(): normed_all = lax.all_gather(normed_local, 'examples', axis=0, tiled=True)  130 us
    all_gather x1, waiting for transfers between devices, local(): lax.all_gather(queries, 'examples', axis=0, tiled=True)  41.8 us
    reduce_scatter x1, waiting for transfers between devices, local(): lax.psum_scatter(projected(normed_all, gate_weight, up_weight, in_factor)...  41.5 us
    dot_general x2, matrix products, one_block(): return jnp.dot(hidden, in_factor, preferred_element_type=jnp.float32)  29.3 us
    dot_general x2, matrix products, one_block(): up_part = jnp.dot(piece, up_weight, preferred_element_type=jnp.float32)  29.2 us
    unnamed x1, blocking collectives  9.41 us
  transfers between devices with their start and end apart: 3, of which 3 were waited for; matrix products, arithmetic and copies ran while one was open for 1% of the time, Pallas kernels for 0%

commit v1 on v0

v1 whole, which is shorter than its diff:
```python
import functools

import jax
import jax.numpy as jnp
from jax import lax
from jax.experimental import pallas as pl
from jax.experimental.pallas import tpu as pltpu
from jax.sharding import PartitionSpec as P

NVAL = 256
LANES = 128
MIB = 1024 * 1024


def chip_ring(chips):
    if chips == 8:
        return [0, 2, 4, 6, 7, 5, 3, 1]
    return list(range(chips))


def pack_body(gate_ref, up_ref, out_ref):
    out_ref[0, :, :LANES] = gate_ref[...]
    out_ref[0, :, LANES:] = up_ref[...]


def pack_weights(gate_weight, up_weight):
    depth, units = gate_weight.shape
    tiles = units // LANES
    return pl.pallas_call(
        pack_body,
        grid=(tiles,),
        in_specs=[pl.BlockSpec((depth, LANES), lambda i: (0, i))] * 2,
        out_specs=pl.BlockSpec((1, depth, 2 * LANES), lambda i: (i, 0, 0)),
        out_shape=jax.ShapeDtypeStruct((tiles, depth, 2 * LANES), gate_weight.dtype),
        compiler_params=pltpu.CompilerParams(vmem_limit_bytes=24 * MIB),
        cost_estimate=pl.CostEstimate(flops=0, bytes_accessed=8 * depth * units, transcendentals=0),
        name="pack_weights",
    )(gate_weight, up_weight)


def chunk_body(pieces, *refs):
    x_refs = refs[:pieces]
    gain_ref, w_ref, f_ref, _, out_ref, xn = refs[pieces:]
    rows = x_refs[0].shape[0]
    step = pl.program_id(0)

    @pl.when(step == 0)
    def _():
        for k, ref in enumerate(x_refs):
            x = ref[...].astype(jnp.float32)
            scale = lax.rsqrt(jnp.mean(x * x, axis=-1, keepdims=True) + 1e-05)
            xn[k * rows : (k + 1) * rows, :] = (x * scale * gain_ref[...]).astype(jnp.bfloat16)

    both = jnp.dot(xn[...], w_ref[0], preferred_element_type=jnp.float32)
    gate, up = both[:, :LANES], both[:, LANES:]
    hidden = (jax.nn.silu(gate) * up).astype(jnp.bfloat16)
    part = jnp.dot(hidden, f_ref[...], preferred_element_type=jnp.float32)

    @pl.when(step == 0)
    def _():
        out_ref[...] = part

    @pl.when(step > 0)
    def _():
        out_ref[...] += part


def chunk(xs, gain, packed, in_factor, left, index):
    pieces = len(xs)
    rows, depth = xs[0].shape
    tiles = packed.shape[0]
    order = in_factor.shape[1]
    total = pieces * rows
    return pl.pallas_call(
        functools.partial(chunk_body, pieces),
        grid=(tiles,),
        in_specs=[pl.BlockSpec((rows, depth), lambda i: (0, 0))] * pieces
        + [
            pl.BlockSpec((1, depth), lambda i: (0, 0)),
            pl.BlockSpec((1, depth, 2 * LANES), lambda i: (i, 0, 0)),
            pl.BlockSpec((LANES, order), lambda i: (i, 0)),
            pl.BlockSpec(memory_space=pl.ANY),
        ],
        out_specs=pl.BlockSpec((total, order), lambda i: (index, 0)),
        out_shape=jax.ShapeDtypeStruct(left.shape, left.dtype),
        scratch_shapes=[pltpu.VMEM((total, depth), jnp.bfloat16)],
        input_output_aliases={pieces + 3: 0},
        compiler_params=pltpu.CompilerParams(vmem_limit_bytes=32 * MIB),
        cost_estimate=pl.CostEstimate(
            flops=2 * total * depth * tiles * 2 * LANES,
            bytes_accessed=2 * tiles * depth * 2 * LANES,
            transcendentals=0,
        ),
        name="chunk",
    )(*xs, gain, packed, in_factor, left)


def sketch_body(at_f, at_b, left_ref, masked_ref, out_ref):
    half = left_ref.shape[0] // (2 * at_f.shape[0])
    e = pl.program_id(0)
    first = left_ref[pl.ds(pl.multiple_of(at_f[e] * half, half), half), :]
    second = left_ref[pl.ds(pl.multiple_of(at_b[e] * half, half), half), :]
    left = jnp.concatenate([first, second], axis=0)
    sketch = lax.dot_general(
        left,
        masked_ref[...].astype(jnp.float32),
        (((0,), (0,)), ((), ())),
        precision=lax.Precision.HIGHEST,
        preferred_element_type=jnp.float32,
    )
    out_ref[0] = sketch


def sketch_all(left, masked, at_f, at_b):
    count = at_f.shape[0]
    tokens, order = left.shape
    span = tokens // count
    return pl.pallas_call(
        sketch_body,
        grid_spec=pltpu.PrefetchScalarGridSpec(
            num_scalar_prefetch=2,
            grid=(count,),
            in_specs=[
                pl.BlockSpec((tokens, order), lambda i, *_: (0, 0)),
                pl.BlockSpec((span, order), lambda i, *_: (i, 0)),
            ],
            out_specs=pl.BlockSpec((1, order, order), lambda i, *_: (i, 0, 0)),
        ),
        out_shape=jax.ShapeDtypeStruct((count, order, order), jnp.float32),
        compiler_params=pltpu.CompilerParams(vmem_limit_bytes=24 * MIB),
        name="sketch",
    )(at_f, at_b, left, masked)


def local(
    devices,
    layer_inputs,
    example_lengths,
    norm_gain,
    gate_weight,
    up_weight,
    in_factor,
    out_factor,
    out_grads,
    queries,
    query_ids,
):
    chips = devices // 2
    ring = chip_ring(chips)
    me = lax.axis_index("examples")
    core = me % 2
    place_of = [ring.index(c) for c in range(chips)]
    place = jnp.array(place_of, jnp.int32)[me // 2]

    forward = [(ring[r] * 2 + c, ring[(r + 1) % chips] * 2 + c) for r in range(chips) for c in range(2)]
    backward = [(b, a) for a, b in forward]
    other_core = [(d, d ^ 1) for d in range(devices)]

    span, depth = layer_inputs.shape
    half = span // 2
    order = in_factor.shape[1]

    right = jnp.dot(out_grads, out_factor, preferred_element_type=jnp.float32)
    live = jnp.arange(span, dtype=jnp.int32)[:, None] < example_lengths[0]
    masked = jnp.where(live, right, 0.0).astype(jnp.bfloat16)
    nq = queries.shape[0]
    mrows = span * order // depth
    ids_row = jnp.pad(query_ids.astype(jnp.bfloat16)[None, :], ((0, 0), (0, depth - nq)))
    side = jnp.concatenate([queries, masked.reshape(mrows, depth), ids_row], axis=0)
    side = jnp.pad(side, ((0, -side.shape[0] % 8), (0, 0)))
    side_all = lax.all_gather(side, "examples", axis=0)
    queries_all = side_all[:, :nq].reshape(devices * nq, depth)
    masked_all = side_all[:, nq : nq + mrows].reshape(devices * span, order)
    ids_all = side_all[:, nq + mrows, :nq].reshape(devices * nq)
    members = (ids_all[:, None] == jnp.arange(NVAL, dtype=jnp.float32)[None, :]).astype(jnp.float32)

    units = gate_weight.shape[1]
    short = -units % LANES
    if short:
        gate_weight = jnp.pad(gate_weight, ((0, 0), (0, short)))
        up_weight = jnp.pad(up_weight, ((0, 0), (0, short)))
        in_factor = jnp.pad(in_factor, ((0, short), (0, 0)))
    packed = pack_weights(gate_weight, up_weight)
    gain = norm_gain[None, :]

    going_f, going_b = layer_inputs[:half], layer_inputs[half:]
    left = jnp.zeros((devices * span, order), jnp.float32)
    for step in range(chips):
        own = (going_f, going_b)
        if step < chips - 1:
            going_f = lax.ppermute(own[0], "examples", forward)
            going_b = lax.ppermute(own[1], "examples", backward)
        swapped = tuple(lax.ppermute(x, "examples", other_core) for x in own)
        left = chunk(own + swapped, gain, packed, in_factor, left, step)

    example = jnp.arange(devices, dtype=jnp.int32)
    origin = jnp.array(place_of, jnp.int32)[example // 2]
    foreign = (example % 2 != core).astype(jnp.int32)
    at_f = ((place - origin) % chips) * 4 + foreign * 2
    at_b = ((origin - place) % chips) * 4 + foreign * 2 + 1

    sketch = sketch_all(left, masked_all, at_f, at_b)
    sketch = sketch.astype(jnp.bfloat16).reshape(devices, order * order)
    scores = jnp.dot(sketch, queries_all.T, preferred_element_type=jnp.float32)
    partial = jnp.dot(scores, members, precision=lax.Precision.HIGHEST)
    shares = lax.all_to_all(partial, "examples", split_axis=0, concat_axis=0, tiled=True)
    return jnp.sum(shares, axis=0, keepdims=True)


def solution(mesh):
    return jax.shard_map(
        functools.partial(local, mesh.shape["examples"]),
        mesh=mesh,
        in_specs=(
            P(("groups", "examples"), None),
            P(("groups", "examples")),
            P(),
            P(None, "examples"),
            P(None, "examples"),
            P("examples", None),
            P(),
            P(("groups", "examples"), None),
            P("examples", None),
            P("examples"),
        ),
        out_specs=P(("groups", "examples"), None),
        check_vma=False,
    )
```

time: 311 us -> 205 us (0.66)
  waiting for transfers between devices: 214 us -> 45.4 us
  Pallas kernels: 0 us -> 73.5 us
  matrix products: 63 us -> 3.99 us
  local copies, waits for them, and re-layouts: 6.22 us -> 28.9 us
  starting transfers between devices: 0.09 us -> 22.6 us
    all_gather x2 -> x1, waiting for transfers between devices: 171 us -> 0.02 us  [local(): side_all = lax.all_gather(side, 'examples', axis=0)]
    pallas_call x0 -> x10, Pallas kernels: none -> 73.5 us  [the longest x8 64 us: chunk(): pl.pallas_call(functools.partial(chunk_body, pieces), grid=(tiles,), in_s...]
    dot_general x7 -> x2, matrix products: 62.5 us -> 2.47 us  [the longest x1 2.24 us: local(): scores = jnp.dot(sketch, queries_all.T, preferred_element_type=jnp.float32)]
    ppermute x0 -> x30, waiting for transfers between devices: none -> 45.4 us  [the longest x7 41.9 us: local(): going_f = lax.ppermute(own[0], 'examples', forward)]
    reduce_scatter x1 -> x0, waiting for transfers between devices: 41.5 us -> none  [local(): lax.psum_scatter(projected(normed_all, gate_weight, up_weight, in_factor)...]
    ppermute x0 -> x30, starting transfers between devices: none -> 22.6 us  [the longest x7 18.3 us: local(): going_f = lax.ppermute(own[0], 'examples', forward)]
    unnamed x14 -> x35, local copies, waits for them, and re-layouts: 1.82 us -> 21.2 us
    all_to_all x0 -> x1, blocking collectives: none -> 11.5 us  [local(): lax.all_to_all(partial, 'examples', split_axis=0, concat_axis=0, tiled=True)]
  transfers between devices with their start and end apart: 3 -> 31, of which waited for: 3 -> 5; matrix products, arithmetic and copies ran while one was open for 1% -> 1% of each run, Pallas kernels for 0% -> 34%
where the time goes in v1:
time: 205 us; the launch traced here: 204 us
  Pallas kernels  73.5 us (36%)
  waiting for transfers between devices  45.4 us (22%)
  local copies, waits for them, and re-layouts  28.9 us (14%)
  starting transfers between devices  22.6 us (11%)
  between operations  14.6 us (7%)
  blocking collectives  11.5 us (6%)
  matrix products  3.99 us (2%)
  other arithmetic  3.69 us (2%)
    pallas_call x8, Pallas kernels, chunk(): pl.pallas_call(functools.partial(chunk_body, pieces), grid=(tiles,), in_s...  64 us
    ppermute x7, waiting for transfers between devices, local(): going_f = lax.ppermute(own[0], 'examples', forward)  41.9 us
    unnamed x35, local copies, waits for them, and re-layouts  21.2 us
    ppermute x7, starting transfers between devices, local(): going_f = lax.ppermute(own[0], 'examples', forward)  18.3 us
    all_to_all x1, blocking collectives, local(): lax.all_to_all(partial, 'examples', split_axis=0, concat_axis=0, tiled=True)  11.5 us
    pallas_call x1, Pallas kernels, pack_weights(): pl.pallas_call(pack_body, grid=(tiles,), in_specs=[pl.BlockSpec((depth, L...  5.17 us
    pallas_call x1, Pallas kernels, sketch_all(): pl.pallas_call(sketch_body, grid_spec=pltpu.PrefetchScalarGridSpec(num_sc...  4.27 us
  transfers between devices with their start and end apart: 31, of which 5 were waited for; matrix products, arithmetic and copies ran while one was open for 1% of the time, Pallas kernels for 34%

profile of v1, /device:TPU:0, one launch (start us, length us, event | category | flops | bytes accessed | tf_op | source)
XLA Modules:
  0.0 204.1 jit_solution(5704396160518030384)
XLA Ops:
  12.3 3.1 %collective-permute-start = (bf16[64,4096]{1,0:T(8,128)(2,1)S(1)}, bf16[64,4096]{1,0:T(8,128)(2,1)S(1)}, u32[]{:S(2)}, u32[]{:S(2)}) collective-permute-start(bf16[64,4096]{1,0:T(8,128)(2,1)S(1)} %get-tuple-element.6.refs_0_), channel_id=1, source_target_pairs={{0,4},{1,5},{4,8},{5,9},{8,12},{9,13},{12,14},{13,15},{14,10},{15,... | collective-permute-start | bytes 1572872 | tf_op jit(solution)/shard_map/ppermute | solution.py:191
  15.4 14.5 %collective-permute-done.refs_0_ = bf16[64,4096]{1,0:T(8,128)(2,1)S(1)} collective-permute-done((bf16[64,4096]{1,0:T(8,128)(2,1)S(1)}, bf16[64,4096]{1,0:T(8,128)(2,1)S(1)}, u32[]{:S(2)}, u32[]{:S(2)}) %collective-permute-start) | collective-permute-done | bytes 524320 | tf_op jit(solution)/shard_map/ppermute | solution.py:191
  29.9 2.5 %collective-permute-start.1 = (bf16[64,4096]{1,0:T(8,128)(2,1)S(1)}, bf16[64,4096]{1,0:T(8,128)(2,1)S(1)}, u32[]{:S(2)}, u32[]{:S(2)}) collective-permute-start(bf16[64,4096]{1,0:T(8,128)(2,1)S(1)} %collective-permute-done.refs_0_), channel_id=1, source_target_pairs={{0,4},{1,5},{4,8},{5,9},{8,12},{9,13},{12,14},{13,15},{14,10},{15,... | collective-permute-start | bytes 1572872 | tf_op jit(solution)/shard_map/ppermute | solution.py:191
  32.7 14.0 %collective-permute-done.1.refs_0_ = bf16[64,4096]{1,0:T(8,128)(2,1)S(1)} collective-permute-done((bf16[64,4096]{1,0:T(8,128)(2,1)S(1)}, bf16[64,4096]{1,0:T(8,128)(2,1)S(1)}, u32[]{:S(2)}, u32[]{:S(2)}) %collective-permute-start.1) | collective-permute-done | bytes 524320 | tf_op jit(solution)/shard_map/ppermute | solution.py:191
  46.7 4.1 %collective-permute-start.2 = (bf16[64,4096]{1,0:T(8,128)(2,1)S(1)}, bf16[64,4096]{1,0:T(8,128)(2,1)}, u32[]{:S(2)}, u32[]{:S(2)}) collective-permute-start(bf16[64,4096]{1,0:T(8,128)(2,1)S(1)} %collective-permute-done.1.refs_0_), channel_id=1, source_target_pairs={{0,4},{1,5},{4,8},{5,9},{8,12},{9,13},{12,14},{13,15},{14,10},{15,... | collective-permute-start | bytes 1572872 | tf_op jit(solution)/shard_map/ppermute | solution.py:191
  50.8 3.2 %collective-permute-done.8.refs_1_ = bf16[64,4096]{1,0:T(8,128)(2,1)} collective-permute-done((bf16[64,4096]{1,0:T(8,128)(2,1)}, bf16[64,4096]{1,0:T(8,128)(2,1)}, u32[]{:S(2)}, u32[]{:S(2)}) %collective-permute-start.8) | collective-permute-done | bytes 524320 | tf_op jit(solution)/shard_map/ppermute | solution.py:192
  54.5 13.5 %collective-permute-done.2.refs_0_ = bf16[64,4096]{1,0:T(8,128)(2,1)} collective-permute-done((bf16[64,4096]{1,0:T(8,128)(2,1)S(1)}, bf16[64,4096]{1,0:T(8,128)(2,1)}, u32[]{:S(2)}, u32[]{:S(2)}) %collective-permute-start.2) | collective-permute-done | bytes 524320 | tf_op jit(solution)/shard_map/ppermute | solution.py:191
  68.0 2.6 %collective-permute-start.3 = (bf16[64,4096]{1,0:T(8,128)(2,1)}, bf16[64,4096]{1,0:T(8,128)(2,1)}, u32[]{:S(2)}, u32[]{:S(2)}) collective-permute-start(bf16[64,4096]{1,0:T(8,128)(2,1)} %collective-permute-done.2.refs_0_), channel_id=1, source_target_pairs={{0,4},{1,5},{4,8},{5,9},{8,12},{9,13},{12,14},{13,15},{14,10},{15,... | collective-permute-start | bytes 1572872 | tf_op jit(solution)/shard_map/ppermute | solution.py:191
  74.5 3.1 %copy-done.3 = bf16[4096,896]{1,0:T(8,128)(2,1)S(1)} copy-done((bf16[4096,896]{1,0:T(8,128)(2,1)S(1)}, bf16[4096,896]{1,0:T(8,128)(2,1)}, u32[]{:S(2)}) %copy-start.3) | copy-done | bytes 7340056
  77.6 3.1 %copy-done.4 = bf16[4096,896]{1,0:T(8,128)(2,1)S(1)} copy-done((bf16[4096,896]{1,0:T(8,128)(2,1)S(1)}, bf16[4096,896]{1,0:T(8,128)(2,1)}, u32[]{:S(2)}) %copy-start.4) | copy-done | bytes 7340056
  80.7 5.2 %pack_weights.1.refs_5_ = bf16[7,4096,256]{2,1,0:T(8,128)(2,1)S(1)} custom-call(bf16[4096,896]{1,0:T(8,128)(2,1)S(1)} %copy-done.3, bf16[4096,896]{1,0:T(8,128)(2,1)S(1)} %copy-done.4), custom_call_target="tpu_custom_call" | custom-call | bytes 29360128 | tf_op jit(solution)/shard_map/pack_weights/pallas_call | solution.py:29
  85.9 5.2 %copy-done.1 = bf16[7,4096,256]{2,1,0:T(8,128)(2,1)} copy-done((bf16[7,4096,256]{2,1,0:T(8,128)(2,1)}, bf16[7,4096,256]{2,1,0:T(8,128)(2,1)S(1)}, u32[]{:S(2)}) %copy-start.1) | copy-done | bytes 14680088
  94.5 5.2 %copy-done.2 = bf16[7,4096,256]{2,1,0:T(8,128)(2,1)S(1)} copy-done((bf16[7,4096,256]{2,1,0:T(8,128)(2,1)S(1)}, bf16[7,4096,256]{2,1,0:T(8,128)(2,1)}, u32[]{:S(2)}) %copy-start.2) | copy-done | bytes 14680088
  101.8 7.4 %chunk.8.refs_7_ = f32[2048,64]{1,0:T(8,128)S(1)} custom-call(bf16[64,4096]{1,0:T(8,128)(2,1)S(1)} %get-tuple-element.6.refs_0_, bf16[64,4096]{1,0:T(8,128)(2,1)S(1)} %get-tuple-element.5.refs_1_, bf16[64,4096]{1,0:T(8,128)(2,1)S(1)} %copy-done.11, bf16[64,4096]{1,0:T(8,128)(2,1)S(1)} %copy-done.13, ...), custom_call_target="tpu_custom_call", output_to_operand_aliasing={{}: (7, {})} | custom-call | flops 3758096384 | bytes 14680064 | tf_op jit(solution)/shard_map/chunk/pallas_call | solution.py:74
  111.4 8.8 %chunk.9.refs_7_ = f32[2048,64]{1,0:T(8,128)S(1)} custom-call(bf16[64,4096]{1,0:T(8,128)(2,1)S(1)} %copy-done.9, bf16[64,4096]{1,0:T(8,128)(2,1)} %collective-permute-done.7.refs_1_, bf16[64,4096]{1,0:T(8,128)(2,1)} %collective-permute-done.26.refs_2_, bf16[64,4096]{1,0:T(8,128)(2,1)} %collective-permute-done.27.refs_3_, ...), custom_call_target="tpu_custom_call", output_to_operand_aliasing={{}: (7, {})} | custom-call | flops 3758096384 | bytes 14680064 | tf_op jit(solution)/shard_map/chunk/pallas_call | solution.py:74
  120.8 8.6 %chunk.10.refs_7_ = f32[2048,64]{1,0:T(8,128)S(1)} custom-call(bf16[64,4096]{1,0:T(8,128)(2,1)S(1)} %copy-done.7, bf16[64,4096]{1,0:T(8,128)(2,1)} %collective-permute-done.8.refs_1_, bf16[64,4096]{1,0:T(8,128)(2,1)} %collective-permute-done.24.refs_2_, bf16[64,4096]{1,0:T(8,128)(2,1)S(1)} %collective-permute-done.25.refs_3_, ...), custom_call_target="tpu_custom_call", output_to_operand_aliasing={{}: (7, {})} | custom-call | flops 3758096384 | bytes 14680064 | tf_op jit(solution)/shard_map/chunk/pallas_call | solution.py:74
  131.6 8.6 %chunk.11.refs_7_ = f32[2048,64]{1,0:T(8,128)S(1)} custom-call(bf16[64,4096]{1,0:T(8,128)(2,1)} %collective-permute-done.2.refs_0_, bf16[64,4096]{1,0:T(8,128)(2,1)} %collective-permute-done.9.refs_1_, bf16[64,4096]{1,0:T(8,128)(2,1)S(1)} %collective-permute-done.22.refs_2_, ...), custom_call_target="tpu_custom_call", output_to_operand_aliasing={{}: (7, {})} | custom-call | flops 3758096384 | bytes 14680064 | tf_op jit(solution)/shard_map/chunk/pallas_call | solution.py:74
  140.8 8.6 %chunk.12.refs_7_ = f32[2048,64]{1,0:T(8,128)S(1)} custom-call(bf16[64,4096]{1,0:T(8,128)(2,1)} %collective-permute-done.3.refs_0_, bf16[64,4096]{1,0:T(8,128)(2,1)} %collective-permute-done.10.refs_1_, bf16[64,4096]{1,0:T(8,128)(2,1)S(1)} %collective-permute-done.20.refs_2_, ...), custom_call_target="tpu_custom_call", output_to_operand_aliasing={{}: (7, {})} | custom-call | flops 3758096384 | bytes 14680064 | tf_op jit(solution)/shard_map/chunk/pallas_call | solution.py:74
  150.0 7.4 %chunk.13.refs_7_ = f32[2048,64]{1,0:T(8,128)S(1)} custom-call(bf16[64,4096]{1,0:T(8,128)(2,1)S(1)} %collective-permute-done.4.refs_0_, bf16[64,4096]{1,0:T(8,128)(2,1)S(1)} %collective-permute-done.11.refs_1_, bf16[64,4096]{1,0:T(8,128)(2,1)S(1)} %collective-permute-done.18.refs_2_, ...), custom_call_target="tpu_custom_call", output_to_operand_aliasing={{}: (7, {})} | custom-call | flops 3758096384 | bytes 14680064 | tf_op jit(solution)/shard_map/chunk/pallas_call | solution.py:74
  157.4 7.4 %chunk.14.refs_7_ = f32[2048,64]{1,0:T(8,128)S(1)} custom-call(bf16[64,4096]{1,0:T(8,128)(2,1)S(1)} %collective-permute-done.5.refs_0_, bf16[64,4096]{1,0:T(8,128)(2,1)S(1)} %collective-permute-done.12.refs_1_, bf16[64,4096]{1,0:T(8,128)(2,1)S(1)} %collective-permute-done.16.refs_2_, ...), custom_call_target="tpu_custom_call", output_to_operand_aliasing={{}: (7, {})} | custom-call | flops 3758096384 | bytes 14680064 | tf_op jit(solution)/shard_map/chunk/pallas_call | solution.py:74
  164.8 7.4 %chunk.15.left_ref = f32[2048,64]{1,0:T(8,128)S(1)} custom-call(bf16[64,4096]{1,0:T(8,128)(2,1)S(1)} %collective-permute-done.6.refs_0_, bf16[64,4096]{1,0:T(8,128)(2,1)S(1)} %collective-permute-done.13.refs_1_, bf16[64,4096]{1,0:T(8,128)(2,1)S(1)} %collective-permute-done.14.refs_2_, ...), custom_call_target="tpu_custom_call", output_to_operand_aliasing={{}: (7, {})} | custom-call | flops 3758096384 | bytes 14680064 | tf_op jit(solution)/shard_map/chunk/pallas_call | solution.py:74
  173.7 3.2 %slice.23 = bf16[16,16,4096]{2,1,0:T(8,128)(2,1)} slice(bf16[16,24,4096]{2,1,0:T(8,128)(2,1)} %bitcast.28), slice={[0:16], [0:16], [0:4096]} | slice | bytes 4194304 | tf_op jit(solution)/shard_map/slice | solution.py:172
  178.0 4.3 %sketch.1 = f32[16,64,64]{2,1,0:T(8,128)S(1)} custom-call(s32[16]{0:T(128)S(1)} %get-tuple-element.8.at_f, s32[16]{0:T(128)S(1)} %get-tuple-element.7.at_b, f32[2048,64]{1,0:T(8,128)S(1)} %chunk.15.left_ref, bf16[2048,64]{1,0:T(8,128)(2,1)S(1)} %reshape.72.masked_ref), custom_call_target="tpu_custom_call" | custom-call | tf_op jit(solution)/shard_map/sketch/pallas_call | solution.py:118
  185.2 11.5 %all_to_all.9 = f32[16,1,256]{2,1,0:T(1,128)S(1)} all-to-all(f32[16,1,256]{2,1,0:T(1,128)S(1)} %copy.58), channel_id=1, replica_groups=mesh['groups'=2,'examples'=16] {'examples'}, dimensions={0} | all-to-all | bytes 32768 | tf_op jit(solution)/shard_map/all_to_all | solution.py:206
  (110 shorter events, 27.4 us)
Async XLA Ops:
  6.5 165.7 %all-gather.3.cloned.1.call-start = ((), (), s32[]{:S(2)}) async-start(), calls=%async_computation.1 | async-start | bytes 3342336 | tf_op jit(solution)/shard_map/all_gather | solution.py:171
  12.3 17.5 %collective-permute-start = (bf16[64,4096]{1,0:T(8,128)(2,1)S(1)}, bf16[64,4096]{1,0:T(8,128)(2,1)S(1)}, u32[]{:S(2)}, u32[]{:S(2)}) collective-permute-start(bf16[64,4096]{1,0:T(8,128)(2,1)S(1)} %get-tuple-element.6.refs_0_), channel_id=1, source_target_pairs={{0,4},{1,5},{4,8},{5,9},{8,12},{9,13},{12,14},{13,15},{14,10},{15,... | collective-permute-start | bytes 1572872 | tf_op jit(solution)/shard_map/ppermute | solution.py:191
  32.3 21.7 %collective-permute-start.8 = (bf16[64,4096]{1,0:T(8,128)(2,1)}, bf16[64,4096]{1,0:T(8,128)(2,1)}, u32[]{:S(2)}, u32[]{:S(2)}) collective-permute-start(bf16[64,4096]{1,0:T(8,128)(2,1)} %collective-permute-done.7.refs_1_), channel_id=1, source_target_pairs={{4,0},{5,1},{8,4},{9,5},{12,8},{13,9},{14,12},{15,13},{10,14},{11,... | collective-permute-start | bytes 1572872 | tf_op jit(solution)/shard_map/ppermute | solution.py:192
  46.7 21.3 %collective-permute-start.2 = (bf16[64,4096]{1,0:T(8,128)(2,1)S(1)}, bf16[64,4096]{1,0:T(8,128)(2,1)}, u32[]{:S(2)}, u32[]{:S(2)}) collective-permute-start(bf16[64,4096]{1,0:T(8,128)(2,1)S(1)} %collective-permute-done.1.refs_0_), channel_id=1, source_target_pairs={{0,4},{1,5},{4,8},{5,9},{8,12},{9,13},{12,14},{13,15},{14,10},{15,... | collective-permute-start | bytes 1572872 | tf_op jit(solution)/shard_map/ppermute | solution.py:191
  54.0 17.7 %collective-permute-start.29 = (bf16[64,4096]{1,0:T(8,128)(2,1)S(1)}, bf16[64,4096]{1,0:T(8,128)(2,1)S(1)}, u32[]{:S(2)}, u32[]{:S(2)}) collective-permute-start(bf16[64,4096]{1,0:T(8,128)(2,1)S(1)} %get-tuple-element.5.refs_1_), channel_id=1, source_target_pairs={{0,1},{1,0},{2,3},{3,2},{4,5},{5,4},{6,7},{7,6},{8,9},{9,8},{10,11... | collective-permute-start | bytes 1572872 | tf_op jit(solution)/shard_map/ppermute | solution.py:193
  54.5 36.5 %collective-permute-start.26 = (bf16[64,4096]{1,0:T(8,128)(2,1)S(1)}, bf16[64,4096]{1,0:T(8,128)(2,1)}, u32[]{:S(2)}, u32[]{:S(2)}) collective-permute-start(bf16[64,4096]{1,0:T(8,128)(2,1)S(1)} %collective-permute-done.refs_0_), channel_id=1, source_target_pairs={{0,1},{1,0},{2,3},{3,2},{4,5},{5,4},{6,7},{7,6},{8,9},{9,8},{10,11... | collective-permute-start | bytes 1572872 | tf_op jit(solution)/shard_map/ppermute | solution.py:193
  68.0 23.1 %collective-permute-start.3 = (bf16[64,4096]{1,0:T(8,128)(2,1)}, bf16[64,4096]{1,0:T(8,128)(2,1)}, u32[]{:S(2)}, u32[]{:S(2)}) collective-permute-start(bf16[64,4096]{1,0:T(8,128)(2,1)} %collective-permute-done.2.refs_0_), channel_id=1, source_target_pairs={{0,4},{1,5},{4,8},{5,9},{8,12},{9,13},{12,14},{13,15},{14,10},{15,... | collective-permute-start | bytes 1572872 | tf_op jit(solution)/shard_map/ppermute | solution.py:191
  70.9 22.3 %collective-permute-start.10 = (bf16[64,4096]{1,0:T(8,128)(2,1)}, bf16[64,4096]{1,0:T(8,128)(2,1)}, u32[]{:S(2)}, u32[]{:S(2)}) collective-permute-start(bf16[64,4096]{1,0:T(8,128)(2,1)} %collective-permute-done.9.refs_1_), channel_id=1, source_target_pairs={{4,0},{5,1},{8,4},{9,5},{12,8},{13,9},{14,12},{15,13},{10,14},{11,... | collective-permute-start | bytes 1572872 | tf_op jit(solution)/shard_map/ppermute | solution.py:192
  71.7 22.1 %collective-permute-start.27 = (bf16[64,4096]{1,0:T(8,128)(2,1)}, bf16[64,4096]{1,0:T(8,128)(2,1)}, u32[]{:S(2)}, u32[]{:S(2)}) collective-permute-start(bf16[64,4096]{1,0:T(8,128)(2,1)} %collective-permute-done.7.refs_1_), channel_id=1, source_target_pairs={{0,1},{1,0},{2,3},{3,2},{4,5},{5,4},{6,7},{7,6},{8,9},{9,8},{10,11... | collective-permute-start | bytes 1572872 | tf_op jit(solution)/shard_map/ppermute | solution.py:193
  72.5 21.6 %collective-permute-start.24 = (bf16[64,4096]{1,0:T(8,128)(2,1)S(1)}, bf16[64,4096]{1,0:T(8,128)(2,1)}, u32[]{:S(2)}, u32[]{:S(2)}) collective-permute-start(bf16[64,4096]{1,0:T(8,128)(2,1)S(1)} %collective-permute-done.1.refs_0_), channel_id=1, source_target_pairs={{0,1},{1,0},{2,3},{3,2},{4,5},{5,4},{6,7},{7,6},{8,9},{9,8},{10,11... | collective-permute-start | bytes 1572872 | tf_op jit(solution)/shard_map/ppermute | solution.py:193
  91.1 18.1 %collective-permute-start.25 = (bf16[64,4096]{1,0:T(8,128)(2,1)}, bf16[64,4096]{1,0:T(8,128)(2,1)S(1)}, u32[]{:S(2)}, u32[]{:S(2)}) collective-permute-start(bf16[64,4096]{1,0:T(8,128)(2,1)} %collective-permute-done.8.refs_1_), channel_id=1, source_target_pairs={{0,1},{1,0},{2,3},{3,2},{4,5},{5,4},{6,7},{7,6},{8,9},{9,8},{10,11... | collective-permute-start | bytes 1572872 | tf_op jit(solution)/shard_map/ppermute | solution.py:193
  91.1 18.3 %collective-permute-start.4 = (bf16[64,4096]{1,0:T(8,128)(2,1)}, bf16[64,4096]{1,0:T(8,128)(2,1)S(1)}, u32[]{:S(2)}, u32[]{:S(2)}) collective-permute-start(bf16[64,4096]{1,0:T(8,128)(2,1)} %collective-permute-done.3.refs_0_), channel_id=1, source_target_pairs={{0,4},{1,5},{4,8},{5,9},{8,12},{9,13},{12,14},{13,15},{14,10},{15,... | collective-permute-start | bytes 1572872 | tf_op jit(solution)/shard_map/ppermute | solution.py:191
  93.2 18.2 %collective-permute-start.11 = (bf16[64,4096]{1,0:T(8,128)(2,1)}, bf16[64,4096]{1,0:T(8,128)(2,1)S(1)}, u32[]{:S(2)}, u32[]{:S(2)}) collective-permute-start(bf16[64,4096]{1,0:T(8,128)(2,1)} %collective-permute-done.10.refs_1_), channel_id=1, source_target_pairs={{4,0},{5,1},{8,4},{9,5},{12,8},{13,9},{14,12},{15,13},{10,14},{11,... | collective-permute-start | bytes 1572872 | tf_op jit(solution)/shard_map/ppermute | solution.py:192
  93.8 26.4 %collective-permute-start.22 = (bf16[64,4096]{1,0:T(8,128)(2,1)}, bf16[64,4096]{1,0:T(8,128)(2,1)S(1)}, u32[]{:S(2)}, u32[]{:S(2)}) collective-permute-start(bf16[64,4096]{1,0:T(8,128)(2,1)} %collective-permute-done.2.refs_0_), channel_id=1, source_target_pairs={{0,1},{1,0},{2,3},{3,2},{4,5},{5,4},{6,7},{7,6},{8,9},{9,8},{10,11... | collective-permute-start | bytes 1572872 | tf_op jit(solution)/shard_map/ppermute | solution.py:193
  94.1 26.3 %collective-permute-start.23 = (bf16[64,4096]{1,0:T(8,128)(2,1)}, bf16[64,4096]{1,0:T(8,128)(2,1)S(1)}, u32[]{:S(2)}, u32[]{:S(2)}) collective-permute-start(bf16[64,4096]{1,0:T(8,128)(2,1)} %collective-permute-done.9.refs_1_), channel_id=1, source_target_pairs={{0,1},{1,0},{2,3},{3,2},{4,5},{5,4},{6,7},{7,6},{8,9},{9,8},{10,11... | collective-permute-start | bytes 1572872 | tf_op jit(solution)/shard_map/ppermute | solution.py:193
  109.2 20.2 %collective-permute-start.20 = (bf16[64,4096]{1,0:T(8,128)(2,1)}, bf16[64,4096]{1,0:T(8,128)(2,1)S(1)}, u32[]{:S(2)}, u32[]{:S(2)}) collective-permute-start(bf16[64,4096]{1,0:T(8,128)(2,1)} %collective-permute-done.3.refs_0_), channel_id=1, source_target_pairs={{0,1},{1,0},{2,3},{3,2},{4,5},{5,4},{6,7},{7,6},{8,9},{9,8},{10,11... | collective-permute-start | bytes 1572872 | tf_op jit(solution)/shard_map/ppermute | solution.py:193
  109.4 20.2 %collective-permute-start.5 = (bf16[64,4096]{1,0:T(8,128)(2,1)S(1)}, bf16[64,4096]{1,0:T(8,128)(2,1)S(1)}, u32[]{:S(2)}, u32[]{:S(2)}) collective-permute-start(bf16[64,4096]{1,0:T(8,128)(2,1)S(1)} %collective-permute-done.4.refs_0_), channel_id=1, source_target_pairs={{0,4},{1,5},{4,8},{5,9},{8,12},{9,13},{12,14},{13,15},{14,10},{15,... | collective-permute-start | bytes 1572872 | tf_op jit(solution)/shard_map/ppermute | solution.py:191
  111.3 20.2 %collective-permute-start.12 = (bf16[64,4096]{1,0:T(8,128)(2,1)S(1)}, bf16[64,4096]{1,0:T(8,128)(2,1)S(1)}, u32[]{:S(2)}, u32[]{:S(2)}) collective-permute-start(bf16[64,4096]{1,0:T(8,128)(2,1)S(1)} %collective-permute-done.11.refs_1_), channel_id=1, source_target_pairs={{4,0},{5,1},{8,4},{9,5},{12,8},{13,9},{14,12},{15,13},{10,14},{11,... | collective-permute-start | bytes 1572872 | tf_op jit(solution)/shard_map/ppermute | solution.py:192
  120.2 20.0 %collective-permute-start.21 = (bf16[64,4096]{1,0:T(8,128)(2,1)}, bf16[64,4096]{1,0:T(8,128)(2,1)S(1)}, u32[]{:S(2)}, u32[]{:S(2)}) collective-permute-start(bf16[64,4096]{1,0:T(8,128)(2,1)} %collective-permute-done.10.refs_1_), channel_id=1, source_target_pairs={{0,1},{1,0},{2,3},{3,2},{4,5},{5,4},{6,7},{7,6},{8,9},{9,8},{10,11... | collective-permute-start | bytes 1572872 | tf_op jit(solution)/shard_map/ppermute | solution.py:193
  120.4 20.0 %collective-permute-start.18 = (bf16[64,4096]{1,0:T(8,128)(2,1)S(1)}, bf16[64,4096]{1,0:T(8,128)(2,1)S(1)}, u32[]{:S(2)}, u32[]{:S(2)}) collective-permute-start(bf16[64,4096]{1,0:T(8,128)(2,1)S(1)} %collective-permute-done.4.refs_0_), channel_id=1, source_target_pairs={{0,1},{1,0},{2,3},{3,2},{4,5},{5,4},{6,7},{7,6},{8,9},{9,8},{10,11... | collective-permute-start | bytes 1572872 | tf_op jit(solution)/shard_map/ppermute | solution.py:193
  129.4 20.6 %collective-permute-start.19 = (bf16[64,4096]{1,0:T(8,128)(2,1)S(1)}, bf16[64,4096]{1,0:T(8,128)(2,1)S(1)}, u32[]{:S(2)}, u32[]{:S(2)}) collective-permute-start(bf16[64,4096]{1,0:T(8,128)(2,1)S(1)} %collective-permute-done.11.refs_1_), channel_id=1, source_target_pairs={{0,1},{1,0},{2,3},{3,2},{4,5},{5,4},{6,7},{7,6},{8,9},{9,8},{10,11... | collective-permute-start | bytes 1572872 | tf_op jit(solution)/shard_map/ppermute | solution.py:193
  129.6 19.8 %collective-permute-start.6 = (bf16[64,4096]{1,0:T(8,128)(2,1)S(1)}, bf16[64,4096]{1,0:T(8,128)(2,1)S(1)}, u32[]{:S(2)}, u32[]{:S(2)}) collective-permute-start(bf16[64,4096]{1,0:T(8,128)(2,1)S(1)} %collective-permute-done.5.refs_0_), channel_id=1, source_target_pairs={{0,4},{1,5},{4,8},{5,9},{8,12},{9,13},{12,14},{13,15},{14,10},{15,... | collective-permute-start | bytes 1572872 | tf_op jit(solution)/shard_map/ppermute | solution.py:191
  131.5 18.1 %collective-permute-start.13 = (bf16[64,4096]{1,0:T(8,128)(2,1)S(1)}, bf16[64,4096]{1,0:T(8,128)(2,1)S(1)}, u32[]{:S(2)}, u32[]{:S(2)}) collective-permute-start(bf16[64,4096]{1,0:T(8,128)(2,1)S(1)} %collective-permute-done.12.refs_1_), channel_id=1, source_target_pairs={{4,0},{5,1},{8,4},{9,5},{12,8},{13,9},{14,12},{15,13},{10,14},{11,... | collective-permute-start | bytes 1572872 | tf_op jit(solution)/shard_map/ppermute | solution.py:192
  140.2 17.1 %collective-permute-start.16 = (bf16[64,4096]{1,0:T(8,128)(2,1)S(1)}, bf16[64,4096]{1,0:T(8,128)(2,1)S(1)}, u32[]{:S(2)}, u32[]{:S(2)}) collective-permute-start(bf16[64,4096]{1,0:T(8,128)(2,1)S(1)} %collective-permute-done.5.refs_0_), channel_id=1, source_target_pairs={{0,1},{1,0},{2,3},{3,2},{4,5},{5,4},{6,7},{7,6},{8,9},{9,8},{10,11... | collective-permute-start | bytes 1572872 | tf_op jit(solution)/shard_map/ppermute | solution.py:193
  (24 other events, 406.1 us)
Sparse Core Ops, SparseCore 0:
  12.3 55.6 all-gather.2

commit v2 on v1

--- a/solution.py
+++ b/solution.py
@@ -18,39 +18,16 @@
     return list(range(chips))
 
 
-def pack_body(gate_ref, up_ref, out_ref):
-    out_ref[0, :, :LANES] = gate_ref[...]
-    out_ref[0, :, LANES:] = up_ref[...]
-
-
-def pack_weights(gate_weight, up_weight):
-    depth, units = gate_weight.shape
-    tiles = units // LANES
-    return pl.pallas_call(
-        pack_body,
-        grid=(tiles,),
-        in_specs=[pl.BlockSpec((depth, LANES), lambda i: (0, i))] * 2,
-        out_specs=pl.BlockSpec((1, depth, 2 * LANES), lambda i: (i, 0, 0)),
-        out_shape=jax.ShapeDtypeStruct((tiles, depth, 2 * LANES), gate_weight.dtype),
-        compiler_params=pltpu.CompilerParams(vmem_limit_bytes=24 * MIB),
-        cost_estimate=pl.CostEstimate(flops=0, bytes_accessed=8 * depth * units, transcendentals=0),
-        name="pack_weights",
-    )(gate_weight, up_weight)
-
-
-def chunk_body(pieces, *refs):
-    x_refs = refs[:pieces]
-    gain_ref, w_ref, f_ref, _, out_ref, xn = refs[pieces:]
+def norm_rows(x_refs, gain_ref, xn):
     rows = x_refs[0].shape[0]
+    for k, ref in enumerate(x_refs):
+        x = ref[...].astype(jnp.float32)
+        scale = lax.rsqrt(jnp.mean(x * x, axis=-1, keepdims=True) + 1e-05)
+        xn[k * rows : (k + 1) * rows, :] = (x * scale * gain_ref[...]).astype(jnp.bfloat16)
+
+
+def project_tile(xn, w_ref, f_ref, out_ref):
     step = pl.program_id(0)
-
-    @pl.when(step == 0)
-    def _():
-        for k, ref in enumerate(x_refs):
-            x = ref[...].astype(jnp.float32)
-            scale = lax.rsqrt(jnp.mean(x * x, axis=-1, keepdims=True) + 1e-05)
-            xn[k * rows : (k + 1) * rows, :] = (x * scale * gain_ref[...]).astype(jnp.bfloat16)
-
     both = jnp.dot(xn[...], w_ref[0], preferred_element_type=jnp.float32)
     gate, up = both[:, :LANES], both[:, LANES:]
     hidden = (jax.nn.silu(gate) * up).astype(jnp.bfloat16)
@@ -63,6 +40,65 @@
     @pl.when(step > 0)
     def _():
         out_ref[...] += part
+
+
+def first_body(pieces, *refs):
+    x_refs = refs[:pieces]
+    gain_ref, gate_ref, up_ref, f_ref, out_ref, w_ref, xn = refs[pieces:]
+
+    @pl.when(pl.program_id(0) == 0)
+    def _():
+        norm_rows(x_refs, gain_ref, xn)
+
+    w_ref[0, :, :LANES] = gate_ref[...]
+    w_ref[0, :, LANES:] = up_ref[...]
+    project_tile(xn, w_ref, f_ref, out_ref)
+
+
+def first_chunk(xs, gain, gate_weight, up_weight, in_factor, tokens):
+    pieces = len(xs)
+    rows, depth = xs[0].shape
+    units, order = in_factor.shape
+    tiles = units // LANES
+    total = pieces * rows
+    return pl.pallas_call(
+        functools.partial(first_body, pieces),
+        grid=(tiles,),
+        in_specs=[pl.BlockSpec((rows, depth), lambda i: (0, 0))] * pieces
+        + [
+            pl.BlockSpec((1, depth), lambda i: (0, 0)),
+            pl.BlockSpec((depth, LANES), lambda i: (0, i)),
+            pl.BlockSpec((depth, LANES), lambda i: (0, i)),
+            pl.BlockSpec((LANES, order), lambda i: (i, 0)),
+        ],
+        out_specs=[
+            pl.BlockSpec((total, order), lambda i: (0, 0)),
+            pl.BlockSpec((1, depth, 2 * LANES), lambda i: (i, 0, 0)),
+        ],
+        out_shape=[
+            jax.ShapeDtypeStruct((tokens, order), jnp.float32),
+            jax.ShapeDtypeStruct((tiles, depth, 2 * LANES), gate_weight.dtype),
+        ],
+        scratch_shapes=[pltpu.VMEM((total, depth), jnp.bfloat16)],
+        compiler_params=pltpu.CompilerParams(vmem_limit_bytes=16 * MIB),
+        cost_estimate=pl.CostEstimate(
+            flops=2 * total * depth * tiles * 2 * LANES,
+            bytes_accessed=8 * depth * units,
+            transcendentals=0,
+        ),
+        name="first_chunk",
+    )(*xs, gain, gate_weight, up_weight, in_factor)
+
+
+def chunk_body(pieces, *refs):
+    x_refs = refs[:pieces]
+    gain_ref, w_ref, f_ref, _, out_ref, xn = refs[pieces:]
+
+    @pl.when(pl.program_id(0) == 0)
+    def _():
+        norm_rows(x_refs, gain_ref, xn)
+
+    project_tile(xn, w_ref, f_ref, out_ref)
 
 
 def chunk(xs, gain, packed, in_factor, left, index):
@@ -85,7 +121,7 @@
         out_shape=jax.ShapeDtypeStruct(left.shape, left.dtype),
         scratch_shapes=[pltpu.VMEM((total, depth), jnp.bfloat16)],
         input_output_aliases={pieces + 3: 0},
-        compiler_params=pltpu.CompilerParams(vmem_limit_bytes=32 * MIB),
+        compiler_params=pltpu.CompilerParams(vmem_limit_bytes=16 * MIB),
         cost_estimate=pl.CostEstimate(
             flops=2 * total * depth * tiles * 2 * LANES,
             bytes_accessed=2 * tiles * depth * 2 * LANES,
@@ -101,12 +137,12 @@
     first = left_ref[pl.ds(pl.multiple_of(at_f[e] * half, half), half), :]
     second = left_ref[pl.ds(pl.multiple_of(at_b[e] * half, half), half), :]
     left = jnp.concatenate([first, second], axis=0)
-    sketch = lax.dot_general(
-        left,
-        masked_ref[...].astype(jnp.float32),
-        (((0,), (0,)), ((), ())),
-        precision=lax.Precision.HIGHEST,
-        preferred_element_type=jnp.float32,
+    high = left.astype(jnp.bfloat16)
+    low = (left - high.astype(jnp.float32)).astype(jnp.bfloat16)
+    masked = masked_ref[...]
+    sketch = sum(
+        lax.dot_general(part, masked, (((0,), (0,)), ((), ())), preferred_element_type=jnp.float32)
+        for part in (low, high)
     )
     out_ref[0] = sketch
 
@@ -180,24 +216,35 @@
         gate_weight = jnp.pad(gate_weight, ((0, 0), (0, short)))
         up_weight = jnp.pad(up_weight, ((0, 0), (0, short)))
         in_factor = jnp.pad(in_factor, ((0, short), (0, 0)))
-    packed = pack_weights(gate_weight, up_weight)
     gain = norm_gain[None, :]
 
-    going_f, going_b = layer_inputs[:half], layer_inputs[half:]
-    left = jnp.zeros((devices * span, order), jnp.float32)
-    for step in range(chips):
-        own = (going_f, going_b)
+    def both_ways(pair):
+        return lax.ppermute(pair[0], "examples", forward), lax.ppermute(pair[1], "examples", backward)
+
+    def swap(pair):
+        return tuple(lax.ppermute(x, "examples", other_core) for x in pair)
+
+    own = (layer_inputs[:half], layer_inputs[half:])
+    coming = both_ways(own)
+    swapped = swap(own)
+    left, packed = first_chunk(own, gain, gate_weight, up_weight, in_factor, devices * span)
+    for step in range(1, chips):
+        own_f, own_b, left = lax.optimization_barrier((*coming, left))
+        own = (own_f, own_b)
         if step < chips - 1:
-            going_f = lax.ppermute(own[0], "examples", forward)
-            going_b = lax.ppermute(own[1], "examples", backward)
-        swapped = tuple(lax.ppermute(x, "examples", other_core) for x in own)
-        left = chunk(own + swapped, gain, packed, in_factor, left, step)
+            coming = both_ways(own)
+        before, swapped = swapped, swap(own)
+        left = chunk(own + before, gain, packed, in_factor, left, step)
+    left = chunk(swapped, gain, packed, in_factor, left, 1)
 
     example = jnp.arange(devices, dtype=jnp.int32)
     origin = jnp.array(place_of, jnp.int32)[example // 2]
     foreign = (example % 2 != core).astype(jnp.int32)
-    at_f = ((place - origin) % chips) * 4 + foreign * 2
-    at_b = ((origin - place) % chips) * 4 + foreign * 2 + 1
+    hops_f = (place - origin) % chips
+    hops_b = (origin - place) % chips
+    here = example % 2 == core
+    at_f = jnp.where(here, 4 * hops_f, 4 * ((hops_f + 1) % chips) + 2)
+    at_b = jnp.where(here, 4 * hops_b, 4 * ((hops_b + 1) % chips) + 2) + 1
 
     sketch = sketch_all(left, masked_all, at_f, at_b)
     sketch = sketch.astype(jnp.bfloat16).reshape(devices, order * order)

time: 205 us -> 178 us (0.87)
  waiting for transfers between devices: 45.4 us -> 22.6 us
  Pallas kernels: 73.5 us -> 77.8 us
  local copies, waits for them, and re-layouts: 28.9 us -> 24.7 us
  starting transfers between devices: 22.6 us -> 19.6 us
    ppermute x30, waiting for transfers between devices: 45.4 us -> 22.5 us  [the longest x7 12.9 us: both_ways(): lax.ppermute(pair[0], 'examples', forward)]
    pallas_call x1, Pallas kernels: 5.17 us -> 9.56 us  [first_chunk(): pl.pallas_call(functools.partial(first_body, pieces), grid=(tiles,), in_s...]
    unnamed x35 -> x21, local copies, waits for them, and re-layouts: 21.2 us -> 17.1 us
    ppermute x30, starting transfers between devices: 22.6 us -> 19.5 us  [the longest x7 11.6 us: both_ways(): lax.ppermute(pair[0], 'examples', forward)]
  transfers between devices with their start and end apart: 31 -> 31, of which waited for: 5 -> 8; matrix products, arithmetic and copies ran while one was open for 1% -> 1% of each run, Pallas kernels for 34% -> 42%
where the time goes in v2:
time: 178 us; the launch traced here: 177 us
  Pallas kernels  77.8 us (44%)
  local copies, waits for them, and re-layouts  24.7 us (14%)
  waiting for transfers between devices  22.6 us (13%)
  starting transfers between devices  19.6 us (11%)
  between operations  14.5 us (8%)
  blocking collectives  10.1 us (6%)
  matrix products  4 us (2%)
  other arithmetic  3.71 us (2%)
    pallas_call x8, Pallas kernels, chunk(): pl.pallas_call(functools.partial(chunk_body, pieces), grid=(tiles,), in_s...  64.8 us
    unnamed x21, local copies, waits for them, and re-layouts  17.1 us
    ppermute x7, waiting for transfers between devices, both_ways(): lax.ppermute(pair[0], 'examples', forward)  12.9 us
    ppermute x7, starting transfers between devices, both_ways(): lax.ppermute(pair[0], 'examples', forward)  11.6 us
    all_to_all x1, blocking collectives, local(): lax.all_to_all(partial, 'examples', split_axis=0, concat_axis=0, tiled=True)  10.1 us
    ppermute x7, waiting for transfers between devices, both_ways(): lax.ppermute(pair[1], 'examples', backward)  9.6 us
    pallas_call x1, Pallas kernels, first_chunk(): pl.pallas_call(functools.partial(first_body, pieces), grid=(tiles,), in_s...  9.56 us
    ppermute x16, starting transfers between devices, swap(): return tuple((lax.ppermute(x, 'examples', other_core) for x in pair))  4.2 us
  transfers between devices with their start and end apart: 31, of which 8 were waited for; matrix products, arithmetic and copies ran while one was open for 1% of the time, Pallas kernels for 42%

profile of v2, /device:TPU:0, one launch (start us, length us, event | category | flops | bytes accessed | tf_op | source)
XLA Modules:
  0.0 177.0 jit_solution(13033104829598455586)
XLA Ops:
  11.9 3.1 %collective-permute-start = (bf16[64,4096]{1,0:T(8,128)(2,1)S(1)}, bf16[64,4096]{1,0:T(8,128)(2,1)}, u32[]{:S(2)}, u32[]{:S(2)}) collective-permute-start(bf16[64,4096]{1,0:T(8,128)(2,1)S(1)} %get-tuple-element.52.refs_0_), channel_id=1, source_target_pairs={{0,4},{1,5},{4,8},{5,9},{8,12},{9,13},{12,14},{13,15},{14,10},{15,... | collective-permute-start | bytes 1572872 | tf_op jit(solution)/shard_map/ppermute | solution.py:222
  15.7 3.1 %copy-done.4 = bf16[4096,896]{1,0:T(8,128)(2,1)S(1)} copy-done((bf16[4096,896]{1,0:T(8,128)(2,1)S(1)}, bf16[4096,896]{1,0:T(8,128)(2,1)}, u32[]{:S(2)}) %copy-start.4) | copy-done | bytes 7340056
  18.8 3.1 %copy-done.5 = bf16[4096,896]{1,0:T(8,128)(2,1)S(1)} copy-done((bf16[4096,896]{1,0:T(8,128)(2,1)S(1)}, bf16[4096,896]{1,0:T(8,128)(2,1)}, u32[]{:S(2)}) %copy-start.5) | copy-done | bytes 7340056
  21.9 9.6 %first_chunk.1 = (f32[2048,64]{1,0:T(8,128)S(1)}, bf16[7,4096,256]{2,1,0:T(8,128)(2,1)S(1)}) custom-call(bf16[64,4096]{1,0:T(8,128)(2,1)S(1)} %get-tuple-element.52.refs_0_, bf16[64,4096]{1,0:T(8,128)(2,1)S(1)} %get-tuple-element.51.refs_1_, f32[1,4096]{1,0:T(1,128)S(1)} %bitcast.18, bf16[4096,896]{1,0:T(8,128)(2,1)S(1)} %copy-done.4, ...), custom_call_target="tpu_custom_call" | custom-call | flops 1879048192 | bytes 29360128 | tf_op jit(solution)/shard_map/first_chunk/pallas_call | solution.py:64
  31.5 2.1 %collective-permute-start.2 = (bf16[64,4096]{1,0:T(8,128)(2,1)}, bf16[64,4096]{1,0:T(8,128)(2,1)S(1)}, u32[]{:S(2)}, u32[]{:S(2)}) collective-permute-start(bf16[64,4096]{1,0:T(8,128)(2,1)} %collective-permute-done.refs_0_), channel_id=1, source_target_pairs={{0,4},{1,5},{4,8},{5,9},{8,12},{9,13},{12,14},{13,15},{14,10},{15,... | collective-permute-start | bytes 1572872 | tf_op jit(solution)/shard_map/ppermute | solution.py:222
  34.1 10.5 %chunk.8.refs_7_ = f32[2048,64]{1,0:T(8,128)S(1)} custom-call(bf16[64,4096]{1,0:T(8,128)(2,1)} %collective-permute-done.refs_0_, bf16[64,4096]{1,0:T(8,128)(2,1)} %collective-permute-done.1.refs_1_, bf16[64,4096]{1,0:T(8,128)(2,1)} %collective-permute-done.4.refs_2_, ...), custom_call_target="tpu_custom_call", output_to_operand_aliasing={{}: (7, {})} | custom-call | flops 3758096384 | bytes 14680064 | tf_op jit(solution)/shard_map/chunk/pallas_call | solution.py:110
  44.6 5.3 %collective-permute-done.2.refs_0_ = bf16[64,4096]{1,0:T(8,128)(2,1)S(1)} collective-permute-done((bf16[64,4096]{1,0:T(8,128)(2,1)}, bf16[64,4096]{1,0:T(8,128)(2,1)S(1)}, u32[]{:S(2)}, u32[]{:S(2)}) %collective-permute-start.2) | collective-permute-done | bytes 524320 | tf_op jit(solution)/shard_map/ppermute | solution.py:222
  49.9 6.5 %collective-permute-done.3.refs_1_ = bf16[64,4096]{1,0:T(8,128)(2,1)S(1)} collective-permute-done((bf16[64,4096]{1,0:T(8,128)(2,1)}, bf16[64,4096]{1,0:T(8,128)(2,1)S(1)}, u32[]{:S(2)}, u32[]{:S(2)}) %collective-permute-start.3) | collective-permute-done | bytes 524320 | tf_op jit(solution)/shard_map/ppermute | solution.py:222
  59.0 7.4 %chunk.9.refs_7_ = f32[2048,64]{1,0:T(8,128)S(1)} custom-call(bf16[64,4096]{1,0:T(8,128)(2,1)S(1)} %collective-permute-done.2.refs_0_, bf16[64,4096]{1,0:T(8,128)(2,1)S(1)} %collective-permute-done.3.refs_1_, bf16[64,4096]{1,0:T(8,128)(2,1)S(1)} %collective-permute-done.8.refs_2_, ...), custom_call_target="tpu_custom_call", output_to_operand_aliasing={{}: (7, {})} | custom-call | flops 3758096384 | bytes 14680064 | tf_op jit(solution)/shard_map/chunk/pallas_call | solution.py:110
  66.4 3.4 %collective-permute-done.6.refs_0_ = bf16[64,4096]{1,0:T(8,128)(2,1)S(1)} collective-permute-done((bf16[64,4096]{1,0:T(8,128)(2,1)S(1)}, bf16[64,4096]{1,0:T(8,128)(2,1)S(1)}, u32[]{:S(2)}, u32[]{:S(2)}) %collective-permute-start.6) | collective-permute-done | bytes 524320 | tf_op jit(solution)/shard_map/ppermute | solution.py:222
  69.8 2.1 %collective-permute-done.7.refs_1_ = bf16[64,4096]{1,0:T(8,128)(2,1)S(1)} collective-permute-done((bf16[64,4096]{1,0:T(8,128)(2,1)S(1)}, bf16[64,4096]{1,0:T(8,128)(2,1)S(1)}, u32[]{:S(2)}, u32[]{:S(2)}) %collective-permute-start.7) | collective-permute-done | bytes 524320 | tf_op jit(solution)/shard_map/ppermute | solution.py:222
  74.5 7.4 %chunk.10.refs_7_ = f32[2048,64]{1,0:T(8,128)S(1)} custom-call(bf16[64,4096]{1,0:T(8,128)(2,1)S(1)} %collective-permute-done.6.refs_0_, bf16[64,4096]{1,0:T(8,128)(2,1)S(1)} %collective-permute-done.7.refs_1_, bf16[64,4096]{1,0:T(8,128)(2,1)S(1)} %collective-permute-done.12.refs_2_, ...), custom_call_target="tpu_custom_call", output_to_operand_aliasing={{}: (7, {})} | custom-call | flops 3758096384 | bytes 14680064 | tf_op jit(solution)/shard_map/chunk/pallas_call | solution.py:110
  81.9 3.1 %collective-permute-done.10.refs_0_ = bf16[64,4096]{1,0:T(8,128)(2,1)} collective-permute-done((bf16[64,4096]{1,0:T(8,128)(2,1)S(1)}, bf16[64,4096]{1,0:T(8,128)(2,1)}, u32[]{:S(2)}, u32[]{:S(2)}) %collective-permute-start.10) | collective-permute-done | bytes 524320 | tf_op jit(solution)/shard_map/ppermute | solution.py:222
  87.7 8.6 %chunk.11.refs_7_ = f32[2048,64]{1,0:T(8,128)S(1)} custom-call(bf16[64,4096]{1,0:T(8,128)(2,1)} %collective-permute-done.10.refs_0_, bf16[64,4096]{1,0:T(8,128)(2,1)} %collective-permute-done.11.refs_1_, bf16[64,4096]{1,0:T(8,128)(2,1)S(1)} %collective-permute-done.16.refs_2_, ...), custom_call_target="tpu_custom_call", output_to_operand_aliasing={{}: (7, {})} | custom-call | flops 3758096384 | bytes 14680064 | tf_op jit(solution)/shard_map/chunk/pallas_call | solution.py:110
  101.2 5.2 %copy-done.2 = bf16[7,4096,256]{2,1,0:T(8,128)(2,1)S(1)} copy-done((bf16[7,4096,256]{2,1,0:T(8,128)(2,1)S(1)}, bf16[7,4096,256]{2,1,0:T(8,128)(2,1)}, u32[]{:S(2)}) %copy-start.2) | copy-done | bytes 14680088
  106.4 8.8 %chunk.12.refs_7_ = f32[2048,64]{1,0:T(8,128)S(1)} custom-call(bf16[64,4096]{1,0:T(8,128)(2,1)} %collective-permute-done.14.refs_0_, bf16[64,4096]{1,0:T(8,128)(2,1)S(1)} %collective-permute-done.15.refs_1_, bf16[64,4096]{1,0:T(8,128)(2,1)} %collective-permute-done.20.refs_2_, ...), custom_call_target="tpu_custom_call", output_to_operand_aliasing={{}: (7, {})} | custom-call | flops 3758096384 | bytes 14680064 | tf_op jit(solution)/shard_map/chunk/pallas_call | solution.py:110
  118.5 5.2 %copy-done.3 = bf16[7,4096,256]{2,1,0:T(8,128)(2,1)S(1)} copy-done((bf16[7,4096,256]{2,1,0:T(8,128)(2,1)S(1)}, bf16[7,4096,256]{2,1,0:T(8,128)(2,1)}, u32[]{:S(2)}) %copy-start.3) | copy-done | bytes 14680088
  123.7 8.8 %chunk.13.refs_7_ = f32[2048,64]{1,0:T(8,128)S(1)} custom-call(bf16[64,4096]{1,0:T(8,128)(2,1)S(1)} %collective-permute-done.18.refs_0_, bf16[64,4096]{1,0:T(8,128)(2,1)} %collective-permute-done.19.refs_1_, bf16[64,4096]{1,0:T(8,128)(2,1)} %collective-permute-done.24.refs_2_, ...), custom_call_target="tpu_custom_call", output_to_operand_aliasing={{}: (7, {})} | custom-call | flops 3758096384 | bytes 14680064 | tf_op jit(solution)/shard_map/chunk/pallas_call | solution.py:110
  133.8 8.6 %chunk.14.refs_5_ = f32[2048,64]{1,0:T(8,128)S(1)} custom-call(bf16[64,4096]{1,0:T(8,128)(2,1)} %collective-permute-done.22.refs_0_, bf16[64,4096]{1,0:T(8,128)(2,1)} %collective-permute-done.23.refs_1_, bf16[64,4096]{1,0:T(8,128)(2,1)S(1)} %collective-permute-done.28.refs_2_, ...), custom_call_target="tpu_custom_call", output_to_operand_aliasing={{}: (7, {})} | custom-call | flops 3758096384 | bytes 14680064 | tf_op jit(solution)/shard_map/chunk/pallas_call | solution.py:110
  142.4 4.8 %chunk.15.left_ref = f32[2048,64]{1,0:T(8,128)S(1)} custom-call(bf16[64,4096]{1,0:T(8,128)(2,1)S(1)} %collective-permute-done.26.refs_0_, bf16[64,4096]{1,0:T(8,128)(2,1)S(1)} %collective-permute-done.27.refs_1_, f32[1,4096]{1,0:T(1,128)S(1)} %bitcast.26, bf16[7,4096,256]{2,1,0:T(8,128)(2,1)S(1)} %copy-done.3, ...), custom_call_target="tpu_custom_call", output_to_operand_aliasing={{}: (5, {})} | custom-call | flops 1879048192 | bytes 14680064 | tf_op jit(solution)/shard_map/chunk/pallas_call | solution.py:110
  148.7 3.2 %slice.23 = bf16[16,16,4096]{2,1,0:T(8,128)(2,1)} slice(bf16[16,24,4096]{2,1,0:T(8,128)(2,1)} %bitcast.29), slice={[0:16], [0:16], [0:4096]} | slice | bytes 4194304 | tf_op jit(solution)/shard_map/slice | solution.py:208
  153.0 3.5 %sketch.1 = f32[16,64,64]{2,1,0:T(8,128)S(1)} custom-call(s32[16]{0:T(128)S(1)} %get-tuple-element.54.at_f, s32[16]{0:T(128)S(1)} %get-tuple-element.53.at_b, f32[2048,64]{1,0:T(8,128)S(1)} %chunk.15.left_ref, bf16[2048,64]{1,0:T(8,128)(2,1)S(1)} %reshape.72.masked_ref), custom_call_target="tpu_custom_call" | custom-call | tf_op jit(solution)/shard_map/sketch/pallas_call | solution.py:154
  156.9 2.2 %fusion.16 = f32[16,256]{1,0:T(8,128)S(1)} fusion(bf16[16,4096]{1,0:T(8,128)(2,1)S(1)} %reshape.73, bf16[256,4096]{1,0:T(8,128)(2,1)} %bitcast.27), kind=kOutput, calls=%fused_computation.45 | convolution fusion | flops 33554432 | bytes 2244608 | tf_op jit(solution)/shard_map/dot_general | solution.py:251
  159.4 10.1 %all_to_all.9 = f32[16,1,256]{2,1,0:T(1,128)S(1)} all-to-all(f32[16,1,256]{2,1,0:T(1,128)S(1)} %copy.50), channel_id=1, replica_groups=mesh['groups'=2,'examples'=16] {'examples'}, dimensions={0} | all-to-all | bytes 32768 | tf_op jit(solution)/shard_map/all_to_all | solution.py:253
  (95 shorter events, 26.9 us)
Async XLA Ops:
  6.5 140.7 %all-gather.3.cloned.1.call-start = ((), (), s32[]{:S(2)}) async-start(), calls=%async_computation.1 | async-start | bytes 3342336 | tf_op jit(solution)/shard_map/all_gather | solution.py:207
  11.9 19.6 %collective-permute-start = (bf16[64,4096]{1,0:T(8,128)(2,1)S(1)}, bf16[64,4096]{1,0:T(8,128)(2,1)}, u32[]{:S(2)}, u32[]{:S(2)}) collective-permute-start(bf16[64,4096]{1,0:T(8,128)(2,1)S(1)} %get-tuple-element.52.refs_0_), channel_id=1, source_target_pairs={{0,4},{1,5},{4,8},{5,9},{8,12},{9,13},{12,14},{13,15},{14,10},{15,... | collective-permute-start | bytes 1572872 | tf_op jit(solution)/shard_map/ppermute | solution.py:222
  15.0 16.5 %collective-permute-start.1 = (bf16[64,4096]{1,0:T(8,128)(2,1)S(1)}, bf16[64,4096]{1,0:T(8,128)(2,1)}, u32[]{:S(2)}, u32[]{:S(2)}) collective-permute-start(bf16[64,4096]{1,0:T(8,128)(2,1)S(1)} %get-tuple-element.51.refs_1_), channel_id=1, source_target_pairs={{4,0},{5,1},{8,4},{9,5},{12,8},{13,9},{14,12},{15,13},{10,14},{11,... | collective-permute-start | bytes 1572872 | tf_op jit(solution)/shard_map/ppermute | solution.py:222
  15.0 18.6 %collective-permute-start.4 = (bf16[64,4096]{1,0:T(8,128)(2,1)S(1)}, bf16[64,4096]{1,0:T(8,128)(2,1)}, u32[]{:S(2)}, u32[]{:S(2)}) collective-permute-start(bf16[64,4096]{1,0:T(8,128)(2,1)S(1)} %get-tuple-element.52.refs_0_), channel_id=1, source_target_pairs={{0,1},{1,0},{2,3},{3,2},{4,5},{5,4},{6,7},{7,6},{8,9},{9,8},{10,11... | collective-permute-start | bytes 1572872 | tf_op jit(solution)/shard_map/ppermute | solution.py:225
  15.0 19.1 %collective-permute-start.5 = (bf16[64,4096]{1,0:T(8,128)(2,1)S(1)}, bf16[64,4096]{1,0:T(8,128)(2,1)}, u32[]{:S(2)}, u32[]{:S(2)}) collective-permute-start(bf16[64,4096]{1,0:T(8,128)(2,1)S(1)} %get-tuple-element.51.refs_1_), channel_id=1, source_target_pairs={{0,1},{1,0},{2,3},{3,2},{4,5},{5,4},{6,7},{7,6},{8,9},{9,8},{10,11... | collective-permute-start | bytes 1572872 | tf_op jit(solution)/shard_map/ppermute | solution.py:225
  31.5 18.4 %collective-permute-start.2 = (bf16[64,4096]{1,0:T(8,128)(2,1)}, bf16[64,4096]{1,0:T(8,128)(2,1)S(1)}, u32[]{:S(2)}, u32[]{:S(2)}) collective-permute-start(bf16[64,4096]{1,0:T(8,128)(2,1)} %collective-permute-done.refs_0_), channel_id=1, source_target_pairs={{0,4},{1,5},{4,8},{5,9},{8,12},{9,13},{12,14},{13,15},{14,10},{15,... | collective-permute-start | bytes 1572872 | tf_op jit(solution)/shard_map/ppermute | solution.py:222
  33.6 22.9 %collective-permute-start.3 = (bf16[64,4096]{1,0:T(8,128)(2,1)}, bf16[64,4096]{1,0:T(8,128)(2,1)S(1)}, u32[]{:S(2)}, u32[]{:S(2)}) collective-permute-start(bf16[64,4096]{1,0:T(8,128)(2,1)} %collective-permute-done.1.refs_1_), channel_id=1, source_target_pairs={{4,0},{5,1},{8,4},{9,5},{12,8},{13,9},{14,12},{15,13},{10,14},{11,... | collective-permute-start | bytes 1572872 | tf_op jit(solution)/shard_map/ppermute | solution.py:222
  33.6 24.9 %collective-permute-start.8 = (bf16[64,4096]{1,0:T(8,128)(2,1)}, bf16[64,4096]{1,0:T(8,128)(2,1)S(1)}, u32[]{:S(2)}, u32[]{:S(2)}) collective-permute-start(bf16[64,4096]{1,0:T(8,128)(2,1)} %collective-permute-done.refs_0_), channel_id=1, source_target_pairs={{0,1},{1,0},{2,3},{3,2},{4,5},{5,4},{6,7},{7,6},{8,9},{9,8},{10,11... | collective-permute-start | bytes 1572872 | tf_op jit(solution)/shard_map/ppermute | solution.py:225
  33.6 25.4 %collective-permute-start.9 = (bf16[64,4096]{1,0:T(8,128)(2,1)}, bf16[64,4096]{1,0:T(8,128)(2,1)S(1)}, u32[]{:S(2)}, u32[]{:S(2)}) collective-permute-start(bf16[64,4096]{1,0:T(8,128)(2,1)} %collective-permute-done.1.refs_1_), channel_id=1, source_target_pairs={{0,1},{1,0},{2,3},{3,2},{4,5},{5,4},{6,7},{7,6},{8,9},{9,8},{10,11... | collective-permute-start | bytes 1572872 | tf_op jit(solution)/shard_map/ppermute | solution.py:225
  56.5 13.4 %collective-permute-start.6 = (bf16[64,4096]{1,0:T(8,128)(2,1)S(1)}, bf16[64,4096]{1,0:T(8,128)(2,1)S(1)}, u32[]{:S(2)}, u32[]{:S(2)}) collective-permute-start(bf16[64,4096]{1,0:T(8,128)(2,1)S(1)} %collective-permute-done.2.refs_0_), channel_id=1, source_target_pairs={{0,4},{1,5},{4,8},{5,9},{8,12},{9,13},{12,14},{13,15},{14,10},{15,... | collective-permute-start | bytes 1572872 | tf_op jit(solution)/shard_map/ppermute | solution.py:222
  56.5 15.5 %collective-permute-start.7 = (bf16[64,4096]{1,0:T(8,128)(2,1)S(1)}, bf16[64,4096]{1,0:T(8,128)(2,1)S(1)}, u32[]{:S(2)}, u32[]{:S(2)}) collective-permute-start(bf16[64,4096]{1,0:T(8,128)(2,1)S(1)} %collective-permute-done.3.refs_1_), channel_id=1, source_target_pairs={{4,0},{5,1},{8,4},{9,5},{12,8},{13,9},{14,12},{15,13},{10,14},{11,... | collective-permute-start | bytes 1572872 | tf_op jit(solution)/shard_map/ppermute | solution.py:222
  58.5 15.5 %collective-permute-start.12 = (bf16[64,4096]{1,0:T(8,128)(2,1)S(1)}, bf16[64,4096]{1,0:T(8,128)(2,1)S(1)}, u32[]{:S(2)}, u32[]{:S(2)}) collective-permute-start(bf16[64,4096]{1,0:T(8,128)(2,1)S(1)} %collective-permute-done.2.refs_0_), channel_id=1, source_target_pairs={{0,1},{1,0},{2,3},{3,2},{4,5},{5,4},{6,7},{7,6},{8,9},{9,8},{10,11... | collective-permute-start | bytes 1572872 | tf_op jit(solution)/shard_map/ppermute | solution.py:225
  58.5 16.0 %collective-permute-start.13 = (bf16[64,4096]{1,0:T(8,128)(2,1)S(1)}, bf16[64,4096]{1,0:T(8,128)(2,1)S(1)}, u32[]{:S(2)}, u32[]{:S(2)}) collective-permute-start(bf16[64,4096]{1,0:T(8,128)(2,1)S(1)} %collective-permute-done.3.refs_1_), channel_id=1, source_target_pairs={{0,1},{1,0},{2,3},{3,2},{4,5},{5,4},{6,7},{7,6},{8,9},{9,8},{10,11... | collective-permute-start | bytes 1572872 | tf_op jit(solution)/shard_map/ppermute | solution.py:225
  74.0 13.8 %collective-permute-start.17 = (bf16[64,4096]{1,0:T(8,128)(2,1)S(1)}, bf16[64,4096]{1,0:T(8,128)(2,1)S(1)}, u32[]{:S(2)}, u32[]{:S(2)}) collective-permute-start(bf16[64,4096]{1,0:T(8,128)(2,1)S(1)} %collective-permute-done.7.refs_1_), channel_id=1, source_target_pairs={{0,1},{1,0},{2,3},{3,2},{4,5},{5,4},{6,7},{7,6},{8,9},{9,8},{10,11... | collective-permute-start | bytes 1572872 | tf_op jit(solution)/shard_map/ppermute | solution.py:225
  87.2 13.5 %collective-permute-start.20 = (bf16[64,4096]{1,0:T(8,128)(2,1)}, bf16[64,4096]{1,0:T(8,128)(2,1)}, u32[]{:S(2)}, u32[]{:S(2)}) collective-permute-start(bf16[64,4096]{1,0:T(8,128)(2,1)} %collective-permute-done.10.refs_0_), channel_id=1, source_target_pairs={{0,1},{1,0},{2,3},{3,2},{4,5},{5,4},{6,7},{7,6},{8,9},{9,8},{10,11... | collective-permute-start | bytes 1572872 | tf_op jit(solution)/shard_map/ppermute | solution.py:225
  87.2 14.0 %collective-permute-start.21 = (bf16[64,4096]{1,0:T(8,128)(2,1)}, bf16[64,4096]{1,0:T(8,128)(2,1)}, u32[]{:S(2)}, u32[]{:S(2)}) collective-permute-start(bf16[64,4096]{1,0:T(8,128)(2,1)} %collective-permute-done.11.refs_1_), channel_id=1, source_target_pairs={{0,1},{1,0},{2,3},{3,2},{4,5},{5,4},{6,7},{7,6},{8,9},{9,8},{10,11... | collective-permute-start | bytes 1572872 | tf_op jit(solution)/shard_map/ppermute | solution.py:225
  98.1 17.1 %collective-permute-start.18 = (bf16[64,4096]{1,0:T(8,128)(2,1)}, bf16[64,4096]{1,0:T(8,128)(2,1)S(1)}, u32[]{:S(2)}, u32[]{:S(2)}) collective-permute-start(bf16[64,4096]{1,0:T(8,128)(2,1)} %collective-permute-done.14.refs_0_), channel_id=1, source_target_pairs={{0,4},{1,5},{4,8},{5,9},{8,12},{9,13},{12,14},{13,15},{14,10},{15,... | collective-permute-start | bytes 1572872 | tf_op jit(solution)/shard_map/ppermute | solution.py:222
  99.8 15.3 %collective-permute-start.19 = (bf16[64,4096]{1,0:T(8,128)(2,1)S(1)}, bf16[64,4096]{1,0:T(8,128)(2,1)}, u32[]{:S(2)}, u32[]{:S(2)}) collective-permute-start(bf16[64,4096]{1,0:T(8,128)(2,1)S(1)} %collective-permute-done.15.refs_1_), channel_id=1, source_target_pairs={{4,0},{5,1},{8,4},{9,5},{12,8},{13,9},{14,12},{15,13},{10,14},{11,... | collective-permute-start | bytes 1572872 | tf_op jit(solution)/shard_map/ppermute | solution.py:222
  100.7 17.3 %collective-permute-start.24 = (bf16[64,4096]{1,0:T(8,128)(2,1)}, bf16[64,4096]{1,0:T(8,128)(2,1)}, u32[]{:S(2)}, u32[]{:S(2)}) collective-permute-start(bf16[64,4096]{1,0:T(8,128)(2,1)} %collective-permute-done.14.refs_0_), channel_id=1, source_target_pairs={{0,1},{1,0},{2,3},{3,2},{4,5},{5,4},{6,7},{7,6},{8,9},{9,8},{10,11... | collective-permute-start | bytes 1572872 | tf_op jit(solution)/shard_map/ppermute | solution.py:225
  100.7 17.8 %collective-permute-start.25 = (bf16[64,4096]{1,0:T(8,128)(2,1)S(1)}, bf16[64,4096]{1,0:T(8,128)(2,1)}, u32[]{:S(2)}, u32[]{:S(2)}) collective-permute-start(bf16[64,4096]{1,0:T(8,128)(2,1)S(1)} %collective-permute-done.15.refs_1_), channel_id=1, source_target_pairs={{0,1},{1,0},{2,3},{3,2},{4,5},{5,4},{6,7},{7,6},{8,9},{9,8},{10,11... | collective-permute-start | bytes 1572872 | tf_op jit(solution)/shard_map/ppermute | solution.py:225
  115.2 17.3 %collective-permute-start.22 = (bf16[64,4096]{1,0:T(8,128)(2,1)S(1)}, bf16[64,4096]{1,0:T(8,128)(2,1)}, u32[]{:S(2)}, u32[]{:S(2)}) collective-permute-start(bf16[64,4096]{1,0:T(8,128)(2,1)S(1)} %collective-permute-done.18.refs_0_), channel_id=1, source_target_pairs={{0,4},{1,5},{4,8},{5,9},{8,12},{9,13},{12,14},{13,15},{14,10},{15,... | collective-permute-start | bytes 1572872 | tf_op jit(solution)/shard_map/ppermute | solution.py:222
  117.0 15.5 %collective-permute-start.23 = (bf16[64,4096]{1,0:T(8,128)(2,1)}, bf16[64,4096]{1,0:T(8,128)(2,1)}, u32[]{:S(2)}, u32[]{:S(2)}) collective-permute-start(bf16[64,4096]{1,0:T(8,128)(2,1)} %collective-permute-done.19.refs_1_), channel_id=1, source_target_pairs={{4,0},{5,1},{8,4},{9,5},{12,8},{13,9},{14,12},{15,13},{10,14},{11,... | collective-permute-start | bytes 1572872 | tf_op jit(solution)/shard_map/ppermute | solution.py:222
  117.9 15.8 %collective-permute-start.28 = (bf16[64,4096]{1,0:T(8,128)(2,1)S(1)}, bf16[64,4096]{1,0:T(8,128)(2,1)S(1)}, u32[]{:S(2)}, u32[]{:S(2)}) collective-permute-start(bf16[64,4096]{1,0:T(8,128)(2,1)S(1)} %collective-permute-done.18.refs_0_), channel_id=1, source_target_pairs={{0,1},{1,0},{2,3},{3,2},{4,5},{5,4},{6,7},{7,6},{8,9},{9,8},{10,11... | collective-permute-start | bytes 1572872 | tf_op jit(solution)/shard_map/ppermute | solution.py:225
  118.0 15.7 %collective-permute-start.29 = (bf16[64,4096]{1,0:T(8,128)(2,1)}, bf16[64,4096]{1,0:T(8,128)(2,1)S(1)}, u32[]{:S(2)}, u32[]{:S(2)}) collective-permute-start(bf16[64,4096]{1,0:T(8,128)(2,1)} %collective-permute-done.19.refs_1_), channel_id=1, source_target_pairs={{0,1},{1,0},{2,3},{3,2},{4,5},{5,4},{6,7},{7,6},{8,9},{9,8},{10,11... | collective-permute-start | bytes 1572872 | tf_op jit(solution)/shard_map/ppermute | solution.py:225
  (17 other events, 197.2 us)
Sparse Core Ops, SparseCore 0:
  12.0 53.6 all-gather.2

commit v3 on v1

v3 whole, which is shorter than its diff:
```python
import functools

import jax
import jax.numpy as jnp
from jax import lax
from jax.experimental import pallas as pl
from jax.experimental.pallas import tpu as pltpu
from jax.sharding import PartitionSpec as P

NVAL = 256
LANES = 128
MIB = 1024 * 1024
NT = (((1,), (1,)), ((), ()))
TN = (((0,), (0,)), ((), ()))


def chip_ring(chips):
    if chips == 8:
        return [0, 2, 4, 6, 7, 5, 3, 1]
    return list(range(chips))


def chunk_body(pieces, *refs):
    x_refs = refs[:pieces]
    gain_ref, gate_ref, up_ref, f_ref, out_ref, xn = refs[pieces], *refs[pieces + 1 : pieces + 4], *refs[-2:]
    rows = x_refs[0].shape[0]
    step = pl.program_id(0)

    @pl.when(step == 0)
    def _():
        for k, ref in enumerate(x_refs):
            x = ref[...].astype(jnp.float32)
            scale = lax.rsqrt(jnp.mean(x * x, axis=-1, keepdims=True) + 1e-05)
            xn[k * rows : (k + 1) * rows, :] = (x * scale * gain_ref[...]).astype(jnp.bfloat16)

    weights = jnp.concatenate([gate_ref[...], up_ref[...]], axis=1)
    both = jnp.dot(xn[...], weights, preferred_element_type=jnp.float32)
    gate, up = both[:, :LANES], both[:, LANES:]
    hidden = (jax.nn.silu(gate) * up).astype(jnp.bfloat16)
    part = jnp.dot(hidden, f_ref[...], preferred_element_type=jnp.float32)

    @pl.when(step == 0)
    def _():
        out_ref[...] = part

    @pl.when(step > 0)
    def _():
        out_ref[...] += part


def chunk(xs, gain, gate_weight, up_weight, in_factor, left, index, tokens):
    pieces = len(xs)
    rows, depth = xs[0].shape
    units, order = in_factor.shape
    tiles = units // LANES
    total = pieces * rows
    operands = [*xs, gain, gate_weight, up_weight, in_factor]
    in_specs = [pl.BlockSpec((rows, depth), lambda i: (0, 0))] * pieces + [
        pl.BlockSpec((1, depth), lambda i: (0, 0)),
        pl.BlockSpec((depth, LANES), lambda i: (0, i)),
        pl.BlockSpec((depth, LANES), lambda i: (0, i)),
        pl.BlockSpec((LANES, order), lambda i: (i, 0)),
    ]
    aliases = {}
    if left is not None:
        aliases = {len(operands): 0}
        operands.append(left)
        in_specs.append(pl.BlockSpec(memory_space=pl.ANY))
    return pl.pallas_call(
        functools.partial(chunk_body, pieces),
        grid=(tiles,),
        in_specs=in_specs,
        out_specs=pl.BlockSpec((total, order), lambda i: (index, 0)),
        out_shape=jax.ShapeDtypeStruct((tokens, order), jnp.float32),
        scratch_shapes=[pltpu.VMEM((total, depth), jnp.bfloat16)],
        input_output_aliases=aliases,
        compiler_params=pltpu.CompilerParams(vmem_limit_bytes=18 * MIB),
        cost_estimate=pl.CostEstimate(
            flops=2 * total * depth * tiles * 2 * LANES,
            bytes_accessed=4 * depth * units,
            transcendentals=0,
        ),
        name="chunk",
    )(*operands)


def one_sketch(left_ref, masked, at, half):
    left = jnp.concatenate([left_ref[p * half : (p + 1) * half, :] for p in at], axis=0)
    high = left.astype(jnp.bfloat16)
    low = (left - high.astype(jnp.float32)).astype(jnp.bfloat16)
    return sum(lax.dot_general(part, masked, TN, preferred_element_type=jnp.float32) for part in (low, high))


def sketch_body(places, half, names, left_ref, side_ref, out_ref):
    for r, at in enumerate(places):
        masked = side_ref[names[r], : 2 * half, :]
        out_ref[r] = one_sketch(left_ref, masked, at, half).astype(out_ref.dtype)


def sketches(places, half, names, left, side):
    order = left.shape[1]
    vmem = pl.BlockSpec(memory_space=pltpu.VMEM)
    made = pl.pallas_call(
        functools.partial(sketch_body, places, half),
        in_specs=[pl.BlockSpec(memory_space=pltpu.SMEM), vmem, vmem],
        out_specs=vmem,
        out_shape=jax.ShapeDtypeStruct((len(places), order, order), jnp.bfloat16),
        compiler_params=pltpu.CompilerParams(vmem_limit_bytes=8 * MIB),
        cost_estimate=pl.CostEstimate(flops=400_000_000 * len(places), bytes_accessed=0, transcendentals=0),
        name="sketches",
    )(names, left, side)
    return made.reshape(len(places), order * order)


def finish_body(places, half, names, left_ref, side_ref, early_ref, queries_ref, ids_ref, out_ref, twice, flat):
    order = left_ref.shape[1]
    early = early_ref.shape[0]
    lane = lax.broadcasted_iota(jnp.int32, (order // 2, 2 * order), 1)
    for r, at in enumerate(places):
        masked = side_ref[names[early + r], : 2 * half, :]
        sketch = one_sketch(left_ref, masked, at, half)
        twice[...] = jnp.concatenate([sketch, sketch], axis=1)
        even = twice[pl.ds(0, order // 2, 2), :]
        odd = twice[pl.ds(1, order // 2, 2), :]
        flat[:, r, :] = jnp.where(lane < order, even, odd)
    late = jnp.concatenate([flat[c] for c in range(order // 2)], axis=1).astype(jnp.bfloat16)
    queries = queries_ref[...]
    count = queries.shape[0]
    value = lax.broadcasted_iota(jnp.int32, (NVAL, count), 0)
    members = (value == ids_ref[...]).astype(jnp.bfloat16)

    def influence(sketch):
        rest = lax.dot_general(sketch, queries, NT, preferred_element_type=jnp.float32)
        total = 0.0
        for _ in range(3):
            part = rest.astype(jnp.bfloat16)
            rest = rest - part.astype(jnp.float32)
            total += lax.dot_general(part, members, NT, preferred_element_type=jnp.float32)
        return total

    rows = influence(jnp.concatenate([late, early_ref[...]], axis=0))
    for r in range(early):
        out_ref[pl.ds(names[r], 1), :] = rows[flat.shape[1] + r : flat.shape[1] + r + 1, :]
    for r in range(len(places)):
        out_ref[pl.ds(names[early + r], 1), :] = rows[r : r + 1, :]


def finish(places, half, names, left, side, early, queries, ids):
    order = left.shape[1]
    vmem = pl.BlockSpec(memory_space=pltpu.VMEM)
    slots = -(-len(places) // 8) * 8
    return pl.pallas_call(
        functools.partial(finish_body, places, half),
        in_specs=[pl.BlockSpec(memory_space=pltpu.SMEM)] + [vmem] * 5,
        out_specs=vmem,
        out_shape=jax.ShapeDtypeStruct((names.shape[0], NVAL), jnp.float32),
        scratch_shapes=[
            pltpu.VMEM((order, 2 * order), jnp.float32),
            pltpu.VMEM((order // 2, slots, 2 * order), jnp.float32),
        ],
        compiler_params=pltpu.CompilerParams(vmem_limit_bytes=16 * MIB),
        name="finish",
    )(names, left, side, early, queries, ids)


def local(
    devices,
    groups,
    layer_inputs,
    example_lengths,
    norm_gain,
    gate_weight,
    up_weight,
    in_factor,
    out_factor,
    out_grads,
    queries,
    query_ids,
):
    chips = devices // 2
    far = chips // 2
    ring = chip_ring(chips)
    me = lax.axis_index("examples")
    core = me % 2
    place = jnp.array([ring.index(c) for c in range(chips)], jnp.int32)[me // 2]

    forward = [(ring[r] * 2 + c, ring[(r + 1) % chips] * 2 + c) for r in range(chips) for c in range(2)]
    backward = [(b, a) for a, b in forward]
    other_core = [(d, d ^ 1) for d in range(devices)]

    span, depth = layer_inputs.shape
    half = span // 2
    order = in_factor.shape[1]
    units = gate_weight.shape[1]
    short = -units % LANES
    if short:
        gate_weight = jnp.pad(gate_weight, ((0, 0), (0, short)))
        up_weight = jnp.pad(up_weight, ((0, 0), (0, short)))
        in_factor = jnp.pad(in_factor, ((0, short), (0, 0)))
    gain = norm_gain[None, :]
    tokens = 2 * span * chips + span

    def send(x, way):
        return lax.ppermute(x, "examples", way)

    def project(xs, left, index):
        return chunk(xs, gain, gate_weight, up_weight, in_factor, left, index, tokens)

    x_a, x_b = layer_inputs[:half], layer_inputs[half:]
    coming = {
        1: (send(x_a, forward), send(x_a, backward)),
        2: (send(x_b, forward), send(x_b, backward)),
    }
    swapped = tuple(send(x, other_core) for x in (x_a, x_b))
    left = project((x_a, x_b), None, 1)

    out_grads, queries, query_ids, left = lax.optimization_barrier((out_grads, queries, query_ids, left))
    right = jnp.dot(out_grads, out_factor, preferred_element_type=jnp.float32)
    live = jnp.arange(span, dtype=jnp.int32)[:, None] < example_lengths[0]
    masked = jnp.where(live, right, 0.0).astype(jnp.bfloat16)
    nq = queries.shape[0]
    ids_row = jnp.pad(query_ids.astype(jnp.bfloat16)[None, :], ((0, 15), (0, order - nq)))
    side = lax.all_gather(jnp.concatenate([masked, ids_row], axis=0), "examples", axis=0)
    share = nq // groups
    mine = lax.dynamic_slice_in_dim(queries, lax.axis_index("groups") * share, share, axis=0)
    mine = lax.all_gather(mine, "examples", axis=0, tiled=True)

    def pair(where):
        first = jnp.array(ring, jnp.int32)[where % chips] * 2
        return [first + core, first + 1 - core]

    names, spots = [], []
    for distance in range(far + 1):
        sides = [(1, 0)] if distance in (0, far) else [(-1, 0), (1, 1)]
        for sign, piece in sides:
            names += pair(place + sign * distance)
            if distance == 0:
                halves = [(0, 0), (0, 1)]
            elif distance == far:
                halves = [(chips - 1, 0), (chips - 1, 1)]
            else:
                halves = [(2 * distance - 1, piece), (2 * distance, piece)]
            spots.append([4 * k + 2 + p for k, p in halves])
            spots.append([4 * k + 4 + p for k, p in halves])
    names = jnp.stack(names)

    for k in range(1, chips):
        own_1, own_2, left = lax.optimization_barrier((*coming.pop(k), left))
        own = (own_1, own_2)
        if k + 2 < chips - 1:
            coming[k + 2] = (send(own_1, forward), send(own_2, backward))
        elif k + 2 == chips - 1:
            opposite = send(own_1, forward)
        elif k + 1 == chips - 1:
            coming[chips - 1] = (opposite, send(own_2, backward))
        before, swapped = swapped, tuple(send(x, other_core) for x in own)
        if k < chips - 1:
            left = project(before + own, left, k)
        if k == chips - 3:
            side, mine, left = lax.optimization_barrier((side, mine, left))
            all_queries = lax.all_gather(mine, "groups", axis=0, tiled=True)
            ids = side[:, span, :nq].reshape(devices, groups, share).swapaxes(0, 1).reshape(1, devices * nq)
            ids = ids.astype(jnp.int32)
            ready = devices - 6
            early = [sketches(spots[:ready], half, names[:ready], left, side)]
        if k == chips - 2:
            left = project(swapped, left, 2 * k + 2)
            early.append(sketches(spots[ready:-2], half, names[ready:-2], left, side))
            early = jnp.concatenate(early, axis=0)
            early, left = lax.optimization_barrier((early, left))
    left = project(own, left, 2 * chips - 1)
    left = project(swapped, left, 2 * chips)

    partial = finish(spots[-2:], half, names, left, side, early, all_queries, ids)
    shares = lax.all_to_all(partial, "examples", split_axis=0, concat_axis=0, tiled=True)
    return jnp.sum(shares, axis=0, keepdims=True)


def solution(mesh):
    return jax.shard_map(
        functools.partial(local, mesh.shape["examples"], mesh.shape["groups"]),
        mesh=mesh,
        in_specs=(
            P(("groups", "examples"), None),
            P(("groups", "examples")),
            P(),
            P(None, "examples"),
            P(None, "examples"),
            P("examples", None),
            P(),
            P(("groups", "examples"), None),
            P("examples", None),
            P("examples"),
        ),
        out_specs=P(("groups", "examples"), None),
        check_vma=False,
    )
```

time: 205 us -> 240 us (1.17)
  waiting for transfers between devices: 45.4 us -> 0.67 us
  Pallas kernels: 73.5 us -> 102 us
  local copies, waits for them, and re-layouts: 28.9 us -> 51.8 us
  blocking collectives: 11.5 us -> 34.3 us
  between operations: 14.6 us -> 26.1 us
  matrix products: 3.99 us -> 1.52 us
    ppermute x30, waiting for transfers between devices: 45.4 us -> 0.6 us  [send(): return lax.ppermute(x, 'examples', way)]
    pallas_call x8 -> x10, Pallas kernels: 64 us -> 98.7 us  [chunk(): pl.pallas_call(functools.partial(chunk_body, pieces), grid=(tiles,), in_s...]
    all_gather x0 -> x1, blocking collectives: none -> 24.9 us  [local(): lax.all_gather(jnp.concatenate([masked, ids_row], axis=0), 'examples', ax...]
    unnamed x35 -> x39, local copies, waits for them, and re-layouts: 21.2 us -> 39.6 us
    optimization_barrier x0 -> x2, local copies, waits for them, and re-layouts: none -> 7.25 us  [local(): side, mine, left = lax.optimization_barrier((side, mine, left))]
    pallas_call x2 -> x3, Pallas kernels: 9.43 us -> 3.52 us  [the longest x1 1.84 us: finish(): pl.pallas_call(functools.partial(finish_body, places, half), in_specs=[pl...]
    slice x3 -> x1, local copies, waits for them, and re-layouts: 4.69 us -> 1.38 us  [local(): x_a, x_b = (layer_inputs[:half], layer_inputs[half:])]
    dot_general x2 -> x0, matrix products: 2.47 us -> none  [the longest x1 2.24 us: local(): scores = jnp.dot(sketch, queries_all.T, preferred_element_type=jnp.float32)]
  transfers between devices with their start and end apart: 31 -> 32, of which waited for: 5 -> 1; matrix products, arithmetic and copies ran while one was open for 1% -> 6% of each run, Pallas kernels for 34% -> 42%
where the time goes in v3:
time: 240 us; the launch traced here: 239 us
  Pallas kernels  102 us (42%)
  local copies, waits for them, and re-layouts  51.8 us (22%)
  blocking collectives  34.3 us (14%)
  between operations  26.1 us (11%)
  starting transfers between devices  20.8 us (9%)
    pallas_call x10, Pallas kernels, chunk(): pl.pallas_call(functools.partial(chunk_body, pieces), grid=(tiles,), in_s...  98.7 us
    unnamed x39, local copies, waits for them, and re-layouts  39.6 us
    all_gather x1, blocking collectives, local(): lax.all_gather(jnp.concatenate([masked, ids_row], axis=0), 'examples', ax...  24.9 us
    ppermute x30, starting transfers between devices, send(): return lax.ppermute(x, 'examples', way)  20.7 us
    all_to_all x1, blocking collectives, local(): lax.all_to_all(partial, 'examples', split_axis=0, concat_axis=0, tiled=True)  9.41 us
    optimization_barrier x2, local copies, waits for them, and re-layouts, local(): side, mine, left = lax.optimization_barrier((side, mine, left))  7.25 us
  transfers between devices with their start and end apart: 32, of which 1 were waited for; matrix products, arithmetic and copies ran while one was open for 6% of the time, Pallas kernels for 42%

profile of v3, /device:TPU:0, one launch (start us, length us, event | category | flops | bytes accessed | tf_op | source)
XLA Modules:
  0.0 238.7 jit_solution(17409428936402481948)
XLA Ops:
  16.8 3.1 %copy-done.7 = bf16[4096,896]{1,0:T(8,128)(2,1)S(1)} copy-done((bf16[4096,896]{1,0:T(8,128)(2,1)S(1)}, bf16[4096,896]{1,0:T(8,128)(2,1)}, u32[]{:S(2)}) %copy-start.7) | copy-done | bytes 7340056
  19.9 7.4 %chunk.10.refs_8_ = f32[2176,64]{1,0:T(8,128)S(1)} custom-call(bf16[64,4096]{1,0:T(8,128)(2,1)S(1)} %get-tuple-element.66.refs_0_, bf16[64,4096]{1,0:T(8,128)(2,1)S(1)} %get-tuple-element.65.refs_1_, f32[1,4096]{1,0:T(1,128)S(1)} %bitcast.43, bf16[4096,896]{1,0:T(8,128)(2,1)S(1)} %copy-done.1, bf16[4096,896]{1,0:T(8,128)(2,1)S(1)} %copy-done.7, ...), custom_call_target="tpu_custom_call" | custom-call | flops 1879048192 | bytes 14680064 | tf_op jit(solution)/shard_map/chunk/pallas_call | solution.py:69
  36.0 3.1 %copy-done.2 = bf16[4096,896]{1,0:T(8,128)(2,1)S(1)} copy-done((bf16[4096,896]{1,0:T(8,128)(2,1)S(1)}, bf16[4096,896]{1,0:T(8,128)(2,1)}, u32[]{:S(2)}) %copy-start.2) | copy-done | bytes 7340056
  39.1 3.1 %copy-done.8 = bf16[4096,896]{1,0:T(8,128)(2,1)S(1)} copy-done((bf16[4096,896]{1,0:T(8,128)(2,1)S(1)}, bf16[4096,896]{1,0:T(8,128)(2,1)}, u32[]{:S(2)}) %copy-start.8) | copy-done | bytes 7340056
  42.2 11.2 %chunk.11.refs_8_ = f32[2176,64]{1,0:T(8,128)S(1)} custom-call(bf16[64,4096]{1,0:T(8,128)(2,1)} %collective-permute-done.8.refs_0_, bf16[64,4096]{1,0:T(8,128)(2,1)} %collective-permute-done.9.refs_1_, bf16[64,4096]{1,0:T(8,128)(2,1)} %collective-permute-done.refs_2_, ...), custom_call_target="tpu_custom_call", output_to_operand_aliasing={{}: (8, {})} | custom-call | flops 3758096384 | bytes 14680064 | tf_op jit(solution)/shard_map/chunk/pallas_call | solution.py:69
  54.1 10.9 %chunk.12.refs_8_ = f32[2176,64]{1,0:T(8,128)S(1)} custom-call(bf16[64,4096]{1,0:T(8,128)(2,1)S(1)} %collective-permute-done.4.refs_0_, bf16[64,4096]{1,0:T(8,128)(2,1)S(1)} %collective-permute-done.5.refs_1_, bf16[64,4096]{1,0:T(8,128)(2,1)} %collective-permute-done.6.refs_2_, ...), custom_call_target="tpu_custom_call", output_to_operand_aliasing={{}: (8, {})} | custom-call | flops 3758096384 | bytes 14680064 | tf_op jit(solution)/shard_map/chunk/pallas_call | solution.py:69
  76.7 3.1 %copy-done.3 = bf16[4096,896]{1,0:T(8,128)(2,1)S(1)} copy-done((bf16[4096,896]{1,0:T(8,128)(2,1)S(1)}, bf16[4096,896]{1,0:T(8,128)(2,1)}, u32[]{:S(2)}) %copy-start.3) | copy-done | bytes 7340056
  79.8 3.1 %copy-done.9 = bf16[4096,896]{1,0:T(8,128)(2,1)S(1)} copy-done((bf16[4096,896]{1,0:T(8,128)(2,1)S(1)}, bf16[4096,896]{1,0:T(8,128)(2,1)}, u32[]{:S(2)}) %copy-start.9) | copy-done | bytes 7340056
  82.8 11.0 %chunk.13.refs_8_ = f32[2176,64]{1,0:T(8,128)S(1)} custom-call(bf16[64,4096]{1,0:T(8,128)(2,1)} %collective-permute-done.16.refs_0_, bf16[64,4096]{1,0:T(8,128)(2,1)} %collective-permute-done.17.refs_1_, bf16[64,4096]{1,0:T(8,128)(2,1)} %collective-permute-done.2.refs_2_, ...), custom_call_target="tpu_custom_call", output_to_operand_aliasing={{}: (8, {})} | custom-call | flops 3758096384 | bytes 14680064 | tf_op jit(solution)/shard_map/chunk/pallas_call | solution.py:69
  99.3 24.9 %all-gather.1 = bf16[16,144,64]{1,2,0:T(8,128)(2,1)} all-gather(bf16[1,144,64]{1,2,0:T(8,128)(2,1)S(1)} %fusion.3), channel_id=2, replica_groups=mesh['groups'=2,'examples'=16] {'examples'}, dimensions={0}, use_global_device_ids=true | all-gather | bytes 313344 | tf_op jit(solution)/shard_map/all_gather | solution.py:223
  126.2 3.1 %copy-done.4 = bf16[4096,896]{1,0:T(8,128)(2,1)S(1)} copy-done((bf16[4096,896]{1,0:T(8,128)(2,1)S(1)}, bf16[4096,896]{1,0:T(8,128)(2,1)}, u32[]{:S(2)}) %copy-start.4) | copy-done | bytes 7340056
  129.3 3.1 %copy-done.10 = bf16[4096,896]{1,0:T(8,128)(2,1)S(1)} copy-done((bf16[4096,896]{1,0:T(8,128)(2,1)S(1)}, bf16[4096,896]{1,0:T(8,128)(2,1)}, u32[]{:S(2)}) %copy-start.10) | copy-done | bytes 7340056
  132.4 11.0 %chunk.14.refs_8_ = f32[2176,64]{1,0:T(8,128)S(1)} custom-call(bf16[64,4096]{1,0:T(8,128)(2,1)S(1)} %collective-permute-done.12.refs_0_, bf16[64,4096]{1,0:T(8,128)(2,1)} %collective-permute-done.13.refs_1_, bf16[64,4096]{1,0:T(8,128)(2,1)} %collective-permute-done.14.refs_2_, ...), custom_call_target="tpu_custom_call", output_to_operand_aliasing={{}: (8, {})} | custom-call | flops 3758096384 | bytes 14680064 | tf_op jit(solution)/shard_map/chunk/pallas_call | solution.py:69
  144.1 11.2 %chunk.15.left_ref.refs_8_ = f32[2176,64]{1,0:T(8,128)S(1)} custom-call(bf16[64,4096]{1,0:T(8,128)(2,1)} %collective-permute-done.21.refs_0_, bf16[64,4096]{1,0:T(8,128)(2,1)} %collective-permute-done.22.refs_1_, bf16[64,4096]{1,0:T(8,128)(2,1)} %collective-permute-done.10.refs_2_, ...), custom_call_target="tpu_custom_call", output_to_operand_aliasing={{}: (8, {})} | custom-call | flops 3758096384 | bytes 14680064 | tf_op jit(solution)/shard_map/chunk/pallas_call | solution.py:69
  160.2 3.4 %copy-done.5 = bf16[4096,896]{1,0:T(8,128)(2,1)S(1)} copy-done((bf16[4096,896]{1,0:T(8,128)(2,1)S(1)}, bf16[4096,896]{1,0:T(8,128)(2,1)}, u32[]{:S(2)}) %copy-start.5) | copy-done | bytes 7340056
  163.6 3.5 %copy-done.11 = bf16[4096,896]{1,0:T(8,128)(2,1)S(1)} copy-done((bf16[4096,896]{1,0:T(8,128)(2,1)S(1)}, bf16[4096,896]{1,0:T(8,128)(2,1)}, u32[]{:S(2)}) %copy-start.11) | copy-done | bytes 7340056
  167.2 11.2 %chunk.16.refs_6_ = f32[2176,64]{1,0:T(8,128)S(1)} custom-call(bf16[64,4096]{1,0:T(8,128)(2,1)} %collective-permute-done.26.refs_0_, bf16[64,4096]{1,0:T(8,128)(2,1)} %collective-permute-done.27.refs_1_, bf16[64,4096]{1,0:T(8,128)(2,1)} %collective-permute-done.19.refs_2_, ...), custom_call_target="tpu_custom_call", output_to_operand_aliasing={{}: (8, {})} | custom-call | flops 3758096384 | bytes 14680064 | tf_op jit(solution)/shard_map/chunk/pallas_call | solution.py:69
  178.4 8.3 %chunk.17.left_ref.refs_6_ = f32[2176,64]{1,0:T(8,128)S(1)} custom-call(bf16[64,4096]{1,0:T(8,128)(2,1)} %collective-permute-done.24.refs_0_, bf16[64,4096]{1,0:T(8,128)(2,1)} %collective-permute-done.25.refs_1_, f32[1,4096]{1,0:T(1,128)S(1)} %bitcast.50, bf16[4096,896]{1,0:T(8,128)(2,1)S(1)} %copy-done.5, ...), custom_call_target="tpu_custom_call", output_to_operand_aliasing={{}: (6, {})} | custom-call | flops 1879048192 | bytes 14680064 | tf_op jit(solution)/shard_map/chunk/pallas_call | solution.py:69
  189.0 5.8 %copy.67 = bf16[16,144,64]{0,2,1:T(8,128)(2,1)} copy(bf16[16,144,64]{1,2,0:T(8,128)(2,1)} %all-gather.1) | data formatting | bytes 589824 | tf_op jit(solution)/shard_map/optimization_barrier | solution.py:260
  195.7 3.1 %copy-done.6 = bf16[4096,896]{1,0:T(8,128)(2,1)S(1)} copy-done((bf16[4096,896]{1,0:T(8,128)(2,1)S(1)}, bf16[4096,896]{1,0:T(8,128)(2,1)}, u32[]{:S(2)}) %copy-start.6) | copy-done | bytes 7340056
  198.8 3.1 %copy-done.12 = bf16[4096,896]{1,0:T(8,128)(2,1)S(1)} copy-done((bf16[4096,896]{1,0:T(8,128)(2,1)S(1)}, bf16[4096,896]{1,0:T(8,128)(2,1)}, u32[]{:S(2)}) %copy-start.12) | copy-done | bytes 7340056
  201.9 8.2 %chunk.18.refs_6_ = f32[2176,64]{1,0:T(8,128)S(1)} custom-call(bf16[64,4096]{1,0:T(8,128)(2,1)} %collective-permute-done.18.refs_0_, bf16[64,4096]{1,0:T(8,128)(2,1)} %collective-permute-done.23.refs_1_, f32[1,4096]{1,0:T(1,128)S(1)} %bitcast.51, bf16[4096,896]{1,0:T(8,128)(2,1)S(1)} %copy-done.6, ...), custom_call_target="tpu_custom_call", output_to_operand_aliasing={{}: (6, {})} | custom-call | flops 1879048192 | bytes 14680064 | tf_op jit(solution)/shard_map/chunk/pallas_call | solution.py:69
  210.1 8.2 %chunk.19.left_ref = f32[2176,64]{1,0:T(8,128)S(1)} custom-call(bf16[64,4096]{1,0:T(8,128)(2,1)} %collective-permute-done.28.refs_0_, bf16[64,4096]{1,0:T(8,128)(2,1)} %collective-permute-done.29.refs_1_, f32[1,4096]{1,0:T(1,128)S(1)} %bitcast.52, bf16[4096,896]{1,0:T(8,128)(2,1)S(1)} %copy-done.6, ...), custom_call_target="tpu_custom_call", output_to_operand_aliasing={{}: (6, {})} | custom-call | flops 1879048192 | bytes 14680064 | tf_op jit(solution)/shard_map/chunk/pallas_call | solution.py:69
  221.9 9.4 %all_to_all.9 = f32[16,1,256]{2,1,0:T(1,128)S(1)} all-to-all(f32[16,1,256]{2,1,0:T(1,128)S(1)} %copy.70), channel_id=1, replica_groups=mesh['groups'=2,'examples'=16] {'examples'}, dimensions={0} | all-to-all | bytes 32768 | tf_op jit(solution)/shard_map/all_to_all | solution.py:275
  (118 shorter events, 39.1 us)
Async XLA Ops:
  6.5 148.8 %all-gather.5.cloned.1.call-start = ((), (), s32[]{:S(2)}) async-start(), calls=%async_computation.1 | async-start | bytes 1114112 | tf_op jit(solution)/shard_map/all_gather | solution.py:226
  11.5 22.7 %collective-permute-start.6 = (bf16[64,4096]{1,0:T(8,128)(2,1)S(1)}, bf16[64,4096]{1,0:T(8,128)(2,1)}, u32[]{:S(2)}, u32[]{:S(2)}) collective-permute-start(bf16[64,4096]{1,0:T(8,128)(2,1)S(1)} %get-tuple-element.65.refs_1_), channel_id=1, source_target_pairs={{0,4},{1,5},{4,8},{5,9},{8,12},{9,13},{12,14},{13,15},{14,10},{15,... | collective-permute-start | bytes 1572872 | tf_op jit(solution)/shard_map/ppermute | solution.py:204
  28.8 189.6 %all-gather.7.cloned.1.call-start = ((), (), s32[]{:S(2)}) async-start(), calls=%async_computation.2 | async-start | bytes 3145728 | tf_op jit(solution)/shard_map/all_gather | solution.py:261
  29.5 24.0 %collective-permute-start.7 = (bf16[64,4096]{1,0:T(8,128)(2,1)S(1)}, bf16[64,4096]{1,0:T(8,128)(2,1)}, u32[]{:S(2)}, u32[]{:S(2)}) collective-permute-start(bf16[64,4096]{1,0:T(8,128)(2,1)S(1)} %get-tuple-element.65.refs_1_), channel_id=1, source_target_pairs={{4,0},{5,1},{8,4},{9,5},{12,8},{13,9},{14,12},{15,13},{10,14},{11,... | collective-permute-start | bytes 1572872 | tf_op jit(solution)/shard_map/ppermute | solution.py:204
  29.6 24.0 %collective-permute-start.4 = (bf16[64,4096]{1,0:T(8,128)(2,1)}, bf16[64,4096]{1,0:T(8,128)(2,1)S(1)}, u32[]{:S(2)}, u32[]{:S(2)}) collective-permute-start(bf16[64,4096]{1,0:T(8,128)(2,1)} %collective-permute-done.refs_2_), channel_id=1, source_target_pairs={{0,1},{1,0},{2,3},{3,2},{4,5},{5,4},{6,7},{7,6},{8,9},{9,8},{10,11... | collective-permute-start | bytes 1572872 | tf_op jit(solution)/shard_map/ppermute | solution.py:204
  29.7 24.2 %collective-permute-start.5 = (bf16[64,4096]{1,0:T(8,128)(2,1)}, bf16[64,4096]{1,0:T(8,128)(2,1)S(1)}, u32[]{:S(2)}, u32[]{:S(2)}) collective-permute-start(bf16[64,4096]{1,0:T(8,128)(2,1)} %collective-permute-done.1.refs_3_), channel_id=1, source_target_pairs={{0,1},{1,0},{2,3},{3,2},{4,5},{5,4},{6,7},{7,6},{8,9},{9,8},{10,11... | collective-permute-start | bytes 1572872 | tf_op jit(solution)/shard_map/ppermute | solution.py:204
  31.7 33.3 %collective-permute-start.2 = (bf16[64,4096]{1,0:T(8,128)(2,1)}, bf16[64,4096]{1,0:T(8,128)(2,1)}, u32[]{:S(2)}, u32[]{:S(2)}) collective-permute-start(bf16[64,4096]{1,0:T(8,128)(2,1)} %collective-permute-done.refs_2_), channel_id=1, source_target_pairs={{0,4},{1,5},{4,8},{5,9},{8,12},{9,13},{12,14},{13,15},{14,10},{15,... | collective-permute-start | bytes 1572872 | tf_op jit(solution)/shard_map/ppermute | solution.py:204
  34.2 32.5 %collective-permute-start.3 = (bf16[64,4096]{1,0:T(8,128)(2,1)}, bf16[64,4096]{1,0:T(8,128)(2,1)S(1)}, u32[]{:S(2)}, u32[]{:S(2)}) collective-permute-start(bf16[64,4096]{1,0:T(8,128)(2,1)} %collective-permute-done.1.refs_3_), channel_id=1, source_target_pairs={{4,0},{5,1},{8,4},{9,5},{12,8},{13,9},{14,12},{15,13},{10,14},{11,... | collective-permute-start | bytes 1572872 | tf_op jit(solution)/shard_map/ppermute | solution.py:204
  53.5 22.6 %collective-permute-start.16 = (bf16[64,4096]{1,0:T(8,128)(2,1)}, bf16[64,4096]{1,0:T(8,128)(2,1)}, u32[]{:S(2)}, u32[]{:S(2)}) collective-permute-start(bf16[64,4096]{1,0:T(8,128)(2,1)} %collective-permute-done.6.refs_2_), channel_id=1, source_target_pairs={{0,1},{1,0},{2,3},{3,2},{4,5},{5,4},{6,7},{7,6},{8,9},{9,8},{10,11... | collective-permute-start | bytes 1572872 | tf_op jit(solution)/shard_map/ppermute | solution.py:204
  53.6 40.3 %collective-permute-start.14 = (bf16[64,4096]{1,0:T(8,128)(2,1)}, bf16[64,4096]{1,0:T(8,128)(2,1)}, u32[]{:S(2)}, u32[]{:S(2)}) collective-permute-start(bf16[64,4096]{1,0:T(8,128)(2,1)} %collective-permute-done.6.refs_2_), channel_id=1, source_target_pairs={{0,4},{1,5},{4,8},{5,9},{8,12},{9,13},{12,14},{13,15},{14,10},{15,... | collective-permute-start | bytes 1572872 | tf_op jit(solution)/shard_map/ppermute | solution.py:204
  53.9 22.7 %collective-permute-start.17 = (bf16[64,4096]{1,0:T(8,128)(2,1)}, bf16[64,4096]{1,0:T(8,128)(2,1)}, u32[]{:S(2)}, u32[]{:S(2)}) collective-permute-start(bf16[64,4096]{1,0:T(8,128)(2,1)} %collective-permute-done.7.refs_3_), channel_id=1, source_target_pairs={{0,1},{1,0},{2,3},{3,2},{4,5},{5,4},{6,7},{7,6},{8,9},{9,8},{10,11... | collective-permute-start | bytes 1572872 | tf_op jit(solution)/shard_map/ppermute | solution.py:204
  65.0 30.6 %collective-permute-start.15 = (bf16[64,4096]{1,0:T(8,128)(2,1)}, bf16[64,4096]{1,0:T(8,128)(2,1)}, u32[]{:S(2)}, u32[]{:S(2)}) collective-permute-start(bf16[64,4096]{1,0:T(8,128)(2,1)} %collective-permute-done.7.refs_3_), channel_id=1, source_target_pairs={{4,0},{5,1},{8,4},{9,5},{12,8},{13,9},{14,12},{15,13},{10,14},{11,... | collective-permute-start | bytes 1572872 | tf_op jit(solution)/shard_map/ppermute | solution.py:204
  66.7 29.0 %collective-permute-start.12 = (bf16[64,4096]{1,0:T(8,128)(2,1)}, bf16[64,4096]{1,0:T(8,128)(2,1)S(1)}, u32[]{:S(2)}, u32[]{:S(2)}) collective-permute-start(bf16[64,4096]{1,0:T(8,128)(2,1)} %collective-permute-done.2.refs_2_), channel_id=1, source_target_pairs={{0,1},{1,0},{2,3},{3,2},{4,5},{5,4},{6,7},{7,6},{8,9},{9,8},{10,11... | collective-permute-start | bytes 1572872 | tf_op jit(solution)/shard_map/ppermute | solution.py:204
  76.1 48.1 %collective-permute-start.10 = (bf16[64,4096]{1,0:T(8,128)(2,1)}, bf16[64,4096]{1,0:T(8,128)(2,1)}, u32[]{:S(2)}, u32[]{:S(2)}) collective-permute-start(bf16[64,4096]{1,0:T(8,128)(2,1)} %collective-permute-done.2.refs_2_), channel_id=1, source_target_pairs={{0,4},{1,5},{4,8},{5,9},{8,12},{9,13},{12,14},{13,15},{14,10},{15,... | collective-permute-start | bytes 1572872 | tf_op jit(solution)/shard_map/ppermute | solution.py:204
  76.6 47.6 %collective-permute-start.13 = (bf16[64,4096]{1,0:T(8,128)(2,1)S(1)}, bf16[64,4096]{1,0:T(8,128)(2,1)}, u32[]{:S(2)}, u32[]{:S(2)}) collective-permute-start(bf16[64,4096]{1,0:T(8,128)(2,1)S(1)} %collective-permute-done.3.refs_3_), channel_id=1, source_target_pairs={{0,1},{1,0},{2,3},{3,2},{4,5},{5,4},{6,7},{7,6},{8,9},{9,8},{10,11... | collective-permute-start | bytes 1572872 | tf_op jit(solution)/shard_map/ppermute | solution.py:204
  93.9 49.5 %collective-permute-start.11 = (bf16[64,4096]{1,0:T(8,128)(2,1)S(1)}, bf16[64,4096]{1,0:T(8,128)(2,1)}, u32[]{:S(2)}, u32[]{:S(2)}) collective-permute-start(bf16[64,4096]{1,0:T(8,128)(2,1)S(1)} %collective-permute-done.3.refs_3_), channel_id=1, source_target_pairs={{4,0},{5,1},{8,4},{9,5},{12,8},{13,9},{14,12},{15,13},{10,14},{11,... | collective-permute-start | bytes 1572872 | tf_op jit(solution)/shard_map/ppermute | solution.py:204
  95.6 47.9 %collective-permute-start.21 = (bf16[64,4096]{1,0:T(8,128)(2,1)}, bf16[64,4096]{1,0:T(8,128)(2,1)}, u32[]{:S(2)}, u32[]{:S(2)}) collective-permute-start(bf16[64,4096]{1,0:T(8,128)(2,1)} %collective-permute-done.14.refs_2_), channel_id=1, source_target_pairs={{0,1},{1,0},{2,3},{3,2},{4,5},{5,4},{6,7},{7,6},{8,9},{9,8},{10,11... | collective-permute-start | bytes 1572872 | tf_op jit(solution)/shard_map/ppermute | solution.py:204
  95.7 48.1 %collective-permute-start.22 = (bf16[64,4096]{1,0:T(8,128)(2,1)}, bf16[64,4096]{1,0:T(8,128)(2,1)}, u32[]{:S(2)}, u32[]{:S(2)}) collective-permute-start(bf16[64,4096]{1,0:T(8,128)(2,1)} %collective-permute-done.15.refs_3_), channel_id=1, source_target_pairs={{0,1},{1,0},{2,3},{3,2},{4,5},{5,4},{6,7},{7,6},{8,9},{9,8},{10,11... | collective-permute-start | bytes 1572872 | tf_op jit(solution)/shard_map/ppermute | solution.py:204
  124.2 32.6 %collective-permute-start.19 = (bf16[64,4096]{1,0:T(8,128)(2,1)}, bf16[64,4096]{1,0:T(8,128)(2,1)}, u32[]{:S(2)}, u32[]{:S(2)}) collective-permute-start(bf16[64,4096]{1,0:T(8,128)(2,1)} %collective-permute-done.14.refs_2_), channel_id=1, source_target_pairs={{0,4},{1,5},{4,8},{5,9},{8,12},{9,13},{12,14},{13,15},{14,10},{15,... | collective-permute-start | bytes 1572872 | tf_op jit(solution)/shard_map/ppermute | solution.py:204
  124.2 32.6 %collective-permute-start.20 = (bf16[64,4096]{1,0:T(8,128)(2,1)}, bf16[64,4096]{1,0:T(8,128)(2,1)}, u32[]{:S(2)}, u32[]{:S(2)}) collective-permute-start(bf16[64,4096]{1,0:T(8,128)(2,1)} %collective-permute-done.15.refs_3_), channel_id=1, source_target_pairs={{4,0},{5,1},{8,4},{9,5},{12,8},{13,9},{14,12},{15,13},{10,14},{11,... | collective-permute-start | bytes 1572872 | tf_op jit(solution)/shard_map/ppermute | solution.py:204
  143.5 44.1 %collective-permute-start.18 = (bf16[64,4096]{1,0:T(8,128)(2,1)}, bf16[64,4096]{1,0:T(8,128)(2,1)}, u32[]{:S(2)}, u32[]{:S(2)}) collective-permute-start(bf16[64,4096]{1,0:T(8,128)(2,1)} %collective-permute-done.10.refs_2_), channel_id=1, source_target_pairs={{0,4},{1,5},{4,8},{5,9},{8,12},{9,13},{12,14},{13,15},{14,10},{15,... | collective-permute-start | bytes 1572872 | tf_op jit(solution)/shard_map/ppermute | solution.py:204
  158.5 29.2 %collective-permute-start.23 = (bf16[64,4096]{1,0:T(8,128)(2,1)}, bf16[64,4096]{1,0:T(8,128)(2,1)}, u32[]{:S(2)}, u32[]{:S(2)}) collective-permute-start(bf16[64,4096]{1,0:T(8,128)(2,1)} %collective-permute-done.20.refs_3_), channel_id=1, source_target_pairs={{4,0},{5,1},{8,4},{9,5},{12,8},{13,9},{14,12},{15,13},{10,14},{11,... | collective-permute-start | bytes 1572872 | tf_op jit(solution)/shard_map/ppermute | solution.py:204
  187.7 22.4 %collective-permute-start.28 = (bf16[64,4096]{1,0:T(8,128)(2,1)}, bf16[64,4096]{1,0:T(8,128)(2,1)}, u32[]{:S(2)}, u32[]{:S(2)}) collective-permute-start(bf16[64,4096]{1,0:T(8,128)(2,1)} %collective-permute-done.18.refs_0_), channel_id=1, source_target_pairs={{0,1},{1,0},{2,3},{3,2},{4,5},{5,4},{6,7},{7,6},{8,9},{9,8},{10,11... | collective-permute-start | bytes 1572872 | tf_op jit(solution)/shard_map/ppermute | solution.py:204
  187.8 22.3 %collective-permute-start.29 = (bf16[64,4096]{1,0:T(8,128)(2,1)}, bf16[64,4096]{1,0:T(8,128)(2,1)}, u32[]{:S(2)}, u32[]{:S(2)}) collective-permute-start(bf16[64,4096]{1,0:T(8,128)(2,1)} %collective-permute-done.23.refs_1_), channel_id=1, source_target_pairs={{0,1},{1,0},{2,3},{3,2},{4,5},{5,4},{6,7},{7,6},{8,9},{9,8},{10,11... | collective-permute-start | bytes 1572872 | tf_op jit(solution)/shard_map/ppermute | solution.py:204
  (27 other events, 278.5 us)
Sparse Core Ops, SparseCore 0:
  28.9 40.3 all-gather.4
  157.5 31.9 all-gather.6

commit v4 on v3

--- a/solution.py
+++ b/solution.py
@@ -20,68 +20,120 @@
     return list(range(chips))
 
 
-def chunk_body(pieces, *refs):
-    x_refs = refs[:pieces]
-    gain_ref, gate_ref, up_ref, f_ref, out_ref, xn = refs[pieces], *refs[pieces + 1 : pieces + 4], *refs[-2:]
+def prepare_body(width, x_ref, gain_ref, queries_ref, a_ref, b_ref, mine_ref):
+    half = a_ref.shape[0]
+    block = 16
+    for start in range(0, 2 * half, block):
+        x = x_ref[start : start + block, :].astype(jnp.float32)
+        scale = lax.rsqrt(jnp.mean(x * x, axis=-1, keepdims=True) + 1e-05)
+        rows = (x * scale * gain_ref[...]).astype(jnp.bfloat16)
+        if start < half:
+            a_ref[start : start + block, :] = rows
+        else:
+            b_ref[start - half : start - half + block, :] = rows
+    offset = pl.multiple_of(lax.axis_index("groups") * width, width)
+    mine_ref[...] = queries_ref[:, pl.ds(offset, width)]
+
+
+def prepare(x, gain, queries, groups):
+    span, depth = x.shape
+    width = depth // groups
+    vmem = pl.BlockSpec(memory_space=pltpu.VMEM)
+    rows = jax.ShapeDtypeStruct((span // 2, depth), jnp.bfloat16)
+    return pl.pallas_call(
+        functools.partial(prepare_body, width),
+        in_specs=[vmem] * 3,
+        out_specs=[vmem] * 3,
+        out_shape=[rows, rows, jax.ShapeDtypeStruct((queries.shape[0], width), queries.dtype)],
+        compiler_params=pltpu.CompilerParams(vmem_limit_bytes=16 * MIB),
+        name="prepare",
+    )(x, gain, queries)
+
+
+def chunk_body(pieces, tiles, packing, *refs):
+    x_refs, refs = refs[:pieces], refs[pieces:]
+    if packing:
+        gate_ref, up_ref, f_ref, out_ref, w_ref, xn, even, odd = refs
+    else:
+        w_ref, f_ref, _, out_ref, xn, even, odd = refs
     rows = x_refs[0].shape[0]
     step = pl.program_id(0)
+
+    def first_product(into):
+        if packing:
+            w_ref[0, :, :LANES] = gate_ref[...]
+            w_ref[0, :, LANES:] = up_ref[...]
+        into[...] = jnp.dot(xn[...], w_ref[0], preferred_element_type=jnp.float32)
+
+    def second_product(source):
+        gate, up = source[:, :LANES], source[:, LANES:]
+        hidden = (jax.nn.silu(gate) * up).astype(jnp.bfloat16)
+        part = jnp.dot(hidden, f_ref[...], preferred_element_type=jnp.float32)
+        out_ref[...] = jnp.where(step == 1, 0.0, out_ref[...]) + part
 
     @pl.when(step == 0)
     def _():
         for k, ref in enumerate(x_refs):
-            x = ref[...].astype(jnp.float32)
-            scale = lax.rsqrt(jnp.mean(x * x, axis=-1, keepdims=True) + 1e-05)
-            xn[k * rows : (k + 1) * rows, :] = (x * scale * gain_ref[...]).astype(jnp.bfloat16)
-
-    weights = jnp.concatenate([gate_ref[...], up_ref[...]], axis=1)
-    both = jnp.dot(xn[...], weights, preferred_element_type=jnp.float32)
-    gate, up = both[:, :LANES], both[:, LANES:]
-    hidden = (jax.nn.silu(gate) * up).astype(jnp.bfloat16)
-    part = jnp.dot(hidden, f_ref[...], preferred_element_type=jnp.float32)
-
-    @pl.when(step == 0)
+            xn[k * rows : (k + 1) * rows, :] = ref[...]
+        first_product(even)
+
+    @pl.when((step > 0) & (step < tiles) & (step % 2 == 1))
     def _():
-        out_ref[...] = part
-
-    @pl.when(step > 0)
+        second_product(even)
+        first_product(odd)
+
+    @pl.when((step > 0) & (step < tiles) & (step % 2 == 0))
     def _():
-        out_ref[...] += part
-
-
-def chunk(xs, gain, gate_weight, up_weight, in_factor, left, index, tokens):
+        second_product(odd)
+        first_product(even)
+
+    @pl.when(step == tiles)
+    def _():
+        second_product(even if tiles % 2 == 1 else odd)
+
+
+def chunk(xs, weights, in_factor, left, index, tokens):
+    packing = left is None
     pieces = len(xs)
     rows, depth = xs[0].shape
     units, order = in_factor.shape
     tiles = units // LANES
     total = pieces * rows
-    operands = [*xs, gain, gate_weight, up_weight, in_factor]
-    in_specs = [pl.BlockSpec((rows, depth), lambda i: (0, 0))] * pieces + [
-        pl.BlockSpec((1, depth), lambda i: (0, 0)),
-        pl.BlockSpec((depth, LANES), lambda i: (0, i)),
-        pl.BlockSpec((depth, LANES), lambda i: (0, i)),
-        pl.BlockSpec((LANES, order), lambda i: (i, 0)),
-    ]
-    aliases = {}
-    if left is not None:
-        aliases = {len(operands): 0}
-        operands.append(left)
+    tile = pl.BlockSpec((1, depth, 2 * LANES), lambda i: (jnp.minimum(i, tiles - 1), 0, 0))
+    in_specs = [pl.BlockSpec((rows, depth), lambda i: (0, 0))] * pieces
+    out_specs = [pl.BlockSpec((total, order), lambda i: (index, 0))]
+    out_shape = [jax.ShapeDtypeStruct((tokens, order), jnp.float32)]
+    if packing:
+        operands = [*xs, *weights, in_factor]
+        in_specs += [pl.BlockSpec((depth, LANES), lambda i: (0, jnp.minimum(i, tiles - 1)))] * 2
+        out_specs.append(tile)
+        out_shape.append(jax.ShapeDtypeStruct((tiles, depth, 2 * LANES), jnp.bfloat16))
+        aliases = {}
+    else:
+        operands = [*xs, weights, in_factor, left]
+        in_specs.append(tile)
+        aliases = {pieces + 2: 0}
+    in_specs.append(pl.BlockSpec((LANES, order), lambda i: (jnp.maximum(i - 1, 0), 0)))
+    if not packing:
         in_specs.append(pl.BlockSpec(memory_space=pl.ANY))
-    return pl.pallas_call(
-        functools.partial(chunk_body, pieces),
-        grid=(tiles,),
+    made = pl.pallas_call(
+        functools.partial(chunk_body, pieces, tiles, packing),
+        grid=(tiles + 1,),
         in_specs=in_specs,
-        out_specs=pl.BlockSpec((total, order), lambda i: (index, 0)),
-        out_shape=jax.ShapeDtypeStruct((tokens, order), jnp.float32),
-        scratch_shapes=[pltpu.VMEM((total, depth), jnp.bfloat16)],
+        out_specs=out_specs,
+        out_shape=out_shape,
+        scratch_shapes=[pltpu.VMEM((total, depth), jnp.bfloat16)]
+        + [pltpu.VMEM((total, 2 * LANES), jnp.float32)] * 2,
         input_output_aliases=aliases,
-        compiler_params=pltpu.CompilerParams(vmem_limit_bytes=18 * MIB),
+        compiler_params=pltpu.CompilerParams(vmem_limit_bytes=50 * MIB),
         cost_estimate=pl.CostEstimate(
             flops=2 * total * depth * tiles * 2 * LANES,
-            bytes_accessed=4 * depth * units,
+            bytes_accessed=(8 if packing else 4) * depth * units,
             transcendentals=0,
         ),
-        name="chunk",
+        name="first_chunk" if packing else "chunk",
     )(*operands)
+    return made if packing else made[0]
 
 
 def one_sketch(left_ref, masked, at, half):
@@ -112,9 +164,11 @@
     return made.reshape(len(places), order * order)
 
 
-def finish_body(places, half, names, left_ref, side_ref, early_ref, queries_ref, ids_ref, out_ref, twice, flat):
+def finish_body(places, half, groups, names, left_ref, side_ref, early_ref, *refs):
+    query_refs, (ids_ref, out_ref, twice, flat, whole) = refs[:groups], refs[groups:]
     order = left_ref.shape[1]
     early = early_ref.shape[0]
+    slots = flat.shape[1]
     lane = lax.broadcasted_iota(jnp.int32, (order // 2, 2 * order), 1)
     for r, at in enumerate(places):
         masked = side_ref[names[early + r], : 2 * half, :]
@@ -124,23 +178,23 @@
         odd = twice[pl.ds(1, order // 2, 2), :]
         flat[:, r, :] = jnp.where(lane < order, even, odd)
     late = jnp.concatenate([flat[c] for c in range(order // 2)], axis=1).astype(jnp.bfloat16)
-    queries = queries_ref[...]
-    count = queries.shape[0]
-    value = lax.broadcasted_iota(jnp.int32, (NVAL, count), 0)
+    whole[...] = jnp.concatenate([late, early_ref[...]], axis=0)
+
+    width = query_refs[0].shape[1]
+    group = lax.axis_index("groups")
+    scores = 0.0
+    for r, ref in enumerate(query_refs):
+        offset = pl.multiple_of(lax.rem(group + r, groups) * width, width)
+        scores += lax.dot_general(whole[:, pl.ds(offset, width)], ref[...], NT, preferred_element_type=jnp.float32)
+    value = lax.broadcasted_iota(jnp.int32, (NVAL, ids_ref.shape[1]), 0)
     members = (value == ids_ref[...]).astype(jnp.bfloat16)
-
-    def influence(sketch):
-        rest = lax.dot_general(sketch, queries, NT, preferred_element_type=jnp.float32)
-        total = 0.0
-        for _ in range(3):
-            part = rest.astype(jnp.bfloat16)
-            rest = rest - part.astype(jnp.float32)
-            total += lax.dot_general(part, members, NT, preferred_element_type=jnp.float32)
-        return total
-
-    rows = influence(jnp.concatenate([late, early_ref[...]], axis=0))
+    rows = 0.0
+    for _ in range(3):
+        part = scores.astype(jnp.bfloat16)
+        scores = scores - part.astype(jnp.float32)
+        rows += lax.dot_general(part, members, NT, preferred_element_type=jnp.float32)
     for r in range(early):
-        out_ref[pl.ds(names[r], 1), :] = rows[flat.shape[1] + r : flat.shape[1] + r + 1, :]
+        out_ref[pl.ds(names[r], 1), :] = rows[slots + r : slots + r + 1, :]
     for r in range(len(places)):
         out_ref[pl.ds(names[early + r], 1), :] = rows[r : r + 1, :]
 
@@ -150,17 +204,18 @@
     vmem = pl.BlockSpec(memory_space=pltpu.VMEM)
     slots = -(-len(places) // 8) * 8
     return pl.pallas_call(
-        functools.partial(finish_body, places, half),
-        in_specs=[pl.BlockSpec(memory_space=pltpu.SMEM)] + [vmem] * 5,
+        functools.partial(finish_body, places, half, len(queries)),
+        in_specs=[pl.BlockSpec(memory_space=pltpu.SMEM)] + [vmem] * (4 + len(queries)),
         out_specs=vmem,
         out_shape=jax.ShapeDtypeStruct((names.shape[0], NVAL), jnp.float32),
         scratch_shapes=[
             pltpu.VMEM((order, 2 * order), jnp.float32),
             pltpu.VMEM((order // 2, slots, 2 * order), jnp.float32),
+            pltpu.VMEM((slots + early.shape[0], order * order), jnp.bfloat16),
         ],
         compiler_params=pltpu.CompilerParams(vmem_limit_bytes=16 * MIB),
         name="finish",
-    )(names, left, side, early, queries, ids)
+    )(names, left, side, early, *queries, ids)
 
 
 def local(
@@ -197,33 +252,33 @@
         gate_weight = jnp.pad(gate_weight, ((0, 0), (0, short)))
         up_weight = jnp.pad(up_weight, ((0, 0), (0, short)))
         in_factor = jnp.pad(in_factor, ((0, short), (0, 0)))
-    gain = norm_gain[None, :]
     tokens = 2 * span * chips + span
 
     def send(x, way):
         return lax.ppermute(x, "examples", way)
 
     def project(xs, left, index):
-        return chunk(xs, gain, gate_weight, up_weight, in_factor, left, index, tokens)
-
-    x_a, x_b = layer_inputs[:half], layer_inputs[half:]
+        return chunk(xs, weights, in_factor, left, index, tokens)
+
+    x_a, x_b, mine = prepare(layer_inputs, norm_gain[None, :], queries, groups)
     coming = {
         1: (send(x_a, forward), send(x_a, backward)),
         2: (send(x_b, forward), send(x_b, backward)),
     }
     swapped = tuple(send(x, other_core) for x in (x_a, x_b))
-    left = project((x_a, x_b), None, 1)
-
-    out_grads, queries, query_ids, left = lax.optimization_barrier((out_grads, queries, query_ids, left))
+    weights = (gate_weight, up_weight)
+    left, weights = project((x_a, x_b), None, 1)
+
+    out_grads, query_ids, mine, left = lax.optimization_barrier((out_grads, query_ids, mine, left))
     right = jnp.dot(out_grads, out_factor, preferred_element_type=jnp.float32)
     live = jnp.arange(span, dtype=jnp.int32)[:, None] < example_lengths[0]
     masked = jnp.where(live, right, 0.0).astype(jnp.bfloat16)
-    nq = queries.shape[0]
-    ids_row = jnp.pad(query_ids.astype(jnp.bfloat16)[None, :], ((0, 15), (0, order - nq)))
-    side = lax.all_gather(jnp.concatenate([masked, ids_row], axis=0), "examples", axis=0)
-    share = nq // groups
-    mine = lax.dynamic_slice_in_dim(queries, lax.axis_index("groups") * share, share, axis=0)
-    mine = lax.all_gather(mine, "examples", axis=0, tiled=True)
+    nq, width = mine.shape
+    masked = masked.reshape(span * order // width, width)
+    ids_row = jnp.pad(query_ids.astype(jnp.bfloat16)[None, :], ((0, 0), (0, width - nq)))
+    more = jnp.concatenate([mine, masked, ids_row], axis=0)
+    more = jnp.pad(more, ((0, -more.shape[0] % 8), (0, 0)))
+    more = lax.all_gather(more, "examples", axis=0)
 
     def pair(where):
         first = jnp.array(ring, jnp.int32)[where % chips] * 2
@@ -257,10 +312,14 @@
         if k < chips - 1:
             left = project(before + own, left, k)
         if k == chips - 3:
-            side, mine, left = lax.optimization_barrier((side, mine, left))
-            all_queries = lax.all_gather(mine, "groups", axis=0, tiled=True)
-            ids = side[:, span, :nq].reshape(devices, groups, share).swapaxes(0, 1).reshape(1, devices * nq)
-            ids = ids.astype(jnp.int32)
+            more, left = lax.optimization_barrier((more, left))
+            mine = more[:, :nq].reshape(devices * nq, width)
+            side = more[:, nq : nq + masked.shape[0]].reshape(devices, span, order)
+            shares = [mine]
+            for r in range(1, groups):
+                way = [((g + r) % groups, g) for g in range(groups)]
+                shares.append(lax.ppermute(mine, "groups", way))
+            ids = more[:, nq + masked.shape[0], :nq].astype(jnp.int32).reshape(1, devices * nq)
             ready = devices - 6
             early = [sketches(spots[:ready], half, names[:ready], left, side)]
         if k == chips - 2:
@@ -271,7 +330,7 @@
     left = project(own, left, 2 * chips - 1)
     left = project(swapped, left, 2 * chips)
 
-    partial = finish(spots[-2:], half, names, left, side, early, all_queries, ids)
+    partial = finish(spots[-2:], half, names, left, side, early, shares, ids)
     shares = lax.all_to_all(partial, "examples", split_axis=0, concat_axis=0, tiled=True)
     return jnp.sum(shares, axis=0, keepdims=True)
 

time: 240 us -> 212 us (0.88)
  local copies, waits for them, and re-layouts: 51.8 us -> 14.9 us
  waiting for transfers between devices: 0.67 us -> 23.4 us
  blocking collectives: 34.3 us -> 12.3 us
  Pallas kernels: 102 us -> 107 us
    unnamed x39 -> x31, local copies, waits for them, and re-layouts: 39.6 us -> 7.31 us
    all_gather x1 -> x0, blocking collectives: 24.9 us -> none  [local(): lax.all_gather(jnp.concatenate([masked, ids_row], axis=0), 'examples', ax...]
    ppermute x30, waiting for transfers between devices: 0.6 us -> 23.4 us  [send(): return lax.ppermute(x, 'examples', way)]
    optimization_barrier x2 -> x0, local copies, waits for them, and re-layouts: 7.25 us -> none  [local(): side, mine, left = lax.optimization_barrier((side, mine, left))]
    pallas_call x11 -> x12, Pallas kernels: 101 us -> 105 us  [the longest x10 102 us: chunk(): pl.pallas_call(functools.partial(chunk_body, pieces, tiles, packing), gri...]
    all_to_all x1, blocking collectives: 9.41 us -> 12.3 us  [local(): lax.all_to_all(partial, 'examples', split_axis=0, concat_axis=0, tiled=True)]
  transfers between devices with their start and end apart: 32 -> 32, of which waited for: 1 -> 3; matrix products, arithmetic and copies ran while one was open for 6% -> 4% of each run, Pallas kernels for 42% -> 42%
where the time goes in v4:
time: 212 us; the launch traced here: 210 us
  Pallas kernels  107 us (50%)
  between operations  26.2 us (12%)
  waiting for transfers between devices  23.4 us (11%)
  starting transfers between devices  22.6 us (11%)
  local copies, waits for them, and re-layouts  14.9 us (7%)
  blocking collectives  12.3 us (6%)
  other arithmetic  3.74 us (2%)
    pallas_call x10, Pallas kernels, chunk(): pl.pallas_call(functools.partial(chunk_body, pieces, tiles, packing), gri...  102 us
    ppermute x30, waiting for transfers between devices, send(): return lax.ppermute(x, 'examples', way)  23.4 us
    ppermute x30, starting transfers between devices, send(): return lax.ppermute(x, 'examples', way)  21.1 us
    all_to_all x1, blocking collectives, local(): lax.all_to_all(partial, 'examples', split_axis=0, concat_axis=0, tiled=True)  12.3 us
    unnamed x31, local copies, waits for them, and re-layouts  7.31 us
  transfers between devices with their start and end apart: 32, of which 3 were waited for; matrix products, arithmetic and copies ran while one was open for 4% of the time, Pallas kernels for 42%

profile of v4, /device:TPU:0, one launch (start us, length us, event | category | flops | bytes accessed | tf_op | source)
XLA Modules:
  0.0 210.4 jit_solution(6925404439017944033)
XLA Ops:
  11.1 15.4 %first_chunk.1 = (f32[2176,64]{1,0:T(8,128)S(1)}, bf16[7,4096,256]{2,1,0:T(8,128)(2,1)}) custom-call(bf16[64,4096]{1,0:T(8,128)(2,1)S(1)} %get-tuple-element.39.refs_0_, bf16[64,4096]{1,0:T(8,128)(2,1)S(1)} %get-tuple-element.41.refs_1_, bf16[4096,896]{1,0:T(8,128)(2,1)} %refs_2_.1, bf16[4096,896]{1,0:T(8,128)(2,1)} %refs_3_.4, ...), custom_call_target="tpu_custom_call" | custom-call | flops 1879048192 | bytes 29360128 | tf_op jit(solution)/shard_map/first_chunk/pallas_call | solution.py:119
  29.2 3.1 %collective-permute-start = (bf16[64,4096]{1,0:T(8,128)(2,1)S(1)}, bf16[64,4096]{1,0:T(8,128)(2,1)S(1)}, u32[]{:S(2)}, u32[]{:S(2)}) collective-permute-start(bf16[64,4096]{1,0:T(8,128)(2,1)S(1)} %get-tuple-element.39.refs_0_), channel_id=1, source_target_pairs={{0,4},{1,5},{4,8},{5,9},{8,12},{9,13},{12,14},{13,15},{14,10},{15,... | collective-permute-start | bytes 1572872 | tf_op jit(solution)/shard_map/ppermute | solution.py:258
  32.8 2.0 collective-permute-start.6
  34.8 11.7 %collective-permute-done.refs_2_ = bf16[64,4096]{1,0:T(8,128)(2,1)S(1)} collective-permute-done((bf16[64,4096]{1,0:T(8,128)(2,1)S(1)}, bf16[64,4096]{1,0:T(8,128)(2,1)S(1)}, u32[]{:S(2)}, u32[]{:S(2)}) %collective-permute-start) | collective-permute-done | bytes 524320 | tf_op jit(solution)/shard_map/ppermute | solution.py:258
  46.5 1.6 collective-permute-start.7
  49.5 10.6 %collective-permute-done.6.refs_2_ = bf16[64,4096]{1,0:T(8,128)(2,1)S(1)} collective-permute-done((bf16[64,4096]{1,0:T(8,128)(2,1)S(1)}, bf16[64,4096]{1,0:T(8,128)(2,1)S(1)}, u32[]{:S(2)}, u32[]{:S(2)}) %collective-permute-start.6) | collective-permute-done | bytes 524320 | tf_op jit(solution)/shard_map/ppermute | solution.py:258
  61.4 9.7 %chunk.9.refs_6_ = f32[2176,64]{1,0:T(8,128)S(1)} custom-call(bf16[64,4096]{1,0:T(8,128)(2,1)S(1)} %collective-permute-done.8.refs_0_, bf16[64,4096]{1,0:T(8,128)(2,1)S(1)} %collective-permute-done.9.refs_1_, bf16[64,4096]{1,0:T(8,128)(2,1)S(1)} %collective-permute-done.refs_2_, ...), custom_call_target="tpu_custom_call", output_to_operand_aliasing={{}: (6, {})} | custom-call | flops 3758096384 | bytes 14680064 | tf_op jit(solution)/shard_map/chunk/pallas_call | solution.py:119
  73.0 9.7 %chunk.10.refs_6_ = f32[2176,64]{1,0:T(8,128)S(1)} custom-call(bf16[64,4096]{1,0:T(8,128)(2,1)S(1)} %collective-permute-done.4.refs_0_, bf16[64,4096]{1,0:T(8,128)(2,1)S(1)} %collective-permute-done.5.refs_1_, bf16[64,4096]{1,0:T(8,128)(2,1)S(1)} %collective-permute-done.6.refs_2_, ...), custom_call_target="tpu_custom_call", output_to_operand_aliasing={{}: (6, {})} | custom-call | flops 3758096384 | bytes 14680064 | tf_op jit(solution)/shard_map/chunk/pallas_call | solution.py:119
  84.1 1.5 collective-permute-start.10
  85.7 9.8 %chunk.11.refs_6_ = f32[2176,64]{1,0:T(8,128)S(1)} custom-call(bf16[64,4096]{1,0:T(8,128)(2,1)S(1)} %collective-permute-done.16.refs_0_, bf16[64,4096]{1,0:T(8,128)(2,1)S(1)} %collective-permute-done.17.refs_1_, bf16[64,4096]{1,0:T(8,128)(2,1)} %collective-permute-done.2.refs_2_, ...), custom_call_target="tpu_custom_call", output_to_operand_aliasing={{}: (6, {})} | custom-call | flops 3758096384 | bytes 14680064 | tf_op jit(solution)/shard_map/chunk/pallas_call | solution.py:119
  110.9 2.1 collective-permute-start.19
  114.0 10.0 %chunk.12.refs_6_ = f32[2176,64]{1,0:T(8,128)S(1)} custom-call(bf16[64,4096]{1,0:T(8,128)(2,1)S(1)} %copy-done.6, bf16[64,4096]{1,0:T(8,128)(2,1)} %collective-permute-done.13.refs_1_, bf16[64,4096]{1,0:T(8,128)(2,1)S(1)} %collective-permute-done.14.refs_2_, bf16[64,4096]{1,0:T(8,128)(2,1)} %collective-permute-done.15.refs_3_, ...), custom_call_target="tpu_custom_call", output_to_operand_aliasing={{}: (6, {})} | custom-call | flops 3758096384 | bytes 14680064 | tf_op jit(solution)/shard_map/chunk/pallas_call | solution.py:119
  124.1 2.1 collective-permute-start.18
  126.3 10.3 %chunk.13.left_ref.refs_6_ = f32[2176,64]{1,0:T(8,128)S(1)} custom-call(bf16[64,4096]{1,0:T(8,128)(2,1)} %collective-permute-done.21.refs_0_, bf16[64,4096]{1,0:T(8,128)(2,1)} %collective-permute-done.22.refs_1_, bf16[64,4096]{1,0:T(8,128)(2,1)} %collective-permute-done.10.refs_2_, ...), custom_call_target="tpu_custom_call", output_to_operand_aliasing={{}: (6, {})} | custom-call | flops 3758096384 | bytes 14680064 | tf_op jit(solution)/shard_map/chunk/pallas_call | solution.py:119
  136.6 1.9 slice.13
  142.9 1.7 reshape.53
  144.7 1.5 collective-permute-start.30
  146.2 10.3 %chunk.14.refs_4_ = f32[2176,64]{1,0:T(8,128)S(1)} custom-call(bf16[64,4096]{1,0:T(8,128)(2,1)} %collective-permute-done.26.refs_0_, bf16[64,4096]{1,0:T(8,128)(2,1)} %collective-permute-done.27.refs_1_, bf16[64,4096]{1,0:T(8,128)(2,1)} %collective-permute-done.19.refs_2_, ...), custom_call_target="tpu_custom_call", output_to_operand_aliasing={{}: (6, {})} | custom-call | flops 3758096384 | bytes 14680064 | tf_op jit(solution)/shard_map/chunk/pallas_call | solution.py:119
  156.5 8.9 %chunk.15.left_ref.refs_4_ = f32[2176,64]{1,0:T(8,128)S(1)} custom-call(bf16[64,4096]{1,0:T(8,128)(2,1)} %collective-permute-done.24.refs_0_, bf16[64,4096]{1,0:T(8,128)(2,1)} %collective-permute-done.25.refs_1_, bf16[7,4096,256]{2,1,0:T(8,128)(2,1)} %get-tuple-element.46.refs_4_.refs_2_, ...), custom_call_target="tpu_custom_call", output_to_operand_aliasing={{}: (4, {})} | custom-call | flops 1879048192 | bytes 14680064 | tf_op jit(solution)/shard_map/chunk/pallas_call | solution.py:119
  166.4 1.6 pad_maximum_fusion.early_ref
  170.1 8.9 %chunk.16.refs_4_ = f32[2176,64]{1,0:T(8,128)S(1)} custom-call(bf16[64,4096]{1,0:T(8,128)(2,1)} %collective-permute-done.18.refs_0_, bf16[64,4096]{1,0:T(8,128)(2,1)} %collective-permute-done.23.refs_1_, bf16[7,4096,256]{2,1,0:T(8,128)(2,1)} %get-tuple-element.46.refs_4_.refs_2_, ...), custom_call_target="tpu_custom_call", output_to_operand_aliasing={{}: (4, {})} | custom-call | flops 1879048192 | bytes 14680064 | tf_op jit(solution)/shard_map/chunk/pallas_call | solution.py:119
  179.0 8.9 %chunk.17.left_ref = f32[2176,64]{1,0:T(8,128)S(1)} custom-call(bf16[64,4096]{1,0:T(8,128)(2,1)} %collective-permute-done.28.refs_0_, bf16[64,4096]{1,0:T(8,128)(2,1)} %collective-permute-done.29.refs_1_, bf16[7,4096,256]{2,1,0:T(8,128)(2,1)} %get-tuple-element.46.refs_4_.refs_2_, ...), custom_call_target="tpu_custom_call", output_to_operand_aliasing={{}: (4, {})} | custom-call | flops 1879048192 | bytes 14680064 | tf_op jit(solution)/shard_map/chunk/pallas_call | solution.py:119
  188.0 2.6 %finish.1 = f32[16,256]{1,0:T(8,128)S(1)} custom-call(s32[16]{0:T(128)S(1)} %stack.71.names, f32[2176,64]{1,0:T(8,128)S(1)} %chunk.17.left_ref, bf16[16,128,64]{2,1,0:T(8,128)(2,1)S(1)} %copy-done.3, bf16[14,4096]{1,0:T(8,128)(2,1)S(1)} %copy-done.7, bf16[256,2048]{1,0:T(8,128)(2,1)S(1)} %bitcast.37, bf16[256,2048]{1,0:T(8,128)(2,1)} %collective-permute-done.30.refs_1_, ...), custom_call_target="tpu_custom_call" | custom-call | tf_op jit(solution)/shard_map/finish/pallas_call | solution.py:206
  190.6 12.3 %all_to_all.9 = f32[16,1,256]{2,1,0:T(1,128)S(1)} all-to-all(f32[16,1,256]{2,1,0:T(1,128)S(1)} %copy.63), channel_id=1, replica_groups=mesh['groups'=2,'examples'=16] {'examples'}, dimensions={0} | all-to-all | bytes 32768 | tf_op jit(solution)/shard_map/all_to_all | solution.py:334
  (109 shorter events, 26.0 us)
Async XLA Ops:
  6.5 130.1 %all-gather.3.cloned.1.call-start = ((), (), s32[]{:S(2)}) async-start(), calls=%async_computation.1 | async-start | bytes 1671168 | tf_op jit(solution)/shard_map/all_gather | solution.py:281
  29.2 17.3 %collective-permute-start = (bf16[64,4096]{1,0:T(8,128)(2,1)S(1)}, bf16[64,4096]{1,0:T(8,128)(2,1)S(1)}, u32[]{:S(2)}, u32[]{:S(2)}) collective-permute-start(bf16[64,4096]{1,0:T(8,128)(2,1)S(1)} %get-tuple-element.39.refs_0_), channel_id=1, source_target_pairs={{0,4},{1,5},{4,8},{5,9},{8,12},{9,13},{12,14},{13,15},{14,10},{15,... | collective-permute-start | bytes 1572872 | tf_op jit(solution)/shard_map/ppermute | solution.py:258
  32.3 16.3 %collective-permute-start.9 = (bf16[64,4096]{1,0:T(8,128)(2,1)S(1)}, bf16[64,4096]{1,0:T(8,128)(2,1)S(1)}, u32[]{:S(2)}, u32[]{:S(2)}) collective-permute-start(bf16[64,4096]{1,0:T(8,128)(2,1)S(1)} %get-tuple-element.41.refs_1_), channel_id=1, source_target_pairs={{0,1},{1,0},{2,3},{3,2},{4,5},{5,4},{6,7},{7,6},{8,9},{9,8},{10,11... | collective-permute-start | bytes 1572872 | tf_op jit(solution)/shard_map/ppermute | solution.py:258
  32.8 27.3 %collective-permute-start.6 = (bf16[64,4096]{1,0:T(8,128)(2,1)S(1)}, bf16[64,4096]{1,0:T(8,128)(2,1)S(1)}, u32[]{:S(2)}, u32[]{:S(2)}) collective-permute-start(bf16[64,4096]{1,0:T(8,128)(2,1)S(1)} %get-tuple-element.41.refs_1_), channel_id=1, source_target_pairs={{0,4},{1,5},{4,8},{5,9},{8,12},{9,13},{12,14},{13,15},{14,10},{15,... | collective-permute-start | bytes 1572872 | tf_op jit(solution)/shard_map/ppermute | solution.py:258
  46.5 24.7 %collective-permute-start.7 = (bf16[64,4096]{1,0:T(8,128)(2,1)S(1)}, bf16[64,4096]{1,0:T(8,128)(2,1)S(1)}, u32[]{:S(2)}, u32[]{:S(2)}) collective-permute-start(bf16[64,4096]{1,0:T(8,128)(2,1)S(1)} %get-tuple-element.41.refs_1_), channel_id=1, source_target_pairs={{4,0},{5,1},{8,4},{9,5},{12,8},{13,9},{14,12},{15,13},{10,14},{11,... | collective-permute-start | bytes 1572872 | tf_op jit(solution)/shard_map/ppermute | solution.py:258
  48.1 23.1 %collective-permute-start.4 = (bf16[64,4096]{1,0:T(8,128)(2,1)S(1)}, bf16[64,4096]{1,0:T(8,128)(2,1)S(1)}, u32[]{:S(2)}, u32[]{:S(2)}) collective-permute-start(bf16[64,4096]{1,0:T(8,128)(2,1)S(1)} %collective-permute-done.refs_2_), channel_id=1, source_target_pairs={{0,1},{1,0},{2,3},{3,2},{4,5},{5,4},{6,7},{7,6},{8,9},{9,8},{10,11... | collective-permute-start | bytes 1572872 | tf_op jit(solution)/shard_map/ppermute | solution.py:258
  48.1 23.6 %collective-permute-start.5 = (bf16[64,4096]{1,0:T(8,128)(2,1)S(1)}, bf16[64,4096]{1,0:T(8,128)(2,1)S(1)}, u32[]{:S(2)}, u32[]{:S(2)}) collective-permute-start(bf16[64,4096]{1,0:T(8,128)(2,1)S(1)} %collective-permute-done.1.refs_3_), channel_id=1, source_target_pairs={{0,1},{1,0},{2,3},{3,2},{4,5},{5,4},{6,7},{7,6},{8,9},{9,8},{10,11... | collective-permute-start | bytes 1572872 | tf_op jit(solution)/shard_map/ppermute | solution.py:258
  48.6 34.1 %collective-permute-start.2 = (bf16[64,4096]{1,0:T(8,128)(2,1)S(1)}, bf16[64,4096]{1,0:T(8,128)(2,1)}, u32[]{:S(2)}, u32[]{:S(2)}) collective-permute-start(bf16[64,4096]{1,0:T(8,128)(2,1)S(1)} %collective-permute-done.refs_2_), channel_id=1, source_target_pairs={{0,4},{1,5},{4,8},{5,9},{8,12},{9,13},{12,14},{13,15},{14,10},{15,... | collective-permute-start | bytes 1572872 | tf_op jit(solution)/shard_map/ppermute | solution.py:258
  60.1 23.5 %collective-permute-start.3 = (bf16[64,4096]{1,0:T(8,128)(2,1)S(1)}, bf16[64,4096]{1,0:T(8,128)(2,1)S(1)}, u32[]{:S(2)}, u32[]{:S(2)}) collective-permute-start(bf16[64,4096]{1,0:T(8,128)(2,1)S(1)} %collective-permute-done.1.refs_3_), channel_id=1, source_target_pairs={{4,0},{5,1},{8,4},{9,5},{12,8},{13,9},{14,12},{15,13},{10,14},{11,... | collective-permute-start | bytes 1572872 | tf_op jit(solution)/shard_map/ppermute | solution.py:258
  71.8 23.7 %collective-permute-start.14 = (bf16[64,4096]{1,0:T(8,128)(2,1)S(1)}, bf16[64,4096]{1,0:T(8,128)(2,1)S(1)}, u32[]{:S(2)}, u32[]{:S(2)}) collective-permute-start(bf16[64,4096]{1,0:T(8,128)(2,1)S(1)} %collective-permute-done.6.refs_2_), channel_id=1, source_target_pairs={{0,4},{1,5},{4,8},{5,9},{8,12},{9,13},{12,14},{13,15},{14,10},{15,... | collective-permute-start | bytes 1572872 | tf_op jit(solution)/shard_map/ppermute | solution.py:258
  83.6 27.3 %collective-permute-start.13 = (bf16[64,4096]{1,0:T(8,128)(2,1)S(1)}, bf16[64,4096]{1,0:T(8,128)(2,1)}, u32[]{:S(2)}, u32[]{:S(2)}) collective-permute-start(bf16[64,4096]{1,0:T(8,128)(2,1)S(1)} %collective-permute-done.3.refs_3_), channel_id=1, source_target_pairs={{0,1},{1,0},{2,3},{3,2},{4,5},{5,4},{6,7},{7,6},{8,9},{9,8},{10,11... | collective-permute-start | bytes 1572872 | tf_op jit(solution)/shard_map/ppermute | solution.py:258
  84.1 28.8 %collective-permute-start.10 = (bf16[64,4096]{1,0:T(8,128)(2,1)}, bf16[64,4096]{1,0:T(8,128)(2,1)}, u32[]{:S(2)}, u32[]{:S(2)}) collective-permute-start(bf16[64,4096]{1,0:T(8,128)(2,1)} %collective-permute-done.2.refs_2_), channel_id=1, source_target_pairs={{0,4},{1,5},{4,8},{5,9},{8,12},{9,13},{12,14},{13,15},{14,10},{15,... | collective-permute-start | bytes 1572872 | tf_op jit(solution)/shard_map/ppermute | solution.py:258
  95.5 28.5 %collective-permute-start.11 = (bf16[64,4096]{1,0:T(8,128)(2,1)S(1)}, bf16[64,4096]{1,0:T(8,128)(2,1)}, u32[]{:S(2)}, u32[]{:S(2)}) collective-permute-start(bf16[64,4096]{1,0:T(8,128)(2,1)S(1)} %collective-permute-done.3.refs_3_), channel_id=1, source_target_pairs={{4,0},{5,1},{8,4},{9,5},{12,8},{13,9},{14,12},{15,13},{10,14},{11,... | collective-permute-start | bytes 1572872 | tf_op jit(solution)/shard_map/ppermute | solution.py:258
  97.0 27.0 %collective-permute-start.21 = (bf16[64,4096]{1,0:T(8,128)(2,1)S(1)}, bf16[64,4096]{1,0:T(8,128)(2,1)}, u32[]{:S(2)}, u32[]{:S(2)}) collective-permute-start(bf16[64,4096]{1,0:T(8,128)(2,1)S(1)} %collective-permute-done.14.refs_2_), channel_id=1, source_target_pairs={{0,1},{1,0},{2,3},{3,2},{4,5},{5,4},{6,7},{7,6},{8,9},{9,8},{10,11... | collective-permute-start | bytes 1572872 | tf_op jit(solution)/shard_map/ppermute | solution.py:258
  97.8 28.3 %collective-permute-start.22 = (bf16[64,4096]{1,0:T(8,128)(2,1)}, bf16[64,4096]{1,0:T(8,128)(2,1)}, u32[]{:S(2)}, u32[]{:S(2)}) collective-permute-start(bf16[64,4096]{1,0:T(8,128)(2,1)} %collective-permute-done.15.refs_3_), channel_id=1, source_target_pairs={{0,1},{1,0},{2,3},{3,2},{4,5},{5,4},{6,7},{7,6},{8,9},{9,8},{10,11... | collective-permute-start | bytes 1572872 | tf_op jit(solution)/shard_map/ppermute | solution.py:258
  110.9 29.0 %collective-permute-start.19 = (bf16[64,4096]{1,0:T(8,128)(2,1)S(1)}, bf16[64,4096]{1,0:T(8,128)(2,1)}, u32[]{:S(2)}, u32[]{:S(2)}) collective-permute-start(bf16[64,4096]{1,0:T(8,128)(2,1)S(1)} %collective-permute-done.14.refs_2_), channel_id=1, source_target_pairs={{0,4},{1,5},{4,8},{5,9},{8,12},{9,13},{12,14},{13,15},{14,10},{15,... | collective-permute-start | bytes 1572872 | tf_op jit(solution)/shard_map/ppermute | solution.py:258
  113.0 27.0 %collective-permute-start.20 = (bf16[64,4096]{1,0:T(8,128)(2,1)}, bf16[64,4096]{1,0:T(8,128)(2,1)}, u32[]{:S(2)}, u32[]{:S(2)}) collective-permute-start(bf16[64,4096]{1,0:T(8,128)(2,1)} %collective-permute-done.15.refs_3_), channel_id=1, source_target_pairs={{4,0},{5,1},{8,4},{9,5},{12,8},{13,9},{14,12},{15,13},{10,14},{11,... | collective-permute-start | bytes 1572872 | tf_op jit(solution)/shard_map/ppermute | solution.py:258
  124.0 20.7 %collective-permute-start.26 = (bf16[64,4096]{1,0:T(8,128)(2,1)}, bf16[64,4096]{1,0:T(8,128)(2,1)}, u32[]{:S(2)}, u32[]{:S(2)}) collective-permute-start(bf16[64,4096]{1,0:T(8,128)(2,1)} %collective-permute-done.10.refs_2_), channel_id=1, source_target_pairs={{0,1},{1,0},{2,3},{3,2},{4,5},{5,4},{6,7},{7,6},{8,9},{9,8},{10,11... | collective-permute-start | bytes 1572872 | tf_op jit(solution)/shard_map/ppermute | solution.py:258
  124.1 43.9 %collective-permute-start.18 = (bf16[64,4096]{1,0:T(8,128)(2,1)}, bf16[64,4096]{1,0:T(8,128)(2,1)}, u32[]{:S(2)}, u32[]{:S(2)}) collective-permute-start(bf16[64,4096]{1,0:T(8,128)(2,1)} %collective-permute-done.10.refs_2_), channel_id=1, source_target_pairs={{0,4},{1,5},{4,8},{5,9},{8,12},{9,13},{12,14},{13,15},{14,10},{15,... | collective-permute-start | bytes 1572872 | tf_op jit(solution)/shard_map/ppermute | solution.py:258
  126.2 18.5 %collective-permute-start.27 = (bf16[64,4096]{1,0:T(8,128)(2,1)}, bf16[64,4096]{1,0:T(8,128)(2,1)}, u32[]{:S(2)}, u32[]{:S(2)}) collective-permute-start(bf16[64,4096]{1,0:T(8,128)(2,1)} %collective-permute-done.11.refs_3_), channel_id=1, source_target_pairs={{0,1},{1,0},{2,3},{3,2},{4,5},{5,4},{6,7},{7,6},{8,9},{9,8},{10,11... | collective-permute-start | bytes 1572872 | tf_op jit(solution)/shard_map/ppermute | solution.py:258
  139.9 16.6 %collective-permute-start.24 = (bf16[64,4096]{1,0:T(8,128)(2,1)}, bf16[64,4096]{1,0:T(8,128)(2,1)}, u32[]{:S(2)}, u32[]{:S(2)}) collective-permute-start(bf16[64,4096]{1,0:T(8,128)(2,1)} %collective-permute-done.19.refs_2_), channel_id=1, source_target_pairs={{0,1},{1,0},{2,3},{3,2},{4,5},{5,4},{6,7},{7,6},{8,9},{9,8},{10,11... | collective-permute-start | bytes 1572872 | tf_op jit(solution)/shard_map/ppermute | solution.py:258
  140.3 16.1 %collective-permute-start.25 = (bf16[64,4096]{1,0:T(8,128)(2,1)}, bf16[64,4096]{1,0:T(8,128)(2,1)}, u32[]{:S(2)}, u32[]{:S(2)}) collective-permute-start(bf16[64,4096]{1,0:T(8,128)(2,1)} %collective-permute-done.20.refs_3_), channel_id=1, source_target_pairs={{0,1},{1,0},{2,3},{3,2},{4,5},{5,4},{6,7},{7,6},{8,9},{9,8},{10,11... | collective-permute-start | bytes 1572872 | tf_op jit(solution)/shard_map/ppermute | solution.py:258
  144.7 23.3 %collective-permute-start.23 = (bf16[64,4096]{1,0:T(8,128)(2,1)}, bf16[64,4096]{1,0:T(8,128)(2,1)}, u32[]{:S(2)}, u32[]{:S(2)}) collective-permute-start(bf16[64,4096]{1,0:T(8,128)(2,1)} %collective-permute-done.20.refs_3_), channel_id=1, source_target_pairs={{4,0},{5,1},{8,4},{9,5},{12,8},{13,9},{14,12},{15,13},{10,14},{11,... | collective-permute-start | bytes 1572872 | tf_op jit(solution)/shard_map/ppermute | solution.py:258
  144.7 43.3 %collective-permute-start.30 = (bf16[256,2048]{1,0:T(8,128)(2,1)S(1)}, bf16[256,2048]{1,0:T(8,128)(2,1)}, u32[]{:S(2)}, u32[]{:S(2)}) collective-permute-start(bf16[256,2048]{1,0:T(8,128)(2,1)S(1)} %bitcast.36), channel_id=1, source_target_pairs={{16,0},{0,16},{17,1},{1,17},{18,2},{2,18},{19,3},{3,19},{20,4},{4,... | collective-permute-start | bytes 3145736 | tf_op jit(solution)/shard_map/ppermute | solution.py:321
  (23 other events, 217.9 us)
Sparse Core Ops, SparseCore 0:
  29.3 46.6 all-gather.2

commit v5 on v4

--- a/solution.py
+++ b/solution.py
@@ -12,6 +12,7 @@
 MIB = 1024 * 1024
 NT = (((1,), (1,)), ((), ()))
 TN = (((0,), (0,)), ((), ()))
+SMALL = pl.CostEstimate(flops=1_000_000, bytes_accessed=100_000, transcendentals=0)
 
 
 def chip_ring(chips):
@@ -50,90 +51,98 @@
     )(x, gain, queries)
 
 
-def chunk_body(pieces, tiles, packing, *refs):
-    x_refs, refs = refs[:pieces], refs[pieces:]
-    if packing:
-        gate_ref, up_ref, f_ref, out_ref, w_ref, xn, even, odd = refs
-    else:
-        w_ref, f_ref, _, out_ref, xn, even, odd = refs
+def tile_product(x, w):
+    return jnp.dot(x, w, preferred_element_type=jnp.float32)
+
+
+def projected(both, factor):
+    gate, up = both[:, :LANES], both[:, LANES:]
+    hidden = (jax.nn.silu(gate) * up).astype(jnp.bfloat16)
+    return jnp.dot(hidden, factor, preferred_element_type=jnp.float32)
+
+
+def gather_rows(x_refs, xn):
     rows = x_refs[0].shape[0]
+    for k, ref in enumerate(x_refs):
+        xn[k * rows : (k + 1) * rows, :] = ref[...]
+
+
+def first_body(pieces, *refs):
+    x_refs, (gate_ref, up_ref, f_ref, out_ref, w_ref, xn) = refs[:pieces], refs[pieces:]
     step = pl.program_id(0)
-
-    def first_product(into):
-        if packing:
-            w_ref[0, :, :LANES] = gate_ref[...]
-            w_ref[0, :, LANES:] = up_ref[...]
-        into[...] = jnp.dot(xn[...], w_ref[0], preferred_element_type=jnp.float32)
-
-    def second_product(source):
-        gate, up = source[:, :LANES], source[:, LANES:]
-        hidden = (jax.nn.silu(gate) * up).astype(jnp.bfloat16)
-        part = jnp.dot(hidden, f_ref[...], preferred_element_type=jnp.float32)
-        out_ref[...] = jnp.where(step == 1, 0.0, out_ref[...]) + part
 
     @pl.when(step == 0)
     def _():
-        for k, ref in enumerate(x_refs):
-            xn[k * rows : (k + 1) * rows, :] = ref[...]
-        first_product(even)
-
-    @pl.when((step > 0) & (step < tiles) & (step % 2 == 1))
-    def _():
-        second_product(even)
-        first_product(odd)
-
-    @pl.when((step > 0) & (step < tiles) & (step % 2 == 0))
-    def _():
-        second_product(odd)
-        first_product(even)
-
-    @pl.when(step == tiles)
-    def _():
-        second_product(even if tiles % 2 == 1 else odd)
-
-
-def chunk(xs, weights, in_factor, left, index, tokens):
-    packing = left is None
+        gather_rows(x_refs, xn)
+
+    w_ref[step, :, :LANES] = gate_ref[...]
+    w_ref[step, :, LANES:] = up_ref[...]
+    part = projected(tile_product(xn[...], w_ref[step]), f_ref[...])
+    out_ref[...] = jnp.where(step == 0, 0.0, out_ref[...]) + part
+
+
+def first_chunk(xs, gate_weight, up_weight, in_factor, index, tokens):
     pieces = len(xs)
     rows, depth = xs[0].shape
     units, order = in_factor.shape
     tiles = units // LANES
     total = pieces * rows
-    tile = pl.BlockSpec((1, depth, 2 * LANES), lambda i: (jnp.minimum(i, tiles - 1), 0, 0))
-    in_specs = [pl.BlockSpec((rows, depth), lambda i: (0, 0))] * pieces
-    out_specs = [pl.BlockSpec((total, order), lambda i: (index, 0))]
-    out_shape = [jax.ShapeDtypeStruct((tokens, order), jnp.float32)]
-    if packing:
-        operands = [*xs, *weights, in_factor]
-        in_specs += [pl.BlockSpec((depth, LANES), lambda i: (0, jnp.minimum(i, tiles - 1)))] * 2
-        out_specs.append(tile)
-        out_shape.append(jax.ShapeDtypeStruct((tiles, depth, 2 * LANES), jnp.bfloat16))
-        aliases = {}
-    else:
-        operands = [*xs, weights, in_factor, left]
-        in_specs.append(tile)
-        aliases = {pieces + 2: 0}
-    in_specs.append(pl.BlockSpec((LANES, order), lambda i: (jnp.maximum(i - 1, 0), 0)))
-    if not packing:
-        in_specs.append(pl.BlockSpec(memory_space=pl.ANY))
-    made = pl.pallas_call(
-        functools.partial(chunk_body, pieces, tiles, packing),
-        grid=(tiles + 1,),
-        in_specs=in_specs,
-        out_specs=out_specs,
-        out_shape=out_shape,
-        scratch_shapes=[pltpu.VMEM((total, depth), jnp.bfloat16)]
-        + [pltpu.VMEM((total, 2 * LANES), jnp.float32)] * 2,
-        input_output_aliases=aliases,
-        compiler_params=pltpu.CompilerParams(vmem_limit_bytes=50 * MIB),
-        cost_estimate=pl.CostEstimate(
-            flops=2 * total * depth * tiles * 2 * LANES,
-            bytes_accessed=(8 if packing else 4) * depth * units,
-            transcendentals=0,
-        ),
-        name="first_chunk" if packing else "chunk",
-    )(*operands)
-    return made if packing else made[0]
+    return pl.pallas_call(
+        functools.partial(first_body, pieces),
+        grid=(tiles,),
+        in_specs=[pl.BlockSpec((rows, depth), lambda i: (0, 0))] * pieces
+        + [
+            pl.BlockSpec((depth, LANES), lambda i: (0, i)),
+            pl.BlockSpec((depth, LANES), lambda i: (0, i)),
+            pl.BlockSpec((LANES, order), lambda i: (i, 0)),
+        ],
+        out_specs=[
+            pl.BlockSpec((total, order), lambda i: (index, 0)),
+            pl.BlockSpec(memory_space=pltpu.VMEM),
+        ],
+        out_shape=[
+            jax.ShapeDtypeStruct((tokens, order), jnp.float32),
+            pltpu.VMEM((tiles, depth, 2 * LANES), jnp.bfloat16),
+        ],
+        scratch_shapes=[pltpu.VMEM((total, depth), jnp.bfloat16)],
+        compiler_params=pltpu.CompilerParams(vmem_limit_bytes=14 * MIB),
+        cost_estimate=SMALL,
+        name="first_chunk",
+    )(*xs, gate_weight, up_weight, in_factor)
+
+
+def chunk_body(pieces, *refs):
+    x_refs, (w_ref, f_ref, _, out_ref, xn) = refs[:pieces], refs[pieces:]
+    gather_rows(x_refs, xn)
+    total = 0.0
+    before = None
+    for tile in range(w_ref.shape[0]):
+        both = tile_product(xn[...], w_ref[tile])
+        if before is not None:
+            total += projected(before, f_ref[(tile - 1) * LANES : tile * LANES, :])
+        before = both
+    out_ref[...] = total + projected(before, f_ref[tile * LANES :, :])
+
+
+def chunk(xs, weights, in_factor, left, index):
+    pieces = len(xs)
+    rows, depth = xs[0].shape
+    order = in_factor.shape[1]
+    total = pieces * rows
+    vmem = pl.BlockSpec(memory_space=pltpu.VMEM)
+    weights = pltpu.with_memory_space_constraint(weights, pltpu.VMEM)
+    return pl.pallas_call(
+        functools.partial(chunk_body, pieces),
+        grid=(1,),
+        in_specs=[vmem] * (pieces + 2) + [pl.BlockSpec(memory_space=pl.ANY)],
+        out_specs=pl.BlockSpec((total, order), lambda i: (index, 0)),
+        out_shape=jax.ShapeDtypeStruct(left.shape, left.dtype),
+        scratch_shapes=[pltpu.VMEM((total, depth), jnp.bfloat16)],
+        input_output_aliases={pieces + 2: 0},
+        compiler_params=pltpu.CompilerParams(vmem_limit_bytes=12 * MIB),
+        cost_estimate=SMALL,
+        name="chunk",
+    )(*xs, weights, in_factor, left)
 
 
 def one_sketch(left_ref, masked, at, half):
@@ -158,7 +167,7 @@
         out_specs=vmem,
         out_shape=jax.ShapeDtypeStruct((len(places), order, order), jnp.bfloat16),
         compiler_params=pltpu.CompilerParams(vmem_limit_bytes=8 * MIB),
-        cost_estimate=pl.CostEstimate(flops=400_000_000 * len(places), bytes_accessed=0, transcendentals=0),
+        cost_estimate=SMALL,
         name="sketches",
     )(names, left, side)
     return made.reshape(len(places), order * order)
@@ -218,6 +227,26 @@
     )(names, left, side, early, *queries, ids)
 
 
+def arrivals(ring, devices):
+    chips = len(ring)
+    far = chips // 2
+    table, spots = [[] for _ in range(devices)], []
+    for distance in range(far + 1):
+        for sign, piece in [(1, 0)] if distance in (0, far) else [(-1, 0), (1, 1)]:
+            for me in range(devices):
+                chip = ring[(ring.index(me // 2) + sign * distance) % chips]
+                table[me] += [2 * chip + me % 2, 2 * chip + 1 - me % 2]
+            if distance == 0:
+                halves = [(0, 0), (0, 1)]
+            elif distance == far:
+                halves = [(chips - 1, 0), (chips - 1, 1)]
+            else:
+                halves = [(2 * distance - 1, piece), (2 * distance, piece)]
+            spots.append([4 * k + 2 + p for k, p in halves])
+            spots.append([4 * k + 4 + p for k, p in halves])
+    return table, spots
+
+
 def local(
     devices,
     groups,
@@ -233,11 +262,8 @@
     query_ids,
 ):
     chips = devices // 2
-    far = chips // 2
     ring = chip_ring(chips)
     me = lax.axis_index("examples")
-    core = me % 2
-    place = jnp.array([ring.index(c) for c in range(chips)], jnp.int32)[me // 2]
 
     forward = [(ring[r] * 2 + c, ring[(r + 1) % chips] * 2 + c) for r in range(chips) for c in range(2)]
     backward = [(b, a) for a, b in forward]
@@ -258,7 +284,7 @@
         return lax.ppermute(x, "examples", way)
 
     def project(xs, left, index):
-        return chunk(xs, weights, in_factor, left, index, tokens)
+        return chunk(xs, weights, in_factor, left, index)
 
     x_a, x_b, mine = prepare(layer_inputs, norm_gain[None, :], queries, groups)
     coming = {
@@ -266,38 +292,19 @@
         2: (send(x_b, forward), send(x_b, backward)),
     }
     swapped = tuple(send(x, other_core) for x in (x_a, x_b))
-    weights = (gate_weight, up_weight)
-    left, weights = project((x_a, x_b), None, 1)
-
-    out_grads, query_ids, mine, left = lax.optimization_barrier((out_grads, query_ids, mine, left))
+    mine = lax.all_gather(mine, "examples", axis=0, tiled=True)
+    left, weights = first_chunk((x_a, x_b), gate_weight, up_weight, in_factor, 1, tokens)
+
+    out_grads, query_ids, left = lax.optimization_barrier((out_grads, query_ids, left))
     right = jnp.dot(out_grads, out_factor, preferred_element_type=jnp.float32)
     live = jnp.arange(span, dtype=jnp.int32)[:, None] < example_lengths[0]
     masked = jnp.where(live, right, 0.0).astype(jnp.bfloat16)
-    nq, width = mine.shape
-    masked = masked.reshape(span * order // width, width)
-    ids_row = jnp.pad(query_ids.astype(jnp.bfloat16)[None, :], ((0, 0), (0, width - nq)))
-    more = jnp.concatenate([mine, masked, ids_row], axis=0)
-    more = jnp.pad(more, ((0, -more.shape[0] % 8), (0, 0)))
-    more = lax.all_gather(more, "examples", axis=0)
-
-    def pair(where):
-        first = jnp.array(ring, jnp.int32)[where % chips] * 2
-        return [first + core, first + 1 - core]
-
-    names, spots = [], []
-    for distance in range(far + 1):
-        sides = [(1, 0)] if distance in (0, far) else [(-1, 0), (1, 1)]
-        for sign, piece in sides:
-            names += pair(place + sign * distance)
-            if distance == 0:
-                halves = [(0, 0), (0, 1)]
-            elif distance == far:
-                halves = [(chips - 1, 0), (chips - 1, 1)]
-            else:
-                halves = [(2 * distance - 1, piece), (2 * distance, piece)]
-            spots.append([4 * k + 2 + p for k, p in halves])
-            spots.append([4 * k + 4 + p for k, p in halves])
-    names = jnp.stack(names)
+    nq = queries.shape[0]
+    ids_row = jnp.pad(query_ids.astype(jnp.bfloat16)[None, :], ((0, 15), (0, order - nq)))
+    side = lax.all_gather(jnp.concatenate([masked, ids_row], axis=0), "examples", axis=0)
+
+    names, spots = arrivals(ring, devices)
+    names = lax.dynamic_index_in_dim(jnp.array(names, jnp.int32), me, keepdims=False)
 
     for k in range(1, chips):
         own_1, own_2, left = lax.optimization_barrier((*coming.pop(k), left))
@@ -309,17 +316,17 @@
         elif k + 1 == chips - 1:
             coming[chips - 1] = (opposite, send(own_2, backward))
         before, swapped = swapped, tuple(send(x, other_core) for x in own)
-        if k < chips - 1:
-            left = project(before + own, left, k)
-        if k == chips - 3:
-            more, left = lax.optimization_barrier((more, left))
-            mine = more[:, :nq].reshape(devices * nq, width)
-            side = more[:, nq : nq + masked.shape[0]].reshape(devices, span, order)
+        if k == chips - 5:
+            mine, left = lax.optimization_barrier((mine, left))
             shares = [mine]
             for r in range(1, groups):
                 way = [((g + r) % groups, g) for g in range(groups)]
                 shares.append(lax.ppermute(mine, "groups", way))
-            ids = more[:, nq + masked.shape[0], :nq].astype(jnp.int32).reshape(1, devices * nq)
+        if k < chips - 1:
+            left = project(before + own, left, k)
+        if k == chips - 3:
+            side, left = lax.optimization_barrier((side, left))
+            ids = side[:, span, :nq].astype(jnp.int32).reshape(1, devices * nq)
             ready = devices - 6
             early = [sketches(spots[:ready], half, names[:ready], left, side)]
         if k == chips - 2:

time: 212 us -> 190 us (0.90)
  Pallas kernels: 107 us -> 61 us
  local copies, waits for them, and re-layouts: 14.9 us -> 41.6 us
  blocking collectives: 12.3 us -> 33.6 us
  waiting for transfers between devices: 23.4 us -> 9.96 us
  between operations: 26.2 us -> 14.4 us
    pallas_call x10, Pallas kernels: 102 us -> 55.2 us  [the longest x9 45.5 us: chunk(): pl.pallas_call(functools.partial(chunk_body, pieces), grid=(1,), in_specs...]
    unnamed x31 -> x39, local copies, waits for them, and re-layouts: 7.31 us -> 38.9 us
    all_gather x0 -> x1, blocking collectives: none -> 24.3 us  [local(): lax.all_gather(jnp.concatenate([masked, ids_row], axis=0), 'examples', ax...]
    ppermute x30, waiting for transfers between devices: 23.4 us -> 9.92 us  [send(): return lax.ppermute(x, 'examples', way)]
    all_to_all x1, blocking collectives: 12.3 us -> 9.31 us  [local(): lax.all_to_all(partial, 'examples', split_axis=0, concat_axis=0, tiled=True)]
  transfers between devices with their start and end apart: 32 -> 32, of which waited for: 3 -> 2; matrix products, arithmetic and copies ran while one was open for 4% -> 3% of each run, Pallas kernels for 42% -> 30%
where the time goes in v5:
time: 190 us; the launch traced here: 189 us
  Pallas kernels  61 us (32%)
  local copies, waits for them, and re-layouts  41.6 us (22%)
  blocking collectives  33.6 us (18%)
  starting transfers between devices  24.2 us (13%)
  between operations  14.4 us (8%)
  waiting for transfers between devices  9.96 us (5%)
  other arithmetic  2.5 us (1%)
    pallas_call x9, Pallas kernels, chunk(): pl.pallas_call(functools.partial(chunk_body, pieces), grid=(1,), in_specs...  45.5 us
    unnamed x39, local copies, waits for them, and re-layouts  38.9 us
    all_gather x1, blocking collectives, local(): lax.all_gather(jnp.concatenate([masked, ids_row], axis=0), 'examples', ax...  24.3 us
    ppermute x30, starting transfers between devices, send(): return lax.ppermute(x, 'examples', way)  22.6 us
    ppermute x30, waiting for transfers between devices, send(): return lax.ppermute(x, 'examples', way)  9.92 us
    pallas_call x1, Pallas kernels, first_chunk(): pl.pallas_call(functools.partial(first_body, pieces), grid=(tiles,), in_s...  9.72 us
    all_to_all x1, blocking collectives, local(): lax.all_to_all(partial, 'examples', split_axis=0, concat_axis=0, tiled=True)  9.31 us
  transfers between devices with their start and end apart: 32, of which 2 were waited for; matrix products, arithmetic and copies ran while one was open for 3% of the time, Pallas kernels for 30%

profile of v5, /device:TPU:0, one launch (start us, length us, event | category | flops | bytes accessed | tf_op | source)
XLA Modules:
  0.0 188.8 jit_solution(10989907282211318000)
XLA Ops:
  10.7 3.1 %collective-permute-start = (bf16[64,4096]{1,0:T(8,128)(2,1)}, bf16[64,4096]{1,0:T(8,128)(2,1)S(1)}, u32[]{:S(2)}, u32[]{:S(2)}) collective-permute-start(bf16[64,4096]{1,0:T(8,128)(2,1)} %get-tuple-element.40.refs_0_), channel_id=1, source_target_pairs={{0,4},{1,5},{4,8},{5,9},{8,12},{9,13},{12,14},{13,15},{14,10},{15,... | collective-permute-start | bytes 1572872 | tf_op jit(solution)/shard_map/ppermute | solution.py:284
  14.3 2.0 %collective-permute-start.6 = (bf16[64,4096]{1,0:T(8,128)(2,1)S(1)}, bf16[64,4096]{1,0:T(8,128)(2,1)}, u32[]{:S(2)}, u32[]{:S(2)}) collective-permute-start(bf16[64,4096]{1,0:T(8,128)(2,1)S(1)} %get-tuple-element.41.refs_1_), channel_id=1, source_target_pairs={{0,4},{1,5},{4,8},{5,9},{8,12},{9,13},{12,14},{13,15},{14,10},{15,... | collective-permute-start | bytes 1572872 | tf_op jit(solution)/shard_map/ppermute | solution.py:284
  16.5 3.1 %copy-done.7 = bf16[4096,896]{1,0:T(8,128)(2,1)S(1)} copy-done((bf16[4096,896]{1,0:T(8,128)(2,1)S(1)}, bf16[4096,896]{1,0:T(8,128)(2,1)}, u32[]{:S(2)}) %copy-start.7) | copy-done | bytes 7340056
  19.6 3.2 %copy-done.8 = bf16[4096,896]{1,0:T(8,128)(2,1)S(1)} copy-done((bf16[4096,896]{1,0:T(8,128)(2,1)S(1)}, bf16[4096,896]{1,0:T(8,128)(2,1)}, u32[]{:S(2)}) %copy-start.8) | copy-done | bytes 7340056
  22.8 9.7 %first_chunk.1 = (f32[2176,64]{1,0:T(8,128)S(1)}, bf16[7,4096,256]{2,1,0:T(8,128)(2,1)S(1)}) custom-call(bf16[64,4096]{1,0:T(8,128)(2,1)} %get-tuple-element.40.refs_0_, bf16[64,4096]{1,0:T(8,128)(2,1)S(1)} %get-tuple-element.41.refs_1_, bf16[4096,896]{1,0:T(8,128)(2,1)S(1)} %copy-done.7, bf16[4096,896]{1,0:T(8,128)(2,1)S(1)} %copy-done.8, ...), custom_call_target="tpu_custom_call" | custom-call | flops 1000000 | bytes 100000 | tf_op jit(solution)/shard_map/first_chunk/pallas_call | solution.py:90
  35.1 6.8 %chunk.9.refs_6_ = f32[2176,64]{1,0:T(8,128)S(1)} custom-call(bf16[64,4096]{1,0:T(8,128)(2,1)} %collective-permute-done.8.refs_0_, bf16[64,4096]{1,0:T(8,128)(2,1)} %collective-permute-done.9.refs_1_, bf16[64,4096]{1,0:T(8,128)(2,1)S(1)} %collective-permute-done.refs_2_, ...), custom_call_target="tpu_custom_call", output_to_operand_aliasing={{}: (6, {})} | custom-call | flops 1000000 | bytes 100000 | tf_op jit(solution)/shard_map/chunk/pallas_call | solution.py:134
  42.3 8.9 %collective-permute-done.7.refs_3_ = bf16[64,4096]{1,0:T(8,128)(2,1)} collective-permute-done((bf16[64,4096]{1,0:T(8,128)(2,1)S(1)}, bf16[64,4096]{1,0:T(8,128)(2,1)}, u32[]{:S(2)}, u32[]{:S(2)}) %collective-permute-start.7) | collective-permute-done | bytes 524320 | tf_op jit(solution)/shard_map/ppermute | solution.py:284
  54.2 3.4 %collective-permute-start.15 = (bf16[64,4096]{1,0:T(8,128)(2,1)}, bf16[64,4096]{1,0:T(8,128)(2,1)S(1)}, u32[]{:S(2)}, u32[]{:S(2)}) collective-permute-start(bf16[64,4096]{1,0:T(8,128)(2,1)} %collective-permute-done.7.refs_3_), channel_id=1, source_target_pairs={{4,0},{5,1},{8,4},{9,5},{12,8},{13,9},{14,12},{15,13},{10,14},{11,... | collective-permute-start | bytes 1572872 | tf_op jit(solution)/shard_map/ppermute | solution.py:284
  57.7 5.5 %chunk.10.refs_6_ = f32[2176,64]{1,0:T(8,128)S(1)} custom-call(bf16[64,4096]{1,0:T(8,128)(2,1)S(1)} %collective-permute-done.4.refs_0_, bf16[64,4096]{1,0:T(8,128)(2,1)S(1)} %collective-permute-done.5.refs_1_, bf16[64,4096]{1,0:T(8,128)(2,1)} %collective-permute-done.6.refs_2_, ...), custom_call_target="tpu_custom_call", output_to_operand_aliasing={{}: (6, {})} | custom-call | flops 1000000 | bytes 100000 | tf_op jit(solution)/shard_map/chunk/pallas_call | solution.py:134
  67.3 5.2 %copy-done.2 = bf16[7,4096,256]{2,1,0:T(8,128)(2,1)S(1)} copy-done((bf16[7,4096,256]{2,1,0:T(8,128)(2,1)S(1)}, bf16[7,4096,256]{2,1,0:T(8,128)(2,1)}, u32[]{:S(2)}) %copy-start.2) | copy-done | bytes 14680088
  74.6 5.5 %chunk.11.refs_6_ = f32[2176,64]{1,0:T(8,128)S(1)} custom-call(bf16[64,4096]{1,0:T(8,128)(2,1)S(1)} %copy-done.11, bf16[64,4096]{1,0:T(8,128)(2,1)S(1)} %copy-done.13, bf16[64,4096]{1,0:T(8,128)(2,1)} %collective-permute-done.2.refs_2_, bf16[64,4096]{1,0:T(8,128)(2,1)} %collective-permute-done.3.refs_3_, ...), custom_call_target="tpu_custom_call", output_to_operand_aliasing={{}: (6, {})} | custom-call | flops 1000000 | bytes 100000 | tf_op jit(solution)/shard_map/chunk/pallas_call | solution.py:134
  84.8 5.2 %copy-done.3 = bf16[7,4096,256]{2,1,0:T(8,128)(2,1)S(1)} copy-done((bf16[7,4096,256]{2,1,0:T(8,128)(2,1)S(1)}, bf16[7,4096,256]{2,1,0:T(8,128)(2,1)}, u32[]{:S(2)}) %copy-start.3) | copy-done | bytes 14680088
  90.0 5.5 %chunk.12.refs_6_ = f32[2176,64]{1,0:T(8,128)S(1)} custom-call(bf16[64,4096]{1,0:T(8,128)(2,1)} %collective-permute-done.12.refs_0_, bf16[64,4096]{1,0:T(8,128)(2,1)} %collective-permute-done.13.refs_1_, bf16[64,4096]{1,0:T(8,128)(2,1)S(1)} %collective-permute-done.14.refs_2_, ...), custom_call_target="tpu_custom_call", output_to_operand_aliasing={{}: (6, {})} | custom-call | flops 1000000 | bytes 100000 | tf_op jit(solution)/shard_map/chunk/pallas_call | solution.py:134
  96.0 24.3 %all-gather.1 = bf16[16,144,64]{1,2,0:T(8,128)(2,1)} all-gather(bf16[1,144,64]{1,2,0:T(8,128)(2,1)S(1)} %fusion.3), channel_id=2, replica_groups=mesh['groups'=2,'examples'=16] {'examples'}, dimensions={0}, use_global_device_ids=true | all-gather | bytes 313344 | tf_op jit(solution)/shard_map/all_gather | solution.py:304
  120.4 5.2 %copy-done.4 = bf16[7,4096,256]{2,1,0:T(8,128)(2,1)S(1)} copy-done((bf16[7,4096,256]{2,1,0:T(8,128)(2,1)S(1)}, bf16[7,4096,256]{2,1,0:T(8,128)(2,1)}, u32[]{:S(2)}) %copy-start.4) | copy-done | bytes 14680088
  125.6 5.8 %chunk.13.left_ref.refs_6_ = f32[2176,64]{1,0:T(8,128)S(1)} custom-call(bf16[64,4096]{1,0:T(8,128)(2,1)} %collective-permute-done.21.refs_0_, bf16[64,4096]{1,0:T(8,128)(2,1)} %collective-permute-done.22.refs_1_, bf16[64,4096]{1,0:T(8,128)(2,1)} %collective-permute-done.10.refs_2_, ...), custom_call_target="tpu_custom_call", output_to_operand_aliasing={{}: (6, {})} | custom-call | flops 1000000 | bytes 100000 | tf_op jit(solution)/shard_map/chunk/pallas_call | solution.py:134
  138.7 5.2 %copy-done.5 = bf16[7,4096,256]{2,1,0:T(8,128)(2,1)S(1)} copy-done((bf16[7,4096,256]{2,1,0:T(8,128)(2,1)S(1)}, bf16[7,4096,256]{2,1,0:T(8,128)(2,1)}, u32[]{:S(2)}) %copy-start.5) | copy-done | bytes 14680088
  143.9 5.8 %chunk.14.refs_4_ = f32[2176,64]{1,0:T(8,128)S(1)} custom-call(bf16[64,4096]{1,0:T(8,128)(2,1)} %collective-permute-done.26.refs_0_, bf16[64,4096]{1,0:T(8,128)(2,1)} %collective-permute-done.27.refs_1_, bf16[64,4096]{1,0:T(8,128)(2,1)} %collective-permute-done.19.refs_2_, ...), custom_call_target="tpu_custom_call", output_to_operand_aliasing={{}: (6, {})} | custom-call | flops 1000000 | bytes 100000 | tf_op jit(solution)/shard_map/chunk/pallas_call | solution.py:134
  149.7 3.6 %chunk.15.left_ref.refs_4_ = f32[2176,64]{1,0:T(8,128)S(1)} custom-call(bf16[64,4096]{1,0:T(8,128)(2,1)} %collective-permute-done.24.refs_0_, bf16[64,4096]{1,0:T(8,128)(2,1)} %collective-permute-done.25.refs_1_, bf16[7,4096,256]{2,1,0:T(8,128)(2,1)S(1)} %copy-done.5, ...), custom_call_target="tpu_custom_call", output_to_operand_aliasing={{}: (4, {})} | custom-call | flops 1000000 | bytes 100000 | tf_op jit(solution)/shard_map/chunk/pallas_call | solution.py:134
  156.7 5.2 %copy-done.6 = bf16[7,4096,256]{2,1,0:T(8,128)(2,1)S(1)} copy-done((bf16[7,4096,256]{2,1,0:T(8,128)(2,1)S(1)}, bf16[7,4096,256]{2,1,0:T(8,128)(2,1)}, u32[]{:S(2)}) %copy-start.6) | copy-done | bytes 14680088
  161.9 3.6 %chunk.16.refs_4_ = f32[2176,64]{1,0:T(8,128)S(1)} custom-call(bf16[64,4096]{1,0:T(8,128)(2,1)} %collective-permute-done.18.refs_0_, bf16[64,4096]{1,0:T(8,128)(2,1)} %collective-permute-done.23.refs_1_, bf16[7,4096,256]{2,1,0:T(8,128)(2,1)S(1)} %copy-done.6, bf16[896,64]{1,0:T(8,128)(2,1)S(1)} %copy.47.refs_4_.refs_5_.refs_3_, ...), custom_call_target="tpu_custom_call", output_to_operand_aliasing={{}: (4, {})} | custom-call | flops 1000000 | bytes 100000 | tf_op jit(solution)/shard_map/chunk/pallas_call | solution.py:134
  165.5 3.5 %chunk.17.left_ref = f32[2176,64]{1,0:T(8,128)S(1)} custom-call(bf16[64,4096]{1,0:T(8,128)(2,1)S(1)} %collective-permute-done.28.refs_0_, bf16[64,4096]{1,0:T(8,128)(2,1)} %collective-permute-done.29.refs_1_, bf16[7,4096,256]{2,1,0:T(8,128)(2,1)S(1)} %copy-done.6, bf16[896,64]{1,0:T(8,128)(2,1)S(1)} %copy.47.refs_4_.refs_5_.refs_3_, ...), custom_call_target="tpu_custom_call", output_to_operand_aliasing={{}: (4, {})} | custom-call | flops 1000000 | bytes 100000 | tf_op jit(solution)/shard_map/chunk/pallas_call | solution.py:134
  169.1 2.9 %finish.1 = f32[16,256]{1,0:T(8,128)S(1)} custom-call(s32[16]{0:T(128)S(1)} %get-tuple-element.76.names, f32[2176,64]{1,0:T(8,128)S(1)} %chunk.17.left_ref, bf16[16,144,64]{2,1,0:T(8,128)(2,1)S(1)} %copy.54.side_ref, bf16[14,4096]{1,0:T(8,128)(2,1)S(1)} %copy-done.14, bf16[256,2048]{1,0:T(8,128)(2,1)} %all-gather.4.cloned.1.call-done.refs_0_, ...), custom_call_target="tpu_custom_call" | custom-call | tf_op jit(solution)/shard_map/finish/pallas_call | solution.py:215
  172.0 9.3 %all_to_all.9 = f32[16,1,256]{2,1,0:T(1,128)S(1)} all-to-all(f32[16,1,256]{2,1,0:T(1,128)S(1)} %copy.61), channel_id=1, replica_groups=mesh['groups'=2,'examples'=16] {'examples'}, dimensions={0} | all-to-all | bytes 32768 | tf_op jit(solution)/shard_map/all_to_all | solution.py:341
  (112 shorter events, 33.1 us)
Async XLA Ops:
  6.5 60.8 %all-gather.4.cloned.1.call-start = ((), (), s32[]{:S(2)}) async-start(), calls=%async_computation.1 | async-start | bytes 1114112 | tf_op jit(solution)/shard_map/all_gather | solution.py:295
  10.7 21.8 %collective-permute-start = (bf16[64,4096]{1,0:T(8,128)(2,1)}, bf16[64,4096]{1,0:T(8,128)(2,1)S(1)}, u32[]{:S(2)}, u32[]{:S(2)}) collective-permute-start(bf16[64,4096]{1,0:T(8,128)(2,1)} %get-tuple-element.40.refs_0_), channel_id=1, source_target_pairs={{0,4},{1,5},{4,8},{5,9},{8,12},{9,13},{12,14},{13,15},{14,10},{15,... | collective-permute-start | bytes 1572872 | tf_op jit(solution)/shard_map/ppermute | solution.py:284
  13.8 18.8 %collective-permute-start.1 = (bf16[64,4096]{1,0:T(8,128)(2,1)}, bf16[64,4096]{1,0:T(8,128)(2,1)}, u32[]{:S(2)}, u32[]{:S(2)}) collective-permute-start(bf16[64,4096]{1,0:T(8,128)(2,1)} %get-tuple-element.40.refs_0_), channel_id=1, source_target_pairs={{4,0},{5,1},{8,4},{9,5},{12,8},{13,9},{14,12},{15,13},{10,14},{11,... | collective-permute-start | bytes 1572872 | tf_op jit(solution)/shard_map/ppermute | solution.py:284
  13.8 18.9 %collective-permute-start.8 = (bf16[64,4096]{1,0:T(8,128)(2,1)}, bf16[64,4096]{1,0:T(8,128)(2,1)}, u32[]{:S(2)}, u32[]{:S(2)}) collective-permute-start(bf16[64,4096]{1,0:T(8,128)(2,1)} %get-tuple-element.40.refs_0_), channel_id=1, source_target_pairs={{0,1},{1,0},{2,3},{3,2},{4,5},{5,4},{6,7},{7,6},{8,9},{9,8},{10,11... | collective-permute-start | bytes 1572872 | tf_op jit(solution)/shard_map/ppermute | solution.py:284
  13.8 19.4 %collective-permute-start.9 = (bf16[64,4096]{1,0:T(8,128)(2,1)S(1)}, bf16[64,4096]{1,0:T(8,128)(2,1)}, u32[]{:S(2)}, u32[]{:S(2)}) collective-permute-start(bf16[64,4096]{1,0:T(8,128)(2,1)S(1)} %get-tuple-element.41.refs_1_), channel_id=1, source_target_pairs={{0,1},{1,0},{2,3},{3,2},{4,5},{5,4},{6,7},{7,6},{8,9},{9,8},{10,11... | collective-permute-start | bytes 1572872 | tf_op jit(solution)/shard_map/ppermute | solution.py:284
  14.3 27.6 %collective-permute-start.6 = (bf16[64,4096]{1,0:T(8,128)(2,1)S(1)}, bf16[64,4096]{1,0:T(8,128)(2,1)}, u32[]{:S(2)}, u32[]{:S(2)}) collective-permute-start(bf16[64,4096]{1,0:T(8,128)(2,1)S(1)} %get-tuple-element.41.refs_1_), channel_id=1, source_target_pairs={{0,4},{1,5},{4,8},{5,9},{8,12},{9,13},{12,14},{13,15},{14,10},{15,... | collective-permute-start | bytes 1572872 | tf_op jit(solution)/shard_map/ppermute | solution.py:284
  32.5 18.7 %collective-permute-start.7 = (bf16[64,4096]{1,0:T(8,128)(2,1)S(1)}, bf16[64,4096]{1,0:T(8,128)(2,1)}, u32[]{:S(2)}, u32[]{:S(2)}) collective-permute-start(bf16[64,4096]{1,0:T(8,128)(2,1)S(1)} %get-tuple-element.41.refs_1_), channel_id=1, source_target_pairs={{4,0},{5,1},{8,4},{9,5},{12,8},{13,9},{14,12},{15,13},{10,14},{11,... | collective-permute-start | bytes 1572872 | tf_op jit(solution)/shard_map/ppermute | solution.py:284
  32.6 18.6 %collective-permute-start.4 = (bf16[64,4096]{1,0:T(8,128)(2,1)S(1)}, bf16[64,4096]{1,0:T(8,128)(2,1)S(1)}, u32[]{:S(2)}, u32[]{:S(2)}) collective-permute-start(bf16[64,4096]{1,0:T(8,128)(2,1)S(1)} %collective-permute-done.refs_2_), channel_id=1, source_target_pairs={{0,1},{1,0},{2,3},{3,2},{4,5},{5,4},{6,7},{7,6},{8,9},{9,8},{10,11... | collective-permute-start | bytes 1572872 | tf_op jit(solution)/shard_map/ppermute | solution.py:284
  32.7 19.0 %collective-permute-start.5 = (bf16[64,4096]{1,0:T(8,128)(2,1)}, bf16[64,4096]{1,0:T(8,128)(2,1)S(1)}, u32[]{:S(2)}, u32[]{:S(2)}) collective-permute-start(bf16[64,4096]{1,0:T(8,128)(2,1)} %collective-permute-done.1.refs_3_), channel_id=1, source_target_pairs={{0,1},{1,0},{2,3},{3,2},{4,5},{5,4},{6,7},{7,6},{8,9},{9,8},{10,11... | collective-permute-start | bytes 1572872 | tf_op jit(solution)/shard_map/ppermute | solution.py:284
  33.2 21.1 %collective-permute-start.2 = (bf16[64,4096]{1,0:T(8,128)(2,1)S(1)}, bf16[64,4096]{1,0:T(8,128)(2,1)}, u32[]{:S(2)}, u32[]{:S(2)}) collective-permute-start(bf16[64,4096]{1,0:T(8,128)(2,1)S(1)} %collective-permute-done.refs_2_), channel_id=1, source_target_pairs={{0,4},{1,5},{4,8},{5,9},{8,12},{9,13},{12,14},{13,15},{14,10},{15,... | collective-permute-start | bytes 1572872 | tf_op jit(solution)/shard_map/ppermute | solution.py:284
  41.9 21.2 %collective-permute-start.3 = (bf16[64,4096]{1,0:T(8,128)(2,1)}, bf16[64,4096]{1,0:T(8,128)(2,1)}, u32[]{:S(2)}, u32[]{:S(2)}) collective-permute-start(bf16[64,4096]{1,0:T(8,128)(2,1)} %collective-permute-done.1.refs_3_), channel_id=1, source_target_pairs={{4,0},{5,1},{8,4},{9,5},{12,8},{13,9},{14,12},{15,13},{10,14},{11,... | collective-permute-start | bytes 1572872 | tf_op jit(solution)/shard_map/ppermute | solution.py:284
  51.7 28.4 %collective-permute-start.14 = (bf16[64,4096]{1,0:T(8,128)(2,1)}, bf16[64,4096]{1,0:T(8,128)(2,1)S(1)}, u32[]{:S(2)}, u32[]{:S(2)}) collective-permute-start(bf16[64,4096]{1,0:T(8,128)(2,1)} %collective-permute-done.6.refs_2_), channel_id=1, source_target_pairs={{0,4},{1,5},{4,8},{5,9},{8,12},{9,13},{12,14},{13,15},{14,10},{15,... | collective-permute-start | bytes 1572872 | tf_op jit(solution)/shard_map/ppermute | solution.py:284
  54.2 26.6 %collective-permute-start.15 = (bf16[64,4096]{1,0:T(8,128)(2,1)}, bf16[64,4096]{1,0:T(8,128)(2,1)S(1)}, u32[]{:S(2)}, u32[]{:S(2)}) collective-permute-start(bf16[64,4096]{1,0:T(8,128)(2,1)} %collective-permute-done.7.refs_3_), channel_id=1, source_target_pairs={{4,0},{5,1},{8,4},{9,5},{12,8},{13,9},{14,12},{15,13},{10,14},{11,... | collective-permute-start | bytes 1572872 | tf_op jit(solution)/shard_map/ppermute | solution.py:284
  64.0 18.2 %collective-permute-start.13 = (bf16[64,4096]{1,0:T(8,128)(2,1)}, bf16[64,4096]{1,0:T(8,128)(2,1)}, u32[]{:S(2)}, u32[]{:S(2)}) collective-permute-start(bf16[64,4096]{1,0:T(8,128)(2,1)} %collective-permute-done.3.refs_3_), channel_id=1, source_target_pairs={{0,1},{1,0},{2,3},{3,2},{4,5},{5,4},{6,7},{7,6},{8,9},{9,8},{10,11... | collective-permute-start | bytes 1572872 | tf_op jit(solution)/shard_map/ppermute | solution.py:284
  80.9 50.5 %collective-permute-start.19 = (bf16[64,4096]{1,0:T(8,128)(2,1)S(1)}, bf16[64,4096]{1,0:T(8,128)(2,1)}, u32[]{:S(2)}, u32[]{:S(2)}) collective-permute-start(bf16[64,4096]{1,0:T(8,128)(2,1)S(1)} %collective-permute-done.14.refs_2_), channel_id=1, source_target_pairs={{0,4},{1,5},{4,8},{5,9},{8,12},{9,13},{12,14},{13,15},{14,10},{15,... | collective-permute-start | bytes 1572872 | tf_op jit(solution)/shard_map/ppermute | solution.py:284
  82.3 38.1 %collective-permute-start.22 = (bf16[64,4096]{1,0:T(8,128)(2,1)S(1)}, bf16[64,4096]{1,0:T(8,128)(2,1)}, u32[]{:S(2)}, u32[]{:S(2)}) collective-permute-start(bf16[64,4096]{1,0:T(8,128)(2,1)S(1)} %collective-permute-done.15.refs_3_), channel_id=1, source_target_pairs={{0,1},{1,0},{2,3},{3,2},{4,5},{5,4},{6,7},{7,6},{8,9},{9,8},{10,11... | collective-permute-start | bytes 1572872 | tf_op jit(solution)/shard_map/ppermute | solution.py:284
  82.5 48.9 %collective-permute-start.20 = (bf16[64,4096]{1,0:T(8,128)(2,1)S(1)}, bf16[64,4096]{1,0:T(8,128)(2,1)}, u32[]{:S(2)}, u32[]{:S(2)}) collective-permute-start(bf16[64,4096]{1,0:T(8,128)(2,1)S(1)} %collective-permute-done.15.refs_3_), channel_id=1, source_target_pairs={{4,0},{5,1},{8,4},{9,5},{12,8},{13,9},{14,12},{15,13},{10,14},{11,... | collective-permute-start | bytes 1572872 | tf_op jit(solution)/shard_map/ppermute | solution.py:284
  95.5 37.2 %collective-permute-start.26 = (bf16[64,4096]{1,0:T(8,128)(2,1)}, bf16[64,4096]{1,0:T(8,128)(2,1)}, u32[]{:S(2)}, u32[]{:S(2)}) collective-permute-start(bf16[64,4096]{1,0:T(8,128)(2,1)} %collective-permute-done.10.refs_2_), channel_id=1, source_target_pairs={{0,1},{1,0},{2,3},{3,2},{4,5},{5,4},{6,7},{7,6},{8,9},{9,8},{10,11... | collective-permute-start | bytes 1572872 | tf_op jit(solution)/shard_map/ppermute | solution.py:284
  95.5 38.6 %collective-permute-start.27 = (bf16[64,4096]{1,0:T(8,128)(2,1)}, bf16[64,4096]{1,0:T(8,128)(2,1)}, u32[]{:S(2)}, u32[]{:S(2)}) collective-permute-start(bf16[64,4096]{1,0:T(8,128)(2,1)} %collective-permute-done.11.refs_3_), channel_id=1, source_target_pairs={{0,1},{1,0},{2,3},{3,2},{4,5},{5,4},{6,7},{7,6},{8,9},{9,8},{10,11... | collective-permute-start | bytes 1572872 | tf_op jit(solution)/shard_map/ppermute | solution.py:284
  131.4 18.3 %collective-permute-start.24 = (bf16[64,4096]{1,0:T(8,128)(2,1)}, bf16[64,4096]{1,0:T(8,128)(2,1)}, u32[]{:S(2)}, u32[]{:S(2)}) collective-permute-start(bf16[64,4096]{1,0:T(8,128)(2,1)} %collective-permute-done.19.refs_2_), channel_id=1, source_target_pairs={{0,1},{1,0},{2,3},{3,2},{4,5},{5,4},{6,7},{7,6},{8,9},{9,8},{10,11... | collective-permute-start | bytes 1572872 | tf_op jit(solution)/shard_map/ppermute | solution.py:284
  131.8 17.9 %collective-permute-start.25 = (bf16[64,4096]{1,0:T(8,128)(2,1)}, bf16[64,4096]{1,0:T(8,128)(2,1)}, u32[]{:S(2)}, u32[]{:S(2)}) collective-permute-start(bf16[64,4096]{1,0:T(8,128)(2,1)} %collective-permute-done.20.refs_3_), channel_id=1, source_target_pairs={{0,1},{1,0},{2,3},{3,2},{4,5},{5,4},{6,7},{7,6},{8,9},{9,8},{10,11... | collective-permute-start | bytes 1572872 | tf_op jit(solution)/shard_map/ppermute | solution.py:284
  132.6 22.3 %collective-permute-start.18 = (bf16[64,4096]{1,0:T(8,128)(2,1)}, bf16[64,4096]{1,0:T(8,128)(2,1)}, u32[]{:S(2)}, u32[]{:S(2)}) collective-permute-start(bf16[64,4096]{1,0:T(8,128)(2,1)} %collective-permute-done.10.refs_2_), channel_id=1, source_target_pairs={{0,4},{1,5},{4,8},{5,9},{8,12},{9,13},{12,14},{13,15},{14,10},{15,... | collective-permute-start | bytes 1572872 | tf_op jit(solution)/shard_map/ppermute | solution.py:284
  132.6 36.4 %collective-permute-start.30 = (bf16[256,2048]{1,0:T(8,128)(2,1)}, bf16[256,2048]{1,0:T(8,128)(2,1)}, u32[]{:S(2)}, u32[]{:S(2)}) collective-permute-start(bf16[256,2048]{1,0:T(8,128)(2,1)} %all-gather.4.cloned.1.call-done.refs_0_), channel_id=1, source_target_pairs={{16,0},{0,16},{17,1},{1,17},{18,2},{2,18},{19,3},{3,19},{20,4},{4,... | collective-permute-start | bytes 3145736 | tf_op jit(solution)/shard_map/ppermute | solution.py:324
  134.2 20.7 %collective-permute-start.23 = (bf16[64,4096]{1,0:T(8,128)(2,1)}, bf16[64,4096]{1,0:T(8,128)(2,1)}, u32[]{:S(2)}, u32[]{:S(2)}) collective-permute-start(bf16[64,4096]{1,0:T(8,128)(2,1)} %collective-permute-done.20.refs_3_), channel_id=1, source_target_pairs={{4,0},{5,1},{8,4},{9,5},{12,8},{13,9},{14,12},{15,13},{10,14},{11,... | collective-permute-start | bytes 1572872 | tf_op jit(solution)/shard_map/ppermute | solution.py:284
  (27 other events, 268.8 us)
Sparse Core Ops, SparseCore 0:
  10.9 43.7 all-gather.3

commit v6 on v5

v6 whole, which is shorter than its diff:
```python
import functools

import jax
import jax.numpy as jnp
from jax import lax
from jax.experimental import pallas as pl
from jax.experimental.pallas import tpu as pltpu
from jax.sharding import PartitionSpec as P

NVAL = 256
LANES = 128
MIB = 1024 * 1024
NT = (((1,), (1,)), ((), ()))
TN = (((0,), (0,)), ((), ()))
SMALL = pl.CostEstimate(flops=1_000_000, bytes_accessed=100_000, transcendentals=0)


def chip_ring(chips):
    if chips == 8:
        return [0, 2, 4, 6, 7, 5, 3, 1]
    return list(range(chips))


def prepare_body(x_ref, gain_ref, a_ref, b_ref):
    half = a_ref.shape[0]
    block = 16
    for start in range(0, 2 * half, block):
        x = x_ref[start : start + block, :].astype(jnp.float32)
        scale = lax.rsqrt(jnp.mean(x * x, axis=-1, keepdims=True) + 1e-05)
        rows = (x * scale * gain_ref[...]).astype(jnp.bfloat16)
        if start < half:
            a_ref[start : start + block, :] = rows
        else:
            b_ref[start - half : start - half + block, :] = rows


def prepare(x, gain):
    span, depth = x.shape
    vmem = pl.BlockSpec(memory_space=pltpu.VMEM)
    rows = jax.ShapeDtypeStruct((span // 2, depth), jnp.bfloat16)
    return pl.pallas_call(
        prepare_body,
        in_specs=[vmem] * 2,
        out_specs=[vmem] * 2,
        out_shape=[rows, rows],
        compiler_params=pltpu.CompilerParams(vmem_limit_bytes=12 * MIB),
        cost_estimate=SMALL,
        name="prepare",
    )(x, gain)


def share_body(lengths_ref, grads_ref, factor_ref, ids_ref, queries_ref, _, out_ref):
    count, width = queries_ref.shape[0], out_ref.shape[1]
    span, order = grads_ref.shape[0], factor_ref.shape[1]
    rows = span * LANES // width
    offset = pl.multiple_of(lax.axis_index("groups") * width, width)
    out_ref[:count, :] = queries_ref[:, pl.ds(offset, width)]
    right = jnp.dot(grads_ref[...], factor_ref[...], preferred_element_type=jnp.float32)
    live = lax.broadcasted_iota(jnp.int32, (span, order), 0) < lengths_ref[0]
    masked = jnp.where(live, right, 0.0)
    both = jnp.concatenate([masked, jnp.broadcast_to(ids_ref[...], (span, LANES - order))], axis=1)
    wide = jnp.concatenate([both[r : r + rows, :] for r in range(0, span, rows)], axis=1)
    out_ref[count : count + rows, :] = wide.astype(out_ref.dtype)
    if count + rows < out_ref.shape[0]:
        out_ref[count + rows :, :] = jnp.zeros((out_ref.shape[0] - count - rows, width), out_ref.dtype)


def own_share(lengths, grads, factor, ids, queries, after, groups):
    count, depth = queries.shape
    width = depth // groups
    span, order = grads.shape[0], factor.shape[1]
    rows = span * LANES // width
    ids = jnp.pad(ids.astype(jnp.float32)[None, :], ((0, 0), (0, LANES - order - count)))
    vmem = pl.BlockSpec(memory_space=pltpu.VMEM)
    return pl.pallas_call(
        share_body,
        in_specs=[pl.BlockSpec(memory_space=pltpu.SMEM)] + [vmem] * 4 + [pl.BlockSpec(memory_space=pl.ANY)],
        out_specs=vmem,
        out_shape=jax.ShapeDtypeStruct((-(-(count + rows) // 8) * 8, width), queries.dtype),
        compiler_params=pltpu.CompilerParams(vmem_limit_bytes=12 * MIB),
        cost_estimate=SMALL,
        name="own_share",
    )(lengths, grads, factor, ids, queries, after)


def gather_rows(x_refs, xn):
    rows = x_refs[0].shape[0]
    for k, ref in enumerate(x_refs):
        xn[k * rows : (k + 1) * rows, :] = ref[...]


def gated(gate, up):
    return (jax.nn.silu(gate) * up).astype(jnp.bfloat16)


def project(xn, gate_ref, up_ref, mix_ref, f_ref):
    units, order = f_ref.shape
    wide = 2 * LANES

    def product(w):
        return jnp.dot(xn[...], w, preferred_element_type=jnp.float32)

    total = jnp.zeros((xn.shape[0], order), jnp.float32)
    hidden, start = None, 0
    for at in range(0, units, wide):
        if at + wide <= units:
            gate = product(gate_ref[:, at : at + wide])
            if hidden is not None:
                total += jnp.dot(hidden, f_ref[start:at, :], preferred_element_type=jnp.float32)
            hidden = gated(gate, product(up_ref[:, at : at + wide]))
        else:
            both = product(mix_ref[...])
            if hidden is not None:
                total += jnp.dot(hidden, f_ref[start:at, :], preferred_element_type=jnp.float32)
            hidden = gated(both[:, :LANES], both[:, LANES:])
        start = at
    return total + jnp.dot(hidden, f_ref[start:, :], preferred_element_type=jnp.float32)


def first_body(pieces, *refs):
    x_refs, (gate_hbm, up_hbm, f_ref, out_ref, gate_ref, up_ref, mix_ref, xn, sems) = refs[:pieces], refs[pieces:]
    depth, units = gate_ref.shape
    parts = sems.shape[1]
    copies = []
    for p in range(parts):
        rows = pl.ds(p * (depth // parts), depth // parts)
        copies.append(pltpu.make_async_copy(gate_hbm.at[rows], gate_ref.at[rows], sems.at[0, p]))
        copies.append(pltpu.make_async_copy(up_hbm.at[rows], up_ref.at[rows], sems.at[1, p]))
    for copy in copies:
        copy.start()
    gather_rows(x_refs, xn)
    for copy in copies:
        copy.wait()
    if units % (2 * LANES):
        mix_ref[:, :LANES] = gate_ref[:, units - LANES :]
        mix_ref[:, LANES:] = up_ref[:, units - LANES :]
    out_ref[...] = project(xn, gate_ref, up_ref, mix_ref, f_ref)


def first_chunk(xs, gate_weight, up_weight, in_factor, index, tokens):
    pieces = len(xs)
    rows, depth = xs[0].shape
    units, order = in_factor.shape
    total = pieces * rows
    vmem = pl.BlockSpec(memory_space=pltpu.VMEM)
    hbm = pl.BlockSpec(memory_space=pltpu.HBM)
    mix = 2 * LANES if units % (2 * LANES) else LANES
    left, *weights = pl.pallas_call(
        functools.partial(first_body, pieces),
        grid=(1,),
        in_specs=[vmem] * pieces + [hbm, hbm, vmem],
        out_specs=[pl.BlockSpec((total, order), lambda i: (index, 0)), vmem, vmem, vmem],
        out_shape=[
            jax.ShapeDtypeStruct((tokens, order), jnp.float32),
            pltpu.VMEM((depth, units), jnp.bfloat16),
            pltpu.VMEM((depth, units), jnp.bfloat16),
            pltpu.VMEM((depth if mix > LANES else 16, mix), jnp.bfloat16),
        ],
        scratch_shapes=[pltpu.VMEM((total, depth), jnp.bfloat16), pltpu.SemaphoreType.DMA((2, 4))],
        compiler_params=pltpu.CompilerParams(vmem_limit_bytes=12 * MIB),
        cost_estimate=SMALL,
        name="first_chunk",
    )(
        *xs,
        pltpu.with_memory_space_constraint(gate_weight, pltpu.HBM),
        pltpu.with_memory_space_constraint(up_weight, pltpu.HBM),
        in_factor,
    )
    return left, weights


def chunk_body(pieces, *refs):
    x_refs, (gate_ref, up_ref, mix_ref, f_ref, _, out_ref, _, _, _, xn) = refs[:pieces], refs[pieces:]
    gather_rows(x_refs, xn)
    out_ref[...] = project(xn, gate_ref, up_ref, mix_ref, f_ref)


def chunk(xs, weights, in_factor, left, index):
    pieces = len(xs)
    rows, depth = xs[0].shape
    order = in_factor.shape[1]
    total = pieces * rows
    vmem = pl.BlockSpec(memory_space=pltpu.VMEM)
    left, *weights = pl.pallas_call(
        functools.partial(chunk_body, pieces),
        grid=(1,),
        in_specs=[vmem] * (pieces + 4) + [pl.BlockSpec(memory_space=pl.ANY)],
        out_specs=[pl.BlockSpec((total, order), lambda i: (index, 0)), vmem, vmem, vmem],
        out_shape=[jax.ShapeDtypeStruct(left.shape, left.dtype)] + [pltpu.VMEM(w.shape, w.dtype) for w in weights],
        scratch_shapes=[pltpu.VMEM((total, depth), jnp.bfloat16)],
        input_output_aliases={pieces + 4: 0, pieces: 1, pieces + 1: 2, pieces + 2: 3},
        compiler_params=pltpu.CompilerParams(vmem_limit_bytes=12 * MIB),
        cost_estimate=SMALL,
        name="chunk",
    )(*xs, *[pltpu.with_memory_space_constraint(w, pltpu.VMEM) for w in weights], in_factor, left)
    return left, weights


def masked_of(side_ref, name, count, span, order):
    width = side_ref.shape[2]
    rows = span * LANES // width
    wide = side_ref[name, count : count + rows, :].astype(jnp.float32)
    both = jnp.concatenate([wide[:, c : c + LANES] for c in range(0, width, LANES)], axis=0)
    return both[:, :order].astype(jnp.bfloat16)


def one_sketch(left_ref, masked, at, half):
    left = jnp.concatenate([left_ref[p * half : (p + 1) * half, :] for p in at], axis=0)
    high = left.astype(jnp.bfloat16)
    low = (left - high.astype(jnp.float32)).astype(jnp.bfloat16)
    return sum(lax.dot_general(part, masked, TN, preferred_element_type=jnp.float32) for part in (low, high))


def sketch_body(places, half, count, names, left_ref, side_ref, out_ref):
    for r, at in enumerate(places):
        masked = masked_of(side_ref, names[r], count, 2 * half, left_ref.shape[1])
        out_ref[r] = one_sketch(left_ref, masked, at, half).astype(out_ref.dtype)


def sketches(places, half, count, names, left, side):
    order = left.shape[1]
    vmem = pl.BlockSpec(memory_space=pltpu.VMEM)
    made = pl.pallas_call(
        functools.partial(sketch_body, places, half, count),
        in_specs=[pl.BlockSpec(memory_space=pltpu.SMEM), vmem, vmem],
        out_specs=vmem,
        out_shape=jax.ShapeDtypeStruct((len(places), order, order), jnp.bfloat16),
        compiler_params=pltpu.CompilerParams(vmem_limit_bytes=8 * MIB),
        cost_estimate=SMALL,
        name="sketches",
    )(names, left, side)
    return made.reshape(len(places), order * order)


def finish_body(places, half, groups, count, names, left_ref, early_ref, *refs):
    share_refs, (ids_ref, out_ref, twice, flat, whole) = refs[:groups], refs[groups:]
    order = left_ref.shape[1]
    early = early_ref.shape[0]
    slots = flat.shape[1]
    lane = lax.broadcasted_iota(jnp.int32, (order // 2, 2 * order), 1)
    for r, at in enumerate(places):
        masked = masked_of(share_refs[0], names[early + r], count, 2 * half, order)
        sketch = one_sketch(left_ref, masked, at, half)
        twice[...] = jnp.concatenate([sketch, sketch], axis=1)
        even = twice[pl.ds(0, order // 2, 2), :]
        odd = twice[pl.ds(1, order // 2, 2), :]
        flat[:, r, :] = jnp.where(lane < order, even, odd)
    late = jnp.concatenate([flat[c] for c in range(order // 2)], axis=1).astype(jnp.bfloat16)
    whole[...] = jnp.concatenate([late, early_ref[...]], axis=0)

    devices, _, width = share_refs[0].shape
    group = lax.axis_index("groups")
    scores = 0.0
    for r, ref in enumerate(share_refs):
        offset = pl.multiple_of(lax.rem(group + r, groups) * width, width)
        queries = ref[:, :count, :].reshape(devices * count, width)
        scores += lax.dot_general(whole[:, pl.ds(offset, width)], queries, NT, preferred_element_type=jnp.float32)
    value = lax.broadcasted_iota(jnp.int32, (NVAL, ids_ref.shape[1]), 0)
    members = (value == ids_ref[...]).astype(jnp.bfloat16)
    rows = 0.0
    for _ in range(3):
        part = scores.astype(jnp.bfloat16)
        scores = scores - part.astype(jnp.float32)
        rows += lax.dot_general(part, members, NT, preferred_element_type=jnp.float32)
    for r in range(early):
        out_ref[pl.ds(names[r], 1), :] = rows[slots + r : slots + r + 1, :]
    for r in range(len(places)):
        out_ref[pl.ds(names[early + r], 1), :] = rows[r : r + 1, :]


def finish(places, half, count, names, left, early, shares, ids):
    order = left.shape[1]
    vmem = pl.BlockSpec(memory_space=pltpu.VMEM)
    slots = -(-len(places) // 8) * 8
    return pl.pallas_call(
        functools.partial(finish_body, places, half, len(shares), count),
        in_specs=[pl.BlockSpec(memory_space=pltpu.SMEM)] + [vmem] * (3 + len(shares)),
        out_specs=vmem,
        out_shape=jax.ShapeDtypeStruct((names.shape[0], NVAL), jnp.float32),
        scratch_shapes=[
            pltpu.VMEM((order, 2 * order), jnp.float32),
            pltpu.VMEM((order // 2, slots, 2 * order), jnp.float32),
            pltpu.VMEM((slots + early.shape[0], order * order), jnp.bfloat16),
        ],
        compiler_params=pltpu.CompilerParams(vmem_limit_bytes=14 * MIB),
        cost_estimate=SMALL,
        name="finish",
    )(names, left, early, *shares, ids)


def arrivals(ring, devices):
    chips = len(ring)
    far = chips // 2
    table, spots = [[] for _ in range(devices)], []
    for distance in range(far + 1):
        for sign, piece in [(1, 0)] if distance in (0, far) else [(-1, 0), (1, 1)]:
            for me in range(devices):
                chip = ring[(ring.index(me // 2) + sign * distance) % chips]
                table[me] += [2 * chip + me % 2, 2 * chip + 1 - me % 2]
            if distance == 0:
                halves = [(0, 0), (0, 1)]
            elif distance == far:
                halves = [(chips - 1, 0), (chips - 1, 1)]
            else:
                halves = [(2 * distance - 1, piece), (2 * distance, piece)]
            spots.append([4 * k + 2 + p for k, p in halves])
            spots.append([4 * k + 4 + p for k, p in halves])
    return table, spots


def local(
    devices,
    groups,
    layer_inputs,
    example_lengths,
    norm_gain,
    gate_weight,
    up_weight,
    in_factor,
    out_factor,
    out_grads,
    queries,
    query_ids,
):
    chips = devices // 2
    ring = chip_ring(chips)
    me = lax.axis_index("examples")

    forward = [(ring[r] * 2 + c, ring[(r + 1) % chips] * 2 + c) for r in range(chips) for c in range(2)]
    backward = [(b, a) for a, b in forward]
    other_core = [(d, d ^ 1) for d in range(devices)]

    span, depth = layer_inputs.shape
    half = span // 2
    order = in_factor.shape[1]
    units = gate_weight.shape[1]
    short = -units % LANES
    if short:
        gate_weight = jnp.pad(gate_weight, ((0, 0), (0, short)))
        up_weight = jnp.pad(up_weight, ((0, 0), (0, short)))
        in_factor = jnp.pad(in_factor, ((0, short), (0, 0)))
    tokens = 2 * span * chips + span

    def send(x, way):
        return lax.ppermute(x, "examples", way)

    x_a, x_b = prepare(layer_inputs, norm_gain[None, :])
    coming = {
        1: (send(x_a, forward), send(x_a, backward)),
        2: (send(x_b, forward), send(x_b, backward)),
    }
    swapped = tuple(send(x, other_core) for x in (x_a, x_b))
    nq = queries.shape[0]
    side = own_share(example_lengths, out_grads, out_factor, query_ids, queries, x_a, groups)
    side, x_a = lax.optimization_barrier((side, x_a))
    side = lax.all_gather(side, "examples", axis=0)
    left, weights = first_chunk((x_a, x_b), gate_weight, up_weight, in_factor, 1, tokens)

    names, spots = arrivals(ring, devices)
    names = lax.dynamic_index_in_dim(jnp.array(names, jnp.int32), me, keepdims=False)

    for k in range(1, chips):
        own_1, own_2, left = lax.optimization_barrier((*coming.pop(k), left))
        own = (own_1, own_2)
        if k + 2 < chips - 1:
            coming[k + 2] = (send(own_1, forward), send(own_2, backward))
        elif k + 2 == chips - 1:
            opposite = send(own_1, forward)
        elif k + 1 == chips - 1:
            coming[chips - 1] = (opposite, send(own_2, backward))
        before, swapped = swapped, tuple(send(x, other_core) for x in own)
        if k < chips - 1:
            left, weights = chunk(before + own, weights, in_factor, left, k)
        if k == chips - 3:
            side, left = lax.optimization_barrier((side, left))
            ids = side[:, nq, order : order + nq].astype(jnp.int32).reshape(1, devices * nq)
            shares = [side]
            for r in range(1, groups):
                way = [((g + r) % groups, g) for g in range(groups)]
                shares.append(lax.ppermute(side, "groups", way))
            ready = devices - 6
            early = [sketches(spots[:ready], half, nq, names[:ready], left, side)]
        if k == chips - 2:
            left, weights = chunk(swapped, weights, in_factor, left, 2 * k + 2)
            early.append(sketches(spots[ready:-2], half, nq, names[ready:-2], left, side))
            early = jnp.concatenate(early, axis=0)
            early, left = lax.optimization_barrier((early, left))
    left, weights = chunk(own, weights, in_factor, left, 2 * chips - 1)
    left, weights = chunk(swapped, weights, in_factor, left, 2 * chips)

    partial = finish(spots[-2:], half, nq, names, left, early, shares, ids)
    shares = lax.all_to_all(partial, "examples", split_axis=0, concat_axis=0, tiled=True)
    return jnp.sum(shares, axis=0, keepdims=True)


def solution(mesh):
    return jax.shard_map(
        functools.partial(local, mesh.shape["examples"], mesh.shape["groups"]),
        mesh=mesh,
        in_specs=(
            P(("groups", "examples"), None),
            P(("groups", "examples")),
            P(),
            P(None, "examples"),
            P(None, "examples"),
            P("examples", None),
            P(),
            P(("groups", "examples"), None),
            P("examples", None),
            P("examples"),
        ),
        out_specs=P(("groups", "examples"), None),
        check_vma=False,
    )
```

time: 190 us -> 177 us (0.932)
  blocking collectives: 33.6 us -> 11.4 us
  waiting for transfers between devices: 9.96 us -> 29.1 us
  local copies, waits for them, and re-layouts: 41.6 us -> 34.8 us
  Pallas kernels: 61 us -> 58.3 us
    all_gather x1 -> x0, blocking collectives: 24.3 us -> none  [local(): lax.all_gather(jnp.concatenate([masked, ids_row], axis=0), 'examples', ax...]
    ppermute x30, waiting for transfers between devices: 9.92 us -> 29 us  [send(): return lax.ppermute(x, 'examples', way)]
    unnamed x39 -> x40, local copies, waits for them, and re-layouts: 38.9 us -> 32.1 us
    pallas_call x9, Pallas kernels: 45.5 us -> 42.5 us  [chunk(): pl.pallas_call(functools.partial(chunk_body, pieces), grid=(1,), in_specs...]
    all_to_all x1, blocking collectives: 9.31 us -> 11.4 us  [local(): lax.all_to_all(partial, 'examples', split_axis=0, concat_axis=0, tiled=True)]
    pallas_call x5 -> x6, Pallas kernels: 15.5 us -> 15.8 us  [the longest x1 8.96 us: first_chunk(): pl.pallas_call(functools.partial(first_body, pieces), grid=(1,), in_specs...]
  transfers between devices with their start and end apart: 32 -> 32, of which waited for: 2 -> 4; matrix products, arithmetic and copies ran while one was open for 3% -> 3% of each run, Pallas kernels for 30% -> 30%
where the time goes in v6:
time: 177 us; the launch traced here: 176 us
  Pallas kernels  58.3 us (33%)
  local copies, waits for them, and re-layouts  34.8 us (20%)
  waiting for transfers between devices  29.1 us (16%)
  starting transfers between devices  24 us (14%)
  between operations  14.4 us (8%)
  blocking collectives  11.4 us (6%)
  other arithmetic  3.71 us (2%)
    pallas_call x9, Pallas kernels, chunk(): pl.pallas_call(functools.partial(chunk_body, pieces), grid=(1,), in_specs...  42.5 us
    unnamed x40, local copies, waits for them, and re-layouts  32.1 us
    ppermute x30, waiting for transfers between devices, send(): return lax.ppermute(x, 'examples', way)  29 us
    ppermute x30, starting transfers between devices, send(): return lax.ppermute(x, 'examples', way)  22.5 us
    all_to_all x1, blocking collectives, local(): lax.all_to_all(partial, 'examples', split_axis=0, concat_axis=0, tiled=True)  11.4 us
    pallas_call x1, Pallas kernels, first_chunk(): pl.pallas_call(functools.partial(first_body, pieces), grid=(1,), in_specs...  8.96 us
  transfers between devices with their start and end apart: 32, of which 4 were waited for; matrix products, arithmetic and copies ran while one was open for 3% of the time, Pallas kernels for 30%

profile of v6, /device:TPU:0, one launch (start us, length us, event | category | flops | bytes accessed | tf_op | source)
XLA Modules:
  0.0 175.6 jit_solution(13516793444334222020)
XLA Ops:
  16.0 3.1 %collective-permute-start = (bf16[64,4096]{1,0:T(8,128)(2,1)}, bf16[64,4096]{1,0:T(8,128)(2,1)}, u32[]{:S(2)}, u32[]{:S(2)}) collective-permute-start(bf16[64,4096]{1,0:T(8,128)(2,1)} %get-tuple-element.72._.refs_0_), channel_id=1, source_target_pairs={{0,4},{1,5},{4,8},{5,9},{8,12},{9,13},{12,14},{13,15},{14,10},{15,... | collective-permute-start | bytes 1572872 | tf_op jit(solution)/shard_map/ppermute | solution.py:345
  21.8 9.0 %first_chunk.1 = (f32[2176,64]{1,0:T(8,128)S(1)}, bf16[4096,896]{1,0:T(8,128)(2,1)S(1)}, bf16[4096,896]{1,0:T(8,128)(2,1)S(1)}, bf16[4096,256]{1,0:T(8,128)(2,1)S(1)}) custom-call(bf16[64,4096]{1,0:T(8,128)(2,1)} %get-tuple-element.72._.refs_0_, bf16[64,4096]{1,0:T(8,128)(2,1)} %get-tuple-element.73.refs_1_, bf16[4096,896]{1,0:T(8,128)(2,1)} %refs_2_.1, ...), custom_call_target="tpu_custom_call" | custom-call | flops 1000000 | bytes 100000 | tf_op jit(solution)/shard_map/first_chunk/pallas_call | solution.py:148
  30.8 3.0 %collective-permute-done.refs_2_ = bf16[64,4096]{1,0:T(8,128)(2,1)} collective-permute-done((bf16[64,4096]{1,0:T(8,128)(2,1)}, bf16[64,4096]{1,0:T(8,128)(2,1)}, u32[]{:S(2)}, u32[]{:S(2)}) %collective-permute-start) | collective-permute-done | bytes 524320 | tf_op jit(solution)/shard_map/ppermute | solution.py:345
  36.8 10.7 %collective-permute-done.6.refs_2_ = bf16[64,4096]{1,0:T(8,128)(2,1)} collective-permute-done((bf16[64,4096]{1,0:T(8,128)(2,1)}, bf16[64,4096]{1,0:T(8,128)(2,1)}, u32[]{:S(2)}, u32[]{:S(2)}) %collective-permute-start.6) | collective-permute-done | bytes 524320 | tf_op jit(solution)/shard_map/ppermute | solution.py:345
  48.7 5.7 %chunk.9 = (f32[2176,64]{1,0:T(8,128)S(1)}, bf16[4096,896]{1,0:T(8,128)(2,1)S(1)}, bf16[4096,896]{1,0:T(8,128)(2,1)S(1)}, bf16[4096,256]{1,0:T(8,128)(2,1)S(1)}) custom-call(bf16[64,4096]{1,0:T(8,128)(2,1)} %collective-permute-done.8.refs_0_, ...), custom_call_target="tpu_custom_call", output_to_operand_aliasing={{0}: (8, {}), {1}: (4, {}), {2}: (5, {}), {3}: (6, {})} | custom-call | flops 1000000 | bytes 100000 | tf_op jit(solution)/shard_map/chunk/pallas_call | solution.py:184
  56.4 7.3 %collective-permute-done.2.refs_2_ = bf16[64,4096]{1,0:T(8,128)(2,1)S(1)} collective-permute-done((bf16[64,4096]{1,0:T(8,128)(2,1)}, bf16[64,4096]{1,0:T(8,128)(2,1)S(1)}, u32[]{:S(2)}, u32[]{:S(2)}) %collective-permute-start.2) | collective-permute-done | bytes 524320 | tf_op jit(solution)/shard_map/ppermute | solution.py:345
  66.0 5.3 %chunk.10 = (f32[2176,64]{1,0:T(8,128)S(1)}, bf16[4096,896]{1,0:T(8,128)(2,1)S(1)}, bf16[4096,896]{1,0:T(8,128)(2,1)S(1)}, bf16[4096,256]{1,0:T(8,128)(2,1)S(1)}) custom-call(bf16[64,4096]{1,0:T(8,128)(2,1)S(1)} %collective-permute-done.4.refs_0_, ...), custom_call_target="tpu_custom_call", output_to_operand_aliasing={{0}: (8, {}), {1}: (4, {}), {2}: (5, {}), {3}: (6, {})} | custom-call | flops 1000000 | bytes 100000 | tf_op jit(solution)/shard_map/chunk/pallas_call | solution.py:184
  71.9 4.2 %chunk.11 = (f32[2176,64]{1,0:T(8,128)S(1)}, bf16[4096,896]{1,0:T(8,128)(2,1)S(1)}, bf16[4096,896]{1,0:T(8,128)(2,1)S(1)}, bf16[4096,256]{1,0:T(8,128)(2,1)S(1)}) custom-call(bf16[64,4096]{1,0:T(8,128)(2,1)S(1)} %collective-permute-done.16.refs_0_, ...), custom_call_target="tpu_custom_call", output_to_operand_aliasing={{0}: (8, {}), {1}: (4, {}), {2}: (5, {}), {3}: (6, {})} | custom-call | flops 1000000 | bytes 100000 | tf_op jit(solution)/shard_map/chunk/pallas_call | solution.py:184
  78.8 7.9 %collective-permute-done.10.refs_2_ = bf16[64,4096]{1,0:T(8,128)(2,1)} collective-permute-done((bf16[64,4096]{1,0:T(8,128)(2,1)S(1)}, bf16[64,4096]{1,0:T(8,128)(2,1)}, u32[]{:S(2)}, u32[]{:S(2)}) %collective-permute-start.10) | collective-permute-done | bytes 524320 | tf_op jit(solution)/shard_map/ppermute | solution.py:345
  88.3 5.4 %chunk.12 = (f32[2176,64]{1,0:T(8,128)S(1)}, bf16[4096,896]{1,0:T(8,128)(2,1)S(1)}, bf16[4096,896]{1,0:T(8,128)(2,1)S(1)}, bf16[4096,256]{1,0:T(8,128)(2,1)S(1)}) custom-call(bf16[64,4096]{1,0:T(8,128)(2,1)S(1)} %collective-permute-done.12.refs_0_, ...), custom_call_target="tpu_custom_call", output_to_operand_aliasing={{0}: (8, {}), {1}: (4, {}), {2}: (5, {}), {3}: (6, {})} | custom-call | flops 1000000 | bytes 100000 | tf_op jit(solution)/shard_map/chunk/pallas_call | solution.py:184
  94.3 5.4 %chunk.13 = (f32[2176,64]{1,0:T(8,128)S(1)}, bf16[4096,896]{1,0:T(8,128)(2,1)S(1)}, bf16[4096,896]{1,0:T(8,128)(2,1)S(1)}, bf16[4096,256]{1,0:T(8,128)(2,1)S(1)}) custom-call(bf16[64,4096]{1,0:T(8,128)(2,1)S(1)} %collective-permute-done.21.refs_0_, ...), custom_call_target="tpu_custom_call", output_to_operand_aliasing={{0}: (8, {}), {1}: (4, {}), {2}: (5, {}), {3}: (6, {})} | custom-call | flops 1000000 | bytes 100000 | tf_op jit(solution)/shard_map/chunk/pallas_call | solution.py:184
  99.7 2.9 %copy-done = bf16[4096,896]{1,0:T(8,128)(2,1)} copy-done((bf16[4096,896]{1,0:T(8,128)(2,1)}, bf16[4096,896]{1,0:T(8,128)(2,1)S(1)}, u32[]{:S(2)}) %copy-start) | copy-done | bytes 7340056
  102.7 3.0 %copy-done.4 = bf16[4096,896]{1,0:T(8,128)(2,1)} copy-done((bf16[4096,896]{1,0:T(8,128)(2,1)}, bf16[4096,896]{1,0:T(8,128)(2,1)S(1)}, u32[]{:S(2)}) %copy-start.4) | copy-done | bytes 7340056
  115.2 3.1 %copy-done.1 = bf16[4096,896]{1,0:T(8,128)(2,1)S(1)} copy-done((bf16[4096,896]{1,0:T(8,128)(2,1)S(1)}, bf16[4096,896]{1,0:T(8,128)(2,1)}, u32[]{:S(2)}) %copy-start.1) | copy-done | bytes 7340056
  118.3 3.1 %copy-done.5 = bf16[4096,896]{1,0:T(8,128)(2,1)S(1)} copy-done((bf16[4096,896]{1,0:T(8,128)(2,1)S(1)}, bf16[4096,896]{1,0:T(8,128)(2,1)}, u32[]{:S(2)}) %copy-start.5) | copy-done | bytes 7340056
  121.4 5.7 %chunk.14 = (f32[2176,64]{1,0:T(8,128)S(1)}, bf16[4096,896]{1,0:T(8,128)(2,1)S(1)}, bf16[4096,896]{1,0:T(8,128)(2,1)S(1)}, bf16[4096,256]{1,0:T(8,128)(2,1)S(1)}) custom-call(bf16[64,4096]{1,0:T(8,128)(2,1)} %collective-permute-done.26.refs_0_, ...), custom_call_target="tpu_custom_call", output_to_operand_aliasing={{0}: (8, {}), {1}: (4, {}), {2}: (5, {}), {3}: (6, {})} | custom-call | flops 1000000 | bytes 100000 | tf_op jit(solution)/shard_map/chunk/pallas_call | solution.py:184
  127.1 3.6 %chunk.15 = (f32[2176,64]{1,0:T(8,128)S(1)}, bf16[4096,896]{1,0:T(8,128)(2,1)S(1)}, bf16[4096,896]{1,0:T(8,128)(2,1)S(1)}, bf16[4096,256]{1,0:T(8,128)(2,1)S(1)}) custom-call(bf16[64,4096]{1,0:T(8,128)(2,1)} %collective-permute-done.24.refs_0_, ...), custom_call_target="tpu_custom_call", output_to_operand_aliasing={{0}: (6, {}), {1}: (2, {}), {2}: (3, {}), {3}: (4, {})} | custom-call | flops 1000000 | bytes 100000 | tf_op jit(solution)/shard_map/chunk/pallas_call | solution.py:184
  130.8 2.9 %copy-done.2 = bf16[4096,896]{1,0:T(8,128)(2,1)} copy-done((bf16[4096,896]{1,0:T(8,128)(2,1)}, bf16[4096,896]{1,0:T(8,128)(2,1)S(1)}, u32[]{:S(2)}) %copy-start.2) | copy-done | bytes 7340056
  133.7 3.0 %copy-done.6 = bf16[4096,896]{1,0:T(8,128)(2,1)} copy-done((bf16[4096,896]{1,0:T(8,128)(2,1)}, bf16[4096,896]{1,0:T(8,128)(2,1)S(1)}, u32[]{:S(2)}) %copy-start.6) | copy-done | bytes 7340056
  140.6 3.1 %copy-done.3 = bf16[4096,896]{1,0:T(8,128)(2,1)S(1)} copy-done((bf16[4096,896]{1,0:T(8,128)(2,1)S(1)}, bf16[4096,896]{1,0:T(8,128)(2,1)}, u32[]{:S(2)}) %copy-start.3) | copy-done | bytes 7340056
  143.7 3.1 %copy-done.7 = bf16[4096,896]{1,0:T(8,128)(2,1)S(1)} copy-done((bf16[4096,896]{1,0:T(8,128)(2,1)S(1)}, bf16[4096,896]{1,0:T(8,128)(2,1)}, u32[]{:S(2)}) %copy-start.7) | copy-done | bytes 7340056
  146.8 3.5 %chunk.16 = (f32[2176,64]{1,0:T(8,128)S(1)}, bf16[4096,896]{1,0:T(8,128)(2,1)S(1)}, bf16[4096,896]{1,0:T(8,128)(2,1)S(1)}, bf16[4096,256]{1,0:T(8,128)(2,1)S(1)}) custom-call(bf16[64,4096]{1,0:T(8,128)(2,1)} %collective-permute-done.18.refs_0_, ...), custom_call_target="tpu_custom_call", output_to_operand_aliasing={{0}: (6, {}), {1}: (2, {}), {2}: (3, {}), {3}: (4, {})} | custom-call | flops 1000000 | bytes 100000 | tf_op jit(solution)/shard_map/chunk/pallas_call | solution.py:184
  150.4 3.6 %chunk.17 = (f32[2176,64]{1,0:T(8,128)S(1)}, bf16[4096,896]{1,0:T(8,128)(2,1)S(1)}, bf16[4096,896]{1,0:T(8,128)(2,1)S(1)}, bf16[4096,256]{1,0:T(8,128)(2,1)S(1)}) custom-call(bf16[64,4096]{1,0:T(8,128)(2,1)} %collective-permute-done.28.refs_0_, ...), custom_call_target="tpu_custom_call", output_to_operand_aliasing={{0}: (6, {}), {1}: (2, {}), {2}: (3, {}), {3}: (4, {})} | custom-call | flops 1000000 | bytes 100000 | tf_op jit(solution)/shard_map/chunk/pallas_call | solution.py:184
  156.8 11.4 %all_to_all.9 = f32[16,1,256]{2,1,0:T(1,128)S(1)} all-to-all(f32[16,1,256]{2,1,0:T(1,128)S(1)} %copy.70), channel_id=1, replica_groups=mesh['groups'=2,'examples'=16] {'examples'}, dimensions={0} | all-to-all | bytes 32768 | tf_op jit(solution)/shard_map/all_to_all | solution.py:392
  (109 shorter events, 42.2 us)
Async XLA Ops:
  6.5 99.1 %all-gather.3.cloned.1.call-start = ((), (), s32[]{:S(2)}) async-start(), calls=%async_computation.1 | async-start | bytes 1671168 | tf_op jit(solution)/shard_map/all_gather | solution.py:356
  16.0 17.8 %collective-permute-start = (bf16[64,4096]{1,0:T(8,128)(2,1)}, bf16[64,4096]{1,0:T(8,128)(2,1)}, u32[]{:S(2)}, u32[]{:S(2)}) collective-permute-start(bf16[64,4096]{1,0:T(8,128)(2,1)} %get-tuple-element.72._.refs_0_), channel_id=1, source_target_pairs={{0,4},{1,5},{4,8},{5,9},{8,12},{9,13},{12,14},{13,15},{14,10},{15,... | collective-permute-start | bytes 1572872 | tf_op jit(solution)/shard_map/ppermute | solution.py:345
  19.1 16.2 %collective-permute-start.1 = (bf16[64,4096]{1,0:T(8,128)(2,1)}, bf16[64,4096]{1,0:T(8,128)(2,1)}, u32[]{:S(2)}, u32[]{:S(2)}) collective-permute-start(bf16[64,4096]{1,0:T(8,128)(2,1)} %get-tuple-element.72._.refs_0_), channel_id=1, source_target_pairs={{4,0},{5,1},{8,4},{9,5},{12,8},{13,9},{14,12},{15,13},{10,14},{11,... | collective-permute-start | bytes 1572872 | tf_op jit(solution)/shard_map/ppermute | solution.py:345
  19.1 16.2 %collective-permute-start.8 = (bf16[64,4096]{1,0:T(8,128)(2,1)}, bf16[64,4096]{1,0:T(8,128)(2,1)}, u32[]{:S(2)}, u32[]{:S(2)}) collective-permute-start(bf16[64,4096]{1,0:T(8,128)(2,1)} %get-tuple-element.72._.refs_0_), channel_id=1, source_target_pairs={{0,1},{1,0},{2,3},{3,2},{4,5},{5,4},{6,7},{7,6},{8,9},{9,8},{10,11... | collective-permute-start | bytes 1572872 | tf_op jit(solution)/shard_map/ppermute | solution.py:345
  19.1 16.7 %collective-permute-start.9 = (bf16[64,4096]{1,0:T(8,128)(2,1)}, bf16[64,4096]{1,0:T(8,128)(2,1)}, u32[]{:S(2)}, u32[]{:S(2)}) collective-permute-start(bf16[64,4096]{1,0:T(8,128)(2,1)} %get-tuple-element.73.refs_1_), channel_id=1, source_target_pairs={{0,1},{1,0},{2,3},{3,2},{4,5},{5,4},{6,7},{7,6},{8,9},{9,8},{10,11... | collective-permute-start | bytes 1572872 | tf_op jit(solution)/shard_map/ppermute | solution.py:345
  19.6 27.9 %collective-permute-start.6 = (bf16[64,4096]{1,0:T(8,128)(2,1)}, bf16[64,4096]{1,0:T(8,128)(2,1)}, u32[]{:S(2)}, u32[]{:S(2)}) collective-permute-start(bf16[64,4096]{1,0:T(8,128)(2,1)} %get-tuple-element.73.refs_1_), channel_id=1, source_target_pairs={{0,4},{1,5},{4,8},{5,9},{8,12},{9,13},{12,14},{13,15},{14,10},{15,... | collective-permute-start | bytes 1572872 | tf_op jit(solution)/shard_map/ppermute | solution.py:345
  33.8 20.7 %collective-permute-start.7 = (bf16[64,4096]{1,0:T(8,128)(2,1)}, bf16[64,4096]{1,0:T(8,128)(2,1)S(1)}, u32[]{:S(2)}, u32[]{:S(2)}) collective-permute-start(bf16[64,4096]{1,0:T(8,128)(2,1)} %get-tuple-element.73.refs_1_), channel_id=1, source_target_pairs={{4,0},{5,1},{8,4},{9,5},{12,8},{13,9},{14,12},{15,13},{10,14},{11,... | collective-permute-start | bytes 1572872 | tf_op jit(solution)/shard_map/ppermute | solution.py:345
  35.3 19.3 %collective-permute-start.4 = (bf16[64,4096]{1,0:T(8,128)(2,1)}, bf16[64,4096]{1,0:T(8,128)(2,1)S(1)}, u32[]{:S(2)}, u32[]{:S(2)}) collective-permute-start(bf16[64,4096]{1,0:T(8,128)(2,1)} %collective-permute-done.refs_2_), channel_id=1, source_target_pairs={{0,1},{1,0},{2,3},{3,2},{4,5},{5,4},{6,7},{7,6},{8,9},{9,8},{10,11... | collective-permute-start | bytes 1572872 | tf_op jit(solution)/shard_map/ppermute | solution.py:345
  35.3 19.8 %collective-permute-start.5 = (bf16[64,4096]{1,0:T(8,128)(2,1)}, bf16[64,4096]{1,0:T(8,128)(2,1)S(1)}, u32[]{:S(2)}, u32[]{:S(2)}) collective-permute-start(bf16[64,4096]{1,0:T(8,128)(2,1)} %collective-permute-done.1.refs_3_), channel_id=1, source_target_pairs={{0,1},{1,0},{2,3},{3,2},{4,5},{5,4},{6,7},{7,6},{8,9},{9,8},{10,11... | collective-permute-start | bytes 1572872 | tf_op jit(solution)/shard_map/ppermute | solution.py:345
  35.8 27.9 %collective-permute-start.2 = (bf16[64,4096]{1,0:T(8,128)(2,1)}, bf16[64,4096]{1,0:T(8,128)(2,1)S(1)}, u32[]{:S(2)}, u32[]{:S(2)}) collective-permute-start(bf16[64,4096]{1,0:T(8,128)(2,1)} %collective-permute-done.refs_2_), channel_id=1, source_target_pairs={{0,4},{1,5},{4,8},{5,9},{8,12},{9,13},{12,14},{13,15},{14,10},{15,... | collective-permute-start | bytes 1572872 | tf_op jit(solution)/shard_map/ppermute | solution.py:345
  47.5 23.7 %collective-permute-start.3 = (bf16[64,4096]{1,0:T(8,128)(2,1)}, bf16[64,4096]{1,0:T(8,128)(2,1)S(1)}, u32[]{:S(2)}, u32[]{:S(2)}) collective-permute-start(bf16[64,4096]{1,0:T(8,128)(2,1)} %collective-permute-done.1.refs_3_), channel_id=1, source_target_pairs={{4,0},{5,1},{8,4},{9,5},{12,8},{13,9},{14,12},{15,13},{10,14},{11,... | collective-permute-start | bytes 1572872 | tf_op jit(solution)/shard_map/ppermute | solution.py:345
  54.5 16.8 %collective-permute-start.16 = (bf16[64,4096]{1,0:T(8,128)(2,1)}, bf16[64,4096]{1,0:T(8,128)(2,1)S(1)}, u32[]{:S(2)}, u32[]{:S(2)}) collective-permute-start(bf16[64,4096]{1,0:T(8,128)(2,1)} %collective-permute-done.6.refs_2_), channel_id=1, source_target_pairs={{0,1},{1,0},{2,3},{3,2},{4,5},{5,4},{6,7},{7,6},{8,9},{9,8},{10,11... | collective-permute-start | bytes 1572872 | tf_op jit(solution)/shard_map/ppermute | solution.py:345
  54.6 17.3 %collective-permute-start.17 = (bf16[64,4096]{1,0:T(8,128)(2,1)S(1)}, bf16[64,4096]{1,0:T(8,128)(2,1)S(1)}, u32[]{:S(2)}, u32[]{:S(2)}) collective-permute-start(bf16[64,4096]{1,0:T(8,128)(2,1)S(1)} %collective-permute-done.7.refs_3_), channel_id=1, source_target_pairs={{0,1},{1,0},{2,3},{3,2},{4,5},{5,4},{6,7},{7,6},{8,9},{9,8},{10,11... | collective-permute-start | bytes 1572872 | tf_op jit(solution)/shard_map/ppermute | solution.py:345
  55.1 21.1 %collective-permute-start.14 = (bf16[64,4096]{1,0:T(8,128)(2,1)}, bf16[64,4096]{1,0:T(8,128)(2,1)}, u32[]{:S(2)}, u32[]{:S(2)}) collective-permute-start(bf16[64,4096]{1,0:T(8,128)(2,1)} %collective-permute-done.6.refs_2_), channel_id=1, source_target_pairs={{0,4},{1,5},{4,8},{5,9},{8,12},{9,13},{12,14},{13,15},{14,10},{15,... | collective-permute-start | bytes 1572872 | tf_op jit(solution)/shard_map/ppermute | solution.py:345
  76.1 17.6 %collective-permute-start.11 = (bf16[64,4096]{1,0:T(8,128)(2,1)S(1)}, bf16[64,4096]{1,0:T(8,128)(2,1)}, u32[]{:S(2)}, u32[]{:S(2)}) collective-permute-start(bf16[64,4096]{1,0:T(8,128)(2,1)S(1)} %collective-permute-done.3.refs_3_), channel_id=1, source_target_pairs={{4,0},{5,1},{8,4},{9,5},{12,8},{13,9},{14,12},{15,13},{10,14},{11,... | collective-permute-start | bytes 1572872 | tf_op jit(solution)/shard_map/ppermute | solution.py:345
  78.1 15.7 %collective-permute-start.21 = (bf16[64,4096]{1,0:T(8,128)(2,1)}, bf16[64,4096]{1,0:T(8,128)(2,1)S(1)}, u32[]{:S(2)}, u32[]{:S(2)}) collective-permute-start(bf16[64,4096]{1,0:T(8,128)(2,1)} %collective-permute-done.14.refs_2_), channel_id=1, source_target_pairs={{0,1},{1,0},{2,3},{3,2},{4,5},{5,4},{6,7},{7,6},{8,9},{9,8},{10,11... | collective-permute-start | bytes 1572872 | tf_op jit(solution)/shard_map/ppermute | solution.py:345
  78.2 16.2 %collective-permute-start.22 = (bf16[64,4096]{1,0:T(8,128)(2,1)}, bf16[64,4096]{1,0:T(8,128)(2,1)S(1)}, u32[]{:S(2)}, u32[]{:S(2)}) collective-permute-start(bf16[64,4096]{1,0:T(8,128)(2,1)} %collective-permute-done.15.refs_3_), channel_id=1, source_target_pairs={{0,1},{1,0},{2,3},{3,2},{4,5},{5,4},{6,7},{7,6},{8,9},{9,8},{10,11... | collective-permute-start | bytes 1572872 | tf_op jit(solution)/shard_map/ppermute | solution.py:345
  78.7 28.5 %collective-permute-start.19 = (bf16[64,4096]{1,0:T(8,128)(2,1)}, bf16[64,4096]{1,0:T(8,128)(2,1)}, u32[]{:S(2)}, u32[]{:S(2)}) collective-permute-start(bf16[64,4096]{1,0:T(8,128)(2,1)} %collective-permute-done.14.refs_2_), channel_id=1, source_target_pairs={{0,4},{1,5},{4,8},{5,9},{8,12},{9,13},{12,14},{13,15},{14,10},{15,... | collective-permute-start | bytes 1572872 | tf_op jit(solution)/shard_map/ppermute | solution.py:345
  86.7 20.4 %collective-permute-start.20 = (bf16[64,4096]{1,0:T(8,128)(2,1)}, bf16[64,4096]{1,0:T(8,128)(2,1)}, u32[]{:S(2)}, u32[]{:S(2)}) collective-permute-start(bf16[64,4096]{1,0:T(8,128)(2,1)} %collective-permute-done.15.refs_3_), channel_id=1, source_target_pairs={{4,0},{5,1},{8,4},{9,5},{12,8},{13,9},{14,12},{15,13},{10,14},{11,... | collective-permute-start | bytes 1572872 | tf_op jit(solution)/shard_map/ppermute | solution.py:345
  105.7 48.3 %collective-permute-start.30 = (bf16[16,24,2048]{2,1,0:T(8,128)(2,1)}, bf16[16,24,2048]{2,1,0:T(8,128)(2,1)}, u32[]{:S(2)}, u32[]{:S(2)}) collective-permute-start(bf16[16,24,2048]{2,1,0:T(8,128)(2,1)} %bitcast.12), channel_id=1, source_target_pairs={{16,0},{0,16},{17,1},{1,17},{18,2},{2,18},{19,3},{3,19},{20,4},{4,... | collective-permute-start | bytes 4718600 | tf_op jit(solution)/shard_map/ppermute | solution.py:380
  107.2 20.0 %collective-permute-start.24 = (bf16[64,4096]{1,0:T(8,128)(2,1)}, bf16[64,4096]{1,0:T(8,128)(2,1)}, u32[]{:S(2)}, u32[]{:S(2)}) collective-permute-start(bf16[64,4096]{1,0:T(8,128)(2,1)} %collective-permute-done.19.refs_2_), channel_id=1, source_target_pairs={{0,1},{1,0},{2,3},{3,2},{4,5},{5,4},{6,7},{7,6},{8,9},{9,8},{10,11... | collective-permute-start | bytes 1572872 | tf_op jit(solution)/shard_map/ppermute | solution.py:345
  107.2 20.0 %collective-permute-start.25 = (bf16[64,4096]{1,0:T(8,128)(2,1)}, bf16[64,4096]{1,0:T(8,128)(2,1)}, u32[]{:S(2)}, u32[]{:S(2)}) collective-permute-start(bf16[64,4096]{1,0:T(8,128)(2,1)} %collective-permute-done.20.refs_3_), channel_id=1, source_target_pairs={{0,1},{1,0},{2,3},{3,2},{4,5},{5,4},{6,7},{7,6},{8,9},{9,8},{10,11... | collective-permute-start | bytes 1572872 | tf_op jit(solution)/shard_map/ppermute | solution.py:345
  108.4 30.8 %collective-permute-start.18 = (bf16[64,4096]{1,0:T(8,128)(2,1)}, bf16[64,4096]{1,0:T(8,128)(2,1)}, u32[]{:S(2)}, u32[]{:S(2)}) collective-permute-start(bf16[64,4096]{1,0:T(8,128)(2,1)} %collective-permute-done.10.refs_2_), channel_id=1, source_target_pairs={{0,4},{1,5},{4,8},{5,9},{8,12},{9,13},{12,14},{13,15},{14,10},{15,... | collective-permute-start | bytes 1572872 | tf_op jit(solution)/shard_map/ppermute | solution.py:345
  108.9 30.3 %collective-permute-start.23 = (bf16[64,4096]{1,0:T(8,128)(2,1)}, bf16[64,4096]{1,0:T(8,128)(2,1)}, u32[]{:S(2)}, u32[]{:S(2)}) collective-permute-start(bf16[64,4096]{1,0:T(8,128)(2,1)} %collective-permute-done.20.refs_3_), channel_id=1, source_target_pairs={{4,0},{5,1},{8,4},{9,5},{12,8},{13,9},{14,12},{15,13},{10,14},{11,... | collective-permute-start | bytes 1572872 | tf_op jit(solution)/shard_map/ppermute | solution.py:345
  (27 other events, 166.6 us)
Sparse Core Ops, SparseCore 0:
  16.1 46.1 all-gather.2

commit v7 on v6

--- a/solution.py
+++ b/solution.py
@@ -51,11 +51,11 @@
 
 def share_body(lengths_ref, grads_ref, factor_ref, ids_ref, queries_ref, _, out_ref):
     count, width = queries_ref.shape[0], out_ref.shape[1]
-    span, order = grads_ref.shape[0], factor_ref.shape[1]
+    span, order = grads_ref.shape[0], factor_ref.shape[0]
     rows = span * LANES // width
     offset = pl.multiple_of(lax.axis_index("groups") * width, width)
     out_ref[:count, :] = queries_ref[:, pl.ds(offset, width)]
-    right = jnp.dot(grads_ref[...], factor_ref[...], preferred_element_type=jnp.float32)
+    right = lax.dot_general(grads_ref[...], factor_ref[...], NT, preferred_element_type=jnp.float32)
     live = lax.broadcasted_iota(jnp.int32, (span, order), 0) < lengths_ref[0]
     masked = jnp.where(live, right, 0.0)
     both = jnp.concatenate([masked, jnp.broadcast_to(ids_ref[...], (span, LANES - order))], axis=1)
@@ -68,7 +68,7 @@
 def own_share(lengths, grads, factor, ids, queries, after, groups):
     count, depth = queries.shape
     width = depth // groups
-    span, order = grads.shape[0], factor.shape[1]
+    span, order = grads.shape[0], factor.shape[0]
     rows = span * LANES // width
     ids = jnp.pad(ids.astype(jnp.float32)[None, :], ((0, 0), (0, LANES - order - count)))
     vmem = pl.BlockSpec(memory_space=pltpu.VMEM)
@@ -94,11 +94,14 @@
 
 
 def project(xn, gate_ref, up_ref, mix_ref, f_ref):
-    units, order = f_ref.shape
+    order, units = f_ref.shape
     wide = 2 * LANES
 
     def product(w):
         return jnp.dot(xn[...], w, preferred_element_type=jnp.float32)
+
+    def left_of(hidden, start, end):
+        return lax.dot_general(hidden, f_ref[:, start:end], NT, preferred_element_type=jnp.float32)
 
     total = jnp.zeros((xn.shape[0], order), jnp.float32)
     hidden, start = None, 0
@@ -106,15 +109,15 @@
         if at + wide <= units:
             gate = product(gate_ref[:, at : at + wide])
             if hidden is not None:
-                total += jnp.dot(hidden, f_ref[start:at, :], preferred_element_type=jnp.float32)
+                total += left_of(hidden, start, at)
             hidden = gated(gate, product(up_ref[:, at : at + wide]))
         else:
             both = product(mix_ref[...])
             if hidden is not None:
-                total += jnp.dot(hidden, f_ref[start:at, :], preferred_element_type=jnp.float32)
+                total += left_of(hidden, start, at)
             hidden = gated(both[:, :LANES], both[:, LANES:])
         start = at
-    return total + jnp.dot(hidden, f_ref[start:, :], preferred_element_type=jnp.float32)
+    return total + left_of(hidden, start, units)
 
 
 def first_body(pieces, *refs):
@@ -140,7 +143,7 @@
 def first_chunk(xs, gate_weight, up_weight, in_factor, index, tokens):
     pieces = len(xs)
     rows, depth = xs[0].shape
-    units, order = in_factor.shape
+    order, units = in_factor.shape
     total = pieces * rows
     vmem = pl.BlockSpec(memory_space=pltpu.VMEM)
     hbm = pl.BlockSpec(memory_space=pltpu.HBM)
@@ -178,7 +181,7 @@
 def chunk(xs, weights, in_factor, left, index):
     pieces = len(xs)
     rows, depth = xs[0].shape
-    order = in_factor.shape[1]
+    order = in_factor.shape[0]
     total = pieces * rows
     vmem = pl.BlockSpec(memory_space=pltpu.VMEM)
     left, *weights = pl.pallas_call(
@@ -196,11 +199,9 @@
     return left, weights
 
 
-def masked_of(side_ref, name, count, span, order):
-    width = side_ref.shape[2]
-    rows = span * LANES // width
-    wide = side_ref[name, count : count + rows, :].astype(jnp.float32)
-    both = jnp.concatenate([wide[:, c : c + LANES] for c in range(0, width, LANES)], axis=0)
+def masked_of(wide, span, order):
+    wide = wide.astype(jnp.float32)
+    both = jnp.concatenate([wide[:, c : c + LANES] for c in range(0, wide.shape[1], LANES)], axis=0)
     return both[:, :order].astype(jnp.bfloat16)
 
 
@@ -211,81 +212,116 @@
     return sum(lax.dot_general(part, masked, TN, preferred_element_type=jnp.float32) for part in (low, high))
 
 
-def sketch_body(places, half, count, names, left_ref, side_ref, out_ref):
+def write_flat(flat, slot, sketch, twice):
+    order = sketch.shape[0]
+    twice[...] = jnp.concatenate([sketch, sketch], axis=1)
+    lane = lax.broadcasted_iota(jnp.int32, (order // 2, 2 * order), 1)
+    even = twice[pl.ds(0, order // 2, 2), :]
+    odd = twice[pl.ds(1, order // 2, 2), :]
+    flat[:, slot, :] = jnp.where(lane < order, even, odd)
+
+
+def sketch_body(places, first, half, count, *refs):
+    names, left_ref, side_hbm = refs[:3]
+    flat, side_ref, twice, sems = refs[-4:]
+    order = left_ref.shape[1]
+    rows = 2 * half * LANES // side_ref.shape[2]
+    copies = [
+        pltpu.make_async_copy(side_hbm.at[names[first + r]], side_ref.at[r], sems.at[r]) for r in range(len(places))
+    ]
+    for copy in copies:
+        copy.start()
+    for copy in copies:
+        copy.wait()
     for r, at in enumerate(places):
-        masked = masked_of(side_ref, names[r], count, 2 * half, left_ref.shape[1])
-        out_ref[r] = one_sketch(left_ref, masked, at, half).astype(out_ref.dtype)
-
-
-def sketches(places, half, count, names, left, side):
+        masked = masked_of(side_ref[r, count : count + rows, :], 2 * half, order)
+        write_flat(flat, first + r, one_sketch(left_ref, masked, at, half), twice)
+
+
+def sketches(places, first, half, count, names, left, side, flat):
     order = left.shape[1]
     vmem = pl.BlockSpec(memory_space=pltpu.VMEM)
-    made = pl.pallas_call(
-        functools.partial(sketch_body, places, half, count),
-        in_specs=[pl.BlockSpec(memory_space=pltpu.SMEM), vmem, vmem],
+    operands = [names, left, pltpu.with_memory_space_constraint(side, pltpu.HBM)]
+    in_specs = [pl.BlockSpec(memory_space=pltpu.SMEM), vmem, pl.BlockSpec(memory_space=pltpu.HBM)]
+    aliases = {}
+    if flat is not None:
+        aliases = {3: 0}
+        operands.append(flat)
+        in_specs.append(vmem)
+    return pl.pallas_call(
+        functools.partial(sketch_body, places, first, half, count),
+        in_specs=in_specs,
         out_specs=vmem,
-        out_shape=jax.ShapeDtypeStruct((len(places), order, order), jnp.bfloat16),
-        compiler_params=pltpu.CompilerParams(vmem_limit_bytes=8 * MIB),
+        out_shape=jax.ShapeDtypeStruct((order // 2, names.shape[0], 2 * order), jnp.float32),
+        scratch_shapes=[
+            pltpu.VMEM((len(places), *side.shape[1:]), side.dtype),
+            pltpu.VMEM((order, 2 * order), jnp.float32),
+            pltpu.SemaphoreType.DMA((len(places),)),
+        ],
+        input_output_aliases=aliases,
+        compiler_params=pltpu.CompilerParams(vmem_limit_bytes=12 * MIB),
         cost_estimate=SMALL,
         name="sketches",
-    )(names, left, side)
-    return made.reshape(len(places), order * order)
-
-
-def finish_body(places, half, groups, count, names, left_ref, early_ref, *refs):
-    share_refs, (ids_ref, out_ref, twice, flat, whole) = refs[:groups], refs[groups:]
+    )(*operands)
+
+
+def finish_body(places, half, groups, count, names, left_ref, flat_ref, ids_ref, *refs):
+    shares_hbm, (out_ref, share_ref, twice, flat, sems) = refs[:groups], refs[groups:]
+    devices, width = share_ref.shape[1], share_ref.shape[3]
     order = left_ref.shape[1]
-    early = early_ref.shape[0]
-    slots = flat.shape[1]
-    lane = lax.broadcasted_iota(jnp.int32, (order // 2, 2 * order), 1)
+    rows = 2 * half * LANES // width
+    parts = sems.shape[1]
+    copies = []
+    for r, ref in enumerate(shares_hbm):
+        for p in range(parts):
+            some = pl.ds(p * (devices // parts), devices // parts)
+            copies.append(pltpu.make_async_copy(ref.at[some], share_ref.at[r, some], sems.at[r, p]))
+    for copy in copies:
+        copy.start()
+    flat[...] = flat_ref[...]
+    value = lax.broadcasted_iota(jnp.int32, (NVAL, ids_ref.shape[1]), 0)
+    members = (value == ids_ref[...]).astype(jnp.bfloat16)
+    for copy in copies:
+        copy.wait()
+    first = names.shape[0] - len(places)
     for r, at in enumerate(places):
-        masked = masked_of(share_refs[0], names[early + r], count, 2 * half, order)
-        sketch = one_sketch(left_ref, masked, at, half)
-        twice[...] = jnp.concatenate([sketch, sketch], axis=1)
-        even = twice[pl.ds(0, order // 2, 2), :]
-        odd = twice[pl.ds(1, order // 2, 2), :]
-        flat[:, r, :] = jnp.where(lane < order, even, odd)
-    late = jnp.concatenate([flat[c] for c in range(order // 2)], axis=1).astype(jnp.bfloat16)
-    whole[...] = jnp.concatenate([late, early_ref[...]], axis=0)
-
-    devices, _, width = share_refs[0].shape
+        masked = masked_of(share_ref[0, names[first + r], count : count + rows, :], 2 * half, order)
+        write_flat(flat, first + r, one_sketch(left_ref, masked, at, half), twice)
     group = lax.axis_index("groups")
     scores = 0.0
-    for r, ref in enumerate(share_refs):
-        offset = pl.multiple_of(lax.rem(group + r, groups) * width, width)
-        queries = ref[:, :count, :].reshape(devices * count, width)
-        scores += lax.dot_general(whole[:, pl.ds(offset, width)], queries, NT, preferred_element_type=jnp.float32)
-    value = lax.broadcasted_iota(jnp.int32, (NVAL, ids_ref.shape[1]), 0)
-    members = (value == ids_ref[...]).astype(jnp.bfloat16)
-    rows = 0.0
+    for r in range(groups):
+        block = lax.rem(group + r, groups) * (width // LANES)
+        sketch = jnp.concatenate([flat[block + c] for c in range(width // LANES)], axis=1).astype(jnp.bfloat16)
+        queries = share_ref[r, :, :count, :].reshape(devices * count, width)
+        scores += lax.dot_general(sketch, queries, NT, preferred_element_type=jnp.float32)
+    total = 0.0
     for _ in range(3):
         part = scores.astype(jnp.bfloat16)
         scores = scores - part.astype(jnp.float32)
-        rows += lax.dot_general(part, members, NT, preferred_element_type=jnp.float32)
-    for r in range(early):
-        out_ref[pl.ds(names[r], 1), :] = rows[slots + r : slots + r + 1, :]
-    for r in range(len(places)):
-        out_ref[pl.ds(names[early + r], 1), :] = rows[r : r + 1, :]
-
-
-def finish(places, half, count, names, left, early, shares, ids):
+        total += lax.dot_general(part, members, NT, preferred_element_type=jnp.float32)
+    for r in range(names.shape[0]):
+        out_ref[pl.ds(names[r], 1), :] = total[r : r + 1, :]
+
+
+def finish(places, half, count, names, left, flat, shares, ids):
     order = left.shape[1]
     vmem = pl.BlockSpec(memory_space=pltpu.VMEM)
-    slots = -(-len(places) // 8) * 8
+    hbm = pl.BlockSpec(memory_space=pltpu.HBM)
     return pl.pallas_call(
         functools.partial(finish_body, places, half, len(shares), count),
-        in_specs=[pl.BlockSpec(memory_space=pltpu.SMEM)] + [vmem] * (3 + len(shares)),
+        in_specs=[pl.BlockSpec(memory_space=pltpu.SMEM)] + [vmem] * 3 + [hbm] + [pl.BlockSpec(memory_space=pl.ANY)] * (len(shares) - 1),
         out_specs=vmem,
         out_shape=jax.ShapeDtypeStruct((names.shape[0], NVAL), jnp.float32),
         scratch_shapes=[
+            pltpu.VMEM((len(shares), *shares[0].shape), shares[0].dtype),
             pltpu.VMEM((order, 2 * order), jnp.float32),
-            pltpu.VMEM((order // 2, slots, 2 * order), jnp.float32),
-            pltpu.VMEM((slots + early.shape[0], order * order), jnp.bfloat16),
+            pltpu.VMEM(flat.shape, jnp.float32),
+            pltpu.SemaphoreType.DMA((len(shares), 4)),
         ],
-        compiler_params=pltpu.CompilerParams(vmem_limit_bytes=14 * MIB),
+        compiler_params=pltpu.CompilerParams(vmem_limit_bytes=20 * MIB),
         cost_estimate=SMALL,
         name="finish",
-    )(names, left, early, *shares, ids)
+    )(names, left, flat, ids, pltpu.with_memory_space_constraint(shares[0], pltpu.HBM), *shares[1:])
 
 
 def arrivals(ring, devices):
@@ -350,11 +386,11 @@
         2: (send(x_b, forward), send(x_b, backward)),
     }
     swapped = tuple(send(x, other_core) for x in (x_a, x_b))
+    left, weights = first_chunk((x_a, x_b), gate_weight, up_weight, in_factor.T, 1, tokens)
     nq = queries.shape[0]
-    side = own_share(example_lengths, out_grads, out_factor, query_ids, queries, x_a, groups)
-    side, x_a = lax.optimization_barrier((side, x_a))
+    side = own_share(example_lengths, out_grads, out_factor.T, query_ids, queries, left, groups)
+    side, left = lax.optimization_barrier((side, left))
     side = lax.all_gather(side, "examples", axis=0)
-    left, weights = first_chunk((x_a, x_b), gate_weight, up_weight, in_factor, 1, tokens)
 
     names, spots = arrivals(ring, devices)
     names = lax.dynamic_index_in_dim(jnp.array(names, jnp.int32), me, keepdims=False)
@@ -370,7 +406,7 @@
             coming[chips - 1] = (opposite, send(own_2, backward))
         before, swapped = swapped, tuple(send(x, other_core) for x in own)
         if k < chips - 1:
-            left, weights = chunk(before + own, weights, in_factor, left, k)
+            left, weights = chunk(before + own, weights, in_factor.T, left, k)
         if k == chips - 3:
             side, left = lax.optimization_barrier((side, left))
             ids = side[:, nq, order : order + nq].astype(jnp.int32).reshape(1, devices * nq)
@@ -379,16 +415,16 @@
                 way = [((g + r) % groups, g) for g in range(groups)]
                 shares.append(lax.ppermute(side, "groups", way))
             ready = devices - 6
-            early = [sketches(spots[:ready], half, nq, names[:ready], left, side)]
+            flat = sketches(spots[:ready], 0, half, nq, names, left, side, None)
+            flat, ids, left = lax.optimization_barrier((flat, ids, left))
         if k == chips - 2:
-            left, weights = chunk(swapped, weights, in_factor, left, 2 * k + 2)
-            early.append(sketches(spots[ready:-2], half, nq, names[ready:-2], left, side))
-            early = jnp.concatenate(early, axis=0)
-            early, left = lax.optimization_barrier((early, left))
-    left, weights = chunk(own, weights, in_factor, left, 2 * chips - 1)
-    left, weights = chunk(swapped, weights, in_factor, left, 2 * chips)
-
-    partial = finish(spots[-2:], half, nq, names, left, early, shares, ids)
+            left, weights = chunk(swapped, weights, in_factor.T, left, 2 * k + 2)
+            flat = sketches(spots[ready:-2], ready, half, nq, names, left, side, flat)
+            flat, left = lax.optimization_barrier((flat, left))
+    left, weights = chunk(own, weights, in_factor.T, left, 2 * chips - 1)
+    left, weights = chunk(swapped, weights, in_factor.T, left, 2 * chips)
+
+    partial = finish(spots[-2:], half, nq, names, left, flat, shares, ids)
     shares = lax.all_to_all(partial, "examples", split_axis=0, concat_axis=0, tiled=True)
     return jnp.sum(shares, axis=0, keepdims=True)
 

time: 177 us -> 176 us (level)
  waiting for transfers between devices: 29.1 us -> 34.6 us
  Pallas kernels: 58.3 us -> 53.7 us
    pallas_call x9, Pallas kernels: 42.5 us -> 36.1 us  [chunk(): pl.pallas_call(functools.partial(chunk_body, pieces), grid=(1,), in_specs...]
    ppermute x30, waiting for transfers between devices: 29 us -> 33.4 us  [send(): return lax.ppermute(x, 'examples', way)]
    pallas_call x2, Pallas kernels: 1.65 us -> 4.33 us  [sketches(): pl.pallas_call(functools.partial(sketch_body, places, first, half, count)...]
    reshape x2 -> x0, local copies, waits for them, and re-layouts: 1.87 us -> none  [sketches(): return made.reshape(len(places), order * order)]
    unnamed x40 -> x38, local copies, waits for them, and re-layouts: 32.1 us -> 33.1 us
  transfers between devices with their start and end apart: 32 -> 32, of which waited for: 4 -> 5; matrix products, arithmetic and copies ran while one was open for 3% -> 1% of each run, Pallas kernels for 30% -> 23%
where the time goes in v7:
time: 176 us; the launch traced here: 175 us
  Pallas kernels  53.7 us (31%)
  waiting for transfers between devices  34.6 us (20%)
  local copies, waits for them, and re-layouts  33.9 us (19%)
  starting transfers between devices  25.1 us (14%)
  between operations  14.4 us (8%)
  blocking collectives  11.7 us (7%)
  other arithmetic  2.11 us (1%)
    pallas_call x9, Pallas kernels, chunk(): pl.pallas_call(functools.partial(chunk_body, pieces), grid=(1,), in_specs...  36.1 us
    ppermute x30, waiting for transfers between devices, send(): return lax.ppermute(x, 'examples', way)  33.4 us
    unnamed x38, local copies, waits for them, and re-layouts  33.1 us
    ppermute x30, starting transfers between devices, send(): return lax.ppermute(x, 'examples', way)  23.6 us
    all_to_all x1, blocking collectives, local(): lax.all_to_all(partial, 'examples', split_axis=0, concat_axis=0, tiled=True)  11.7 us
    pallas_call x1, Pallas kernels, first_chunk(): pl.pallas_call(functools.partial(first_body, pieces), grid=(1,), in_specs...  7.97 us
    pallas_call x2, Pallas kernels, sketches(): pl.pallas_call(functools.partial(sketch_body, places, first, half, count)...  4.33 us
    pallas_call x1, Pallas kernels, finish(): pl.pallas_call(functools.partial(finish_body, places, half, len(shares),...  3.75 us
  transfers between devices with their start and end apart: 32, of which 5 were waited for; matrix products, arithmetic and copies ran while one was open for 1% of the time, Pallas kernels for 23%

profile of v7, /device:TPU:0, one launch (start us, length us, event | category | flops | bytes accessed | tf_op | source)
XLA Modules:
  0.0 175.5 jit_solution(6085928535033111464)
XLA Ops:
  11.4 8.0 %first_chunk.1 = (f32[2176,64]{1,0:T(8,128)S(1)}, bf16[4096,896]{1,0:T(8,128)(2,1)S(1)}, bf16[4096,896]{1,0:T(8,128)(2,1)S(1)}, bf16[4096,256]{1,0:T(8,128)(2,1)S(1)}) custom-call(bf16[64,4096]{1,0:T(8,128)(2,1)S(1)} %get-tuple-element.74.refs_0_, bf16[64,4096]{1,0:T(8,128)(2,1)S(1)} %get-tuple-element.75.refs_1_, bf16[4096,896]{1,0:T(8,128)(2,1)} %refs_2_.1, ...), custom_call_target="tpu_custom_call" | custom-call | flops 1000000 | bytes 100000 | tf_op jit(solution)/shard_map/first_chunk/pallas_call | solution.py:151
  19.4 2.9 %copy-done = bf16[4096,896]{1,0:T(8,128)(2,1)} copy-done((bf16[4096,896]{1,0:T(8,128)(2,1)}, bf16[4096,896]{1,0:T(8,128)(2,1)S(1)}, u32[]{:S(2)}) %copy-start) | copy-done | bytes 7340056
  22.3 3.0 %copy-done.6 = bf16[4096,896]{1,0:T(8,128)(2,1)} copy-done((bf16[4096,896]{1,0:T(8,128)(2,1)}, bf16[4096,896]{1,0:T(8,128)(2,1)S(1)}, u32[]{:S(2)}) %copy-start.6) | copy-done | bytes 7340056
  26.4 3.1 %collective-permute-start = (bf16[64,4096]{1,0:T(8,128)(2,1)}, bf16[64,4096]{1,0:T(8,128)(2,1)S(1)}, u32[]{:S(2)}, u32[]{:S(2)}) collective-permute-start(bf16[64,4096]{1,0:T(8,128)(2,1)} %copy-done.15), channel_id=1, source_target_pairs={{0,4},{1,5},{4,8},{5,9},{8,12},{9,13},{12,14},{13,15},{14,10},{15,... | collective-permute-start | bytes 1572872 | tf_op jit(solution)/shard_map/ppermute | solution.py:381
  32.0 12.2 %collective-permute-done.refs_2_ = bf16[64,4096]{1,0:T(8,128)(2,1)S(1)} collective-permute-done((bf16[64,4096]{1,0:T(8,128)(2,1)}, bf16[64,4096]{1,0:T(8,128)(2,1)S(1)}, u32[]{:S(2)}, u32[]{:S(2)}) %collective-permute-start) | collective-permute-done | bytes 524320 | tf_op jit(solution)/shard_map/ppermute | solution.py:381
  47.1 10.9 %collective-permute-done.6.refs_2_ = bf16[64,4096]{1,0:T(8,128)(2,1)S(1)} collective-permute-done((bf16[64,4096]{1,0:T(8,128)(2,1)}, bf16[64,4096]{1,0:T(8,128)(2,1)S(1)}, u32[]{:S(2)}, u32[]{:S(2)}) %collective-permute-start.6) | collective-permute-done | bytes 524320 | tf_op jit(solution)/shard_map/ppermute | solution.py:381
  59.0 3.1 %copy-done.1 = bf16[4096,896]{1,0:T(8,128)(2,1)S(1)} copy-done((bf16[4096,896]{1,0:T(8,128)(2,1)S(1)}, bf16[4096,896]{1,0:T(8,128)(2,1)}, u32[]{:S(2)}) %copy-start.1) | copy-done | bytes 7340056
  62.1 3.1 %copy-done.7 = bf16[4096,896]{1,0:T(8,128)(2,1)S(1)} copy-done((bf16[4096,896]{1,0:T(8,128)(2,1)S(1)}, bf16[4096,896]{1,0:T(8,128)(2,1)}, u32[]{:S(2)}) %copy-start.7) | copy-done | bytes 7340056
  65.2 4.2 %chunk.9 = (f32[2176,64]{1,0:T(8,128)S(1)}, bf16[4096,896]{1,0:T(8,128)(2,1)S(1)}, bf16[4096,896]{1,0:T(8,128)(2,1)S(1)}, bf16[4096,256]{1,0:T(8,128)(2,1)S(1)}) custom-call(bf16[64,4096]{1,0:T(8,128)(2,1)S(1)} %collective-permute-done.8.refs_0_, ...), custom_call_target="tpu_custom_call", output_to_operand_aliasing={{0}: (8, {}), {1}: (4, {}), {2}: (5, {}), {3}: (6, {})} | custom-call | flops 1000000 | bytes 100000 | tf_op jit(solution)/shard_map/chunk/pallas_call | solution.py:187
  71.4 2.6 %collective-permute-done.2.refs_2_ = bf16[64,4096]{1,0:T(8,128)(2,1)S(1)} collective-permute-done((bf16[64,4096]{1,0:T(8,128)(2,1)S(1)}, bf16[64,4096]{1,0:T(8,128)(2,1)S(1)}, u32[]{:S(2)}, u32[]{:S(2)}) %collective-permute-start.2) | collective-permute-done | bytes 524320 | tf_op jit(solution)/shard_map/ppermute | solution.py:381
  76.0 4.2 %chunk.10 = (f32[2176,64]{1,0:T(8,128)S(1)}, bf16[4096,896]{1,0:T(8,128)(2,1)S(1)}, bf16[4096,896]{1,0:T(8,128)(2,1)S(1)}, bf16[4096,256]{1,0:T(8,128)(2,1)S(1)}) custom-call(bf16[64,4096]{1,0:T(8,128)(2,1)S(1)} %collective-permute-done.4.refs_0_, ...), custom_call_target="tpu_custom_call", output_to_operand_aliasing={{0}: (8, {}), {1}: (4, {}), {2}: (5, {}), {3}: (6, {})} | custom-call | flops 1000000 | bytes 100000 | tf_op jit(solution)/shard_map/chunk/pallas_call | solution.py:187
  81.2 4.2 %chunk.11 = (f32[2176,64]{1,0:T(8,128)S(1)}, bf16[4096,896]{1,0:T(8,128)(2,1)S(1)}, bf16[4096,896]{1,0:T(8,128)(2,1)S(1)}, bf16[4096,256]{1,0:T(8,128)(2,1)S(1)}) custom-call(bf16[64,4096]{1,0:T(8,128)(2,1)S(1)} %collective-permute-done.16.refs_0_, ...), custom_call_target="tpu_custom_call", output_to_operand_aliasing={{0}: (8, {}), {1}: (4, {}), {2}: (5, {}), {3}: (6, {})} | custom-call | flops 1000000 | bytes 100000 | tf_op jit(solution)/shard_map/chunk/pallas_call | solution.py:187
  88.7 7.7 %collective-permute-done.10.refs_2_ = bf16[64,4096]{1,0:T(8,128)(2,1)} collective-permute-done((bf16[64,4096]{1,0:T(8,128)(2,1)S(1)}, bf16[64,4096]{1,0:T(8,128)(2,1)}, u32[]{:S(2)}, u32[]{:S(2)}) %collective-permute-start.10) | collective-permute-done | bytes 524320 | tf_op jit(solution)/shard_map/ppermute | solution.py:381
  98.5 5.4 %chunk.12 = (f32[2176,64]{1,0:T(8,128)S(1)}, bf16[4096,896]{1,0:T(8,128)(2,1)S(1)}, bf16[4096,896]{1,0:T(8,128)(2,1)S(1)}, bf16[4096,256]{1,0:T(8,128)(2,1)S(1)}) custom-call(bf16[64,4096]{1,0:T(8,128)(2,1)S(1)} %collective-permute-done.12.refs_0_, ...), custom_call_target="tpu_custom_call", output_to_operand_aliasing={{0}: (8, {}), {1}: (4, {}), {2}: (5, {}), {3}: (6, {})} | custom-call | flops 1000000 | bytes 100000 | tf_op jit(solution)/shard_map/chunk/pallas_call | solution.py:187
  104.5 5.4 %chunk.13 = (f32[2176,64]{1,0:T(8,128)S(1)}, bf16[4096,896]{1,0:T(8,128)(2,1)S(1)}, bf16[4096,896]{1,0:T(8,128)(2,1)S(1)}, bf16[4096,256]{1,0:T(8,128)(2,1)S(1)}) custom-call(bf16[64,4096]{1,0:T(8,128)(2,1)S(1)} %collective-permute-done.21.refs_0_, ...), custom_call_target="tpu_custom_call", output_to_operand_aliasing={{0}: (8, {}), {1}: (4, {}), {2}: (5, {}), {3}: (6, {})} | custom-call | flops 1000000 | bytes 100000 | tf_op jit(solution)/shard_map/chunk/pallas_call | solution.py:187
  110.0 2.9 %copy-done.2 = bf16[4096,896]{1,0:T(8,128)(2,1)} copy-done((bf16[4096,896]{1,0:T(8,128)(2,1)}, bf16[4096,896]{1,0:T(8,128)(2,1)S(1)}, u32[]{:S(2)}) %copy-start.2) | copy-done | bytes 7340056
  112.9 3.0 %copy-done.8 = bf16[4096,896]{1,0:T(8,128)(2,1)} copy-done((bf16[4096,896]{1,0:T(8,128)(2,1)}, bf16[4096,896]{1,0:T(8,128)(2,1)S(1)}, u32[]{:S(2)}) %copy-start.8) | copy-done | bytes 7340056
  124.0 3.1 %copy-done.3 = bf16[4096,896]{1,0:T(8,128)(2,1)S(1)} copy-done((bf16[4096,896]{1,0:T(8,128)(2,1)S(1)}, bf16[4096,896]{1,0:T(8,128)(2,1)}, u32[]{:S(2)}) %copy-start.3) | copy-done | bytes 7340056
  127.1 3.1 %copy-done.9 = bf16[4096,896]{1,0:T(8,128)(2,1)S(1)} copy-done((bf16[4096,896]{1,0:T(8,128)(2,1)S(1)}, bf16[4096,896]{1,0:T(8,128)(2,1)}, u32[]{:S(2)}) %copy-start.9) | copy-done | bytes 7340056
  130.2 5.7 %chunk.14 = (f32[2176,64]{1,0:T(8,128)S(1)}, bf16[4096,896]{1,0:T(8,128)(2,1)S(1)}, bf16[4096,896]{1,0:T(8,128)(2,1)S(1)}, bf16[4096,256]{1,0:T(8,128)(2,1)S(1)}) custom-call(bf16[64,4096]{1,0:T(8,128)(2,1)} %collective-permute-done.26.refs_0_, ...), custom_call_target="tpu_custom_call", output_to_operand_aliasing={{0}: (8, {}), {1}: (4, {}), {2}: (5, {}), {3}: (6, {})} | custom-call | flops 1000000 | bytes 100000 | tf_op jit(solution)/shard_map/chunk/pallas_call | solution.py:187
  138.2 2.9 %copy-done.4 = bf16[4096,896]{1,0:T(8,128)(2,1)} copy-done((bf16[4096,896]{1,0:T(8,128)(2,1)}, bf16[4096,896]{1,0:T(8,128)(2,1)S(1)}, u32[]{:S(2)}) %copy-start.4) | copy-done | bytes 7340056
  143.7 3.1 %copy-done.5 = bf16[4096,896]{1,0:T(8,128)(2,1)S(1)} copy-done((bf16[4096,896]{1,0:T(8,128)(2,1)S(1)}, bf16[4096,896]{1,0:T(8,128)(2,1)}, u32[]{:S(2)}) %copy-start.5) | copy-done | bytes 7340056
  152.6 3.8 %finish.1 = f32[16,256]{1,0:T(8,128)S(1)} custom-call(s32[16]{0:T(128)S(1)} %dynamic-slice_bitcast_fusion.refs_0_.names, f32[2176,64]{1,0:T(8,128)S(1)} %get-tuple-element.140.left_ref, f32[32,16,128]{2,1,0:T(8,128)S(1)} %sketches.3.flat_ref, s32[1,256]{1,0:T(1,128)S(1)} %reshape.15.ids_ref, bf16[16,24,2048]{2,1,0:T(8,128)(2,1)} %bitcast.27, ...), custom_call_target="tpu_custom_call" | custom-call | flops 1000000 | bytes 100000 | tf_op jit(solution)/shard_map/finish/pallas_call | solution.py:310
  156.4 11.7 %all_to_all.9 = f32[16,1,256]{2,1,0:T(1,128)S(1)} all-to-all(f32[16,1,256]{2,1,0:T(1,128)S(1)} %copy.49), channel_id=1, replica_groups=mesh['groups'=2,'examples'=16] {'examples'}, dimensions={0} | all-to-all | bytes 32768 | tf_op jit(solution)/shard_map/all_to_all | solution.py:428
  (102 shorter events, 41.9 us)
Async XLA Ops:
  6.5 109.3 %all-gather.3.cloned.1.call-start = ((), (), s32[]{:S(2)}) async-start(), calls=%async_computation.1 | async-start | bytes 1671168 | tf_op jit(solution)/shard_map/all_gather | solution.py:393
  26.4 17.8 %collective-permute-start = (bf16[64,4096]{1,0:T(8,128)(2,1)}, bf16[64,4096]{1,0:T(8,128)(2,1)S(1)}, u32[]{:S(2)}, u32[]{:S(2)}) collective-permute-start(bf16[64,4096]{1,0:T(8,128)(2,1)} %copy-done.15), channel_id=1, source_target_pairs={{0,4},{1,5},{4,8},{5,9},{8,12},{9,13},{12,14},{13,15},{14,10},{15,... | collective-permute-start | bytes 1572872 | tf_op jit(solution)/shard_map/ppermute | solution.py:381
  29.4 16.1 %collective-permute-start.1 = (bf16[64,4096]{1,0:T(8,128)(2,1)}, bf16[64,4096]{1,0:T(8,128)(2,1)S(1)}, u32[]{:S(2)}, u32[]{:S(2)}) collective-permute-start(bf16[64,4096]{1,0:T(8,128)(2,1)} %copy-done.15), channel_id=1, source_target_pairs={{4,0},{5,1},{8,4},{9,5},{12,8},{13,9},{14,12},{15,13},{10,14},{11,... | collective-permute-start | bytes 1572872 | tf_op jit(solution)/shard_map/ppermute | solution.py:381
  29.5 16.1 %collective-permute-start.8 = (bf16[64,4096]{1,0:T(8,128)(2,1)}, bf16[64,4096]{1,0:T(8,128)(2,1)S(1)}, u32[]{:S(2)}, u32[]{:S(2)}) collective-permute-start(bf16[64,4096]{1,0:T(8,128)(2,1)} %copy-done.15), channel_id=1, source_target_pairs={{0,1},{1,0},{2,3},{3,2},{4,5},{5,4},{6,7},{7,6},{8,9},{9,8},{10,11... | collective-permute-start | bytes 1572872 | tf_op jit(solution)/shard_map/ppermute | solution.py:381
  29.5 16.6 %collective-permute-start.9 = (bf16[64,4096]{1,0:T(8,128)(2,1)}, bf16[64,4096]{1,0:T(8,128)(2,1)S(1)}, u32[]{:S(2)}, u32[]{:S(2)}) collective-permute-start(bf16[64,4096]{1,0:T(8,128)(2,1)} %copy-done.14), channel_id=1, source_target_pairs={{0,1},{1,0},{2,3},{3,2},{4,5},{5,4},{6,7},{7,6},{8,9},{9,8},{10,11... | collective-permute-start | bytes 1572872 | tf_op jit(solution)/shard_map/ppermute | solution.py:381
  30.0 28.0 %collective-permute-start.6 = (bf16[64,4096]{1,0:T(8,128)(2,1)}, bf16[64,4096]{1,0:T(8,128)(2,1)S(1)}, u32[]{:S(2)}, u32[]{:S(2)}) collective-permute-start(bf16[64,4096]{1,0:T(8,128)(2,1)} %copy-done.14), channel_id=1, source_target_pairs={{0,4},{1,5},{4,8},{5,9},{8,12},{9,13},{12,14},{13,15},{14,10},{15,... | collective-permute-start | bytes 1572872 | tf_op jit(solution)/shard_map/ppermute | solution.py:381
  44.2 25.3 %collective-permute-start.7 = (bf16[64,4096]{1,0:T(8,128)(2,1)}, bf16[64,4096]{1,0:T(8,128)(2,1)S(1)}, u32[]{:S(2)}, u32[]{:S(2)}) collective-permute-start(bf16[64,4096]{1,0:T(8,128)(2,1)} %copy-done.14), channel_id=1, source_target_pairs={{4,0},{5,1},{8,4},{9,5},{12,8},{13,9},{14,12},{15,13},{10,14},{11,... | collective-permute-start | bytes 1572872 | tf_op jit(solution)/shard_map/ppermute | solution.py:381
  45.5 24.0 %collective-permute-start.4 = (bf16[64,4096]{1,0:T(8,128)(2,1)S(1)}, bf16[64,4096]{1,0:T(8,128)(2,1)S(1)}, u32[]{:S(2)}, u32[]{:S(2)}) collective-permute-start(bf16[64,4096]{1,0:T(8,128)(2,1)S(1)} %collective-permute-done.refs_2_), channel_id=1, source_target_pairs={{0,1},{1,0},{2,3},{3,2},{4,5},{5,4},{6,7},{7,6},{8,9},{9,8},{10,11... | collective-permute-start | bytes 1572872 | tf_op jit(solution)/shard_map/ppermute | solution.py:381
  45.5 24.5 %collective-permute-start.5 = (bf16[64,4096]{1,0:T(8,128)(2,1)S(1)}, bf16[64,4096]{1,0:T(8,128)(2,1)S(1)}, u32[]{:S(2)}, u32[]{:S(2)}) collective-permute-start(bf16[64,4096]{1,0:T(8,128)(2,1)S(1)} %collective-permute-done.1.refs_3_), channel_id=1, source_target_pairs={{0,1},{1,0},{2,3},{3,2},{4,5},{5,4},{6,7},{7,6},{8,9},{9,8},{10,11... | collective-permute-start | bytes 1572872 | tf_op jit(solution)/shard_map/ppermute | solution.py:381
  46.1 27.9 %collective-permute-start.2 = (bf16[64,4096]{1,0:T(8,128)(2,1)S(1)}, bf16[64,4096]{1,0:T(8,128)(2,1)S(1)}, u32[]{:S(2)}, u32[]{:S(2)}) collective-permute-start(bf16[64,4096]{1,0:T(8,128)(2,1)S(1)} %collective-permute-done.refs_2_), channel_id=1, source_target_pairs={{0,4},{1,5},{4,8},{5,9},{8,12},{9,13},{12,14},{13,15},{14,10},{15,... | collective-permute-start | bytes 1572872 | tf_op jit(solution)/shard_map/ppermute | solution.py:381
  57.9 22.2 %collective-permute-start.3 = (bf16[64,4096]{1,0:T(8,128)(2,1)S(1)}, bf16[64,4096]{1,0:T(8,128)(2,1)S(1)}, u32[]{:S(2)}, u32[]{:S(2)}) collective-permute-start(bf16[64,4096]{1,0:T(8,128)(2,1)S(1)} %collective-permute-done.1.refs_3_), channel_id=1, source_target_pairs={{4,0},{5,1},{8,4},{9,5},{12,8},{13,9},{14,12},{15,13},{10,14},{11,... | collective-permute-start | bytes 1572872 | tf_op jit(solution)/shard_map/ppermute | solution.py:381
  70.0 15.4 %collective-permute-start.14 = (bf16[64,4096]{1,0:T(8,128)(2,1)S(1)}, bf16[64,4096]{1,0:T(8,128)(2,1)}, u32[]{:S(2)}, u32[]{:S(2)}) collective-permute-start(bf16[64,4096]{1,0:T(8,128)(2,1)S(1)} %collective-permute-done.6.refs_2_), channel_id=1, source_target_pairs={{0,4},{1,5},{4,8},{5,9},{8,12},{9,13},{12,14},{13,15},{14,10},{15,... | collective-permute-start | bytes 1572872 | tf_op jit(solution)/shard_map/ppermute | solution.py:381
  80.8 15.6 %collective-permute-start.10 = (bf16[64,4096]{1,0:T(8,128)(2,1)S(1)}, bf16[64,4096]{1,0:T(8,128)(2,1)}, u32[]{:S(2)}, u32[]{:S(2)}) collective-permute-start(bf16[64,4096]{1,0:T(8,128)(2,1)S(1)} %collective-permute-done.2.refs_2_), channel_id=1, source_target_pairs={{0,4},{1,5},{4,8},{5,9},{8,12},{9,13},{12,14},{13,15},{14,10},{15,... | collective-permute-start | bytes 1572872 | tf_op jit(solution)/shard_map/ppermute | solution.py:381
  85.5 18.5 %collective-permute-start.11 = (bf16[64,4096]{1,0:T(8,128)(2,1)S(1)}, bf16[64,4096]{1,0:T(8,128)(2,1)}, u32[]{:S(2)}, u32[]{:S(2)}) collective-permute-start(bf16[64,4096]{1,0:T(8,128)(2,1)S(1)} %collective-permute-done.3.refs_3_), channel_id=1, source_target_pairs={{4,0},{5,1},{8,4},{9,5},{12,8},{13,9},{14,12},{15,13},{10,14},{11,... | collective-permute-start | bytes 1572872 | tf_op jit(solution)/shard_map/ppermute | solution.py:381
  87.3 16.7 %collective-permute-start.21 = (bf16[64,4096]{1,0:T(8,128)(2,1)}, bf16[64,4096]{1,0:T(8,128)(2,1)S(1)}, u32[]{:S(2)}, u32[]{:S(2)}) collective-permute-start(bf16[64,4096]{1,0:T(8,128)(2,1)} %collective-permute-done.14.refs_2_), channel_id=1, source_target_pairs={{0,1},{1,0},{2,3},{3,2},{4,5},{5,4},{6,7},{7,6},{8,9},{9,8},{10,11... | collective-permute-start | bytes 1572872 | tf_op jit(solution)/shard_map/ppermute | solution.py:381
  87.3 17.2 %collective-permute-start.22 = (bf16[64,4096]{1,0:T(8,128)(2,1)}, bf16[64,4096]{1,0:T(8,128)(2,1)S(1)}, u32[]{:S(2)}, u32[]{:S(2)}) collective-permute-start(bf16[64,4096]{1,0:T(8,128)(2,1)} %collective-permute-done.15.refs_3_), channel_id=1, source_target_pairs={{0,1},{1,0},{2,3},{3,2},{4,5},{5,4},{6,7},{7,6},{8,9},{9,8},{10,11... | collective-permute-start | bytes 1572872 | tf_op jit(solution)/shard_map/ppermute | solution.py:381
  87.8 33.6 %collective-permute-start.19 = (bf16[64,4096]{1,0:T(8,128)(2,1)}, bf16[64,4096]{1,0:T(8,128)(2,1)}, u32[]{:S(2)}, u32[]{:S(2)}) collective-permute-start(bf16[64,4096]{1,0:T(8,128)(2,1)} %collective-permute-done.14.refs_2_), channel_id=1, source_target_pairs={{0,4},{1,5},{4,8},{5,9},{8,12},{9,13},{12,14},{13,15},{14,10},{15,... | collective-permute-start | bytes 1572872 | tf_op jit(solution)/shard_map/ppermute | solution.py:381
  96.4 25.0 %collective-permute-start.20 = (bf16[64,4096]{1,0:T(8,128)(2,1)}, bf16[64,4096]{1,0:T(8,128)(2,1)}, u32[]{:S(2)}, u32[]{:S(2)}) collective-permute-start(bf16[64,4096]{1,0:T(8,128)(2,1)} %collective-permute-done.15.refs_3_), channel_id=1, source_target_pairs={{4,0},{5,1},{8,4},{9,5},{12,8},{13,9},{14,12},{15,13},{10,14},{11,... | collective-permute-start | bytes 1572872 | tf_op jit(solution)/shard_map/ppermute | solution.py:381
  104.0 18.0 %collective-permute-start.26 = (bf16[64,4096]{1,0:T(8,128)(2,1)}, bf16[64,4096]{1,0:T(8,128)(2,1)}, u32[]{:S(2)}, u32[]{:S(2)}) collective-permute-start(bf16[64,4096]{1,0:T(8,128)(2,1)} %collective-permute-done.10.refs_2_), channel_id=1, source_target_pairs={{0,1},{1,0},{2,3},{3,2},{4,5},{5,4},{6,7},{7,6},{8,9},{9,8},{10,11... | collective-permute-start | bytes 1572872 | tf_op jit(solution)/shard_map/ppermute | solution.py:381
  104.1 18.4 %collective-permute-start.27 = (bf16[64,4096]{1,0:T(8,128)(2,1)}, bf16[64,4096]{1,0:T(8,128)(2,1)}, u32[]{:S(2)}, u32[]{:S(2)}) collective-permute-start(bf16[64,4096]{1,0:T(8,128)(2,1)} %collective-permute-done.11.refs_3_), channel_id=1, source_target_pairs={{0,1},{1,0},{2,3},{3,2},{4,5},{5,4},{6,7},{7,6},{8,9},{9,8},{10,11... | collective-permute-start | bytes 1572872 | tf_op jit(solution)/shard_map/ppermute | solution.py:381
  115.9 36.7 %collective-permute-start.30 = (bf16[16,24,2048]{2,1,0:T(8,128)(2,1)}, bf16[16,24,2048]{2,1,0:T(8,128)(2,1)}, u32[]{:S(2)}, u32[]{:S(2)}) collective-permute-start(bf16[16,24,2048]{2,1,0:T(8,128)(2,1)} %bitcast.23), channel_id=1, source_target_pairs={{16,0},{0,16},{17,1},{1,17},{18,2},{2,18},{19,3},{3,19},{20,4},{4,... | collective-permute-start | bytes 4718600 | tf_op jit(solution)/shard_map/ppermute | solution.py:416
  121.4 14.5 %collective-permute-start.24 = (bf16[64,4096]{1,0:T(8,128)(2,1)}, bf16[64,4096]{1,0:T(8,128)(2,1)S(1)}, u32[]{:S(2)}, u32[]{:S(2)}) collective-permute-start(bf16[64,4096]{1,0:T(8,128)(2,1)} %collective-permute-done.19.refs_2_), channel_id=1, source_target_pairs={{0,1},{1,0},{2,3},{3,2},{4,5},{5,4},{6,7},{7,6},{8,9},{9,8},{10,11... | collective-permute-start | bytes 1572872 | tf_op jit(solution)/shard_map/ppermute | solution.py:381
  122.0 21.1 %collective-permute-start.18 = (bf16[64,4096]{1,0:T(8,128)(2,1)}, bf16[64,4096]{1,0:T(8,128)(2,1)S(1)}, u32[]{:S(2)}, u32[]{:S(2)}) collective-permute-start(bf16[64,4096]{1,0:T(8,128)(2,1)} %collective-permute-done.10.refs_2_), channel_id=1, source_target_pairs={{0,4},{1,5},{4,8},{5,9},{8,12},{9,13},{12,14},{13,15},{14,10},{15,... | collective-permute-start | bytes 1572872 | tf_op jit(solution)/shard_map/ppermute | solution.py:381
  122.5 20.7 %collective-permute-start.23 = (bf16[64,4096]{1,0:T(8,128)(2,1)}, bf16[64,4096]{1,0:T(8,128)(2,1)S(1)}, u32[]{:S(2)}, u32[]{:S(2)}) collective-permute-start(bf16[64,4096]{1,0:T(8,128)(2,1)} %collective-permute-done.20.refs_3_), channel_id=1, source_target_pairs={{4,0},{5,1},{8,4},{9,5},{12,8},{13,9},{14,12},{15,13},{10,14},{11,... | collective-permute-start | bytes 1572872 | tf_op jit(solution)/shard_map/ppermute | solution.py:381
  (27 other events, 203.1 us)
Sparse Core Ops, SparseCore 0:
  26.5 46.3 all-gather.2

commit v8 on v7

--- a/solution.py
+++ b/solution.py
@@ -21,66 +21,73 @@
     return list(range(chips))
 
 
-def prepare_body(x_ref, gain_ref, a_ref, b_ref):
-    half = a_ref.shape[0]
-    block = 16
-    for start in range(0, 2 * half, block):
-        x = x_ref[start : start + block, :].astype(jnp.float32)
-        scale = lax.rsqrt(jnp.mean(x * x, axis=-1, keepdims=True) + 1e-05)
-        rows = (x * scale * gain_ref[...]).astype(jnp.bfloat16)
-        if start < half:
-            a_ref[start : start + block, :] = rows
-        else:
-            b_ref[start - half : start - half + block, :] = rows
-
-
-def prepare(x, gain):
-    span, depth = x.shape
-    vmem = pl.BlockSpec(memory_space=pltpu.VMEM)
-    rows = jax.ShapeDtypeStruct((span // 2, depth), jnp.bfloat16)
-    return pl.pallas_call(
-        prepare_body,
-        in_specs=[vmem] * 2,
-        out_specs=[vmem] * 2,
-        out_shape=[rows, rows],
-        compiler_params=pltpu.CompilerParams(vmem_limit_bytes=12 * MIB),
-        cost_estimate=SMALL,
-        name="prepare",
-    )(x, gain)
-
-
-def share_body(lengths_ref, grads_ref, factor_ref, ids_ref, queries_ref, _, out_ref):
+def prepare_body(lengths_ref, ids_ref, x_hbm, gain_hbm, grads_hbm, factor_hbm, queries_hbm, *refs):
+    a_ref, b_ref, out_ref, x_ref, gain_ref, grads_ref, factor_ref, queries_ref, sems = refs
+    half, span = a_ref.shape[0], x_ref.shape[0]
+    block = 32
+    starts = range(0, span, block)
+    x_copies = []
+    for k, start in enumerate(starts):
+        some = pl.ds(start, block)
+        x_copies.append(pltpu.make_async_copy(x_hbm.at[some], x_ref.at[some], sems.at[k]))
+    copies = []
+    pairs = [(gain_hbm, gain_ref), (grads_hbm, grads_ref), (factor_hbm, factor_ref), (queries_hbm, queries_ref)]
+    for k, (source, target) in enumerate(pairs):
+        copies.append(pltpu.make_async_copy(source, target, sems.at[len(x_copies) + k]))
+    copies[0].start()
+    for copy in x_copies + copies[1:]:
+        copy.start()
+    copies[0].wait()
+    for start, copy in zip(starts, x_copies):
+        copy.wait()
+        for at in range(start, start + block, 16):
+            x = x_ref[at : at + 16, :].astype(jnp.float32)
+            scale = lax.rsqrt(jnp.mean(x * x, axis=-1, keepdims=True) + 1e-05)
+            rows = (x * scale * gain_ref[...]).astype(jnp.bfloat16)
+            if at < half:
+                a_ref[at : at + 16, :] = rows
+            else:
+                b_ref[at - half : at - half + 16, :] = rows
+    for copy in copies[1:]:
+        copy.wait()
+
     count, width = queries_ref.shape[0], out_ref.shape[1]
-    span, order = grads_ref.shape[0], factor_ref.shape[0]
+    order = factor_ref.shape[0]
     rows = span * LANES // width
     offset = pl.multiple_of(lax.axis_index("groups") * width, width)
     out_ref[:count, :] = queries_ref[:, pl.ds(offset, width)]
     right = lax.dot_general(grads_ref[...], factor_ref[...], NT, preferred_element_type=jnp.float32)
     live = lax.broadcasted_iota(jnp.int32, (span, order), 0) < lengths_ref[0]
     masked = jnp.where(live, right, 0.0)
-    both = jnp.concatenate([masked, jnp.broadcast_to(ids_ref[...], (span, LANES - order))], axis=1)
+    ids = jnp.concatenate([ids_ref[...], jnp.zeros((1, LANES - order - count), jnp.int32)], axis=1)
+    ids = jnp.broadcast_to(ids.astype(jnp.float32), (span, LANES - order))
+    both = jnp.concatenate([masked, ids], axis=1)
     wide = jnp.concatenate([both[r : r + rows, :] for r in range(0, span, rows)], axis=1)
     out_ref[count : count + rows, :] = wide.astype(out_ref.dtype)
     if count + rows < out_ref.shape[0]:
         out_ref[count + rows :, :] = jnp.zeros((out_ref.shape[0] - count - rows, width), out_ref.dtype)
 
 
-def own_share(lengths, grads, factor, ids, queries, after, groups):
-    count, depth = queries.shape
+def prepare(x, gain, lengths, grads, factor, ids, queries, groups):
+    span, depth = x.shape
+    count = queries.shape[0]
     width = depth // groups
-    span, order = grads.shape[0], factor.shape[0]
-    rows = span * LANES // width
-    ids = jnp.pad(ids.astype(jnp.float32)[None, :], ((0, 0), (0, LANES - order - count)))
     vmem = pl.BlockSpec(memory_space=pltpu.VMEM)
+    hbm = pl.BlockSpec(memory_space=pltpu.HBM)
+    rows = jax.ShapeDtypeStruct((span // 2, depth), jnp.bfloat16)
+    share = -(-(count + span * LANES // width) // 8) * 8
+    operands = [x, gain, grads, factor, queries]
     return pl.pallas_call(
-        share_body,
-        in_specs=[pl.BlockSpec(memory_space=pltpu.SMEM)] + [vmem] * 4 + [pl.BlockSpec(memory_space=pl.ANY)],
-        out_specs=vmem,
-        out_shape=jax.ShapeDtypeStruct((-(-(count + rows) // 8) * 8, width), queries.dtype),
+        prepare_body,
+        in_specs=[pl.BlockSpec(memory_space=pltpu.SMEM), vmem] + [hbm] * len(operands),
+        out_specs=[vmem] * 3,
+        out_shape=[rows, rows, jax.ShapeDtypeStruct((share, width), queries.dtype)],
+        scratch_shapes=[pltpu.VMEM(o.shape, o.dtype) for o in operands]
+        + [pltpu.SemaphoreType.DMA((span // 32 + len(operands) - 1,))],
         compiler_params=pltpu.CompilerParams(vmem_limit_bytes=12 * MIB),
         cost_estimate=SMALL,
-        name="own_share",
-    )(lengths, grads, factor, ids, queries, after)
+        name="prepare",
+    )(lengths, ids, *[pltpu.with_memory_space_constraint(o, pltpu.HBM) for o in operands])
 
 
 def gather_rows(x_refs, xn):
@@ -93,7 +100,7 @@
     return (jax.nn.silu(gate) * up).astype(jnp.bfloat16)
 
 
-def project(xn, gate_ref, up_ref, mix_ref, f_ref):
+def project(xn, gate_ref, up_ref, f_ref):
     order, units = f_ref.shape
     wide = 2 * LANES
 
@@ -106,38 +113,39 @@
     total = jnp.zeros((xn.shape[0], order), jnp.float32)
     hidden, start = None, 0
     for at in range(0, units, wide):
+        both = product(gate_ref[:, at : at + wide])
+        if hidden is not None:
+            total += left_of(hidden, start, at)
         if at + wide <= units:
-            gate = product(gate_ref[:, at : at + wide])
-            if hidden is not None:
-                total += left_of(hidden, start, at)
-            hidden = gated(gate, product(up_ref[:, at : at + wide]))
+            hidden = gated(both, product(up_ref[:, at : at + wide]))
         else:
-            both = product(mix_ref[...])
-            if hidden is not None:
-                total += left_of(hidden, start, at)
             hidden = gated(both[:, :LANES], both[:, LANES:])
         start = at
     return total + left_of(hidden, start, units)
 
 
 def first_body(pieces, *refs):
-    x_refs, (gate_hbm, up_hbm, f_ref, out_ref, gate_ref, up_ref, mix_ref, xn, sems) = refs[:pieces], refs[pieces:]
-    depth, units = gate_ref.shape
+    x_refs, (gate_hbm, up_hbm, f_ref, out_ref, gate_ref, up_ref, xn, sems) = refs[:pieces], refs[pieces:]
+    depth, units = gate_hbm.shape
+    even = up_ref.shape[1]
     parts = sems.shape[1]
     copies = []
     for p in range(parts):
         rows = pl.ds(p * (depth // parts), depth // parts)
-        copies.append(pltpu.make_async_copy(gate_hbm.at[rows], gate_ref.at[rows], sems.at[0, p]))
-        copies.append(pltpu.make_async_copy(up_hbm.at[rows], up_ref.at[rows], sems.at[1, p]))
+        moves = [
+            (gate_hbm.at[rows], gate_ref.at[rows, pl.ds(0, units)]),
+            (up_hbm.at[rows, pl.ds(0, even)], up_ref.at[rows]),
+        ]
+        if even < units:
+            moves.append((up_hbm.at[rows, pl.ds(even, LANES)], gate_ref.at[rows, pl.ds(units, LANES)]))
+        for k, (source, target) in enumerate(moves):
+            copies.append(pltpu.make_async_copy(source, target, sems.at[k, p]))
     for copy in copies:
         copy.start()
     gather_rows(x_refs, xn)
     for copy in copies:
         copy.wait()
-    if units % (2 * LANES):
-        mix_ref[:, :LANES] = gate_ref[:, units - LANES :]
-        mix_ref[:, LANES:] = up_ref[:, units - LANES :]
-    out_ref[...] = project(xn, gate_ref, up_ref, mix_ref, f_ref)
+    out_ref[...] = project(xn, gate_ref, up_ref, f_ref)
 
 
 def first_chunk(xs, gate_weight, up_weight, in_factor, index, tokens):
@@ -147,19 +155,18 @@
     total = pieces * rows
     vmem = pl.BlockSpec(memory_space=pltpu.VMEM)
     hbm = pl.BlockSpec(memory_space=pltpu.HBM)
-    mix = 2 * LANES if units % (2 * LANES) else LANES
+    rest = units % (2 * LANES)
     left, *weights = pl.pallas_call(
         functools.partial(first_body, pieces),
         grid=(1,),
         in_specs=[vmem] * pieces + [hbm, hbm, vmem],
-        out_specs=[pl.BlockSpec((total, order), lambda i: (index, 0)), vmem, vmem, vmem],
+        out_specs=[pl.BlockSpec((total, order), lambda i: (index, 0)), vmem, vmem],
         out_shape=[
             jax.ShapeDtypeStruct((tokens, order), jnp.float32),
-            pltpu.VMEM((depth, units), jnp.bfloat16),
-            pltpu.VMEM((depth, units), jnp.bfloat16),
-            pltpu.VMEM((depth if mix > LANES else 16, mix), jnp.bfloat16),
+            pltpu.VMEM((depth, units + rest), jnp.bfloat16),
+            pltpu.VMEM((depth, units - rest), jnp.bfloat16),
         ],
-        scratch_shapes=[pltpu.VMEM((total, depth), jnp.bfloat16), pltpu.SemaphoreType.DMA((2, 4))],
+        scratch_shapes=[pltpu.VMEM((total, depth), jnp.bfloat16), pltpu.SemaphoreType.DMA((3, 4))],
         compiler_params=pltpu.CompilerParams(vmem_limit_bytes=12 * MIB),
         cost_estimate=SMALL,
         name="first_chunk",
@@ -173,9 +180,9 @@
 
 
 def chunk_body(pieces, *refs):
-    x_refs, (gate_ref, up_ref, mix_ref, f_ref, _, out_ref, _, _, _, xn) = refs[:pieces], refs[pieces:]
+    x_refs, (gate_ref, up_ref, f_ref, _, out_ref, _, _, xn) = refs[:pieces], refs[pieces:]
     gather_rows(x_refs, xn)
-    out_ref[...] = project(xn, gate_ref, up_ref, mix_ref, f_ref)
+    out_ref[...] = project(xn, gate_ref, up_ref, f_ref)
 
 
 def chunk(xs, weights, in_factor, left, index):
@@ -187,11 +194,11 @@
     left, *weights = pl.pallas_call(
         functools.partial(chunk_body, pieces),
         grid=(1,),
-        in_specs=[vmem] * (pieces + 4) + [pl.BlockSpec(memory_space=pl.ANY)],
-        out_specs=[pl.BlockSpec((total, order), lambda i: (index, 0)), vmem, vmem, vmem],
+        in_specs=[vmem] * (pieces + 3) + [pl.BlockSpec(memory_space=pl.ANY)],
+        out_specs=[pl.BlockSpec((total, order), lambda i: (index, 0)), vmem, vmem],
         out_shape=[jax.ShapeDtypeStruct(left.shape, left.dtype)] + [pltpu.VMEM(w.shape, w.dtype) for w in weights],
         scratch_shapes=[pltpu.VMEM((total, depth), jnp.bfloat16)],
-        input_output_aliases={pieces + 4: 0, pieces: 1, pieces + 1: 2, pieces + 2: 3},
+        input_output_aliases={pieces + 3: 0, pieces: 1, pieces + 1: 2},
         compiler_params=pltpu.CompilerParams(vmem_limit_bytes=12 * MIB),
         cost_estimate=SMALL,
         name="chunk",
@@ -380,17 +387,24 @@
     def send(x, way):
         return lax.ppermute(x, "examples", way)
 
-    x_a, x_b = prepare(layer_inputs, norm_gain[None, :])
+    nq = queries.shape[0]
+    x_a, x_b, side = prepare(
+        layer_inputs,
+        norm_gain[None, :],
+        example_lengths,
+        out_grads,
+        out_factor.T,
+        query_ids[None, :],
+        queries,
+        groups,
+    )
+    side = lax.all_gather(side, "examples", axis=0)
     coming = {
         1: (send(x_a, forward), send(x_a, backward)),
         2: (send(x_b, forward), send(x_b, backward)),
     }
     swapped = tuple(send(x, other_core) for x in (x_a, x_b))
     left, weights = first_chunk((x_a, x_b), gate_weight, up_weight, in_factor.T, 1, tokens)
-    nq = queries.shape[0]
-    side = own_share(example_lengths, out_grads, out_factor.T, query_ids, queries, left, groups)
-    side, left = lax.optimization_barrier((side, left))
-    side = lax.all_gather(side, "examples", axis=0)
 
     names, spots = arrivals(ring, devices)
     names = lax.dynamic_index_in_dim(jnp.array(names, jnp.int32), me, keepdims=False)
@@ -407,16 +421,18 @@
         before, swapped = swapped, tuple(send(x, other_core) for x in own)
         if k < chips - 1:
             left, weights = chunk(before + own, weights, in_factor.T, left, k)
-        if k == chips - 3:
+        if k == chips - 4:
             side, left = lax.optimization_barrier((side, left))
             ids = side[:, nq, order : order + nq].astype(jnp.int32).reshape(1, devices * nq)
+            ids, left = lax.optimization_barrier((ids, left))
             shares = [side]
             for r in range(1, groups):
                 way = [((g + r) % groups, g) for g in range(groups)]
                 shares.append(lax.ppermute(side, "groups", way))
+        if k == chips - 3:
             ready = devices - 6
             flat = sketches(spots[:ready], 0, half, nq, names, left, side, None)
-            flat, ids, left = lax.optimization_barrier((flat, ids, left))
+            flat, left = lax.optimization_barrier((flat, left))
         if k == chips - 2:
             left, weights = chunk(swapped, weights, in_factor.T, left, 2 * k + 2)
             flat = sketches(spots[ready:-2], ready, half, nq, names, left, side, flat)

time: 176 us -> 161 us (0.915)
  waiting for transfers between devices: 34.6 us -> 22.4 us
  local copies, waits for them, and re-layouts: 33.9 us -> 29.7 us
    ppermute x30, waiting for transfers between devices: 33.4 us -> 22.3 us  [send(): return lax.ppermute(x, 'examples', way)]
    unnamed x38 -> x26, local copies, waits for them, and re-layouts: 33.1 us -> 28.9 us
  transfers between devices with their start and end apart: 32 -> 32, of which waited for: 5 -> 3; matrix products, arithmetic and copies ran while one was open for 1% -> 1% of each run, Pallas kernels for 23% -> 30%
where the time goes in v8:
time: 161 us; the launch traced here: 160 us
  Pallas kernels  54.9 us (34%)
  local copies, waits for them, and re-layouts  29.7 us (18%)
  starting transfers between devices  25.9 us (16%)
  waiting for transfers between devices  22.4 us (14%)
  between operations  14.4 us (9%)
  blocking collectives  11.3 us (7%)
    pallas_call x9, Pallas kernels, chunk(): pl.pallas_call(functools.partial(chunk_body, pieces), grid=(1,), in_specs...  36.8 us
    unnamed x26, local copies, waits for them, and re-layouts  28.9 us
    ppermute x30, starting transfers between devices, send(): return lax.ppermute(x, 'examples', way)  24.4 us
    ppermute x30, waiting for transfers between devices, send(): return lax.ppermute(x, 'examples', way)  22.3 us
    all_to_all x1, blocking collectives, local(): lax.all_to_all(partial, 'examples', split_axis=0, concat_axis=0, tiled=True)  11.3 us
    pallas_call x1, Pallas kernels, first_chunk(): pl.pallas_call(functools.partial(first_body, pieces), grid=(1,), in_specs...  7.6 us
    pallas_call x2, Pallas kernels, sketches(): pl.pallas_call(functools.partial(sketch_body, places, first, half, count)...  4.33 us
    pallas_call x1, Pallas kernels, finish(): pl.pallas_call(functools.partial(finish_body, places, half, len(shares),...  3.28 us
  transfers between devices with their start and end apart: 32, of which 3 were waited for; matrix products, arithmetic and copies ran while one was open for 1% of the time, Pallas kernels for 30%

profile of v8, /device:TPU:0, one launch (start us, length us, event | category | flops | bytes accessed | tf_op | source)
XLA Modules:
  0.0 160.0 jit_solution(16855058073196439332)
XLA Ops:
  7.8 2.8 %prepare.1 = (bf16[64,4096]{1,0:T(8,128)(2,1)S(1)}, bf16[64,4096]{1,0:T(8,128)(2,1)S(1)}, bf16[24,2048]{1,0:T(8,128)(2,1)}) custom-call(s32[1]{0:T(128)S(6)} %copy.69.lengths_ref, s32[1,16]{1,0:T(1,128)S(1)} %bitcast.20, bf16[128,4096]{1,0:T(8,128)(2,1)} %x_hbm.1, f32[1,4096]{1,0:T(1,128)} %bitcast.27, bf16[128,4096]{1,0:T(8,128)(2,1)} %grads_hbm.1, ...), custom_call_target="tpu_custom_call" | custom-call | flops 1000000 | bytes 100000 | tf_op jit(solution)/shard_map/prepare/pallas_call | solution.py:80
  10.7 3.1 %collective-permute-start = (bf16[64,4096]{1,0:T(8,128)(2,1)S(1)}, bf16[64,4096]{1,0:T(8,128)(2,1)S(1)}, u32[]{:S(2)}, u32[]{:S(2)}) collective-permute-start(bf16[64,4096]{1,0:T(8,128)(2,1)S(1)} %get-tuple-element.65.refs_0_), channel_id=1, source_target_pairs={{0,4},{1,5},{4,8},{5,9},{8,12},{9,13},{12,14},{13,15},{14,10},{15,... | collective-permute-start | bytes 1572872 | tf_op jit(solution)/shard_map/ppermute | solution.py:388
  16.3 11.7 %collective-permute-done.refs_2_ = bf16[64,4096]{1,0:T(8,128)(2,1)S(1)} collective-permute-done((bf16[64,4096]{1,0:T(8,128)(2,1)S(1)}, bf16[64,4096]{1,0:T(8,128)(2,1)S(1)}, u32[]{:S(2)}, u32[]{:S(2)}) %collective-permute-start) | collective-permute-done | bytes 524320 | tf_op jit(solution)/shard_map/ppermute | solution.py:388
  30.5 7.6 %first_chunk.1 = (f32[2176,64]{1,0:T(8,128)S(1)}, bf16[4096,1024]{1,0:T(8,128)(2,1)S(1)}, bf16[4096,768]{1,0:T(8,128)(2,1)S(1)}) custom-call(bf16[64,4096]{1,0:T(8,128)(2,1)S(1)} %get-tuple-element.65.refs_0_, bf16[64,4096]{1,0:T(8,128)(2,1)S(1)} %get-tuple-element.66.refs_1_, bf16[4096,896]{1,0:T(8,128)(2,1)} %refs_2_.1, bf16[4096,896]{1,0:T(8,128)(2,1)} %refs_3_.1, ...), custom_call_target="tpu_custom_call" | custom-call | flops 1000000 | bytes 100000 | tf_op jit(solution)/shard_map/first_chunk/pallas_call | solution.py:159
  41.8 4.2 %chunk.9 = (f32[2176,64]{1,0:T(8,128)S(1)}, bf16[4096,1024]{1,0:T(8,128)(2,1)S(1)}, bf16[4096,768]{1,0:T(8,128)(2,1)S(1)}) custom-call(bf16[64,4096]{1,0:T(8,128)(2,1)S(1)} %collective-permute-done.8.refs_0_, bf16[64,4096]{1,0:T(8,128)(2,1)S(1)} %collective-permute-done.9.refs_1_, ...), custom_call_target="tpu_custom_call", output_to_operand_aliasing={{0}: (7, {}), {1}: (4, {}), {2}: (5, {})} | custom-call | flops 1000000 | bytes 100000 | tf_op jit(solution)/shard_map/chunk/pallas_call | solution.py:194
  46.8 10.5 %collective-permute-done.2.refs_2_ = bf16[64,4096]{1,0:T(8,128)(2,1)S(1)} collective-permute-done((bf16[64,4096]{1,0:T(8,128)(2,1)S(1)}, bf16[64,4096]{1,0:T(8,128)(2,1)S(1)}, u32[]{:S(2)}, u32[]{:S(2)}) %collective-permute-start.2) | collective-permute-done | bytes 524320 | tf_op jit(solution)/shard_map/ppermute | solution.py:388
  57.3 3.2 %collective-permute-start.15 = (bf16[64,4096]{1,0:T(8,128)(2,1)S(1)}, bf16[64,4096]{1,0:T(8,128)(2,1)}, u32[]{:S(2)}, u32[]{:S(2)}) collective-permute-start(bf16[64,4096]{1,0:T(8,128)(2,1)S(1)} %collective-permute-done.7.refs_3_), channel_id=1, source_target_pairs={{4,0},{5,1},{8,4},{9,5},{12,8},{13,9},{14,12},{15,13},{10,14},{11,... | collective-permute-start | bytes 1572872 | tf_op jit(solution)/shard_map/ppermute | solution.py:388
  60.5 4.2 %chunk.10 = (f32[2176,64]{1,0:T(8,128)S(1)}, bf16[4096,1024]{1,0:T(8,128)(2,1)S(1)}, bf16[4096,768]{1,0:T(8,128)(2,1)S(1)}) custom-call(bf16[64,4096]{1,0:T(8,128)(2,1)S(1)} %collective-permute-done.4.refs_0_, bf16[64,4096]{1,0:T(8,128)(2,1)S(1)} %collective-permute-done.5.refs_1_, ...), custom_call_target="tpu_custom_call", output_to_operand_aliasing={{0}: (7, {}), {1}: (4, {}), {2}: (5, {})} | custom-call | flops 1000000 | bytes 100000 | tf_op jit(solution)/shard_map/chunk/pallas_call | solution.py:194
  65.3 4.2 %chunk.11 = (f32[2176,64]{1,0:T(8,128)S(1)}, bf16[4096,1024]{1,0:T(8,128)(2,1)S(1)}, bf16[4096,768]{1,0:T(8,128)(2,1)S(1)}) custom-call(bf16[64,4096]{1,0:T(8,128)(2,1)S(1)} %collective-permute-done.16.refs_0_, bf16[64,4096]{1,0:T(8,128)(2,1)S(1)} %collective-permute-done.17.refs_1_, ...), custom_call_target="tpu_custom_call", output_to_operand_aliasing={{0}: (7, {}), {1}: (4, {}), {2}: (5, {})} | custom-call | flops 1000000 | bytes 100000 | tf_op jit(solution)/shard_map/chunk/pallas_call | solution.py:194
  73.6 5.5 %chunk.12 = (f32[2176,64]{1,0:T(8,128)S(1)}, bf16[4096,1024]{1,0:T(8,128)(2,1)S(1)}, bf16[4096,768]{1,0:T(8,128)(2,1)S(1)}) custom-call(bf16[64,4096]{1,0:T(8,128)(2,1)S(1)} %collective-permute-done.12.refs_0_, bf16[64,4096]{1,0:T(8,128)(2,1)S(1)} %collective-permute-done.13.refs_1_, ...), custom_call_target="tpu_custom_call", output_to_operand_aliasing={{0}: (7, {}), {1}: (4, {}), {2}: (5, {})} | custom-call | flops 1000000 | bytes 100000 | tf_op jit(solution)/shard_map/chunk/pallas_call | solution.py:194
  79.1 3.3 %copy-done = bf16[4096,1024]{1,0:T(8,128)(2,1)} copy-done((bf16[4096,1024]{1,0:T(8,128)(2,1)}, bf16[4096,1024]{1,0:T(8,128)(2,1)S(1)}, u32[]{:S(2)}) %copy-start) | copy-done | bytes 8388632
  82.4 2.7 %copy-done.6 = bf16[4096,768]{1,0:T(8,128)(2,1)} copy-done((bf16[4096,768]{1,0:T(8,128)(2,1)}, bf16[4096,768]{1,0:T(8,128)(2,1)S(1)}, u32[]{:S(2)}) %copy-start.6) | copy-done | bytes 6291480
  91.0 3.4 %copy-done.1 = bf16[4096,1024]{1,0:T(8,128)(2,1)S(1)} copy-done((bf16[4096,1024]{1,0:T(8,128)(2,1)S(1)}, bf16[4096,1024]{1,0:T(8,128)(2,1)}, u32[]{:S(2)}) %copy-start.1) | copy-done | bytes 8388632
  94.4 2.8 %copy-done.7 = bf16[4096,768]{1,0:T(8,128)(2,1)S(1)} copy-done((bf16[4096,768]{1,0:T(8,128)(2,1)S(1)}, bf16[4096,768]{1,0:T(8,128)(2,1)}, u32[]{:S(2)}) %copy-start.7) | copy-done | bytes 6291480
  98.2 5.5 %chunk.13 = (f32[2176,64]{1,0:T(8,128)S(1)}, bf16[4096,1024]{1,0:T(8,128)(2,1)S(1)}, bf16[4096,768]{1,0:T(8,128)(2,1)S(1)}) custom-call(bf16[64,4096]{1,0:T(8,128)(2,1)S(1)} %copy-done.11, bf16[64,4096]{1,0:T(8,128)(2,1)} %collective-permute-done.22.refs_1_, ...), custom_call_target="tpu_custom_call", output_to_operand_aliasing={{0}: (7, {}), {1}: (4, {}), {2}: (5, {})} | custom-call | flops 1000000 | bytes 100000 | tf_op jit(solution)/shard_map/chunk/pallas_call | solution.py:194
  103.8 3.3 %copy-done.2 = bf16[4096,1024]{1,0:T(8,128)(2,1)} copy-done((bf16[4096,1024]{1,0:T(8,128)(2,1)}, bf16[4096,1024]{1,0:T(8,128)(2,1)S(1)}, u32[]{:S(2)}) %copy-start.2) | copy-done | bytes 8388632
  112.1 3.4 %copy-done.3 = bf16[4096,1024]{1,0:T(8,128)(2,1)S(1)} copy-done((bf16[4096,1024]{1,0:T(8,128)(2,1)S(1)}, bf16[4096,1024]{1,0:T(8,128)(2,1)}, u32[]{:S(2)}) %copy-start.3) | copy-done | bytes 8388632
  115.4 5.8 %chunk.14 = (f32[2176,64]{1,0:T(8,128)S(1)}, bf16[4096,1024]{1,0:T(8,128)(2,1)S(1)}, bf16[4096,768]{1,0:T(8,128)(2,1)S(1)}) custom-call(bf16[64,4096]{1,0:T(8,128)(2,1)} %collective-permute-done.26.refs_0_, bf16[64,4096]{1,0:T(8,128)(2,1)} %collective-permute-done.27.refs_1_, ...), custom_call_target="tpu_custom_call", output_to_operand_aliasing={{0}: (7, {}), {1}: (4, {}), {2}: (5, {})} | custom-call | flops 1000000 | bytes 100000 | tf_op jit(solution)/shard_map/chunk/pallas_call | solution.py:194
  121.3 2.4 %chunk.15 = (f32[2176,64]{1,0:T(8,128)S(1)}, bf16[4096,1024]{1,0:T(8,128)(2,1)S(1)}, bf16[4096,768]{1,0:T(8,128)(2,1)S(1)}) custom-call(bf16[64,4096]{1,0:T(8,128)(2,1)S(1)} %collective-permute-done.24.refs_0_, bf16[64,4096]{1,0:T(8,128)(2,1)S(1)} %collective-permute-done.25.refs_1_, ...), custom_call_target="tpu_custom_call", output_to_operand_aliasing={{0}: (5, {}), {1}: (2, {}), {2}: (3, {})} | custom-call | flops 1000000 | bytes 100000 | tf_op jit(solution)/shard_map/chunk/pallas_call | solution.py:194
  123.8 3.3 %copy-done.4 = bf16[4096,1024]{1,0:T(8,128)(2,1)} copy-done((bf16[4096,1024]{1,0:T(8,128)(2,1)}, bf16[4096,1024]{1,0:T(8,128)(2,1)S(1)}, u32[]{:S(2)}) %copy-start.4) | copy-done | bytes 8388632
  129.6 3.4 %copy-done.5 = bf16[4096,1024]{1,0:T(8,128)(2,1)S(1)} copy-done((bf16[4096,1024]{1,0:T(8,128)(2,1)S(1)}, bf16[4096,1024]{1,0:T(8,128)(2,1)}, u32[]{:S(2)}) %copy-start.5) | copy-done | bytes 8388632
  135.5 2.4 %chunk.17 = (f32[2176,64]{1,0:T(8,128)S(1)}, bf16[4096,1024]{1,0:T(8,128)(2,1)S(1)}, bf16[4096,768]{1,0:T(8,128)(2,1)S(1)}) custom-call(bf16[64,4096]{1,0:T(8,128)(2,1)S(1)} %collective-permute-done.28.refs_0_, bf16[64,4096]{1,0:T(8,128)(2,1)S(1)} %collective-permute-done.29.refs_1_, ...), custom_call_target="tpu_custom_call", output_to_operand_aliasing={{0}: (5, {}), {1}: (2, {}), {2}: (3, {})} | custom-call | flops 1000000 | bytes 100000 | tf_op jit(solution)/shard_map/chunk/pallas_call | solution.py:194
  137.9 3.3 %finish.1 = f32[16,256]{1,0:T(8,128)S(1)} custom-call(s32[16]{0:T(128)S(1)} %dynamic-slice_bitcast_fusion.refs_0_.names, f32[2176,64]{1,0:T(8,128)S(1)} %get-tuple-element.122.left_ref, f32[32,16,128]{2,1,0:T(8,128)S(1)} %sketches.3.flat_ref, s32[1,256]{1,0:T(1,128)S(1)} %reshape.15.ids_ref, bf16[16,24,2048]{2,1,0:T(8,128)(2,1)} %bitcast.25, ...), custom_call_target="tpu_custom_call" | custom-call | flops 1000000 | bytes 100000 | tf_op jit(solution)/shard_map/finish/pallas_call | solution.py:317
  141.2 11.3 %all_to_all.9 = f32[16,1,256]{2,1,0:T(1,128)S(1)} all-to-all(f32[16,1,256]{2,1,0:T(1,128)S(1)} %copy.40), channel_id=1, replica_groups=mesh['groups'=2,'examples'=16] {'examples'}, dimensions={0} | all-to-all | bytes 32768 | tf_op jit(solution)/shard_map/all_to_all | solution.py:444
  (87 shorter events, 32.2 us)
Async XLA Ops:
  6.5 78.6 %all-gather.3.cloned.1.call-start = ((), (), s32[]{:S(2)}) async-start(), calls=%async_computation.1 | async-start | bytes 1671168 | tf_op jit(solution)/shard_map/all_gather | solution.py:401
  10.7 17.3 %collective-permute-start = (bf16[64,4096]{1,0:T(8,128)(2,1)S(1)}, bf16[64,4096]{1,0:T(8,128)(2,1)S(1)}, u32[]{:S(2)}, u32[]{:S(2)}) collective-permute-start(bf16[64,4096]{1,0:T(8,128)(2,1)S(1)} %get-tuple-element.65.refs_0_), channel_id=1, source_target_pairs={{0,4},{1,5},{4,8},{5,9},{8,12},{9,13},{12,14},{13,15},{14,10},{15,... | collective-permute-start | bytes 1572872 | tf_op jit(solution)/shard_map/ppermute | solution.py:388
  13.8 24.4 %collective-permute-start.1 = (bf16[64,4096]{1,0:T(8,128)(2,1)S(1)}, bf16[64,4096]{1,0:T(8,128)(2,1)S(1)}, u32[]{:S(2)}, u32[]{:S(2)}) collective-permute-start(bf16[64,4096]{1,0:T(8,128)(2,1)S(1)} %get-tuple-element.65.refs_0_), channel_id=1, source_target_pairs={{4,0},{5,1},{8,4},{9,5},{12,8},{13,9},{14,12},{15,13},{10,14},{11,... | collective-permute-start | bytes 1572872 | tf_op jit(solution)/shard_map/ppermute | solution.py:388
  13.8 24.4 %collective-permute-start.8 = (bf16[64,4096]{1,0:T(8,128)(2,1)S(1)}, bf16[64,4096]{1,0:T(8,128)(2,1)S(1)}, u32[]{:S(2)}, u32[]{:S(2)}) collective-permute-start(bf16[64,4096]{1,0:T(8,128)(2,1)S(1)} %get-tuple-element.65.refs_0_), channel_id=1, source_target_pairs={{0,1},{1,0},{2,3},{3,2},{4,5},{5,4},{6,7},{7,6},{8,9},{9,8},{10,11... | collective-permute-start | bytes 1572872 | tf_op jit(solution)/shard_map/ppermute | solution.py:388
  13.8 24.9 %collective-permute-start.9 = (bf16[64,4096]{1,0:T(8,128)(2,1)S(1)}, bf16[64,4096]{1,0:T(8,128)(2,1)S(1)}, u32[]{:S(2)}, u32[]{:S(2)}) collective-permute-start(bf16[64,4096]{1,0:T(8,128)(2,1)S(1)} %get-tuple-element.66.refs_1_), channel_id=1, source_target_pairs={{0,1},{1,0},{2,3},{3,2},{4,5},{5,4},{6,7},{7,6},{8,9},{9,8},{10,11... | collective-permute-start | bytes 1572872 | tf_op jit(solution)/shard_map/ppermute | solution.py:388
  14.3 25.3 %collective-permute-start.6 = (bf16[64,4096]{1,0:T(8,128)(2,1)S(1)}, bf16[64,4096]{1,0:T(8,128)(2,1)S(1)}, u32[]{:S(2)}, u32[]{:S(2)}) collective-permute-start(bf16[64,4096]{1,0:T(8,128)(2,1)S(1)} %get-tuple-element.66.refs_1_), channel_id=1, source_target_pairs={{0,4},{1,5},{4,8},{5,9},{8,12},{9,13},{12,14},{13,15},{14,10},{15,... | collective-permute-start | bytes 1572872 | tf_op jit(solution)/shard_map/ppermute | solution.py:388
  28.0 18.0 %collective-permute-start.7 = (bf16[64,4096]{1,0:T(8,128)(2,1)S(1)}, bf16[64,4096]{1,0:T(8,128)(2,1)S(1)}, u32[]{:S(2)}, u32[]{:S(2)}) collective-permute-start(bf16[64,4096]{1,0:T(8,128)(2,1)S(1)} %get-tuple-element.66.refs_1_), channel_id=1, source_target_pairs={{4,0},{5,1},{8,4},{9,5},{12,8},{13,9},{14,12},{15,13},{10,14},{11,... | collective-permute-start | bytes 1572872 | tf_op jit(solution)/shard_map/ppermute | solution.py:388
  38.7 18.5 %collective-permute-start.2 = (bf16[64,4096]{1,0:T(8,128)(2,1)S(1)}, bf16[64,4096]{1,0:T(8,128)(2,1)S(1)}, u32[]{:S(2)}, u32[]{:S(2)}) collective-permute-start(bf16[64,4096]{1,0:T(8,128)(2,1)S(1)} %collective-permute-done.refs_2_), channel_id=1, source_target_pairs={{0,4},{1,5},{4,8},{5,9},{8,12},{9,13},{12,14},{13,15},{14,10},{15,... | collective-permute-start | bytes 1572872 | tf_op jit(solution)/shard_map/ppermute | solution.py:388
  39.6 25.1 %collective-permute-start.3 = (bf16[64,4096]{1,0:T(8,128)(2,1)S(1)}, bf16[64,4096]{1,0:T(8,128)(2,1)S(1)}, u32[]{:S(2)}, u32[]{:S(2)}) collective-permute-start(bf16[64,4096]{1,0:T(8,128)(2,1)S(1)} %collective-permute-done.1.refs_3_), channel_id=1, source_target_pairs={{4,0},{5,1},{8,4},{9,5},{12,8},{13,9},{14,12},{15,13},{10,14},{11,... | collective-permute-start | bytes 1572872 | tf_op jit(solution)/shard_map/ppermute | solution.py:388
  46.0 18.8 %collective-permute-start.16 = (bf16[64,4096]{1,0:T(8,128)(2,1)S(1)}, bf16[64,4096]{1,0:T(8,128)(2,1)S(1)}, u32[]{:S(2)}, u32[]{:S(2)}) collective-permute-start(bf16[64,4096]{1,0:T(8,128)(2,1)S(1)} %collective-permute-done.6.refs_2_), channel_id=1, source_target_pairs={{0,1},{1,0},{2,3},{3,2},{4,5},{5,4},{6,7},{7,6},{8,9},{9,8},{10,11... | collective-permute-start | bytes 1572872 | tf_op jit(solution)/shard_map/ppermute | solution.py:388
  46.1 19.2 %collective-permute-start.17 = (bf16[64,4096]{1,0:T(8,128)(2,1)S(1)}, bf16[64,4096]{1,0:T(8,128)(2,1)S(1)}, u32[]{:S(2)}, u32[]{:S(2)}) collective-permute-start(bf16[64,4096]{1,0:T(8,128)(2,1)S(1)} %collective-permute-done.7.refs_3_), channel_id=1, source_target_pairs={{0,1},{1,0},{2,3},{3,2},{4,5},{5,4},{6,7},{7,6},{8,9},{9,8},{10,11... | collective-permute-start | bytes 1572872 | tf_op jit(solution)/shard_map/ppermute | solution.py:388
  46.6 22.9 %collective-permute-start.14 = (bf16[64,4096]{1,0:T(8,128)(2,1)S(1)}, bf16[64,4096]{1,0:T(8,128)(2,1)}, u32[]{:S(2)}, u32[]{:S(2)}) collective-permute-start(bf16[64,4096]{1,0:T(8,128)(2,1)S(1)} %collective-permute-done.6.refs_2_), channel_id=1, source_target_pairs={{0,4},{1,5},{4,8},{5,9},{8,12},{9,13},{12,14},{13,15},{14,10},{15,... | collective-permute-start | bytes 1572872 | tf_op jit(solution)/shard_map/ppermute | solution.py:388
  57.3 14.6 %collective-permute-start.15 = (bf16[64,4096]{1,0:T(8,128)(2,1)S(1)}, bf16[64,4096]{1,0:T(8,128)(2,1)}, u32[]{:S(2)}, u32[]{:S(2)}) collective-permute-start(bf16[64,4096]{1,0:T(8,128)(2,1)S(1)} %collective-permute-done.7.refs_3_), channel_id=1, source_target_pairs={{4,0},{5,1},{8,4},{9,5},{12,8},{13,9},{14,12},{15,13},{10,14},{11,... | collective-permute-start | bytes 1572872 | tf_op jit(solution)/shard_map/ppermute | solution.py:388
  65.3 19.8 %collective-permute-start.10 = (bf16[64,4096]{1,0:T(8,128)(2,1)S(1)}, bf16[64,4096]{1,0:T(8,128)(2,1)S(1)}, u32[]{:S(2)}, u32[]{:S(2)}) collective-permute-start(bf16[64,4096]{1,0:T(8,128)(2,1)S(1)} %collective-permute-done.2.refs_2_), channel_id=1, source_target_pairs={{0,4},{1,5},{4,8},{5,9},{8,12},{9,13},{12,14},{13,15},{14,10},{15,... | collective-permute-start | bytes 1572872 | tf_op jit(solution)/shard_map/ppermute | solution.py:388
  69.6 17.9 %collective-permute-start.11 = (bf16[64,4096]{1,0:T(8,128)(2,1)S(1)}, bf16[64,4096]{1,0:T(8,128)(2,1)}, u32[]{:S(2)}, u32[]{:S(2)}) collective-permute-start(bf16[64,4096]{1,0:T(8,128)(2,1)S(1)} %collective-permute-done.3.refs_3_), channel_id=1, source_target_pairs={{4,0},{5,1},{8,4},{9,5},{12,8},{13,9},{14,12},{15,13},{10,14},{11,... | collective-permute-start | bytes 1572872 | tf_op jit(solution)/shard_map/ppermute | solution.py:388
  71.9 15.6 %collective-permute-start.21 = (bf16[64,4096]{1,0:T(8,128)(2,1)}, bf16[64,4096]{1,0:T(8,128)(2,1)S(1)}, u32[]{:S(2)}, u32[]{:S(2)}) collective-permute-start(bf16[64,4096]{1,0:T(8,128)(2,1)} %collective-permute-done.14.refs_2_), channel_id=1, source_target_pairs={{0,1},{1,0},{2,3},{3,2},{4,5},{5,4},{6,7},{7,6},{8,9},{9,8},{10,11... | collective-permute-start | bytes 1572872 | tf_op jit(solution)/shard_map/ppermute | solution.py:388
  71.9 16.9 %collective-permute-start.22 = (bf16[64,4096]{1,0:T(8,128)(2,1)}, bf16[64,4096]{1,0:T(8,128)(2,1)}, u32[]{:S(2)}, u32[]{:S(2)}) collective-permute-start(bf16[64,4096]{1,0:T(8,128)(2,1)} %collective-permute-done.15.refs_3_), channel_id=1, source_target_pairs={{0,1},{1,0},{2,3},{3,2},{4,5},{5,4},{6,7},{7,6},{8,9},{9,8},{10,11... | collective-permute-start | bytes 1572872 | tf_op jit(solution)/shard_map/ppermute | solution.py:388
  72.4 37.0 %collective-permute-start.19 = (bf16[64,4096]{1,0:T(8,128)(2,1)}, bf16[64,4096]{1,0:T(8,128)(2,1)}, u32[]{:S(2)}, u32[]{:S(2)}) collective-permute-start(bf16[64,4096]{1,0:T(8,128)(2,1)} %collective-permute-done.14.refs_2_), channel_id=1, source_target_pairs={{0,4},{1,5},{4,8},{5,9},{8,12},{9,13},{12,14},{13,15},{14,10},{15,... | collective-permute-start | bytes 1572872 | tf_op jit(solution)/shard_map/ppermute | solution.py:388
  85.1 24.3 %collective-permute-start.20 = (bf16[64,4096]{1,0:T(8,128)(2,1)}, bf16[64,4096]{1,0:T(8,128)(2,1)}, u32[]{:S(2)}, u32[]{:S(2)}) collective-permute-start(bf16[64,4096]{1,0:T(8,128)(2,1)} %collective-permute-done.15.refs_3_), channel_id=1, source_target_pairs={{4,0},{5,1},{8,4},{9,5},{12,8},{13,9},{14,12},{15,13},{10,14},{11,... | collective-permute-start | bytes 1572872 | tf_op jit(solution)/shard_map/ppermute | solution.py:388
  87.4 22.6 %collective-permute-start.26 = (bf16[64,4096]{1,0:T(8,128)(2,1)S(1)}, bf16[64,4096]{1,0:T(8,128)(2,1)}, u32[]{:S(2)}, u32[]{:S(2)}) collective-permute-start(bf16[64,4096]{1,0:T(8,128)(2,1)S(1)} %collective-permute-done.10.refs_2_), channel_id=1, source_target_pairs={{0,1},{1,0},{2,3},{3,2},{4,5},{5,4},{6,7},{7,6},{8,9},{9,8},{10,11... | collective-permute-start | bytes 1572872 | tf_op jit(solution)/shard_map/ppermute | solution.py:388
  88.3 23.7 %collective-permute-start.27 = (bf16[64,4096]{1,0:T(8,128)(2,1)}, bf16[64,4096]{1,0:T(8,128)(2,1)}, u32[]{:S(2)}, u32[]{:S(2)}) collective-permute-start(bf16[64,4096]{1,0:T(8,128)(2,1)} %collective-permute-done.11.refs_3_), channel_id=1, source_target_pairs={{0,1},{1,0},{2,3},{3,2},{4,5},{5,4},{6,7},{7,6},{8,9},{9,8},{10,11... | collective-permute-start | bytes 1572872 | tf_op jit(solution)/shard_map/ppermute | solution.py:388
  88.8 49.1 %collective-permute-start.30 = (bf16[16,24,2048]{2,1,0:T(8,128)(2,1)}, bf16[16,24,2048]{2,1,0:T(8,128)(2,1)S(1)}, u32[]{:S(2)}, u32[]{:S(2)}) collective-permute-start(bf16[16,24,2048]{2,1,0:T(8,128)(2,1)} %bitcast.22), channel_id=1, source_target_pairs={{16,0},{0,16},{17,1},{1,17},{18,2},{2,18},{19,3},{3,19},{20,4},{4,... | collective-permute-start | bytes 4718600 | tf_op jit(solution)/shard_map/ppermute | solution.py:431
  110.0 19.0 %collective-permute-start.23 = (bf16[64,4096]{1,0:T(8,128)(2,1)}, bf16[64,4096]{1,0:T(8,128)(2,1)S(1)}, u32[]{:S(2)}, u32[]{:S(2)}) collective-permute-start(bf16[64,4096]{1,0:T(8,128)(2,1)} %collective-permute-done.20.refs_3_), channel_id=1, source_target_pairs={{4,0},{5,1},{8,4},{9,5},{12,8},{13,9},{14,12},{15,13},{10,14},{11,... | collective-permute-start | bytes 1572872 | tf_op jit(solution)/shard_map/ppermute | solution.py:388
  112.1 17.0 %collective-permute-start.18 = (bf16[64,4096]{1,0:T(8,128)(2,1)S(1)}, bf16[64,4096]{1,0:T(8,128)(2,1)S(1)}, u32[]{:S(2)}, u32[]{:S(2)}) collective-permute-start(bf16[64,4096]{1,0:T(8,128)(2,1)S(1)} %collective-permute-done.10.refs_2_), channel_id=1, source_target_pairs={{0,4},{1,5},{4,8},{5,9},{8,12},{9,13},{12,14},{13,15},{14,10},{15,... | collective-permute-start | bytes 1572872 | tf_op jit(solution)/shard_map/ppermute | solution.py:388
  (21 other events, 113.8 us)
Sparse Core Ops, SparseCore 0:
  10.8 46.6 all-gather.2

commit v9 on v8

--- a/solution.py
+++ b/solution.py
@@ -228,43 +228,32 @@
     flat[:, slot, :] = jnp.where(lane < order, even, odd)
 
 
-def sketch_body(places, first, half, count, *refs):
-    names, left_ref, side_hbm = refs[:3]
-    flat, side_ref, twice, sems = refs[-4:]
+def sketch_body(places, first, half, count, table, left_ref, mine_ref, other_ref, *refs):
+    flat, twice = refs[-2:]
+    me = lax.axis_index("examples")
     order = left_ref.shape[1]
-    rows = 2 * half * LANES // side_ref.shape[2]
-    copies = [
-        pltpu.make_async_copy(side_hbm.at[names[first + r]], side_ref.at[r], sems.at[r]) for r in range(len(places))
-    ]
-    for copy in copies:
-        copy.start()
-    for copy in copies:
-        copy.wait()
-    for r, at in enumerate(places):
-        masked = masked_of(side_ref[r, count : count + rows, :], 2 * half, order)
-        write_flat(flat, first + r, one_sketch(left_ref, masked, at, half), twice)
-
-
-def sketches(places, first, half, count, names, left, side, flat):
+    rows = 2 * half * LANES // mine_ref.shape[2]
+    total = table.shape[1] // 2
+    for r, at in enumerate(places, first):
+        ref = mine_ref if r % 2 == 0 else other_ref
+        masked = masked_of(ref[table[me, total + r], count : count + rows, :], 2 * half, order)
+        write_flat(flat, r, one_sketch(left_ref, masked, at, half), twice)
+
+
+def sketches(places, first, half, count, table, left, mine, other, flat):
     order = left.shape[1]
     vmem = pl.BlockSpec(memory_space=pltpu.VMEM)
-    operands = [names, left, pltpu.with_memory_space_constraint(side, pltpu.HBM)]
-    in_specs = [pl.BlockSpec(memory_space=pltpu.SMEM), vmem, pl.BlockSpec(memory_space=pltpu.HBM)]
+    operands = [table, left, mine, other]
     aliases = {}
     if flat is not None:
-        aliases = {3: 0}
+        aliases = {4: 0}
         operands.append(flat)
-        in_specs.append(vmem)
     return pl.pallas_call(
         functools.partial(sketch_body, places, first, half, count),
-        in_specs=in_specs,
+        in_specs=[pl.BlockSpec(memory_space=pltpu.SMEM)] + [vmem] * (len(operands) - 1),
         out_specs=vmem,
-        out_shape=jax.ShapeDtypeStruct((order // 2, names.shape[0], 2 * order), jnp.float32),
-        scratch_shapes=[
-            pltpu.VMEM((len(places), *side.shape[1:]), side.dtype),
-            pltpu.VMEM((order, 2 * order), jnp.float32),
-            pltpu.SemaphoreType.DMA((len(places),)),
-        ],
+        out_shape=jax.ShapeDtypeStruct((order // 2, table.shape[0], 2 * order), jnp.float32),
+        scratch_shapes=[pltpu.VMEM((order, 2 * order), jnp.float32)],
         input_output_aliases=aliases,
         compiler_params=pltpu.CompilerParams(vmem_limit_bytes=12 * MIB),
         cost_estimate=SMALL,
@@ -272,63 +261,65 @@
     )(*operands)
 
 
-def finish_body(places, half, groups, count, names, left_ref, flat_ref, ids_ref, *refs):
-    shares_hbm, (out_ref, share_ref, twice, flat, sems) = refs[:groups], refs[groups:]
-    devices, width = share_ref.shape[1], share_ref.shape[3]
+def members_of(share_ref, count, order):
+    devices = share_ref.shape[0]
+    first = share_ref[:, count : count + 8, :LANES].astype(jnp.float32)[:, 0, :].astype(jnp.bfloat16)
+    shape = (LANES, devices * count)
+    place = lax.broadcasted_iota(jnp.int32, shape, 0) - order
+    query = lax.broadcasted_iota(jnp.int32, shape, 1)
+    spread = (place >= 0) & (place < count) & (((query - place) & (count - 1)) == 0)
+    ids = jnp.dot(first, spread.astype(jnp.bfloat16), preferred_element_type=jnp.float32)
+    place = lax.broadcasted_iota(jnp.int32, ids.shape, 1) - count * lax.broadcasted_iota(jnp.int32, ids.shape, 0)
+    ids = jnp.sum(jnp.where((place >= 0) & (place < count), ids, 0.0), axis=0, keepdims=True)
+    value = lax.broadcasted_iota(jnp.int32, (NVAL, devices * count), 0).astype(jnp.float32)
+    return (value == ids).astype(jnp.bfloat16)
+
+
+def finish_body(places, half, groups, count, table, left_ref, flat_ref, *refs):
+    share_refs, (out_ref, twice, flat) = (refs[:groups], refs[groups : 2 * groups]), refs[2 * groups :]
+    chips, _, width = share_refs[0][0].shape
     order = left_ref.shape[1]
     rows = 2 * half * LANES // width
-    parts = sems.shape[1]
-    copies = []
-    for r, ref in enumerate(shares_hbm):
-        for p in range(parts):
-            some = pl.ds(p * (devices // parts), devices // parts)
-            copies.append(pltpu.make_async_copy(ref.at[some], share_ref.at[r, some], sems.at[r, p]))
-    for copy in copies:
-        copy.start()
+    me, group = lax.axis_index("examples"), lax.axis_index("groups")
+    examples = table.shape[0]
     flat[...] = flat_ref[...]
-    value = lax.broadcasted_iota(jnp.int32, (NVAL, ids_ref.shape[1]), 0)
-    members = (value == ids_ref[...]).astype(jnp.bfloat16)
-    for copy in copies:
-        copy.wait()
-    first = names.shape[0] - len(places)
-    for r, at in enumerate(places):
-        masked = masked_of(share_ref[0, names[first + r], count : count + rows, :], 2 * half, order)
-        write_flat(flat, first + r, one_sketch(left_ref, masked, at, half), twice)
-    group = lax.axis_index("groups")
-    scores = 0.0
+    members = [members_of(refs[0], count, order) for refs in share_refs]
+    first = examples - len(places)
+    for r, at in enumerate(places, first):
+        masked = masked_of(share_refs[r % 2][0][table[me, examples + r], count : count + rows, :], 2 * half, order)
+        write_flat(flat, r, one_sketch(left_ref, masked, at, half), twice)
+    scores = [0.0, 0.0]
     for r in range(groups):
         block = lax.rem(group + r, groups) * (width // LANES)
         sketch = jnp.concatenate([flat[block + c] for c in range(width // LANES)], axis=1).astype(jnp.bfloat16)
-        queries = share_ref[r, :, :count, :].reshape(devices * count, width)
-        scores += lax.dot_general(sketch, queries, NT, preferred_element_type=jnp.float32)
+        for kind in range(2):
+            queries = share_refs[kind][r][:, :count, :].reshape(chips * count, width)
+            scores[kind] += lax.dot_general(sketch, queries, NT, preferred_element_type=jnp.float32)
     total = 0.0
-    for _ in range(3):
-        part = scores.astype(jnp.bfloat16)
-        scores = scores - part.astype(jnp.float32)
-        total += lax.dot_general(part, members, NT, preferred_element_type=jnp.float32)
-    for r in range(names.shape[0]):
-        out_ref[pl.ds(names[r], 1), :] = total[r : r + 1, :]
-
-
-def finish(places, half, count, names, left, flat, shares, ids):
+    for kind in range(2):
+        rest = scores[kind]
+        for _ in range(3):
+            part = rest.astype(jnp.bfloat16)
+            rest = rest - part.astype(jnp.float32)
+            total += lax.dot_general(part, members[kind], NT, preferred_element_type=jnp.float32)
+    for r in range(examples):
+        out_ref[pl.ds(table[me, r], 1), :] = total[r : r + 1, :]
+
+
+def finish(places, half, count, table, left, flat, mine, other):
     order = left.shape[1]
+    groups = len(mine)
     vmem = pl.BlockSpec(memory_space=pltpu.VMEM)
-    hbm = pl.BlockSpec(memory_space=pltpu.HBM)
     return pl.pallas_call(
-        functools.partial(finish_body, places, half, len(shares), count),
-        in_specs=[pl.BlockSpec(memory_space=pltpu.SMEM)] + [vmem] * 3 + [hbm] + [pl.BlockSpec(memory_space=pl.ANY)] * (len(shares) - 1),
+        functools.partial(finish_body, places, half, groups, count),
+        in_specs=[pl.BlockSpec(memory_space=pltpu.SMEM)] + [vmem] * (2 + 2 * groups),
         out_specs=vmem,
-        out_shape=jax.ShapeDtypeStruct((names.shape[0], NVAL), jnp.float32),
-        scratch_shapes=[
-            pltpu.VMEM((len(shares), *shares[0].shape), shares[0].dtype),
-            pltpu.VMEM((order, 2 * order), jnp.float32),
-            pltpu.VMEM(flat.shape, jnp.float32),
-            pltpu.SemaphoreType.DMA((len(shares), 4)),
-        ],
-        compiler_params=pltpu.CompilerParams(vmem_limit_bytes=20 * MIB),
+        out_shape=jax.ShapeDtypeStruct((table.shape[0], NVAL), jnp.float32),
+        scratch_shapes=[pltpu.VMEM((order, 2 * order), jnp.float32), pltpu.VMEM(flat.shape, jnp.float32)],
+        compiler_params=pltpu.CompilerParams(vmem_limit_bytes=12 * MIB),
         cost_estimate=SMALL,
         name="finish",
-    )(names, left, flat, ids, pltpu.with_memory_space_constraint(shares[0], pltpu.HBM), *shares[1:])
+    )(table, left, flat, *mine, *other)
 
 
 def arrivals(ring, devices):
@@ -348,6 +339,10 @@
                 halves = [(2 * distance - 1, piece), (2 * distance, piece)]
             spots.append([4 * k + 2 + p for k, p in halves])
             spots.append([4 * k + 4 + p for k, p in halves])
+    bits = chips.bit_length() - 1
+    for me, row in enumerate(table):
+        apart = [(example // 2) ^ (me // 2) for example in row]
+        row += [sum(((x >> b) & 1) << (bits - 1 - b) for b in range(bits)) for x in apart]
     return table, spots
 
 
@@ -367,8 +362,6 @@
 ):
     chips = devices // 2
     ring = chip_ring(chips)
-    me = lax.axis_index("examples")
-
     forward = [(ring[r] * 2 + c, ring[(r + 1) % chips] * 2 + c) for r in range(chips) for c in range(2)]
     backward = [(b, a) for a, b in forward]
     other_core = [(d, d ^ 1) for d in range(devices)]
@@ -398,7 +391,10 @@
         queries,
         groups,
     )
-    side = lax.all_gather(side, "examples", axis=0)
+    distances = [chips >> b for b in range(1, chips.bit_length())]
+    apart = [[(d, 2 * ((d // 2) ^ distance) + d % 2) for d in range(devices)] for distance in distances]
+    side = side[None]
+    pending = [send(side, apart[0])]
     coming = {
         1: (send(x_a, forward), send(x_a, backward)),
         2: (send(x_b, forward), send(x_b, backward)),
@@ -406,11 +402,11 @@
     swapped = tuple(send(x, other_core) for x in (x_a, x_b))
     left, weights = first_chunk((x_a, x_b), gate_weight, up_weight, in_factor.T, 1, tokens)
 
-    names, spots = arrivals(ring, devices)
-    names = lax.dynamic_index_in_dim(jnp.array(names, jnp.int32), me, keepdims=False)
+    table, spots = arrivals(ring, devices)
+    table = jnp.array(table, jnp.int32)
 
     for k in range(1, chips):
-        own_1, own_2, left = lax.optimization_barrier((*coming.pop(k), left))
+        own_1, own_2, left, *pending = lax.optimization_barrier((*coming.pop(k), left, *pending))
         own = (own_1, own_2)
         if k + 2 < chips - 1:
             coming[k + 2] = (send(own_1, forward), send(own_2, backward))
@@ -421,26 +417,32 @@
         before, swapped = swapped, tuple(send(x, other_core) for x in own)
         if k < chips - 1:
             left, weights = chunk(before + own, weights, in_factor.T, left, k)
-        if k == chips - 4:
-            side, left = lax.optimization_barrier((side, left))
-            ids = side[:, nq, order : order + nq].astype(jnp.int32).reshape(1, devices * nq)
-            ids, left = lax.optimization_barrier((ids, left))
-            shares = [side]
+        if k <= len(distances):
+            side = jnp.concatenate([side, *pending], axis=0)
+            pending = []
+        if k < len(distances):
+            pending = [send(side, apart[k])]
+        if k == len(distances):
+            other = [send(side, other_core)]
+            mine = [side]
             for r in range(1, groups):
                 way = [((g + r) % groups, g) for g in range(groups)]
-                shares.append(lax.ppermute(side, "groups", way))
+                pending.append(lax.ppermute(side, "groups", way))
         if k == chips - 3:
+            mine += pending
+            other += [send(x, other_core) for x in pending]
+            pending = []
             ready = devices - 6
-            flat = sketches(spots[:ready], 0, half, nq, names, left, side, None)
+            flat = sketches(spots[:ready], 0, half, nq, table, left, mine[0], other[0], None)
             flat, left = lax.optimization_barrier((flat, left))
         if k == chips - 2:
             left, weights = chunk(swapped, weights, in_factor.T, left, 2 * k + 2)
-            flat = sketches(spots[ready:-2], ready, half, nq, names, left, side, flat)
+            flat = sketches(spots[ready:-2], ready, half, nq, table, left, mine[0], other[0], flat)
             flat, left = lax.optimization_barrier((flat, left))
     left, weights = chunk(own, weights, in_factor.T, left, 2 * chips - 1)
     left, weights = chunk(swapped, weights, in_factor.T, left, 2 * chips)
 
-    partial = finish(spots[-2:], half, nq, names, left, flat, shares, ids)
+    partial = finish(spots[-2:], half, nq, table, left, flat, mine, other)
     shares = lax.all_to_all(partial, "examples", split_axis=0, concat_axis=0, tiled=True)
     return jnp.sum(shares, axis=0, keepdims=True)
 

time: 161 us -> 140 us (0.87)
  waiting for transfers between devices: 22.4 us -> 55.4 us
  local copies, waits for them, and re-layouts: 29.7 us -> 1.57 us
  between operations: 14.4 us -> 0.97 us
  Pallas kernels: 54.9 us -> 46.2 us
  starting transfers between devices: 25.9 us -> 24.1 us
    ppermute x30 -> x35, waiting for transfers between devices: 22.3 us -> 55.4 us  [send(): return lax.ppermute(x, 'examples', way)]
    unnamed x26 -> x8, local copies, waits for them, and re-layouts: 28.9 us -> 1.56 us
    pallas_call x9, Pallas kernels: 36.8 us -> 32.4 us  [chunk(): pl.pallas_call(functools.partial(chunk_body, pieces), grid=(1,), in_specs...]
    pallas_call x2, Pallas kernels: 4.33 us -> 2.16 us  [sketches(): pl.pallas_call(functools.partial(sketch_body, places, first, half, count)...]
    ppermute x30 -> x35, starting transfers between devices: 24.4 us -> 22.5 us  [send(): return lax.ppermute(x, 'examples', way)]
  transfers between devices with their start and end apart: 32 -> 36, of which waited for: 3 -> 10; matrix products, arithmetic and copies ran while one was open for 1% -> 0% of each run, Pallas kernels for 30% -> 30%
where the time goes in v9:
time: 140 us; the launch traced here: 139 us
  waiting for transfers between devices  55.4 us (40%)
  Pallas kernels  46.2 us (33%)
  starting transfers between devices  24.1 us (17%)
  blocking collectives  10.4 us (7%)
  local copies, waits for them, and re-layouts  1.57 us (1%)
    ppermute x35, waiting for transfers between devices, send(): return lax.ppermute(x, 'examples', way)  55.4 us
    pallas_call x9, Pallas kernels, chunk(): pl.pallas_call(functools.partial(chunk_body, pieces), grid=(1,), in_specs...  32.4 us
    ppermute x35, starting transfers between devices, send(): return lax.ppermute(x, 'examples', way)  22.5 us
    all_to_all x1, blocking collectives, local(): lax.all_to_all(partial, 'examples', split_axis=0, concat_axis=0, tiled=True)  10.4 us
    pallas_call x1, Pallas kernels, first_chunk(): pl.pallas_call(functools.partial(first_body, pieces), grid=(1,), in_specs...  7.59 us
  transfers between devices with their start and end apart: 36, of which 10 were waited for; matrix products, arithmetic and copies ran while one was open for 0% of the time, Pallas kernels for 30%

profile of v9, /device:TPU:0, one launch (start us, length us, event | category | flops | bytes accessed | tf_op | source)
XLA Modules:
  0.0 139.3 jit_solution(11994788704194537288)
XLA Ops:
  1.3 2.2 %prepare.1 = (bf16[64,4096]{1,0:T(8,128)(2,1)S(1)}, bf16[64,4096]{1,0:T(8,128)(2,1)S(1)}, bf16[24,2048]{1,0:T(8,128)(2,1)S(1)}) custom-call(s32[1]{0:T(128)S(6)} %copy.69.lengths_ref, s32[1,16]{1,0:T(1,128)S(1)} %bitcast.22, bf16[128,4096]{1,0:T(8,128)(2,1)} %x_hbm.1, f32[1,4096]{1,0:T(1,128)} %bitcast.24, bf16[128,4096]{1,0:T(8,128)(2,1)} %grads_hbm.1, ...), custom_call_target="tpu_custom_call" | custom-call | flops 1000000 | bytes 100000 | tf_op jit(solution)/shard_map/prepare/pallas_call | solution.py:80
  3.5 3.1 %collective-permute-start = (bf16[64,4096]{1,0:T(8,128)(2,1)S(1)}, bf16[64,4096]{1,0:T(8,128)(2,1)S(1)}, u32[]{:S(2)}, u32[]{:S(2)}) collective-permute-start(bf16[64,4096]{1,0:T(8,128)(2,1)S(1)} %get-tuple-element.66.refs_0_), channel_id=1, source_target_pairs={{0,4},{1,5},{4,8},{5,9},{8,12},{9,13},{12,14},{13,15},{14,10},{15,... | collective-permute-start | bytes 1572872 | tf_op jit(solution)/shard_map/ppermute | solution.py:381
  6.6 3.0 %collective-permute-start.2 = (bf16[1,24,2048]{2,1,0:T(8,128)(2,1)S(1)}, bf16[1,24,2048]{2,1,0:T(8,128)(2,1)S(1)}, u32[]{:S(2)}, u32[]{:S(2)}) collective-permute-start(bf16[1,24,2048]{2,1,0:T(8,128)(2,1)S(1)} %bitcast.17), channel_id=1, source_target_pairs={{0,8},{1,9},{2,10},{3,11},{4,12},{5,13},{6,14},{7,15},{8,0},{9,1},... | collective-permute-start | bytes 294920 | tf_op jit(solution)/shard_map/ppermute | solution.py:381
  10.1 15.1 %collective-permute-done.2 = bf16[1,24,2048]{2,1,0:T(8,128)(2,1)S(1)} collective-permute-done((bf16[1,24,2048]{2,1,0:T(8,128)(2,1)S(1)}, bf16[1,24,2048]{2,1,0:T(8,128)(2,1)S(1)}, u32[]{:S(2)}, u32[]{:S(2)}) %collective-permute-start.2) | collective-permute-done | bytes 98336 | tf_op jit(solution)/shard_map/ppermute | solution.py:381
  25.2 2.0 %collective-permute-start.8 = (bf16[64,4096]{1,0:T(8,128)(2,1)S(1)}, bf16[64,4096]{1,0:T(8,128)(2,1)S(1)}, u32[]{:S(2)}, u32[]{:S(2)}) collective-permute-start(bf16[64,4096]{1,0:T(8,128)(2,1)S(1)} %get-tuple-element.67.refs_1_), channel_id=1, source_target_pairs={{4,0},{5,1},{8,4},{9,5},{12,8},{13,9},{14,12},{15,13},{10,14},{11,... | collective-permute-start | bytes 1572872 | tf_op jit(solution)/shard_map/ppermute | solution.py:381
  28.1 7.6 %first_chunk.1 = (f32[2176,64]{1,0:T(8,128)S(1)}, bf16[4096,1024]{1,0:T(8,128)(2,1)S(1)}, bf16[4096,768]{1,0:T(8,128)(2,1)S(1)}) custom-call(bf16[64,4096]{1,0:T(8,128)(2,1)S(1)} %get-tuple-element.66.refs_0_, bf16[64,4096]{1,0:T(8,128)(2,1)S(1)} %get-tuple-element.67.refs_1_, bf16[4096,896]{1,0:T(8,128)(2,1)} %refs_2_.1, bf16[4096,896]{1,0:T(8,128)(2,1)} %refs_3_.1, ...), custom_call_target="tpu_custom_call" | custom-call | flops 1000000 | bytes 100000 | tf_op jit(solution)/shard_map/first_chunk/pallas_call | solution.py:159
  36.4 4.2 %chunk.9 = (f32[2176,64]{1,0:T(8,128)S(1)}, bf16[4096,1024]{1,0:T(8,128)(2,1)S(1)}, bf16[4096,768]{1,0:T(8,128)(2,1)S(1)}) custom-call(bf16[64,4096]{1,0:T(8,128)(2,1)S(1)} %collective-permute-done.9.refs_0_, bf16[64,4096]{1,0:T(8,128)(2,1)S(1)} %collective-permute-done.10.refs_1_, ...), custom_call_target="tpu_custom_call", output_to_operand_aliasing={{0}: (7, {}), {1}: (4, {}), {2}: (5, {})} | custom-call | flops 1000000 | bytes 100000 | tf_op jit(solution)/shard_map/chunk/pallas_call | solution.py:194
  40.7 2.0 %collective-permute-start.3 = (bf16[64,4096]{1,0:T(8,128)(2,1)S(1)}, bf16[64,4096]{1,0:T(8,128)(2,1)S(1)}, u32[]{:S(2)}, u32[]{:S(2)}) collective-permute-start(bf16[64,4096]{1,0:T(8,128)(2,1)S(1)} %collective-permute-done.refs_2_), channel_id=1, source_target_pairs={{0,4},{1,5},{4,8},{5,9},{8,12},{9,13},{12,14},{13,15},{14,10},{15,... | collective-permute-start | bytes 1572872 | tf_op jit(solution)/shard_map/ppermute | solution.py:381
  43.1 4.2 %chunk.10 = (f32[2176,64]{1,0:T(8,128)S(1)}, bf16[4096,1024]{1,0:T(8,128)(2,1)S(1)}, bf16[4096,768]{1,0:T(8,128)(2,1)S(1)}) custom-call(bf16[64,4096]{1,0:T(8,128)(2,1)S(1)} %collective-permute-done.5.refs_0_, bf16[64,4096]{1,0:T(8,128)(2,1)S(1)} %collective-permute-done.6.refs_1_, ...), custom_call_target="tpu_custom_call", output_to_operand_aliasing={{0}: (7, {}), {1}: (4, {}), {2}: (5, {})} | custom-call | flops 1000000 | bytes 100000 | tf_op jit(solution)/shard_map/chunk/pallas_call | solution.py:194
  47.4 8.2 %collective-permute-done.3.refs_2_ = bf16[64,4096]{1,0:T(8,128)(2,1)S(1)} collective-permute-done((bf16[64,4096]{1,0:T(8,128)(2,1)S(1)}, bf16[64,4096]{1,0:T(8,128)(2,1)S(1)}, u32[]{:S(2)}, u32[]{:S(2)}) %collective-permute-start.3) | collective-permute-done | bytes 524320 | tf_op jit(solution)/shard_map/ppermute | solution.py:381
  56.3 6.8 %collective-permute-done.12 = bf16[4,24,2048]{2,1,0:T(8,128)(2,1)S(1)} collective-permute-done((bf16[4,24,2048]{2,1,0:T(8,128)(2,1)S(1)}, bf16[4,24,2048]{2,1,0:T(8,128)(2,1)S(1)}, u32[]{:S(2)}, u32[]{:S(2)}) %collective-permute-start.12) | collective-permute-done | bytes 393248 | tf_op jit(solution)/shard_map/ppermute | solution.py:381
  64.7 2.0 %collective-permute-start.18 = (bf16[64,4096]{1,0:T(8,128)(2,1)S(1)}, bf16[64,4096]{1,0:T(8,128)(2,1)S(1)}, u32[]{:S(2)}, u32[]{:S(2)}) collective-permute-start(bf16[64,4096]{1,0:T(8,128)(2,1)S(1)} %collective-permute-done.8.refs_3_), channel_id=1, source_target_pairs={{4,0},{5,1},{8,4},{9,5},{12,8},{13,9},{14,12},{15,13},{10,14},{11,... | collective-permute-start | bytes 1572872 | tf_op jit(solution)/shard_map/ppermute | solution.py:381
  67.3 12.0 %collective-permute-done.17.refs_2_ = bf16[64,4096]{1,0:T(8,128)(2,1)S(1)} collective-permute-done((bf16[64,4096]{1,0:T(8,128)(2,1)S(1)}, bf16[64,4096]{1,0:T(8,128)(2,1)S(1)}, u32[]{:S(2)}, u32[]{:S(2)}) %collective-permute-start.17) | collective-permute-done | bytes 524320 | tf_op jit(solution)/shard_map/ppermute | solution.py:381
  79.3 1.9 %collective-permute-start.14 = (bf16[64,4096]{1,0:T(8,128)(2,1)S(1)}, bf16[64,4096]{1,0:T(8,128)(2,1)S(1)}, u32[]{:S(2)}, u32[]{:S(2)}) collective-permute-start(bf16[64,4096]{1,0:T(8,128)(2,1)S(1)} %collective-permute-done.4.refs_3_), channel_id=1, source_target_pairs={{4,0},{5,1},{8,4},{9,5},{12,8},{13,9},{14,12},{15,13},{10,14},{11,... | collective-permute-start | bytes 1572872 | tf_op jit(solution)/shard_map/ppermute | solution.py:381
  81.3 4.2 %chunk.11 = (f32[2176,64]{1,0:T(8,128)S(1)}, bf16[4096,1024]{1,0:T(8,128)(2,1)S(1)}, bf16[4096,768]{1,0:T(8,128)(2,1)S(1)}) custom-call(bf16[64,4096]{1,0:T(8,128)(2,1)S(1)} %collective-permute-done.19.refs_0_, bf16[64,4096]{1,0:T(8,128)(2,1)S(1)} %collective-permute-done.20.refs_1_, ...), custom_call_target="tpu_custom_call", output_to_operand_aliasing={{0}: (7, {}), {1}: (4, {}), {2}: (5, {})} | custom-call | flops 1000000 | bytes 100000 | tf_op jit(solution)/shard_map/chunk/pallas_call | solution.py:194
  86.2 6.7 %collective-permute-done.13.refs_2_ = bf16[64,4096]{1,0:T(8,128)(2,1)S(1)} collective-permute-done((bf16[64,4096]{1,0:T(8,128)(2,1)S(1)}, bf16[64,4096]{1,0:T(8,128)(2,1)S(1)}, u32[]{:S(2)}, u32[]{:S(2)}) %collective-permute-start.13) | collective-permute-done | bytes 524320 | tf_op jit(solution)/shard_map/ppermute | solution.py:381
  94.9 4.2 %chunk.12 = (f32[2176,64]{1,0:T(8,128)S(1)}, bf16[4096,1024]{1,0:T(8,128)(2,1)S(1)}, bf16[4096,768]{1,0:T(8,128)(2,1)S(1)}) custom-call(bf16[64,4096]{1,0:T(8,128)(2,1)S(1)} %collective-permute-done.15.refs_0_, bf16[64,4096]{1,0:T(8,128)(2,1)S(1)} %collective-permute-done.16.refs_1_, ...), custom_call_target="tpu_custom_call", output_to_operand_aliasing={{0}: (7, {}), {1}: (4, {}), {2}: (5, {})} | custom-call | flops 1000000 | bytes 100000 | tf_op jit(solution)/shard_map/chunk/pallas_call | solution.py:194
  99.8 4.2 %chunk.13 = (f32[2176,64]{1,0:T(8,128)S(1)}, bf16[4096,1024]{1,0:T(8,128)(2,1)S(1)}, bf16[4096,768]{1,0:T(8,128)(2,1)S(1)}) custom-call(bf16[64,4096]{1,0:T(8,128)(2,1)S(1)} %collective-permute-done.25.refs_0_, bf16[64,4096]{1,0:T(8,128)(2,1)S(1)} %collective-permute-done.26.refs_1_, ...), custom_call_target="tpu_custom_call", output_to_operand_aliasing={{0}: (7, {}), {1}: (4, {}), {2}: (5, {})} | custom-call | flops 1000000 | bytes 100000 | tf_op jit(solution)/shard_map/chunk/pallas_call | solution.py:194
  108.5 4.2 %chunk.14 = (f32[2176,64]{1,0:T(8,128)S(1)}, bf16[4096,1024]{1,0:T(8,128)(2,1)S(1)}, bf16[4096,768]{1,0:T(8,128)(2,1)S(1)}) custom-call(bf16[64,4096]{1,0:T(8,128)(2,1)S(1)} %collective-permute-done.31.refs_0_, bf16[64,4096]{1,0:T(8,128)(2,1)S(1)} %collective-permute-done.32.refs_1_, ...), custom_call_target="tpu_custom_call", output_to_operand_aliasing={{0}: (7, {}), {1}: (4, {}), {2}: (5, {})} | custom-call | flops 1000000 | bytes 100000 | tf_op jit(solution)/shard_map/chunk/pallas_call | solution.py:194
  112.7 2.3 %chunk.15 = (f32[2176,64]{1,0:T(8,128)S(1)}, bf16[4096,1024]{1,0:T(8,128)(2,1)S(1)}, bf16[4096,768]{1,0:T(8,128)(2,1)S(1)}) custom-call(bf16[64,4096]{1,0:T(8,128)(2,1)S(1)} %collective-permute-done.29.refs_0_, bf16[64,4096]{1,0:T(8,128)(2,1)S(1)} %collective-permute-done.30.refs_1_, ...), custom_call_target="tpu_custom_call", output_to_operand_aliasing={{0}: (5, {}), {1}: (2, {}), {2}: (3, {})} | custom-call | flops 1000000 | bytes 100000 | tf_op jit(solution)/shard_map/chunk/pallas_call | solution.py:194
  116.1 4.2 %collective-permute-done.22.refs_0_ = bf16[64,4096]{1,0:T(8,128)(2,1)S(1)} collective-permute-done((bf16[64,4096]{1,0:T(8,128)(2,1)S(1)}, bf16[64,4096]{1,0:T(8,128)(2,1)S(1)}, u32[]{:S(2)}, u32[]{:S(2)}) %collective-permute-start.22) | collective-permute-done | bytes 524320 | tf_op jit(solution)/shard_map/ppermute | solution.py:381
  121.7 2.3 %chunk.16 = (f32[2176,64]{1,0:T(8,128)S(1)}, bf16[4096,1024]{1,0:T(8,128)(2,1)S(1)}, bf16[4096,768]{1,0:T(8,128)(2,1)S(1)}) custom-call(bf16[64,4096]{1,0:T(8,128)(2,1)S(1)} %collective-permute-done.22.refs_0_, bf16[64,4096]{1,0:T(8,128)(2,1)S(1)} %collective-permute-done.28.refs_1_, ...), custom_call_target="tpu_custom_call", output_to_operand_aliasing={{0}: (5, {}), {1}: (2, {}), {2}: (3, {})} | custom-call | flops 1000000 | bytes 100000 | tf_op jit(solution)/shard_map/chunk/pallas_call | solution.py:194
  124.1 2.3 %chunk.17 = (f32[2176,64]{1,0:T(8,128)S(1)}, bf16[4096,1024]{1,0:T(8,128)(2,1)S(1)}, bf16[4096,768]{1,0:T(8,128)(2,1)S(1)}) custom-call(bf16[64,4096]{1,0:T(8,128)(2,1)S(1)} %collective-permute-done.33.refs_0_, bf16[64,4096]{1,0:T(8,128)(2,1)S(1)} %collective-permute-done.34.refs_1_, ...), custom_call_target="tpu_custom_call", output_to_operand_aliasing={{0}: (5, {}), {1}: (2, {}), {2}: (3, {})} | custom-call | flops 1000000 | bytes 100000 | tf_op jit(solution)/shard_map/chunk/pallas_call | solution.py:194
  128.4 10.4 %all_to_all.9 = f32[16,1,256]{2,1,0:T(1,128)S(1)} all-to-all(f32[16,1,256]{2,1,0:T(1,128)S(1)} %copy.40), channel_id=1, replica_groups=mesh['groups'=2,'examples'=16] {'examples'}, dimensions={0} | all-to-all | bytes 32768 | tf_op jit(solution)/shard_map/all_to_all | solution.py:446
  (76 shorter events, 18.9 us)
Async XLA Ops:
  3.5 21.7 %collective-permute-start = (bf16[64,4096]{1,0:T(8,128)(2,1)S(1)}, bf16[64,4096]{1,0:T(8,128)(2,1)S(1)}, u32[]{:S(2)}, u32[]{:S(2)}) collective-permute-start(bf16[64,4096]{1,0:T(8,128)(2,1)S(1)} %get-tuple-element.66.refs_0_), channel_id=1, source_target_pairs={{0,4},{1,5},{4,8},{5,9},{8,12},{9,13},{12,14},{13,15},{14,10},{15,... | collective-permute-start | bytes 1572872 | tf_op jit(solution)/shard_map/ppermute | solution.py:381
  6.6 29.1 %collective-permute-start.1 = (bf16[64,4096]{1,0:T(8,128)(2,1)S(1)}, bf16[64,4096]{1,0:T(8,128)(2,1)S(1)}, u32[]{:S(2)}, u32[]{:S(2)}) collective-permute-start(bf16[64,4096]{1,0:T(8,128)(2,1)S(1)} %get-tuple-element.66.refs_0_), channel_id=1, source_target_pairs={{4,0},{5,1},{8,4},{9,5},{12,8},{13,9},{14,12},{15,13},{10,14},{11,... | collective-permute-start | bytes 1572872 | tf_op jit(solution)/shard_map/ppermute | solution.py:381
  6.6 18.6 %collective-permute-start.2 = (bf16[1,24,2048]{2,1,0:T(8,128)(2,1)S(1)}, bf16[1,24,2048]{2,1,0:T(8,128)(2,1)S(1)}, u32[]{:S(2)}, u32[]{:S(2)}) collective-permute-start(bf16[1,24,2048]{2,1,0:T(8,128)(2,1)S(1)} %bitcast.17), channel_id=1, source_target_pairs={{0,8},{1,9},{2,10},{3,11},{4,12},{5,13},{6,14},{7,15},{8,0},{9,1},... | collective-permute-start | bytes 294920 | tf_op jit(solution)/shard_map/ppermute | solution.py:381
  9.6 26.2 %collective-permute-start.10 = (bf16[64,4096]{1,0:T(8,128)(2,1)S(1)}, bf16[64,4096]{1,0:T(8,128)(2,1)S(1)}, u32[]{:S(2)}, u32[]{:S(2)}) collective-permute-start(bf16[64,4096]{1,0:T(8,128)(2,1)S(1)} %get-tuple-element.67.refs_1_), channel_id=1, source_target_pairs={{0,1},{1,0},{2,3},{3,2},{4,5},{5,4},{6,7},{7,6},{8,9},{9,8},{10,11... | collective-permute-start | bytes 1572872 | tf_op jit(solution)/shard_map/ppermute | solution.py:381
  9.6 26.3 %collective-permute-start.9 = (bf16[64,4096]{1,0:T(8,128)(2,1)S(1)}, bf16[64,4096]{1,0:T(8,128)(2,1)S(1)}, u32[]{:S(2)}, u32[]{:S(2)}) collective-permute-start(bf16[64,4096]{1,0:T(8,128)(2,1)S(1)} %get-tuple-element.66.refs_0_), channel_id=1, source_target_pairs={{0,1},{1,0},{2,3},{3,2},{4,5},{5,4},{6,7},{7,6},{8,9},{9,8},{10,11... | collective-permute-start | bytes 1572872 | tf_op jit(solution)/shard_map/ppermute | solution.py:381
  25.2 15.5 %collective-permute-start.7 = (bf16[64,4096]{1,0:T(8,128)(2,1)S(1)}, bf16[64,4096]{1,0:T(8,128)(2,1)S(1)}, u32[]{:S(2)}, u32[]{:S(2)}) collective-permute-start(bf16[64,4096]{1,0:T(8,128)(2,1)S(1)} %get-tuple-element.67.refs_1_), channel_id=1, source_target_pairs={{0,4},{1,5},{4,8},{5,9},{8,12},{9,13},{12,14},{13,15},{14,10},{15,... | collective-permute-start | bytes 1572872 | tf_op jit(solution)/shard_map/ppermute | solution.py:381
  25.2 17.5 %collective-permute-start.8 = (bf16[64,4096]{1,0:T(8,128)(2,1)S(1)}, bf16[64,4096]{1,0:T(8,128)(2,1)S(1)}, u32[]{:S(2)}, u32[]{:S(2)}) collective-permute-start(bf16[64,4096]{1,0:T(8,128)(2,1)S(1)} %get-tuple-element.67.refs_1_), channel_id=1, source_target_pairs={{4,0},{5,1},{8,4},{9,5},{12,8},{13,9},{14,12},{15,13},{10,14},{11,... | collective-permute-start | bytes 1572872 | tf_op jit(solution)/shard_map/ppermute | solution.py:381
  40.7 14.8 %collective-permute-start.3 = (bf16[64,4096]{1,0:T(8,128)(2,1)S(1)}, bf16[64,4096]{1,0:T(8,128)(2,1)S(1)}, u32[]{:S(2)}, u32[]{:S(2)}) collective-permute-start(bf16[64,4096]{1,0:T(8,128)(2,1)S(1)} %collective-permute-done.refs_2_), channel_id=1, source_target_pairs={{0,4},{1,5},{4,8},{5,9},{8,12},{9,13},{12,14},{13,15},{14,10},{15,... | collective-permute-start | bytes 1572872 | tf_op jit(solution)/shard_map/ppermute | solution.py:381
  42.7 13.6 %collective-permute-start.4 = (bf16[64,4096]{1,0:T(8,128)(2,1)S(1)}, bf16[64,4096]{1,0:T(8,128)(2,1)S(1)}, u32[]{:S(2)}, u32[]{:S(2)}) collective-permute-start(bf16[64,4096]{1,0:T(8,128)(2,1)S(1)} %collective-permute-done.1.refs_3_), channel_id=1, source_target_pairs={{4,0},{5,1},{8,4},{9,5},{12,8},{13,9},{14,12},{15,13},{10,14},{11,... | collective-permute-start | bytes 1572872 | tf_op jit(solution)/shard_map/ppermute | solution.py:381
  42.8 20.3 %collective-permute-start.12 = (bf16[4,24,2048]{2,1,0:T(8,128)(2,1)S(1)}, bf16[4,24,2048]{2,1,0:T(8,128)(2,1)S(1)}, u32[]{:S(2)}, u32[]{:S(2)}) collective-permute-start(bf16[4,24,2048]{2,1,0:T(8,128)(2,1)S(1)} %pad_maximum_fusion.1), channel_id=1, source_target_pairs={{0,2},{1,3},{2,0},{3,1},{4,6},{5,7},{6,4},{7,5},{8,10},{9,11},{10,... | collective-permute-start | bytes 1179656 | tf_op jit(solution)/shard_map/ppermute | solution.py:381
  43.1 23.7 %collective-permute-start.19 = (bf16[64,4096]{1,0:T(8,128)(2,1)S(1)}, bf16[64,4096]{1,0:T(8,128)(2,1)S(1)}, u32[]{:S(2)}, u32[]{:S(2)}) collective-permute-start(bf16[64,4096]{1,0:T(8,128)(2,1)S(1)} %collective-permute-done.7.refs_2_), channel_id=1, source_target_pairs={{0,1},{1,0},{2,3},{3,2},{4,5},{5,4},{6,7},{7,6},{8,9},{9,8},{10,11... | collective-permute-start | bytes 1572872 | tf_op jit(solution)/shard_map/ppermute | solution.py:381
  63.2 22.3 %collective-permute-start.21 = (bf16[8,24,2048]{2,1,0:T(8,128)(2,1)S(1)}, bf16[8,24,2048]{2,1,0:T(8,128)(2,1)S(1)}, u32[]{:S(2)}, u32[]{:S(2)}) collective-permute-start(bf16[8,24,2048]{2,1,0:T(8,128)(2,1)S(1)} %pad_maximum_fusion.mine_ref.refs_0_), channel_id=1, source_target_pairs={{16,0},{0,16},{17,1},{1,17},{18,2},{2,18},{19,3},{3,19},{20,4},{4,... | collective-permute-start | bytes 2359304 | tf_op jit(solution)/shard_map/ppermute | solution.py:430
  64.7 14.5 %collective-permute-start.17 = (bf16[64,4096]{1,0:T(8,128)(2,1)S(1)}, bf16[64,4096]{1,0:T(8,128)(2,1)S(1)}, u32[]{:S(2)}, u32[]{:S(2)}) collective-permute-start(bf16[64,4096]{1,0:T(8,128)(2,1)S(1)} %collective-permute-done.7.refs_2_), channel_id=1, source_target_pairs={{0,4},{1,5},{4,8},{5,9},{8,12},{9,13},{12,14},{13,15},{14,10},{15,... | collective-permute-start | bytes 1572872 | tf_op jit(solution)/shard_map/ppermute | solution.py:381
  64.7 14.6 %collective-permute-start.18 = (bf16[64,4096]{1,0:T(8,128)(2,1)S(1)}, bf16[64,4096]{1,0:T(8,128)(2,1)S(1)}, u32[]{:S(2)}, u32[]{:S(2)}) collective-permute-start(bf16[64,4096]{1,0:T(8,128)(2,1)S(1)} %collective-permute-done.8.refs_3_), channel_id=1, source_target_pairs={{4,0},{5,1},{8,4},{9,5},{12,8},{13,9},{14,12},{15,13},{10,14},{11,... | collective-permute-start | bytes 1572872 | tf_op jit(solution)/shard_map/ppermute | solution.py:381
  66.8 18.8 %collective-permute-start.15 = (bf16[64,4096]{1,0:T(8,128)(2,1)S(1)}, bf16[64,4096]{1,0:T(8,128)(2,1)S(1)}, u32[]{:S(2)}, u32[]{:S(2)}) collective-permute-start(bf16[64,4096]{1,0:T(8,128)(2,1)S(1)} %collective-permute-done.3.refs_2_), channel_id=1, source_target_pairs={{0,1},{1,0},{2,3},{3,2},{4,5},{5,4},{6,7},{7,6},{8,9},{9,8},{10,11... | collective-permute-start | bytes 1572872 | tf_op jit(solution)/shard_map/ppermute | solution.py:381
  66.9 19.2 %collective-permute-start.16 = (bf16[64,4096]{1,0:T(8,128)(2,1)S(1)}, bf16[64,4096]{1,0:T(8,128)(2,1)S(1)}, u32[]{:S(2)}, u32[]{:S(2)}) collective-permute-start(bf16[64,4096]{1,0:T(8,128)(2,1)S(1)} %collective-permute-done.4.refs_3_), channel_id=1, source_target_pairs={{0,1},{1,0},{2,3},{3,2},{4,5},{5,4},{6,7},{7,6},{8,9},{9,8},{10,11... | collective-permute-start | bytes 1572872 | tf_op jit(solution)/shard_map/ppermute | solution.py:381
  79.2 13.7 %collective-permute-start.13 = (bf16[64,4096]{1,0:T(8,128)(2,1)S(1)}, bf16[64,4096]{1,0:T(8,128)(2,1)S(1)}, u32[]{:S(2)}, u32[]{:S(2)}) collective-permute-start(bf16[64,4096]{1,0:T(8,128)(2,1)S(1)} %collective-permute-done.3.refs_2_), channel_id=1, source_target_pairs={{0,4},{1,5},{4,8},{5,9},{8,12},{9,13},{12,14},{13,15},{14,10},{15,... | collective-permute-start | bytes 1572872 | tf_op jit(solution)/shard_map/ppermute | solution.py:381
  79.3 13.8 %collective-permute-start.14 = (bf16[64,4096]{1,0:T(8,128)(2,1)S(1)}, bf16[64,4096]{1,0:T(8,128)(2,1)S(1)}, u32[]{:S(2)}, u32[]{:S(2)}) collective-permute-start(bf16[64,4096]{1,0:T(8,128)(2,1)S(1)} %collective-permute-done.4.refs_3_), channel_id=1, source_target_pairs={{4,0},{5,1},{8,4},{9,5},{12,8},{13,9},{14,12},{15,13},{10,14},{11,... | collective-permute-start | bytes 1572872 | tf_op jit(solution)/shard_map/ppermute | solution.py:381
  85.5 13.7 %collective-permute-start.25 = (bf16[64,4096]{1,0:T(8,128)(2,1)S(1)}, bf16[64,4096]{1,0:T(8,128)(2,1)S(1)}, u32[]{:S(2)}, u32[]{:S(2)}) collective-permute-start(bf16[64,4096]{1,0:T(8,128)(2,1)S(1)} %collective-permute-done.17.refs_2_), channel_id=1, source_target_pairs={{0,1},{1,0},{2,3},{3,2},{4,5},{5,4},{6,7},{7,6},{8,9},{9,8},{10,11... | collective-permute-start | bytes 1572872 | tf_op jit(solution)/shard_map/ppermute | solution.py:381
  85.6 18.4 %collective-permute-start.27 = (bf16[8,24,2048]{2,1,0:T(8,128)(2,1)S(1)}, bf16[8,24,2048]{2,1,0:T(8,128)(2,1)S(1)}, u32[]{:S(2)}, u32[]{:S(2)}) collective-permute-start(bf16[8,24,2048]{2,1,0:T(8,128)(2,1)S(1)} %pad_maximum_fusion.mine_ref.refs_0_), channel_id=1, source_target_pairs={{0,1},{1,0},{2,3},{3,2},{4,5},{5,4},{6,7},{7,6},{8,9},{9,8},{10,11... | collective-permute-start | bytes 2359304 | tf_op jit(solution)/shard_map/ppermute | solution.py:381
  86.1 13.2 %collective-permute-start.26 = (bf16[64,4096]{1,0:T(8,128)(2,1)S(1)}, bf16[64,4096]{1,0:T(8,128)(2,1)S(1)}, u32[]{:S(2)}, u32[]{:S(2)}) collective-permute-start(bf16[64,4096]{1,0:T(8,128)(2,1)S(1)} %collective-permute-done.18.refs_3_), channel_id=1, source_target_pairs={{0,1},{1,0},{2,3},{3,2},{4,5},{5,4},{6,7},{7,6},{8,9},{9,8},{10,11... | collective-permute-start | bytes 1572872 | tf_op jit(solution)/shard_map/ppermute | solution.py:381
  106.4 13.8 %collective-permute-start.22 = (bf16[64,4096]{1,0:T(8,128)(2,1)S(1)}, bf16[64,4096]{1,0:T(8,128)(2,1)S(1)}, u32[]{:S(2)}, u32[]{:S(2)}) collective-permute-start(bf16[64,4096]{1,0:T(8,128)(2,1)S(1)} %collective-permute-done.13.refs_2_), channel_id=1, source_target_pairs={{0,4},{1,5},{4,8},{5,9},{8,12},{9,13},{12,14},{13,15},{14,10},{15,... | collective-permute-start | bytes 1572872 | tf_op jit(solution)/shard_map/ppermute | solution.py:381
  107.7 13.6 %collective-permute-start.28 = (bf16[64,4096]{1,0:T(8,128)(2,1)S(1)}, bf16[64,4096]{1,0:T(8,128)(2,1)S(1)}, u32[]{:S(2)}, u32[]{:S(2)}) collective-permute-start(bf16[64,4096]{1,0:T(8,128)(2,1)S(1)} %collective-permute-done.24.refs_3_), channel_id=1, source_target_pairs={{4,0},{5,1},{8,4},{9,5},{12,8},{13,9},{14,12},{15,13},{10,14},{11,... | collective-permute-start | bytes 1572872 | tf_op jit(solution)/shard_map/ppermute | solution.py:381
  108.5 18.0 %collective-permute-start.35 = (bf16[8,24,2048]{2,1,0:T(8,128)(2,1)S(1)}, bf16[8,24,2048]{2,1,0:T(8,128)(2,1)S(1)}, u32[]{:S(2)}, u32[]{:S(2)}) collective-permute-start(bf16[8,24,2048]{2,1,0:T(8,128)(2,1)S(1)} %collective-permute-done.21.refs_1_), channel_id=1, source_target_pairs={{0,1},{1,0},{2,3},{3,2},{4,5},{5,4},{6,7},{7,6},{8,9},{9,8},{10,11... | collective-permute-start | bytes 2359304 | tf_op jit(solution)/shard_map/ppermute | solution.py:381
  (16 other events, 130.0 us)

commit v10 on v9

--- a/solution.py
+++ b/solution.py
@@ -22,8 +22,8 @@
 
 
 def prepare_body(lengths_ref, ids_ref, x_hbm, gain_hbm, grads_hbm, factor_hbm, queries_hbm, *refs):
-    a_ref, b_ref, out_ref, x_ref, gain_ref, grads_ref, factor_ref, queries_ref, sems = refs
-    half, span = a_ref.shape[0], x_ref.shape[0]
+    rows_ref, out_ref, x_ref, gain_ref, grads_ref, factor_ref, queries_ref, sems = refs
+    span = x_ref.shape[0]
     block = 32
     starts = range(0, span, block)
     x_copies = []
@@ -43,11 +43,7 @@
         for at in range(start, start + block, 16):
             x = x_ref[at : at + 16, :].astype(jnp.float32)
             scale = lax.rsqrt(jnp.mean(x * x, axis=-1, keepdims=True) + 1e-05)
-            rows = (x * scale * gain_ref[...]).astype(jnp.bfloat16)
-            if at < half:
-                a_ref[at : at + 16, :] = rows
-            else:
-                b_ref[at - half : at - half + 16, :] = rows
+            rows_ref[at : at + 16, :] = (x * scale * gain_ref[...]).astype(jnp.bfloat16)
     for copy in copies[1:]:
         copy.wait()
 
@@ -74,14 +70,16 @@
     width = depth // groups
     vmem = pl.BlockSpec(memory_space=pltpu.VMEM)
     hbm = pl.BlockSpec(memory_space=pltpu.HBM)
-    rows = jax.ShapeDtypeStruct((span // 2, depth), jnp.bfloat16)
     share = -(-(count + span * LANES // width) // 8) * 8
     operands = [x, gain, grads, factor, queries]
     return pl.pallas_call(
         prepare_body,
         in_specs=[pl.BlockSpec(memory_space=pltpu.SMEM), vmem] + [hbm] * len(operands),
-        out_specs=[vmem] * 3,
-        out_shape=[rows, rows, jax.ShapeDtypeStruct((share, width), queries.dtype)],
+        out_specs=[vmem] * 2,
+        out_shape=[
+            jax.ShapeDtypeStruct((span, depth), jnp.bfloat16),
+            jax.ShapeDtypeStruct((share, width), queries.dtype),
+        ],
         scratch_shapes=[pltpu.VMEM(o.shape, o.dtype) for o in operands]
         + [pltpu.SemaphoreType.DMA((span // 32 + len(operands) - 1,))],
         compiler_params=pltpu.CompilerParams(vmem_limit_bytes=12 * MIB),
@@ -91,9 +89,12 @@
 
 
 def gather_rows(x_refs, xn):
+    if len(x_refs) == 1:
+        return x_refs[0]
     rows = x_refs[0].shape[0]
     for k, ref in enumerate(x_refs):
         xn[k * rows : (k + 1) * rows, :] = ref[...]
+    return xn
 
 
 def gated(gate, up):
@@ -142,10 +143,9 @@
             copies.append(pltpu.make_async_copy(source, target, sems.at[k, p]))
     for copy in copies:
         copy.start()
-    gather_rows(x_refs, xn)
     for copy in copies:
         copy.wait()
-    out_ref[...] = project(xn, gate_ref, up_ref, f_ref)
+    out_ref[...] = project(gather_rows(x_refs, xn), gate_ref, up_ref, f_ref)
 
 
 def first_chunk(xs, gate_weight, up_weight, in_factor, index, tokens):
@@ -181,8 +181,7 @@
 
 def chunk_body(pieces, *refs):
     x_refs, (gate_ref, up_ref, f_ref, _, out_ref, _, _, xn) = refs[:pieces], refs[pieces:]
-    gather_rows(x_refs, xn)
-    out_ref[...] = project(xn, gate_ref, up_ref, f_ref)
+    out_ref[...] = project(gather_rows(x_refs, xn), gate_ref, up_ref, f_ref)
 
 
 def chunk(xs, weights, in_factor, left, index):
@@ -228,37 +227,37 @@
     flat[:, slot, :] = jnp.where(lane < order, even, odd)
 
 
-def sketch_body(places, first, half, count, table, left_ref, mine_ref, other_ref, *refs):
-    flat, twice = refs[-2:]
+def share_of(refs, at):
+    first, second = refs
+    count = first.shape[0]
+    inside = lax.rem(at, count)
+    return jnp.where(at < count, first[inside].astype(jnp.float32), second[inside].astype(jnp.float32))
+
+
+def sketch_body(places, half, count, table, left_ref, *refs):
+    share_refs, (flat, twice) = (refs[:2], refs[2:4]), refs[4:]
     me = lax.axis_index("examples")
     order = left_ref.shape[1]
-    rows = 2 * half * LANES // mine_ref.shape[2]
+    rows = 2 * half * LANES // refs[0].shape[2]
     total = table.shape[1] // 2
-    for r, at in enumerate(places, first):
-        ref = mine_ref if r % 2 == 0 else other_ref
-        masked = masked_of(ref[table[me, total + r], count : count + rows, :], 2 * half, order)
+    for r, at in enumerate(places):
+        masked = masked_of(share_of(share_refs[r % 2], table[me, total + r])[count : count + rows], 2 * half, order)
         write_flat(flat, r, one_sketch(left_ref, masked, at, half), twice)
 
 
-def sketches(places, first, half, count, table, left, mine, other, flat):
+def sketches(places, half, count, table, left, mine, other):
     order = left.shape[1]
     vmem = pl.BlockSpec(memory_space=pltpu.VMEM)
-    operands = [table, left, mine, other]
-    aliases = {}
-    if flat is not None:
-        aliases = {4: 0}
-        operands.append(flat)
     return pl.pallas_call(
-        functools.partial(sketch_body, places, first, half, count),
-        in_specs=[pl.BlockSpec(memory_space=pltpu.SMEM)] + [vmem] * (len(operands) - 1),
+        functools.partial(sketch_body, places, half, count),
+        in_specs=[pl.BlockSpec(memory_space=pltpu.SMEM)] + [vmem] * 5,
         out_specs=vmem,
         out_shape=jax.ShapeDtypeStruct((order // 2, table.shape[0], 2 * order), jnp.float32),
         scratch_shapes=[pltpu.VMEM((order, 2 * order), jnp.float32)],
-        input_output_aliases=aliases,
         compiler_params=pltpu.CompilerParams(vmem_limit_bytes=12 * MIB),
         cost_estimate=SMALL,
         name="sketches",
-    )(*operands)
+    )(table, left, *mine, *other)
 
 
 def members_of(share_ref, count, order):
@@ -276,50 +275,51 @@
 
 
 def finish_body(places, half, groups, count, table, left_ref, flat_ref, *refs):
-    share_refs, (out_ref, twice, flat) = (refs[:groups], refs[groups : 2 * groups]), refs[2 * groups :]
-    chips, _, width = share_refs[0][0].shape
+    share_refs, (out_ref, twice, flat) = refs[:-3], refs[-3:]
+    kinds = 4
+    chips, _, width = share_refs[0].shape
     order = left_ref.shape[1]
     rows = 2 * half * LANES // width
     me, group = lax.axis_index("examples"), lax.axis_index("groups")
     examples = table.shape[0]
     flat[...] = flat_ref[...]
-    members = [members_of(refs[0], count, order) for refs in share_refs]
     first = examples - len(places)
     for r, at in enumerate(places, first):
-        masked = masked_of(share_refs[r % 2][0][table[me, examples + r], count : count + rows, :], 2 * half, order)
+        side = share_of(share_refs[2 * (r % 2) : 2 * (r % 2) + 2], table[me, examples + r])
+        masked = masked_of(side[count : count + rows], 2 * half, order)
         write_flat(flat, r, one_sketch(left_ref, masked, at, half), twice)
-    scores = [0.0, 0.0]
+    scores = [0.0] * kinds
     for r in range(groups):
         block = lax.rem(group + r, groups) * (width // LANES)
         sketch = jnp.concatenate([flat[block + c] for c in range(width // LANES)], axis=1).astype(jnp.bfloat16)
-        for kind in range(2):
-            queries = share_refs[kind][r][:, :count, :].reshape(chips * count, width)
+        for kind in range(kinds):
+            queries = share_refs[kinds * r + kind][:, :count, :].reshape(chips * count, width)
             scores[kind] += lax.dot_general(sketch, queries, NT, preferred_element_type=jnp.float32)
     total = 0.0
-    for kind in range(2):
+    for kind in range(kinds):
+        members = members_of(share_refs[kind], count, order)
         rest = scores[kind]
         for _ in range(3):
             part = rest.astype(jnp.bfloat16)
             rest = rest - part.astype(jnp.float32)
-            total += lax.dot_general(part, members[kind], NT, preferred_element_type=jnp.float32)
+            total += lax.dot_general(part, members, NT, preferred_element_type=jnp.float32)
     for r in range(examples):
         out_ref[pl.ds(table[me, r], 1), :] = total[r : r + 1, :]
 
 
-def finish(places, half, count, table, left, flat, mine, other):
+def finish(places, half, groups, count, table, left, flat, shares):
     order = left.shape[1]
-    groups = len(mine)
     vmem = pl.BlockSpec(memory_space=pltpu.VMEM)
     return pl.pallas_call(
         functools.partial(finish_body, places, half, groups, count),
-        in_specs=[pl.BlockSpec(memory_space=pltpu.SMEM)] + [vmem] * (2 + 2 * groups),
+        in_specs=[pl.BlockSpec(memory_space=pltpu.SMEM)] + [vmem] * (2 + len(shares)),
         out_specs=vmem,
         out_shape=jax.ShapeDtypeStruct((table.shape[0], NVAL), jnp.float32),
         scratch_shapes=[pltpu.VMEM((order, 2 * order), jnp.float32), pltpu.VMEM(flat.shape, jnp.float32)],
         compiler_params=pltpu.CompilerParams(vmem_limit_bytes=12 * MIB),
         cost_estimate=SMALL,
         name="finish",
-    )(table, left, flat, *mine, *other)
+    )(table, left, flat, *shares)
 
 
 def arrivals(ring, devices):
@@ -332,13 +332,13 @@
                 chip = ring[(ring.index(me // 2) + sign * distance) % chips]
                 table[me] += [2 * chip + me % 2, 2 * chip + 1 - me % 2]
             if distance == 0:
-                halves = [(0, 0), (0, 1)]
+                spots += [[0, 1], [2, 3]]
             elif distance == far:
-                halves = [(chips - 1, 0), (chips - 1, 1)]
+                at = 4 * (2 * far - 1)
+                spots += [[at, at + 1], [at + 2, at + 3]]
             else:
-                halves = [(2 * distance - 1, piece), (2 * distance, piece)]
-            spots.append([4 * k + 2 + p for k, p in halves])
-            spots.append([4 * k + 4 + p for k, p in halves])
+                at = 4 * (2 * distance - 1) + 2 * piece
+                spots += [[at, at + 1], [at + 4, at + 5]]
     bits = chips.bit_length() - 1
     for me, row in enumerate(table):
         apart = [(example // 2) ^ (me // 2) for example in row]
@@ -375,13 +375,20 @@
         gate_weight = jnp.pad(gate_weight, ((0, 0), (0, short)))
         up_weight = jnp.pad(up_weight, ((0, 0), (0, short)))
         in_factor = jnp.pad(in_factor, ((0, short), (0, 0)))
-    tokens = 2 * span * chips + span
+    far = chips // 2
+    tokens = devices * span
+    table, spots = arrivals(ring, devices)
+    table = jnp.array(table, jnp.int32)
+    nq = queries.shape[0]
 
     def send(x, way):
         return lax.ppermute(x, "examples", way)
 
-    nq = queries.shape[0]
-    x_a, x_b, side = prepare(
+    def across(x):
+        ways = [[((g + r) % groups, g) for g in range(groups)] for r in range(1, groups)]
+        return [lax.ppermute(x, "groups", way) for way in ways]
+
+    rows, side = prepare(
         layer_inputs,
         norm_gain[None, :],
         example_lengths,
@@ -391,60 +398,55 @@
         queries,
         groups,
     )
+
     distances = [chips >> b for b in range(1, chips.bit_length())]
+    stages = len(distances)
     apart = [[(d, 2 * ((d // 2) ^ distance) + d % 2) for d in range(devices)] for distance in distances]
+
+    coming = (send(rows, forward), send(rows, backward))
+    swapped = send(rows, other_core)
     side = side[None]
     pending = [send(side, apart[0])]
-    coming = {
-        1: (send(x_a, forward), send(x_a, backward)),
-        2: (send(x_b, forward), send(x_b, backward)),
-    }
-    swapped = tuple(send(x, other_core) for x in (x_a, x_b))
-    left, weights = first_chunk((x_a, x_b), gate_weight, up_weight, in_factor.T, 1, tokens)
-
-    table, spots = arrivals(ring, devices)
-    table = jnp.array(table, jnp.int32)
-
-    for k in range(1, chips):
-        own_1, own_2, left, *pending = lax.optimization_barrier((*coming.pop(k), left, *pending))
-        own = (own_1, own_2)
-        if k + 2 < chips - 1:
-            coming[k + 2] = (send(own_1, forward), send(own_2, backward))
-        elif k + 2 == chips - 1:
-            opposite = send(own_1, forward)
-        elif k + 1 == chips - 1:
-            coming[chips - 1] = (opposite, send(own_2, backward))
-        before, swapped = swapped, tuple(send(x, other_core) for x in own)
-        if k < chips - 1:
-            left, weights = chunk(before + own, weights, in_factor.T, left, k)
-        if k <= len(distances):
+    left, weights = first_chunk((rows,), gate_weight, up_weight, in_factor.T, 0, tokens)
+    left, weights = chunk((swapped,), weights, in_factor.T, left, 1)
+    first, second = [], []
+    for r in range(1, far + 1):
+        own_f, own_b, left, *pending = lax.optimization_barrier((*coming, left, *pending))
+        if r < far - 1:
+            coming = (send(own_f, forward), send(own_b, backward))
+        elif r == far - 1:
+            coming = (send(own_f[:half], forward), send(own_b[half:], backward))
+        swapped = (send(own_f, other_core), send(own_b, other_core))
+        if r < stages:
             side = jnp.concatenate([side, *pending], axis=0)
+            pending = [send(side, apart[r])]
+            if r == stages - 1:
+                first = [side, send(side, other_core)]
+                pending += across(side)
+        elif r == stages:
+            side, *others = pending
+            second = [side, send(side, other_core)]
+            for x in others:
+                first += [x, send(x, other_core)]
+            pending = across(side)
+        elif r == stages + 1:
+            for x in pending:
+                second += [x, send(x, other_core)]
             pending = []
-        if k < len(distances):
-            pending = [send(side, apart[k])]
-        if k == len(distances):
-            other = [send(side, other_core)]
-            mine = [side]
-            for r in range(1, groups):
-                way = [((g + r) % groups, g) for g in range(groups)]
-                pending.append(lax.ppermute(side, "groups", way))
-        if k == chips - 3:
-            mine += pending
-            other += [send(x, other_core) for x in pending]
-            pending = []
-            ready = devices - 6
-            flat = sketches(spots[:ready], 0, half, nq, table, left, mine[0], other[0], None)
+        if r < far:
+            left, weights = chunk((own_f, own_b), weights, in_factor.T, left, 2 * r - 1)
+            left, weights = chunk(swapped, weights, in_factor.T, left, 2 * r)
+        else:
+            left, weights = chunk((own_f, own_b), weights, in_factor.T, left, 2 * (2 * far - 1))
+            left, weights = chunk(swapped, weights, in_factor.T, left, 2 * (2 * far - 1) + 1)
+        if r == far - 1:
+            flat = sketches(spots[:-2], half, nq, table, left, (first[0], second[0]), (first[1], second[1]))
             flat, left = lax.optimization_barrier((flat, left))
-        if k == chips - 2:
-            left, weights = chunk(swapped, weights, in_factor.T, left, 2 * k + 2)
-            flat = sketches(spots[ready:-2], ready, half, nq, table, left, mine[0], other[0], flat)
-            flat, left = lax.optimization_barrier((flat, left))
-    left, weights = chunk(own, weights, in_factor.T, left, 2 * chips - 1)
-    left, weights = chunk(swapped, weights, in_factor.T, left, 2 * chips)
-
-    partial = finish(spots[-2:], half, nq, table, left, flat, mine, other)
-    shares = lax.all_to_all(partial, "examples", split_axis=0, concat_axis=0, tiled=True)
-    return jnp.sum(shares, axis=0, keepdims=True)
+
+    shares = [x for pair in zip(first, second) for x in pair]
+    partial = finish(spots[-2:], half, groups, nq, table, left, flat, shares)
+    parts = lax.all_to_all(partial, "examples", split_axis=0, concat_axis=0, tiled=True)
+    return jnp.sum(parts, axis=0, keepdims=True)
 
 
 def solution(mesh):

time: 140 us -> 137 us (0.979)
  starting transfers between devices: 24.1 us -> 18.8 us
  Pallas kernels: 46.2 us -> 47.8 us
    ppermute x35 -> x24, starting transfers between devices: 22.5 us -> 15.8 us  [send(): return lax.ppermute(x, 'examples', way)]
    pallas_call x9, Pallas kernels: 32.4 us -> 34.3 us  [chunk(): pl.pallas_call(functools.partial(chunk_body, pieces), grid=(1,), in_specs...]
    ppermute x1 -> x2, starting transfers between devices: 1.55 us -> 2.98 us  [across(): return [lax.ppermute(x, 'groups', way) for way in ways]]
    ppermute x35 -> x24, waiting for transfers between devices: 55.4 us -> 56.3 us  [send(): return lax.ppermute(x, 'examples', way)]
  transfers between devices with their start and end apart: 36 -> 26, of which waited for: 10 -> 4; matrix products, arithmetic and copies ran while one was open for 0% -> 0% of each run, Pallas kernels for 30% -> 32%
where the time goes in v10:
time: 137 us; the launch traced here: 136 us
  waiting for transfers between devices  56.3 us (41%)
  Pallas kernels  47.8 us (35%)
  starting transfers between devices  18.8 us (14%)
  blocking collectives  10 us (7%)
  local copies, waits for them, and re-layouts  1.65 us (1%)
    ppermute x24, waiting for transfers between devices, send(): return lax.ppermute(x, 'examples', way)  56.3 us
    pallas_call x9, Pallas kernels, chunk(): pl.pallas_call(functools.partial(chunk_body, pieces), grid=(1,), in_specs...  34.3 us
    ppermute x24, starting transfers between devices, send(): return lax.ppermute(x, 'examples', way)  15.8 us
    all_to_all x1, blocking collectives, local(): lax.all_to_all(partial, 'examples', split_axis=0, concat_axis=0, tiled=True)  10 us
    pallas_call x1, Pallas kernels, first_chunk(): pl.pallas_call(functools.partial(first_body, pieces), grid=(1,), in_specs...  7.76 us
    ppermute x2, starting transfers between devices, across(): return [lax.ppermute(x, 'groups', way) for way in ways]  2.98 us
  transfers between devices with their start and end apart: 26, of which 4 were waited for; matrix products, arithmetic and copies ran while one was open for 0% of the time, Pallas kernels for 32%

profile of v10, /device:TPU:0, one launch (start us, length us, event | category | flops | bytes accessed | tf_op | source)
XLA Modules:
  0.0 136.3 jit_solution(10766065556051171729)
XLA Ops:
  1.3 2.2 %prepare.1 = (bf16[128,4096]{1,0:T(8,128)(2,1)S(1)}, bf16[24,2048]{1,0:T(8,128)(2,1)S(1)}) custom-call(s32[1]{0:T(128)S(6)} %copy.67.lengths_ref, s32[1,16]{1,0:T(1,128)S(1)} %bitcast.21, bf16[128,4096]{1,0:T(8,128)(2,1)} %x_hbm.1, f32[1,4096]{1,0:T(1,128)} %bitcast.23, bf16[128,4096]{1,0:T(8,128)(2,1)} %grads_hbm.1, bf16[64,4096]{1,0:T(8,128)(2,1)} %bitcast.22, ...), custom_call_target="tpu_custom_call" | custom-call | flops 1000000 | bytes 100000 | tf_op jit(solution)/shard_map/prepare/pallas_call | solution.py:75
  4.0 2.6 %collective-permute-start = (bf16[128,4096]{1,0:T(8,128)(2,1)S(1)}, bf16[128,4096]{1,0:T(8,128)(2,1)S(1)}, u32[]{:S(2)}, u32[]{:S(2)}) collective-permute-start(bf16[128,4096]{1,0:T(8,128)(2,1)S(1)} %get-tuple-element.54.refs_0_), channel_id=1, source_target_pairs={{0,4},{1,5},{4,8},{5,9},{8,12},{9,13},{12,14},{13,15},{14,10},{15,... | collective-permute-start | bytes 3145736 | tf_op jit(solution)/shard_map/ppermute | solution.py:385
  6.7 3.0 %collective-permute-start.3 = (bf16[1,24,2048]{2,1,0:T(8,128)(2,1)S(1)}, bf16[1,24,2048]{2,1,0:T(8,128)(2,1)S(1)}, u32[]{:S(2)}, u32[]{:S(2)}) collective-permute-start(bf16[1,24,2048]{2,1,0:T(8,128)(2,1)S(1)} %bitcast.17), channel_id=1, source_target_pairs={{0,8},{1,9},{2,10},{3,11},{4,12},{5,13},{6,14},{7,15},{8,0},{9,1},... | collective-permute-start | bytes 294920 | tf_op jit(solution)/shard_map/ppermute | solution.py:385
  10.6 7.8 %first_chunk.1 = (f32[2048,64]{1,0:T(8,128)S(1)}, bf16[4096,1024]{1,0:T(8,128)(2,1)S(1)}, bf16[4096,768]{1,0:T(8,128)(2,1)S(1)}) custom-call(bf16[128,4096]{1,0:T(8,128)(2,1)S(1)} %get-tuple-element.54.refs_0_, bf16[4096,896]{1,0:T(8,128)(2,1)} %refs_1_.1, bf16[4096,896]{1,0:T(8,128)(2,1)} %refs_2_.1, bf16[64,896]{1,0:T(8,128)(2,1)S(1)} %bitcast.7), custom_call_target="tpu_custom_call" | custom-call | flops 1000000 | bytes 100000 | tf_op jit(solution)/shard_map/first_chunk/pallas_call | solution.py:159
  18.4 2.5 %chunk.9 = (f32[2048,64]{1,0:T(8,128)S(1)}, bf16[4096,1024]{1,0:T(8,128)(2,1)S(1)}, bf16[4096,768]{1,0:T(8,128)(2,1)S(1)}) custom-call(bf16[128,4096]{1,0:T(8,128)(2,1)S(1)} %collective-permute-done.2.refs_0_, bf16[4096,1024]{1,0:T(8,128)(2,1)S(1)} %get-tuple-element.55.refs_1_, ...), custom_call_target="tpu_custom_call", output_to_operand_aliasing={{0}: (4, {}), {1}: (1, {}), {2}: (2, {})} | custom-call | flops 1000000 | bytes 100000 | tf_op jit(solution)/shard_map/chunk/pallas_call | solution.py:193
  20.9 16.3 %collective-permute-done.3 = bf16[1,24,2048]{2,1,0:T(8,128)(2,1)S(1)} collective-permute-done((bf16[1,24,2048]{2,1,0:T(8,128)(2,1)S(1)}, bf16[1,24,2048]{2,1,0:T(8,128)(2,1)S(1)}, u32[]{:S(2)}, u32[]{:S(2)}) %collective-permute-start.3) | collective-permute-done | bytes 98336 | tf_op jit(solution)/shard_map/ppermute | solution.py:385
  37.6 2.0 %collective-permute-start.5 = (bf16[128,4096]{1,0:T(8,128)(2,1)S(1)}, bf16[128,4096]{1,0:T(8,128)(2,1)S(1)}, u32[]{:S(2)}, u32[]{:S(2)}) collective-permute-start(bf16[128,4096]{1,0:T(8,128)(2,1)S(1)} %collective-permute-done.1.refs_1_), channel_id=1, source_target_pairs={{4,0},{5,1},{8,4},{9,5},{12,8},{13,9},{14,12},{15,13},{10,14},{11,... | collective-permute-start | bytes 3145736 | tf_op jit(solution)/shard_map/ppermute | solution.py:385
  39.8 4.5 %chunk.10 = (f32[2048,64]{1,0:T(8,128)S(1)}, bf16[4096,1024]{1,0:T(8,128)(2,1)S(1)}, bf16[4096,768]{1,0:T(8,128)(2,1)S(1)}) custom-call(bf16[128,4096]{1,0:T(8,128)(2,1)S(1)} %collective-permute-done.refs_0_, bf16[128,4096]{1,0:T(8,128)(2,1)S(1)} %collective-permute-done.1.refs_1_, ...), custom_call_target="tpu_custom_call", output_to_operand_aliasing={{0}: (5, {}), {1}: (2, {}), {2}: (3, {})} | custom-call | flops 1000000 | bytes 100000 | tf_op jit(solution)/shard_map/chunk/pallas_call | solution.py:193
  44.3 4.5 %chunk.11 = (f32[2048,64]{1,0:T(8,128)S(1)}, bf16[4096,1024]{1,0:T(8,128)(2,1)S(1)}, bf16[4096,768]{1,0:T(8,128)(2,1)S(1)}) custom-call(bf16[128,4096]{1,0:T(8,128)(2,1)S(1)} %collective-permute-done.6.refs_0_, bf16[128,4096]{1,0:T(8,128)(2,1)S(1)} %collective-permute-done.7.refs_1_, ...), custom_call_target="tpu_custom_call", output_to_operand_aliasing={{0}: (5, {}), {1}: (2, {}), {2}: (3, {})} | custom-call | flops 1000000 | bytes 100000 | tf_op jit(solution)/shard_map/chunk/pallas_call | solution.py:193
  48.7 18.3 %collective-permute-done.8 = bf16[2,24,2048]{2,1,0:T(8,128)(2,1)S(1)} collective-permute-done((bf16[2,24,2048]{2,1,0:T(8,128)(2,1)S(1)}, bf16[2,24,2048]{2,1,0:T(8,128)(2,1)S(1)}, u32[]{:S(2)}, u32[]{:S(2)}) %collective-permute-start.8) | collective-permute-done | bytes 196640 | tf_op jit(solution)/shard_map/ppermute | solution.py:385
  67.7 1.8 %collective-permute-start.9 = (bf16[128,4096]{1,0:T(8,128)(2,1)S(1)}, bf16[128,4096]{1,0:T(8,128)(2,1)S(1)}, u32[]{:S(2)}, u32[]{:S(2)}) collective-permute-start(bf16[128,4096]{1,0:T(8,128)(2,1)S(1)} %collective-permute-done.4.refs_0_), channel_id=1, source_target_pairs={{0,4},{1,5},{4,8},{5,9},{8,12},{9,13},{12,14},{13,15},{14,10},{15,... | collective-permute-start | bytes 3145736 | tf_op jit(solution)/shard_map/ppermute | solution.py:385
  69.9 1.5 %collective-permute-start.14 = (bf16[4,24,2048]{2,1,0:T(8,128)(2,1)S(1)}, bf16[4,24,2048]{2,1,0:T(8,128)(2,1)S(1)}, u32[]{:S(2)}, u32[]{:S(2)}) collective-permute-start(bf16[4,24,2048]{2,1,0:T(8,128)(2,1)S(1)} %pad_maximum_fusion.refs_0_), channel_id=1, source_target_pairs={{16,0},{0,16},{17,1},{1,17},{18,2},{2,18},{19,3},{3,19},{20,4},{4,... | collective-permute-start | bytes 1179656 | tf_op jit(solution)/shard_map/ppermute | solution.py:389
  71.4 4.5 %chunk.12 = (f32[2048,64]{1,0:T(8,128)S(1)}, bf16[4096,1024]{1,0:T(8,128)(2,1)S(1)}, bf16[4096,768]{1,0:T(8,128)(2,1)S(1)}) custom-call(bf16[128,4096]{1,0:T(8,128)(2,1)S(1)} %collective-permute-done.4.refs_0_, bf16[128,4096]{1,0:T(8,128)(2,1)S(1)} %collective-permute-done.5.refs_1_, ...), custom_call_target="tpu_custom_call", output_to_operand_aliasing={{0}: (5, {}), {1}: (2, {}), {2}: (3, {})} | custom-call | flops 1000000 | bytes 100000 | tf_op jit(solution)/shard_map/chunk/pallas_call | solution.py:193
  75.9 4.5 %chunk.13 = (f32[2048,64]{1,0:T(8,128)S(1)}, bf16[4096,1024]{1,0:T(8,128)(2,1)S(1)}, bf16[4096,768]{1,0:T(8,128)(2,1)S(1)}) custom-call(bf16[128,4096]{1,0:T(8,128)(2,1)S(1)} %collective-permute-done.11.refs_0_, bf16[128,4096]{1,0:T(8,128)(2,1)S(1)} %collective-permute-done.12.refs_1_, ...), custom_call_target="tpu_custom_call", output_to_operand_aliasing={{0}: (5, {}), {1}: (2, {}), {2}: (3, {})} | custom-call | flops 1000000 | bytes 100000 | tf_op jit(solution)/shard_map/chunk/pallas_call | solution.py:193
  80.3 20.8 %collective-permute-done.13.refs_1_ = bf16[4,24,2048]{2,1,0:T(8,128)(2,1)S(1)} collective-permute-done((bf16[4,24,2048]{2,1,0:T(8,128)(2,1)S(1)}, bf16[4,24,2048]{2,1,0:T(8,128)(2,1)S(1)}, u32[]{:S(2)}, u32[]{:S(2)}) %collective-permute-start.13) | collective-permute-done | bytes 393248 | tf_op jit(solution)/shard_map/ppermute | solution.py:385
  101.8 2.0 %collective-permute-start.16 = (bf16[64,4096]{1,0:T(8,128)(2,1)S(1)}, bf16[64,4096]{1,0:T(8,128)(2,1)S(1)}, u32[]{:S(2)}, u32[]{:S(2)}) collective-permute-start(bf16[64,4096]{1,0:T(8,128)(2,1)S(1)} %slice.7), channel_id=1, source_target_pairs={{4,0},{5,1},{8,4},{9,5},{12,8},{13,9},{14,12},{15,13},{10,14},{11,... | collective-permute-start | bytes 1572872 | tf_op jit(solution)/shard_map/ppermute | solution.py:385
  105.3 1.5 %collective-permute-start.21 = (bf16[4,24,2048]{2,1,0:T(8,128)(2,1)S(1)}, bf16[4,24,2048]{2,1,0:T(8,128)(2,1)S(1)}, u32[]{:S(2)}, u32[]{:S(2)}) collective-permute-start(bf16[4,24,2048]{2,1,0:T(8,128)(2,1)S(1)} %collective-permute-done.13.refs_1_), channel_id=1, source_target_pairs={{16,0},{0,16},{17,1},{1,17},{18,2},{2,18},{19,3},{3,19},{20,4},{4,... | collective-permute-start | bytes 1179656 | tf_op jit(solution)/shard_map/ppermute | solution.py:389
  106.8 4.5 %chunk.14 = (f32[2048,64]{1,0:T(8,128)S(1)}, bf16[4096,1024]{1,0:T(8,128)(2,1)S(1)}, bf16[4096,768]{1,0:T(8,128)(2,1)S(1)}) custom-call(bf16[128,4096]{1,0:T(8,128)(2,1)S(1)} %collective-permute-done.9.refs_0_, bf16[128,4096]{1,0:T(8,128)(2,1)S(1)} %collective-permute-done.10.refs_1_, ...), custom_call_target="tpu_custom_call", output_to_operand_aliasing={{0}: (5, {}), {1}: (2, {}), {2}: (3, {})} | custom-call | flops 1000000 | bytes 100000 | tf_op jit(solution)/shard_map/chunk/pallas_call | solution.py:193
  111.3 4.5 %chunk.15 = (f32[2048,64]{1,0:T(8,128)S(1)}, bf16[4096,1024]{1,0:T(8,128)(2,1)S(1)}, bf16[4096,768]{1,0:T(8,128)(2,1)S(1)}) custom-call(bf16[128,4096]{1,0:T(8,128)(2,1)S(1)} %collective-permute-done.17.refs_0_, bf16[128,4096]{1,0:T(8,128)(2,1)S(1)} %collective-permute-done.18.refs_1_, ...), custom_call_target="tpu_custom_call", output_to_operand_aliasing={{0}: (5, {}), {1}: (2, {}), {2}: (3, {})} | custom-call | flops 1000000 | bytes 100000 | tf_op jit(solution)/shard_map/chunk/pallas_call | solution.py:193
  115.8 1.2 sketches.1.flat_ref
  118.2 2.5 %chunk.16 = (f32[2048,64]{1,0:T(8,128)S(1)}, bf16[4096,1024]{1,0:T(8,128)(2,1)S(1)}, bf16[4096,768]{1,0:T(8,128)(2,1)S(1)}) custom-call(bf16[64,4096]{1,0:T(8,128)(2,1)S(1)} %collective-permute-done.15.refs_0_, bf16[64,4096]{1,0:T(8,128)(2,1)S(1)} %collective-permute-done.16.refs_1_, ...), custom_call_target="tpu_custom_call", output_to_operand_aliasing={{0}: (5, {}), {1}: (2, {}), {2}: (3, {})} | custom-call | flops 1000000 | bytes 100000 | tf_op jit(solution)/shard_map/chunk/pallas_call | solution.py:193
  120.7 2.5 %chunk.17 = (f32[2048,64]{1,0:T(8,128)S(1)}, bf16[4096,1024]{1,0:T(8,128)(2,1)S(1)}, bf16[4096,768]{1,0:T(8,128)(2,1)S(1)}) custom-call(bf16[64,4096]{1,0:T(8,128)(2,1)S(1)} %collective-permute-done.22.refs_0_, bf16[64,4096]{1,0:T(8,128)(2,1)S(1)} %collective-permute-done.23.refs_1_, ...), custom_call_target="tpu_custom_call", output_to_operand_aliasing={{0}: (5, {}), {1}: (2, {}), {2}: (3, {})} | custom-call | flops 1000000 | bytes 100000 | tf_op jit(solution)/shard_map/chunk/pallas_call | solution.py:193
  123.2 2.4 %finish.1 = f32[16,256]{1,0:T(8,128)S(1)} custom-call(s32[16,32]{1,0:T(8,128)S(1)} %copy-done.2, f32[2048,64]{1,0:T(8,128)S(1)} %get-tuple-element.99.left_ref, f32[32,16,128]{2,1,0:T(8,128)S(1)} %sketches.1.flat_ref, bf16[4,24,2048]{2,1,0:T(8,128)(2,1)S(1)} %pad_maximum_fusion.refs_0_, bf16[4,24,2048]{2,1,0:T(8,128)(2,1)S(1)} %collective-permute-done.13.refs_1_, ...), custom_call_target="tpu_custom_call" | custom-call | flops 1000000 | bytes 100000 | tf_op jit(solution)/shard_map/finish/pallas_call | solution.py:313
  125.6 10.0 %all_to_all.9 = f32[16,1,256]{2,1,0:T(1,128)S(1)} all-to-all(f32[16,1,256]{2,1,0:T(1,128)S(1)} %copy.39), channel_id=1, replica_groups=mesh['groups'=2,'examples'=16] {'examples'}, dimensions={0} | all-to-all | bytes 32768 | tf_op jit(solution)/shard_map/all_to_all | solution.py:448
  (56 shorter events, 7.7 us)
Async XLA Ops:
  3.5 14.9 %collective-permute-start.2 = (bf16[128,4096]{1,0:T(8,128)(2,1)S(1)}, bf16[128,4096]{1,0:T(8,128)(2,1)S(1)}, u32[]{:S(2)}, u32[]{:S(2)}) collective-permute-start(bf16[128,4096]{1,0:T(8,128)(2,1)S(1)} %get-tuple-element.54.refs_0_), channel_id=1, source_target_pairs={{0,1},{1,0},{2,3},{3,2},{4,5},{5,4},{6,7},{7,6},{8,9},{9,8},{10,11... | collective-permute-start | bytes 3145736 | tf_op jit(solution)/shard_map/ppermute | solution.py:385
  4.0 33.1 %collective-permute-start = (bf16[128,4096]{1,0:T(8,128)(2,1)S(1)}, bf16[128,4096]{1,0:T(8,128)(2,1)S(1)}, u32[]{:S(2)}, u32[]{:S(2)}) collective-permute-start(bf16[128,4096]{1,0:T(8,128)(2,1)S(1)} %get-tuple-element.54.refs_0_), channel_id=1, source_target_pairs={{0,4},{1,5},{4,8},{5,9},{8,12},{9,13},{12,14},{13,15},{14,10},{15,... | collective-permute-start | bytes 3145736 | tf_op jit(solution)/shard_map/ppermute | solution.py:385
  6.7 30.5 %collective-permute-start.1 = (bf16[128,4096]{1,0:T(8,128)(2,1)S(1)}, bf16[128,4096]{1,0:T(8,128)(2,1)S(1)}, u32[]{:S(2)}, u32[]{:S(2)}) collective-permute-start(bf16[128,4096]{1,0:T(8,128)(2,1)S(1)} %get-tuple-element.54.refs_0_), channel_id=1, source_target_pairs={{4,0},{5,1},{8,4},{9,5},{12,8},{13,9},{14,12},{15,13},{10,14},{11,... | collective-permute-start | bytes 3145736 | tf_op jit(solution)/shard_map/ppermute | solution.py:385
  6.7 30.4 %collective-permute-start.3 = (bf16[1,24,2048]{2,1,0:T(8,128)(2,1)S(1)}, bf16[1,24,2048]{2,1,0:T(8,128)(2,1)S(1)}, u32[]{:S(2)}, u32[]{:S(2)}) collective-permute-start(bf16[1,24,2048]{2,1,0:T(8,128)(2,1)S(1)} %bitcast.17), channel_id=1, source_target_pairs={{0,8},{1,9},{2,10},{3,11},{4,12},{5,13},{6,14},{7,15},{8,0},{9,1},... | collective-permute-start | bytes 294920 | tf_op jit(solution)/shard_map/ppermute | solution.py:385
  37.1 7.1 %collective-permute-start.6 = (bf16[128,4096]{1,0:T(8,128)(2,1)S(1)}, bf16[128,4096]{1,0:T(8,128)(2,1)S(1)}, u32[]{:S(2)}, u32[]{:S(2)}) collective-permute-start(bf16[128,4096]{1,0:T(8,128)(2,1)S(1)} %collective-permute-done.refs_0_), channel_id=1, source_target_pairs={{0,1},{1,0},{2,3},{3,2},{4,5},{5,4},{6,7},{7,6},{8,9},{9,8},{10,11... | collective-permute-start | bytes 3145736 | tf_op jit(solution)/shard_map/ppermute | solution.py:385
  37.1 7.1 %collective-permute-start.7 = (bf16[128,4096]{1,0:T(8,128)(2,1)S(1)}, bf16[128,4096]{1,0:T(8,128)(2,1)S(1)}, u32[]{:S(2)}, u32[]{:S(2)}) collective-permute-start(bf16[128,4096]{1,0:T(8,128)(2,1)S(1)} %collective-permute-done.1.refs_1_), channel_id=1, source_target_pairs={{0,1},{1,0},{2,3},{3,2},{4,5},{5,4},{6,7},{7,6},{8,9},{9,8},{10,11... | collective-permute-start | bytes 3145736 | tf_op jit(solution)/shard_map/ppermute | solution.py:385
  37.6 29.4 %collective-permute-start.4 = (bf16[128,4096]{1,0:T(8,128)(2,1)S(1)}, bf16[128,4096]{1,0:T(8,128)(2,1)S(1)}, u32[]{:S(2)}, u32[]{:S(2)}) collective-permute-start(bf16[128,4096]{1,0:T(8,128)(2,1)S(1)} %collective-permute-done.refs_0_), channel_id=1, source_target_pairs={{0,4},{1,5},{4,8},{5,9},{8,12},{9,13},{12,14},{13,15},{14,10},{15,... | collective-permute-start | bytes 3145736 | tf_op jit(solution)/shard_map/ppermute | solution.py:385
  37.6 29.4 %collective-permute-start.5 = (bf16[128,4096]{1,0:T(8,128)(2,1)S(1)}, bf16[128,4096]{1,0:T(8,128)(2,1)S(1)}, u32[]{:S(2)}, u32[]{:S(2)}) collective-permute-start(bf16[128,4096]{1,0:T(8,128)(2,1)S(1)} %collective-permute-done.1.refs_1_), channel_id=1, source_target_pairs={{4,0},{5,1},{8,4},{9,5},{12,8},{13,9},{14,12},{15,13},{10,14},{11,... | collective-permute-start | bytes 3145736 | tf_op jit(solution)/shard_map/ppermute | solution.py:385
  39.7 27.3 %collective-permute-start.8 = (bf16[2,24,2048]{2,1,0:T(8,128)(2,1)S(1)}, bf16[2,24,2048]{2,1,0:T(8,128)(2,1)S(1)}, u32[]{:S(2)}, u32[]{:S(2)}) collective-permute-start(bf16[2,24,2048]{2,1,0:T(8,128)(2,1)S(1)} %pad_maximum_fusion.1), channel_id=1, source_target_pairs={{0,4},{1,5},{2,6},{3,7},{4,0},{5,1},{6,2},{7,3},{8,12},{9,13},{10,... | collective-permute-start | bytes 589832 | tf_op jit(solution)/shard_map/ppermute | solution.py:385
  67.0 8.8 %collective-permute-start.12 = (bf16[128,4096]{1,0:T(8,128)(2,1)S(1)}, bf16[128,4096]{1,0:T(8,128)(2,1)S(1)}, u32[]{:S(2)}, u32[]{:S(2)}) collective-permute-start(bf16[128,4096]{1,0:T(8,128)(2,1)S(1)} %collective-permute-done.5.refs_1_), channel_id=1, source_target_pairs={{0,1},{1,0},{2,3},{3,2},{4,5},{5,4},{6,7},{7,6},{8,9},{9,8},{10,11... | collective-permute-start | bytes 3145736 | tf_op jit(solution)/shard_map/ppermute | solution.py:385
  67.5 33.6 %collective-permute-start.10 = (bf16[128,4096]{1,0:T(8,128)(2,1)S(1)}, bf16[128,4096]{1,0:T(8,128)(2,1)S(1)}, u32[]{:S(2)}, u32[]{:S(2)}) collective-permute-start(bf16[128,4096]{1,0:T(8,128)(2,1)S(1)} %collective-permute-done.5.refs_1_), channel_id=1, source_target_pairs={{4,0},{5,1},{8,4},{9,5},{12,8},{13,9},{14,12},{15,13},{10,14},{11,... | collective-permute-start | bytes 3145736 | tf_op jit(solution)/shard_map/ppermute | solution.py:385
  67.7 33.4 %collective-permute-start.9 = (bf16[128,4096]{1,0:T(8,128)(2,1)S(1)}, bf16[128,4096]{1,0:T(8,128)(2,1)S(1)}, u32[]{:S(2)}, u32[]{:S(2)}) collective-permute-start(bf16[128,4096]{1,0:T(8,128)(2,1)S(1)} %collective-permute-done.4.refs_0_), channel_id=1, source_target_pairs={{0,4},{1,5},{4,8},{5,9},{8,12},{9,13},{12,14},{13,15},{14,10},{15,... | collective-permute-start | bytes 3145736 | tf_op jit(solution)/shard_map/ppermute | solution.py:385
  69.6 31.5 %collective-permute-start.13 = (bf16[4,24,2048]{2,1,0:T(8,128)(2,1)S(1)}, bf16[4,24,2048]{2,1,0:T(8,128)(2,1)S(1)}, u32[]{:S(2)}, u32[]{:S(2)}) collective-permute-start(bf16[4,24,2048]{2,1,0:T(8,128)(2,1)S(1)} %pad_maximum_fusion.refs_0_), channel_id=1, source_target_pairs={{0,2},{1,3},{2,0},{3,1},{4,6},{5,7},{6,4},{7,5},{8,10},{9,11},{10,... | collective-permute-start | bytes 1179656 | tf_op jit(solution)/shard_map/ppermute | solution.py:385
  69.9 31.2 %collective-permute-start.14 = (bf16[4,24,2048]{2,1,0:T(8,128)(2,1)S(1)}, bf16[4,24,2048]{2,1,0:T(8,128)(2,1)S(1)}, u32[]{:S(2)}, u32[]{:S(2)}) collective-permute-start(bf16[4,24,2048]{2,1,0:T(8,128)(2,1)S(1)} %pad_maximum_fusion.refs_0_), channel_id=1, source_target_pairs={{16,0},{0,16},{17,1},{1,17},{18,2},{2,18},{19,3},{3,19},{20,4},{4,... | collective-permute-start | bytes 1179656 | tf_op jit(solution)/shard_map/ppermute | solution.py:389
  101.2 4.1 %collective-permute-start.18 = (bf16[128,4096]{1,0:T(8,128)(2,1)S(1)}, bf16[128,4096]{1,0:T(8,128)(2,1)S(1)}, u32[]{:S(2)}, u32[]{:S(2)}) collective-permute-start(bf16[128,4096]{1,0:T(8,128)(2,1)S(1)} %collective-permute-done.10.refs_1_), channel_id=1, source_target_pairs={{0,1},{1,0},{2,3},{3,2},{4,5},{5,4},{6,7},{7,6},{8,9},{9,8},{10,11... | collective-permute-start | bytes 3145736 | tf_op jit(solution)/shard_map/ppermute | solution.py:385
  101.8 15.3 %collective-permute-start.15 = (bf16[64,4096]{1,0:T(8,128)(2,1)S(1)}, bf16[64,4096]{1,0:T(8,128)(2,1)S(1)}, u32[]{:S(2)}, u32[]{:S(2)}) collective-permute-start(bf16[64,4096]{1,0:T(8,128)(2,1)S(1)} %slice.6), channel_id=1, source_target_pairs={{0,4},{1,5},{4,8},{5,9},{8,12},{9,13},{12,14},{13,15},{14,10},{15,... | collective-permute-start | bytes 1572872 | tf_op jit(solution)/shard_map/ppermute | solution.py:385
  101.8 15.3 %collective-permute-start.16 = (bf16[64,4096]{1,0:T(8,128)(2,1)S(1)}, bf16[64,4096]{1,0:T(8,128)(2,1)S(1)}, u32[]{:S(2)}, u32[]{:S(2)}) collective-permute-start(bf16[64,4096]{1,0:T(8,128)(2,1)S(1)} %slice.7), channel_id=1, source_target_pairs={{4,0},{5,1},{8,4},{9,5},{12,8},{13,9},{14,12},{15,13},{10,14},{11,... | collective-permute-start | bytes 1572872 | tf_op jit(solution)/shard_map/ppermute | solution.py:385
  103.8 12.0 %collective-permute-start.19 = (bf16[4,24,2048]{2,1,0:T(8,128)(2,1)S(1)}, bf16[4,24,2048]{2,1,0:T(8,128)(2,1)S(1)}, u32[]{:S(2)}, u32[]{:S(2)}) collective-permute-start(bf16[4,24,2048]{2,1,0:T(8,128)(2,1)S(1)} %pad_maximum_fusion.refs_0_), channel_id=1, source_target_pairs={{0,1},{1,0},{2,3},{3,2},{4,5},{5,4},{6,7},{7,6},{8,9},{9,8},{10,11... | collective-permute-start | bytes 1179656 | tf_op jit(solution)/shard_map/ppermute | solution.py:385
  103.8 12.0 %collective-permute-start.20 = (bf16[4,24,2048]{2,1,0:T(8,128)(2,1)S(1)}, bf16[4,24,2048]{2,1,0:T(8,128)(2,1)S(1)}, u32[]{:S(2)}, u32[]{:S(2)}) collective-permute-start(bf16[4,24,2048]{2,1,0:T(8,128)(2,1)S(1)} %collective-permute-done.13.refs_1_), channel_id=1, source_target_pairs={{0,1},{1,0},{2,3},{3,2},{4,5},{5,4},{6,7},{7,6},{8,9},{9,8},{10,11... | collective-permute-start | bytes 1179656 | tf_op jit(solution)/shard_map/ppermute | solution.py:385
  105.3 11.7 %collective-permute-start.21 = (bf16[4,24,2048]{2,1,0:T(8,128)(2,1)S(1)}, bf16[4,24,2048]{2,1,0:T(8,128)(2,1)S(1)}, u32[]{:S(2)}, u32[]{:S(2)}) collective-permute-start(bf16[4,24,2048]{2,1,0:T(8,128)(2,1)S(1)} %collective-permute-done.13.refs_1_), channel_id=1, source_target_pairs={{16,0},{0,16},{17,1},{1,17},{18,2},{2,18},{19,3},{3,19},{20,4},{4,... | collective-permute-start | bytes 1179656 | tf_op jit(solution)/shard_map/ppermute | solution.py:389
  117.1 3.6 %collective-permute-start.22 = (bf16[64,4096]{1,0:T(8,128)(2,1)S(1)}, bf16[64,4096]{1,0:T(8,128)(2,1)S(1)}, u32[]{:S(2)}, u32[]{:S(2)}) collective-permute-start(bf16[64,4096]{1,0:T(8,128)(2,1)S(1)} %collective-permute-done.15.refs_0_), channel_id=1, source_target_pairs={{0,1},{1,0},{2,3},{3,2},{4,5},{5,4},{6,7},{7,6},{8,9},{9,8},{10,11... | collective-permute-start | bytes 1572872 | tf_op jit(solution)/shard_map/ppermute | solution.py:385
  117.2 3.5 %collective-permute-start.23 = (bf16[64,4096]{1,0:T(8,128)(2,1)S(1)}, bf16[64,4096]{1,0:T(8,128)(2,1)S(1)}, u32[]{:S(2)}, u32[]{:S(2)}) collective-permute-start(bf16[64,4096]{1,0:T(8,128)(2,1)S(1)} %collective-permute-done.16.refs_1_), channel_id=1, source_target_pairs={{0,1},{1,0},{2,3},{3,2},{4,5},{5,4},{6,7},{7,6},{8,9},{9,8},{10,11... | collective-permute-start | bytes 1572872 | tf_op jit(solution)/shard_map/ppermute | solution.py:385
  117.7 5.5 %collective-permute-start.24 = (bf16[4,24,2048]{2,1,0:T(8,128)(2,1)S(1)}, bf16[4,24,2048]{2,1,0:T(8,128)(2,1)S(1)}, u32[]{:S(2)}, u32[]{:S(2)}) collective-permute-start(bf16[4,24,2048]{2,1,0:T(8,128)(2,1)S(1)} %collective-permute-done.14.refs_4_), channel_id=1, source_target_pairs={{0,1},{1,0},{2,3},{3,2},{4,5},{5,4},{6,7},{7,6},{8,9},{9,8},{10,11... | collective-permute-start | bytes 1179656 | tf_op jit(solution)/shard_map/ppermute | solution.py:385
  117.7 5.5 %collective-permute-start.25 = (bf16[4,24,2048]{2,1,0:T(8,128)(2,1)S(1)}, bf16[4,24,2048]{2,1,0:T(8,128)(2,1)S(1)}, u32[]{:S(2)}, u32[]{:S(2)}) collective-permute-start(bf16[4,24,2048]{2,1,0:T(8,128)(2,1)S(1)} %collective-permute-done.21.refs_5_), channel_id=1, source_target_pairs={{0,1},{1,0},{2,3},{3,2},{4,5},{5,4},{6,7},{7,6},{8,9},{9,8},{10,11... | collective-permute-start | bytes 1179656 | tf_op jit(solution)/shard_map/ppermute | solution.py:385
  (6 other events, 18.6 us)

commit v11 on v10

v11 whole, which is shorter than its diff:
```python
import functools

import jax
import jax.numpy as jnp
from jax import lax
from jax.experimental import pallas as pl
from jax.experimental.pallas import tpu as pltpu
from jax.sharding import PartitionSpec as P

NVAL = 256
LANES = 128
MIB = 1024 * 1024
NT = (((1,), (1,)), ((), ()))
TN = (((0,), (0,)), ((), ()))
SMALL = pl.CostEstimate(flops=1_000_000, bytes_accessed=100_000, transcendentals=0)


def chip_ring(chips):
    if chips == 8:
        return [0, 2, 4, 6, 7, 5, 3, 1]
    return list(range(chips))


def prepare_body(lengths_ref, ids_ref, x_hbm, gain_hbm, grads_hbm, factor_hbm, queries_hbm, *refs):
    rows_ref, share_ref, x_ref, gain_ref, grads_ref, factor_ref, queries_ref, sems = refs
    span = x_ref.shape[0]
    block = 32
    starts = range(0, span, block)
    x_copies = []
    for k, start in enumerate(starts):
        some = pl.ds(start, block)
        x_copies.append(pltpu.make_async_copy(x_hbm.at[some], x_ref.at[some], sems.at[k]))
    copies = []
    pairs = [(gain_hbm, gain_ref), (grads_hbm, grads_ref), (factor_hbm, factor_ref), (queries_hbm, queries_ref)]
    for k, (source, target) in enumerate(pairs):
        copies.append(pltpu.make_async_copy(source, target, sems.at[len(x_copies) + k]))
    copies[0].start()
    for copy in x_copies + copies[1:]:
        copy.start()
    copies[0].wait()
    for start, copy in zip(starts, x_copies):
        copy.wait()
        for at in range(start, start + block, 16):
            x = x_ref[at : at + 16, :].astype(jnp.float32)
            scale = lax.rsqrt(jnp.mean(x * x, axis=-1, keepdims=True) + 1e-05)
            rows_ref[at : at + 16, :] = (x * scale * gain_ref[...]).astype(jnp.bfloat16)
    for copy in copies[1:]:
        copy.wait()

    count, width = share_ref.shape[1:]
    depth, order = factor_ref.shape[1], factor_ref.shape[0]
    rows = span * LANES // width
    extra = rows_ref.shape[0] - span
    offset = pl.multiple_of(lax.axis_index("groups") * width, width)
    share_ref[0] = queries_ref[:, pl.ds(offset, width)]
    right = lax.dot_general(grads_ref[...], factor_ref[...], NT, preferred_element_type=jnp.float32)
    live = lax.broadcasted_iota(jnp.int32, (span, order), 0) < lengths_ref[0]
    masked = jnp.where(live, right, 0.0)
    ids = jnp.concatenate([ids_ref[...], jnp.zeros((1, LANES - order - count), jnp.int32)], axis=1)
    ids = jnp.broadcast_to(ids.astype(jnp.float32), (span, LANES - order))
    both = jnp.concatenate([masked, ids], axis=1)
    wide = jnp.concatenate([both[r : r + rows, :] for r in range(0, span, rows)], axis=1)
    if rows < extra:
        wide = jnp.concatenate([wide, jnp.zeros((extra - rows, width), jnp.float32)], axis=0)
    rows_ref[span:, :width] = queries_ref[:, pl.ds(offset, width)]
    rows_ref[span:, width : 2 * width] = wide.astype(rows_ref.dtype)
    if 2 * width < depth:
        rows_ref[span:, 2 * width :] = jnp.zeros((extra, depth - 2 * width), rows_ref.dtype)


def prepare(x, gain, lengths, grads, factor, ids, queries, groups):
    span, depth = x.shape
    count = queries.shape[0]
    width = depth // groups
    vmem = pl.BlockSpec(memory_space=pltpu.VMEM)
    hbm = pl.BlockSpec(memory_space=pltpu.HBM)
    operands = [x, gain, grads, factor, queries]
    return pl.pallas_call(
        prepare_body,
        in_specs=[pl.BlockSpec(memory_space=pltpu.SMEM), vmem] + [hbm] * len(operands),
        out_specs=[vmem] * 2,
        out_shape=[
            jax.ShapeDtypeStruct((span + count, depth), jnp.bfloat16),
            jax.ShapeDtypeStruct((1, count, width), queries.dtype),
        ],
        scratch_shapes=[pltpu.VMEM(o.shape, o.dtype) for o in operands]
        + [pltpu.SemaphoreType.DMA((span // 32 + len(operands) - 1,))],
        compiler_params=pltpu.CompilerParams(vmem_limit_bytes=12 * MIB),
        cost_estimate=SMALL,
        name="prepare",
    )(lengths, ids, *[pltpu.with_memory_space_constraint(o, pltpu.HBM) for o in operands])


def gather_rows(x_refs, xn, shares_ref, slots, extra):
    at = 0
    for ref, slot in zip(x_refs, slots):
        rows = ref.shape[0] - (0 if slot is None else extra)
        xn[at : at + rows, :] = ref[:rows, :]
        if slot is not None:
            shares_ref[slot] = ref[rows:, :]
        at += rows
    return xn


def gated(gate, up):
    return (jax.nn.silu(gate) * up).astype(jnp.bfloat16)


def project(xn, gate_ref, up_ref, f_ref):
    order, units = f_ref.shape
    wide = 2 * LANES

    def product(w):
        return jnp.dot(xn[...], w, preferred_element_type=jnp.float32)

    def left_of(hidden, start, end):
        return lax.dot_general(hidden, f_ref[:, start:end], NT, preferred_element_type=jnp.float32)

    total = jnp.zeros((xn.shape[0], order), jnp.float32)
    hidden, start = None, 0
    for at in range(0, units, wide):
        both = product(gate_ref[:, at : at + wide])
        if hidden is not None:
            total += left_of(hidden, start, at)
        if at + wide <= units:
            hidden = gated(both, product(up_ref[:, at : at + wide]))
        else:
            hidden = gated(both[:, :LANES], both[:, LANES:])
        start = at
    return total + left_of(hidden, start, units)


def first_body(x_ref, gate_hbm, up_hbm, f_ref, out_ref, gate_ref, up_ref, shares_ref, xn, sems):
    depth, units = gate_hbm.shape
    even = up_ref.shape[1]
    parts = sems.shape[1]
    copies = []
    for p in range(parts):
        rows = pl.ds(p * (depth // parts), depth // parts)
        moves = [
            (gate_hbm.at[rows], gate_ref.at[rows, pl.ds(0, units)]),
            (up_hbm.at[rows, pl.ds(0, even)], up_ref.at[rows]),
        ]
        if even < units:
            moves.append((up_hbm.at[rows, pl.ds(even, LANES)], gate_ref.at[rows, pl.ds(units, LANES)]))
        for k, (source, target) in enumerate(moves):
            copies.append(pltpu.make_async_copy(source, target, sems.at[k, p]))
    for copy in copies:
        copy.start()
    gather_rows([x_ref], xn, shares_ref, [0], shares_ref.shape[1])
    for copy in copies:
        copy.wait()
    out_ref[...] = project(xn, gate_ref, up_ref, f_ref)


def first_chunk(rows, gate_weight, up_weight, in_factor, devices, extra):
    total, depth = rows.shape[0] - extra, rows.shape[1]
    order, units = in_factor.shape
    vmem = pl.BlockSpec(memory_space=pltpu.VMEM)
    hbm = pl.BlockSpec(memory_space=pltpu.HBM)
    rest = units % (2 * LANES)
    left, *kept = pl.pallas_call(
        first_body,
        grid=(1,),
        in_specs=[vmem, hbm, hbm, vmem],
        out_specs=[pl.BlockSpec((total, order), lambda i: (0, 0)), vmem, vmem, vmem],
        out_shape=[
            jax.ShapeDtypeStruct((devices * total, order), jnp.float32),
            pltpu.VMEM((depth, units + rest), jnp.bfloat16),
            pltpu.VMEM((depth, units - rest), jnp.bfloat16),
            pltpu.VMEM((devices, extra, depth), jnp.bfloat16),
        ],
        scratch_shapes=[pltpu.VMEM((total, depth), jnp.bfloat16), pltpu.SemaphoreType.DMA((3, 4))],
        compiler_params=pltpu.CompilerParams(vmem_limit_bytes=12 * MIB),
        cost_estimate=SMALL,
        name="first_chunk",
    )(
        rows,
        pltpu.with_memory_space_constraint(gate_weight, pltpu.HBM),
        pltpu.with_memory_space_constraint(up_weight, pltpu.HBM),
        in_factor,
    )
    return left, kept


def chunk_body(slots, *refs):
    pieces = len(slots)
    x_refs, (gate_ref, up_ref, _, f_ref, _, out_ref, _, _, shares_ref, xn) = refs[:pieces], refs[pieces:]
    gather_rows(x_refs, xn, shares_ref, slots, shares_ref.shape[1])
    out_ref[...] = project(xn, gate_ref, up_ref, f_ref)


def chunk(xs, slots, kept, in_factor, left, index):
    pieces = len(xs)
    depth = xs[0].shape[1]
    order = in_factor.shape[0]
    extra = kept[2].shape[1]
    total = sum(x.shape[0] - (0 if slot is None else extra) for x, slot in zip(xs, slots))
    vmem = pl.BlockSpec(memory_space=pltpu.VMEM)
    left, *kept = pl.pallas_call(
        functools.partial(chunk_body, slots),
        grid=(1,),
        in_specs=[vmem] * (pieces + 4) + [pl.BlockSpec(memory_space=pl.ANY)],
        out_specs=[pl.BlockSpec((total, order), lambda i: (index, 0)), vmem, vmem, vmem],
        out_shape=[jax.ShapeDtypeStruct(left.shape, left.dtype)] + [pltpu.VMEM(w.shape, w.dtype) for w in kept],
        scratch_shapes=[pltpu.VMEM((total, depth), jnp.bfloat16)],
        input_output_aliases={pieces + 4: 0, pieces: 1, pieces + 1: 2, pieces + 2: 3},
        compiler_params=pltpu.CompilerParams(vmem_limit_bytes=12 * MIB),
        cost_estimate=SMALL,
        name="chunk",
    )(*xs, *[pltpu.with_memory_space_constraint(w, pltpu.VMEM) for w in kept], in_factor, left)
    return left, kept


def masked_of(wide, span, order):
    wide = wide.astype(jnp.float32)
    both = jnp.concatenate([wide[:, c : c + LANES] for c in range(0, wide.shape[1], LANES)], axis=0)
    return both[:, :order].astype(jnp.bfloat16)


def one_sketch(left_ref, masked, at, half):
    left = jnp.concatenate([left_ref[p * half : (p + 1) * half, :] for p in at], axis=0)
    high = left.astype(jnp.bfloat16)
    low = (left - high.astype(jnp.float32)).astype(jnp.bfloat16)
    return sum(lax.dot_general(part, masked, TN, preferred_element_type=jnp.float32) for part in (low, high))


def write_flat(flat, slot, sketch, twice):
    order = sketch.shape[0]
    twice[...] = jnp.concatenate([sketch, sketch], axis=1)
    lane = lax.broadcasted_iota(jnp.int32, (order // 2, 2 * order), 1)
    even = twice[pl.ds(0, order // 2, 2), :]
    odd = twice[pl.ds(1, order // 2, 2), :]
    flat[:, slot, :] = jnp.where(lane < order, even, odd)


def masked_in(shares_ref, slot, width, span, order):
    return masked_of(shares_ref[slot, : span * LANES // width, width : 2 * width], span, order)


def sketch_body(places, half, width, left_ref, shares_ref, flat, twice):
    for r, at in enumerate(places):
        masked = masked_in(shares_ref, r, width, 2 * half, left_ref.shape[1])
        write_flat(flat, r, one_sketch(left_ref, masked, at, half), twice)


def sketches(places, half, width, left, shares):
    order = left.shape[1]
    vmem = pl.BlockSpec(memory_space=pltpu.VMEM)
    return pl.pallas_call(
        functools.partial(sketch_body, places, half, width),
        in_specs=[vmem] * 2,
        out_specs=vmem,
        out_shape=jax.ShapeDtypeStruct((order // 2, shares.shape[0], 2 * order), jnp.float32),
        scratch_shapes=[pltpu.VMEM((order, 2 * order), jnp.float32)],
        compiler_params=pltpu.CompilerParams(vmem_limit_bytes=12 * MIB),
        cost_estimate=SMALL,
        name="sketches",
    )(left, pltpu.with_memory_space_constraint(shares, pltpu.VMEM))


def members_of(shares_ref, count, width, order):
    devices = shares_ref.shape[0]
    first = shares_ref[:, :8, width : width + LANES].astype(jnp.float32)[:, 0, :].astype(jnp.bfloat16)
    shape = (LANES, devices * count)
    place = lax.broadcasted_iota(jnp.int32, shape, 0) - order
    query = lax.broadcasted_iota(jnp.int32, shape, 1)
    spread = (place >= 0) & (place < count) & (((query - place) & (count - 1)) == 0)
    ids = jnp.dot(first, spread.astype(jnp.bfloat16), preferred_element_type=jnp.float32)
    place = lax.broadcasted_iota(jnp.int32, ids.shape, 1) - count * lax.broadcasted_iota(jnp.int32, ids.shape, 0)
    ids = jnp.sum(jnp.where((place >= 0) & (place < count), ids, 0.0), axis=0, keepdims=True)
    value = lax.broadcasted_iota(jnp.int32, (NVAL, devices * count), 0).astype(jnp.float32)
    return (value == ids).astype(jnp.bfloat16)


def finish_body(places, half, groups, width, table, left_ref, flat_ref, shares_ref, *refs):
    query_refs, (out_ref, twice, flat) = refs[:-3], refs[-3:]
    examples, count, _ = shares_ref.shape
    order = left_ref.shape[1]
    me, group = lax.axis_index("examples"), lax.axis_index("groups")
    flat[...] = flat_ref[...]
    for r, at in enumerate(places, examples - len(places)):
        masked = masked_in(shares_ref, r, width, 2 * half, order)
        write_flat(flat, r, one_sketch(left_ref, masked, at, half), twice)
    scores = 0.0
    for r in range(groups):
        block = lax.rem(group + r, groups) * (width // LANES)
        sketch = jnp.concatenate([flat[block + c] for c in range(width // LANES)], axis=1).astype(jnp.bfloat16)
        if r == 0:
            queries = shares_ref[:, :, :width].reshape(examples * count, width)
        else:
            parts = []
            for mine, other in zip(query_refs[2 * r - 2 :: 2 * groups - 2], query_refs[2 * r - 1 :: 2 * groups - 2]):
                for k in range(mine.shape[0]):
                    parts += [mine[k], other[k]]
            queries = jnp.concatenate(parts, axis=0)
        scores += lax.dot_general(sketch, queries, NT, preferred_element_type=jnp.float32)
    members = members_of(shares_ref, count, width, order)
    total = 0.0
    for _ in range(3):
        part = scores.astype(jnp.bfloat16)
        scores = scores - part.astype(jnp.float32)
        total += lax.dot_general(part, members, NT, preferred_element_type=jnp.float32)
    for r in range(examples):
        out_ref[pl.ds(table[me, r], 1), :] = total[r : r + 1, :]


def finish(places, half, groups, width, table, left, flat, shares, queries):
    order = left.shape[1]
    vmem = pl.BlockSpec(memory_space=pltpu.VMEM)
    return pl.pallas_call(
        functools.partial(finish_body, places, half, groups, width),
        in_specs=[pl.BlockSpec(memory_space=pltpu.SMEM)] + [vmem] * (3 + len(queries)),
        out_specs=vmem,
        out_shape=jax.ShapeDtypeStruct((table.shape[0], NVAL), jnp.float32),
        scratch_shapes=[pltpu.VMEM((order, 2 * order), jnp.float32), pltpu.VMEM(flat.shape, jnp.float32)],
        compiler_params=pltpu.CompilerParams(vmem_limit_bytes=14 * MIB),
        cost_estimate=SMALL,
        name="finish",
    )(table, left, flat, pltpu.with_memory_space_constraint(shares, pltpu.VMEM), *queries)


def arrivals(ring, devices):
    chips = len(ring)
    far = chips // 2
    table, spots = [[] for _ in range(devices)], []
    for distance in range(far + 1):
        for sign, piece in [(1, 0)] if distance in (0, far) else [(-1, 0), (1, 1)]:
            for me in range(devices):
                chip = ring[(ring.index(me // 2) + sign * distance) % chips]
                table[me] += [2 * chip + me % 2, 2 * chip + 1 - me % 2]
            if distance == 0:
                spots += [[0, 1], [2, 3]]
            elif distance == far:
                at = 4 * (2 * far - 1)
                spots += [[at, at + 1], [at + 2, at + 3]]
            else:
                at = 4 * (2 * distance - 1) + 2 * piece
                spots += [[at, at + 1], [at + 4, at + 5]]
    return table, spots


def local(
    devices,
    groups,
    layer_inputs,
    example_lengths,
    norm_gain,
    gate_weight,
    up_weight,
    in_factor,
    out_factor,
    out_grads,
    queries,
    query_ids,
):
    chips = devices // 2
    ring = chip_ring(chips)
    forward = [(ring[r] * 2 + c, ring[(r + 1) % chips] * 2 + c) for r in range(chips) for c in range(2)]
    backward = [(b, a) for a, b in forward]
    other_core = [(d, d ^ 1) for d in range(devices)]

    span, depth = layer_inputs.shape
    half = span // 2
    order = in_factor.shape[1]
    units = gate_weight.shape[1]
    short = -units % LANES
    if short:
        gate_weight = jnp.pad(gate_weight, ((0, 0), (0, short)))
        up_weight = jnp.pad(up_weight, ((0, 0), (0, short)))
        in_factor = jnp.pad(in_factor, ((0, short), (0, 0)))
    far = chips // 2
    table, spots = arrivals(ring, devices)
    table = jnp.array(table, jnp.int32)

    def send(x, way):
        return lax.ppermute(x, "examples", way)

    def across(x):
        ways = [[((g + r) % groups, g) for g in range(groups)] for r in range(1, groups)]
        return [lax.ppermute(x, "groups", way) for way in ways]

    rows, share = prepare(
        layer_inputs,
        norm_gain[None, :],
        example_lengths,
        out_grads,
        out_factor.T,
        query_ids[None, :],
        queries,
        groups,
    )
    width = share.shape[2]
    extra = rows.shape[0] - span

    coming = (send(rows, forward), send(rows, backward))
    swapped = send(rows, other_core)
    pending, crossed = across(share), []
    left, kept = first_chunk(rows, gate_weight, up_weight, in_factor.T, devices, extra)
    left, kept = chunk((swapped,), (1,), kept, in_factor.T, left, 1)
    for r in range(1, far + 1):
        due = len(pending)
        own_f, own_b, left, *rest = lax.optimization_barrier((*coming, left, *pending, *crossed))
        pending, crossed = rest[:due], rest[due:]
        if r < far - 1:
            coming = (send(own_f, forward), send(own_b, backward))
        elif r == far - 1:
            coming = (send(own_f[:half], forward), send(own_b[half:], backward))
        swapped = (send(own_f, other_core), send(own_b, other_core))
        crossed += [y for x in pending for y in (x, send(x, other_core))]
        if r < far:
            pending = across(jnp.stack([own_f[span:, :width], own_b[span:, :width]]))
            slot = 4 * r - 2
            left, kept = chunk((own_f, own_b), (slot, slot + 2), kept, in_factor.T, left, 2 * r - 1)
            left, kept = chunk(swapped, (slot + 1, slot + 3), kept, in_factor.T, left, 2 * r)
        else:
            pending = across(own_b[half:, :width][None])
            crossed += [y for x in pending for y in (x, send(x, other_core))]
            slot, at = devices - 2, 2 * (2 * far - 1)
            left, kept = chunk((own_f, own_b), (None, slot), kept, in_factor.T, left, at)
            left, kept = chunk(swapped, (None, slot + 1), kept, in_factor.T, left, at + 1)
        if r == far - 1:
            flat = sketches(spots[:-2], half, width, left, kept[2])
            flat, left = lax.optimization_barrier((flat, left))

    partial = finish(spots[-2:], half, groups, width, table, left, flat, kept[2], crossed)
    parts = lax.all_to_all(partial, "examples", split_axis=0, concat_axis=0, tiled=True)
    return jnp.sum(parts, axis=0, keepdims=True)


def solution(mesh):
    return jax.shard_map(
        functools.partial(local, mesh.shape["examples"], mesh.shape["groups"]),
        mesh=mesh,
        in_specs=(
            P(("groups", "examples"), None),
            P(("groups", "examples")),
            P(),
            P(None, "examples"),
            P(None, "examples"),
            P("examples", None),
            P(),
            P(("groups", "examples"), None),
            P("examples", None),
            P("examples"),
        ),
        out_specs=P(("groups", "examples"), None),
        check_vma=False,
    )
```

time: 137 us -> 135 us (0.985)
  Pallas kernels: 47.8 us -> 44.8 us
    ppermute x2 -> x5, starting transfers between devices: 2.98 us -> 8.18 us  [across(): return [lax.ppermute(x, 'groups', way) for way in ways]]
    ppermute x24 -> x22, starting transfers between devices: 15.8 us -> 11.2 us  [send(): return lax.ppermute(x, 'examples', way)]
    pallas_call x12, Pallas kernels: 45.6 us -> 42.6 us  [the longest x9 32.5 us: chunk(): pl.pallas_call(functools.partial(chunk_body, slots), grid=(1,), in_specs=...]
    ppermute x2 -> x5, waiting for transfers between devices: 0.01 us -> 2.78 us  [across(): return [lax.ppermute(x, 'groups', way) for way in ways]]
    ppermute x24 -> x22, waiting for transfers between devices: 56.3 us -> 54.7 us  [send(): return lax.ppermute(x, 'examples', way)]
  transfers between devices with their start and end apart: 26 -> 27, of which waited for: 4 -> 9; matrix products, arithmetic and copies ran while one was open for 0% -> 0% of each run, Pallas kernels for 32% -> 30%
where the time goes in v11:
time: 135 us; the launch traced here: 134 us
  waiting for transfers between devices  57.5 us (43%)
  Pallas kernels  44.8 us (33%)
  starting transfers between devices  19.3 us (14%)
  blocking collectives  10.4 us (8%)
    ppermute x22, waiting for transfers between devices, send(): return lax.ppermute(x, 'examples', way)  54.7 us
    pallas_call x9, Pallas kernels, chunk(): pl.pallas_call(functools.partial(chunk_body, slots), grid=(1,), in_specs=...  32.5 us
    ppermute x22, starting transfers between devices, send(): return lax.ppermute(x, 'examples', way)  11.2 us
    all_to_all x1, blocking collectives, local(): lax.all_to_all(partial, 'examples', split_axis=0, concat_axis=0, tiled=True)  10.4 us
    ppermute x5, starting transfers between devices, across(): return [lax.ppermute(x, 'groups', way) for way in ways]  8.18 us
    pallas_call x1, Pallas kernels, first_chunk(): pl.pallas_call(first_body, grid=(1,), in_specs=[vmem, hbm, hbm, vmem], ou...  7.6 us
    ppermute x5, waiting for transfers between devices, across(): return [lax.ppermute(x, 'groups', way) for way in ways]  2.78 us
  transfers between devices with their start and end apart: 27, of which 9 were waited for; matrix products, arithmetic and copies ran while one was open for 0% of the time, Pallas kernels for 30%

profile of v11, /device:TPU:0, one launch (start us, length us, event | category | flops | bytes accessed | tf_op | source)
XLA Modules:
  0.0 134.4 jit_solution(12163529496610731277)
XLA Ops:
  1.3 2.2 %prepare.1 = (bf16[144,4096]{1,0:T(8,128)(2,1)S(1)}, bf16[1,16,2048]{2,1,0:T(8,128)(2,1)S(1)}) custom-call(s32[1]{0:T(128)S(6)} %copy.85.lengths_ref, s32[1,16]{1,0:T(1,128)S(1)} %bitcast.31, bf16[128,4096]{1,0:T(8,128)(2,1)} %x_hbm.1, f32[1,4096]{1,0:T(1,128)} %bitcast.33, bf16[128,4096]{1,0:T(8,128)(2,1)} %grads_hbm.1, bf16[64,4096]{1,0:T(8,128)(2,1)} %bitcast.32, ...), custom_call_target="tpu_custom_call" | custom-call | flops 1000000 | bytes 100000 | tf_op jit(solution)/shard_map/prepare/pallas_call | solution.py:78
  4.1 2.6 %collective-permute-start.1 = (bf16[144,4096]{1,0:T(8,128)(2,1)S(1)}, bf16[144,4096]{1,0:T(8,128)(2,1)S(1)}, u32[]{:S(2)}, u32[]{:S(2)}) collective-permute-start(bf16[144,4096]{1,0:T(8,128)(2,1)S(1)} %get-tuple-element.75.x_ref), channel_id=1, source_target_pairs={{4,0},{5,1},{8,4},{9,5},{12,8},{13,9},{14,12},{15,13},{10,14},{11,... | collective-permute-start | bytes 3538952 | tf_op jit(solution)/shard_map/ppermute | solution.py:377
  6.8 1.9 %collective-permute-start.3 = (bf16[1,16,2048]{2,1,0:T(8,128)(2,1)S(1)}, bf16[1,16,2048]{2,1,0:T(8,128)(2,1)S(1)}, u32[]{:S(2)}, u32[]{:S(2)}) collective-permute-start(bf16[1,16,2048]{2,1,0:T(8,128)(2,1)S(1)} %get-tuple-element.81), channel_id=1, source_target_pairs={{16,0},{0,16},{17,1},{1,17},{18,2},{2,18},{19,3},{3,19},{20,4},{4,... | collective-permute-start | bytes 196616 | tf_op jit(solution)/shard_map/ppermute | solution.py:381
  8.7 7.6 %first_chunk.1 = (f32[2048,64]{1,0:T(8,128)S(1)}, bf16[4096,1024]{1,0:T(8,128)(2,1)S(1)}, bf16[4096,768]{1,0:T(8,128)(2,1)S(1)}, bf16[16,16,4096]{2,1,0:T(8,128)(2,1)S(1)}) custom-call(bf16[144,4096]{1,0:T(8,128)(2,1)S(1)} %get-tuple-element.75.x_ref, bf16[4096,896]{1,0:T(8,128)(2,1)} %gate_hbm.1, bf16[4096,896]{1,0:T(8,128)(2,1)} %up_hbm.1, ...), custom_call_target="tpu_custom_call" | custom-call | flops 1000000 | bytes 100000 | tf_op jit(solution)/shard_map/first_chunk/pallas_call | solution.py:162
  16.3 2.3 %chunk.9 = (f32[2048,64]{1,0:T(8,128)S(1)}, bf16[4096,1024]{1,0:T(8,128)(2,1)S(1)}, bf16[4096,768]{1,0:T(8,128)(2,1)S(1)}, bf16[16,16,4096]{2,1,0:T(8,128)(2,1)S(1)}) custom-call(bf16[144,4096]{1,0:T(8,128)(2,1)S(1)} %collective-permute-done.2.refs_0_, ...), custom_call_target="tpu_custom_call", output_to_operand_aliasing={{0}: (5, {}), {1}: (1, {}), {2}: (2, {}), {3}: (3, {})} | custom-call | flops 1000000 | bytes 100000 | tf_op jit(solution)/shard_map/chunk/pallas_call | solution.py:200
  18.6 14.7 %collective-permute-done.1.refs_1_ = bf16[144,4096]{1,0:T(8,128)(2,1)S(1)} collective-permute-done((bf16[144,4096]{1,0:T(8,128)(2,1)S(1)}, bf16[144,4096]{1,0:T(8,128)(2,1)S(1)}, u32[]{:S(2)}, u32[]{:S(2)}) %collective-permute-start.1) | collective-permute-done | bytes 1179680 | tf_op jit(solution)/shard_map/ppermute | solution.py:377
  35.5 1.7 %collective-permute-start.5 = (bf16[144,4096]{1,0:T(8,128)(2,1)S(1)}, bf16[144,4096]{1,0:T(8,128)(2,1)S(1)}, u32[]{:S(2)}, u32[]{:S(2)}) collective-permute-start(bf16[144,4096]{1,0:T(8,128)(2,1)S(1)} %collective-permute-done.1.refs_1_), channel_id=1, source_target_pairs={{4,0},{5,1},{8,4},{9,5},{12,8},{13,9},{14,12},{15,13},{10,14},{11,... | collective-permute-start | bytes 3538952 | tf_op jit(solution)/shard_map/ppermute | solution.py:377
  38.8 4.2 %chunk.10 = (f32[2048,64]{1,0:T(8,128)S(1)}, bf16[4096,1024]{1,0:T(8,128)(2,1)S(1)}, bf16[4096,768]{1,0:T(8,128)(2,1)S(1)}, bf16[16,16,4096]{2,1,0:T(8,128)(2,1)S(1)}) custom-call(bf16[144,4096]{1,0:T(8,128)(2,1)S(1)} %collective-permute-done.refs_0_, ...), custom_call_target="tpu_custom_call", output_to_operand_aliasing={{0}: (6, {}), {1}: (2, {}), {2}: (3, {}), {3}: (4, {})} | custom-call | flops 1000000 | bytes 100000 | tf_op jit(solution)/shard_map/chunk/pallas_call | solution.py:200
  43.1 4.3 %chunk.11 = (f32[2048,64]{1,0:T(8,128)S(1)}, bf16[4096,1024]{1,0:T(8,128)(2,1)S(1)}, bf16[4096,768]{1,0:T(8,128)(2,1)S(1)}, bf16[16,16,4096]{2,1,0:T(8,128)(2,1)S(1)}) custom-call(bf16[144,4096]{1,0:T(8,128)(2,1)S(1)} %collective-permute-done.6.refs_0_, ...), custom_call_target="tpu_custom_call", output_to_operand_aliasing={{0}: (6, {}), {1}: (2, {}), {2}: (3, {}), {3}: (4, {})} | custom-call | flops 1000000 | bytes 100000 | tf_op jit(solution)/shard_map/chunk/pallas_call | solution.py:200
  47.4 15.7 %collective-permute-done.4.refs_0_ = bf16[144,4096]{1,0:T(8,128)(2,1)S(1)} collective-permute-done((bf16[144,4096]{1,0:T(8,128)(2,1)S(1)}, bf16[144,4096]{1,0:T(8,128)(2,1)S(1)}, u32[]{:S(2)}, u32[]{:S(2)}) %collective-permute-start.4) | collective-permute-done | bytes 1179680 | tf_op jit(solution)/shard_map/ppermute | solution.py:377
  63.1 1.7 %collective-permute-start.10 = (bf16[144,4096]{1,0:T(8,128)(2,1)S(1)}, bf16[144,4096]{1,0:T(8,128)(2,1)S(1)}, u32[]{:S(2)}, u32[]{:S(2)}) collective-permute-start(bf16[144,4096]{1,0:T(8,128)(2,1)S(1)} %collective-permute-done.4.refs_0_), channel_id=1, source_target_pairs={{0,4},{1,5},{4,8},{5,9},{8,12},{9,13},{12,14},{13,15},{14,10},{15,... | collective-permute-start | bytes 3538952 | tf_op jit(solution)/shard_map/ppermute | solution.py:377
  65.4 1.7 %collective-permute-start.14 = (bf16[2,16,2048]{2,1,0:T(8,128)(2,1)S(1)}, bf16[2,16,2048]{2,1,0:T(8,128)(2,1)S(1)}, u32[]{:S(2)}, u32[]{:S(2)}) collective-permute-start(bf16[2,16,2048]{2,1,0:T(8,128)(2,1)S(1)} %pad_maximum_fusion.1), channel_id=1, source_target_pairs={{16,0},{0,16},{17,1},{1,17},{18,2},{2,18},{19,3},{3,19},{20,4},{4,... | collective-permute-start | bytes 393224 | tf_op jit(solution)/shard_map/ppermute | solution.py:381
  67.2 4.2 %chunk.12 = (f32[2048,64]{1,0:T(8,128)S(1)}, bf16[4096,1024]{1,0:T(8,128)(2,1)S(1)}, bf16[4096,768]{1,0:T(8,128)(2,1)S(1)}, bf16[16,16,4096]{2,1,0:T(8,128)(2,1)S(1)}) custom-call(bf16[144,4096]{1,0:T(8,128)(2,1)S(1)} %collective-permute-done.4.refs_0_, ...), custom_call_target="tpu_custom_call", output_to_operand_aliasing={{0}: (6, {}), {1}: (2, {}), {2}: (3, {}), {3}: (4, {})} | custom-call | flops 1000000 | bytes 100000 | tf_op jit(solution)/shard_map/chunk/pallas_call | solution.py:200
  71.4 4.3 %chunk.13 = (f32[2048,64]{1,0:T(8,128)S(1)}, bf16[4096,1024]{1,0:T(8,128)(2,1)S(1)}, bf16[4096,768]{1,0:T(8,128)(2,1)S(1)}, bf16[16,16,4096]{2,1,0:T(8,128)(2,1)S(1)}) custom-call(bf16[144,4096]{1,0:T(8,128)(2,1)S(1)} %collective-permute-done.12.refs_0_, ...), custom_call_target="tpu_custom_call", output_to_operand_aliasing={{0}: (6, {}), {1}: (2, {}), {2}: (3, {}), {3}: (4, {})} | custom-call | flops 1000000 | bytes 100000 | tf_op jit(solution)/shard_map/chunk/pallas_call | solution.py:200
  75.7 15.8 %collective-permute-done.10.refs_0_ = bf16[144,4096]{1,0:T(8,128)(2,1)S(1)} collective-permute-done((bf16[144,4096]{1,0:T(8,128)(2,1)S(1)}, bf16[144,4096]{1,0:T(8,128)(2,1)S(1)}, u32[]{:S(2)}, u32[]{:S(2)}) %collective-permute-start.10) | collective-permute-done | bytes 1179680 | tf_op jit(solution)/shard_map/ppermute | solution.py:377
  91.5 1.7 %collective-permute-done.11.refs_1_ = bf16[144,4096]{1,0:T(8,128)(2,1)S(1)} collective-permute-done((bf16[144,4096]{1,0:T(8,128)(2,1)S(1)}, bf16[144,4096]{1,0:T(8,128)(2,1)S(1)}, u32[]{:S(2)}, u32[]{:S(2)}) %collective-permute-start.11) | collective-permute-done | bytes 1179680 | tf_op jit(solution)/shard_map/ppermute | solution.py:377
  97.6 4.2 %chunk.14 = (f32[2048,64]{1,0:T(8,128)S(1)}, bf16[4096,1024]{1,0:T(8,128)(2,1)S(1)}, bf16[4096,768]{1,0:T(8,128)(2,1)S(1)}, bf16[16,16,4096]{2,1,0:T(8,128)(2,1)S(1)}) custom-call(bf16[144,4096]{1,0:T(8,128)(2,1)S(1)} %collective-permute-done.10.refs_0_, ...), custom_call_target="tpu_custom_call", output_to_operand_aliasing={{0}: (6, {}), {1}: (2, {}), {2}: (3, {}), {3}: (4, {})} | custom-call | flops 1000000 | bytes 100000 | tf_op jit(solution)/shard_map/chunk/pallas_call | solution.py:200
  101.8 4.2 %chunk.15 = (f32[2048,64]{1,0:T(8,128)S(1)}, bf16[4096,1024]{1,0:T(8,128)(2,1)S(1)}, bf16[4096,768]{1,0:T(8,128)(2,1)S(1)}, bf16[16,16,4096]{2,1,0:T(8,128)(2,1)S(1)}) custom-call(bf16[144,4096]{1,0:T(8,128)(2,1)S(1)} %collective-permute-done.18.refs_0_, ...), custom_call_target="tpu_custom_call", output_to_operand_aliasing={{0}: (6, {}), {1}: (2, {}), {2}: (3, {}), {3}: (4, {})} | custom-call | flops 1000000 | bytes 100000 | tf_op jit(solution)/shard_map/chunk/pallas_call | solution.py:200
  107.8 4.1 %collective-permute-done.17.refs_1_ = bf16[80,4096]{1,0:T(8,128)(2,1)S(1)} collective-permute-done((bf16[80,4096]{1,0:T(8,128)(2,1)S(1)}, bf16[80,4096]{1,0:T(8,128)(2,1)S(1)}, u32[]{:S(2)}, u32[]{:S(2)}) %collective-permute-start.17) | collective-permute-done | bytes 655392 | tf_op jit(solution)/shard_map/ppermute | solution.py:377
  113.9 2.8 %collective-permute-done.25.refs_8_ = bf16[1,16,2048]{2,1,0:T(8,128)(2,1)S(1)} collective-permute-done((bf16[1,16,2048]{2,1,0:T(8,128)(2,1)S(1)}, bf16[1,16,2048]{2,1,0:T(8,128)(2,1)S(1)}, u32[]{:S(2)}, u32[]{:S(2)}) %collective-permute-start.25) | collective-permute-done | bytes 65568 | tf_op jit(solution)/shard_map/ppermute | solution.py:381
  116.7 2.3 %chunk.16 = (f32[2048,64]{1,0:T(8,128)S(1)}, bf16[4096,1024]{1,0:T(8,128)(2,1)S(1)}, bf16[4096,768]{1,0:T(8,128)(2,1)S(1)}, bf16[16,16,4096]{2,1,0:T(8,128)(2,1)S(1)}) custom-call(bf16[64,4096]{1,0:T(8,128)(2,1)S(1)} %collective-permute-done.16.refs_0_, ...), custom_call_target="tpu_custom_call", output_to_operand_aliasing={{0}: (6, {}), {1}: (2, {}), {2}: (3, {}), {3}: (4, {})} | custom-call | flops 1000000 | bytes 100000 | tf_op jit(solution)/shard_map/chunk/pallas_call | solution.py:200
  119.1 2.3 %chunk.17 = (f32[2048,64]{1,0:T(8,128)S(1)}, bf16[4096,1024]{1,0:T(8,128)(2,1)S(1)}, bf16[4096,768]{1,0:T(8,128)(2,1)S(1)}, bf16[16,16,4096]{2,1,0:T(8,128)(2,1)S(1)}) custom-call(bf16[64,4096]{1,0:T(8,128)(2,1)S(1)} %collective-permute-done.22.refs_0_, ...), custom_call_target="tpu_custom_call", output_to_operand_aliasing={{0}: (6, {}), {1}: (2, {}), {2}: (3, {}), {3}: (4, {})} | custom-call | flops 1000000 | bytes 100000 | tf_op jit(solution)/shard_map/chunk/pallas_call | solution.py:200
  121.5 2.0 %finish.1 = f32[16,256]{1,0:T(8,128)S(1)} custom-call(s32[16,16]{1,0:T(8,128)S(1)} %copy-done.1, f32[2048,64]{1,0:T(8,128)S(1)} %get-tuple-element.135.left_ref, f32[32,16,128]{2,1,0:T(8,128)S(1)} %sketches.1.flat_ref, bf16[16,16,4096]{2,1,0:T(8,128)(2,1)S(1)} %get-tuple-element.137.shares_ref, bf16[1,16,2048]{2,1,0:T(8,128)(2,1)S(1)} %collective-permute-done.3.refs_0_, ...), custom_call_target="tpu_custom_call" | custom-call | flops 1000000 | bytes 100000 | tf_op jit(solution)/shard_map/finish/pallas_call | solution.py:311
  123.5 10.4 %all_to_all.9 = f32[16,1,256]{2,1,0:T(1,128)S(1)} all-to-all(f32[16,1,256]{2,1,0:T(1,128)S(1)} %copy.48), channel_id=1, replica_groups=mesh['groups'=2,'examples'=16] {'examples'}, dimensions={0} | all-to-all | bytes 32768 | tf_op jit(solution)/shard_map/all_to_all | solution.py:427
  (63 shorter events, 14.5 us)
Async XLA Ops:
  3.6 12.7 %collective-permute-start.2 = (bf16[144,4096]{1,0:T(8,128)(2,1)S(1)}, bf16[144,4096]{1,0:T(8,128)(2,1)S(1)}, u32[]{:S(2)}, u32[]{:S(2)}) collective-permute-start(bf16[144,4096]{1,0:T(8,128)(2,1)S(1)} %get-tuple-element.75.x_ref), channel_id=1, source_target_pairs={{0,1},{1,0},{2,3},{3,2},{4,5},{5,4},{6,7},{7,6},{8,9},{9,8},{10,11... | collective-permute-start | bytes 3538952 | tf_op jit(solution)/shard_map/ppermute | solution.py:377
  4.1 29.2 %collective-permute-start.1 = (bf16[144,4096]{1,0:T(8,128)(2,1)S(1)}, bf16[144,4096]{1,0:T(8,128)(2,1)S(1)}, u32[]{:S(2)}, u32[]{:S(2)}) collective-permute-start(bf16[144,4096]{1,0:T(8,128)(2,1)S(1)} %get-tuple-element.75.x_ref), channel_id=1, source_target_pairs={{4,0},{5,1},{8,4},{9,5},{12,8},{13,9},{14,12},{15,13},{10,14},{11,... | collective-permute-start | bytes 3538952 | tf_op jit(solution)/shard_map/ppermute | solution.py:377
  6.7 28.0 %collective-permute-start = (bf16[144,4096]{1,0:T(8,128)(2,1)S(1)}, bf16[144,4096]{1,0:T(8,128)(2,1)S(1)}, u32[]{:S(2)}, u32[]{:S(2)}) collective-permute-start(bf16[144,4096]{1,0:T(8,128)(2,1)S(1)} %get-tuple-element.75.x_ref), channel_id=1, source_target_pairs={{0,4},{1,5},{4,8},{5,9},{8,12},{9,13},{12,14},{13,15},{14,10},{15,... | collective-permute-start | bytes 3538952 | tf_op jit(solution)/shard_map/ppermute | solution.py:377
  6.8 11.8 %collective-permute-start.3 = (bf16[1,16,2048]{2,1,0:T(8,128)(2,1)S(1)}, bf16[1,16,2048]{2,1,0:T(8,128)(2,1)S(1)}, u32[]{:S(2)}, u32[]{:S(2)}) collective-permute-start(bf16[1,16,2048]{2,1,0:T(8,128)(2,1)S(1)} %get-tuple-element.81), channel_id=1, source_target_pairs={{16,0},{0,16},{17,1},{1,17},{18,2},{2,18},{19,3},{3,19},{20,4},{4,... | collective-permute-start | bytes 196616 | tf_op jit(solution)/shard_map/ppermute | solution.py:381
  34.7 8.4 %collective-permute-start.7 = (bf16[144,4096]{1,0:T(8,128)(2,1)S(1)}, bf16[144,4096]{1,0:T(8,128)(2,1)S(1)}, u32[]{:S(2)}, u32[]{:S(2)}) collective-permute-start(bf16[144,4096]{1,0:T(8,128)(2,1)S(1)} %collective-permute-done.1.refs_1_), channel_id=1, source_target_pairs={{0,1},{1,0},{2,3},{3,2},{4,5},{5,4},{6,7},{7,6},{8,9},{9,8},{10,11... | collective-permute-start | bytes 3538952 | tf_op jit(solution)/shard_map/ppermute | solution.py:377
  35.2 27.9 %collective-permute-start.4 = (bf16[144,4096]{1,0:T(8,128)(2,1)S(1)}, bf16[144,4096]{1,0:T(8,128)(2,1)S(1)}, u32[]{:S(2)}, u32[]{:S(2)}) collective-permute-start(bf16[144,4096]{1,0:T(8,128)(2,1)S(1)} %collective-permute-done.refs_0_), channel_id=1, source_target_pairs={{0,4},{1,5},{4,8},{5,9},{8,12},{9,13},{12,14},{13,15},{14,10},{15,... | collective-permute-start | bytes 3538952 | tf_op jit(solution)/shard_map/ppermute | solution.py:377
  35.5 27.6 %collective-permute-start.5 = (bf16[144,4096]{1,0:T(8,128)(2,1)S(1)}, bf16[144,4096]{1,0:T(8,128)(2,1)S(1)}, u32[]{:S(2)}, u32[]{:S(2)}) collective-permute-start(bf16[144,4096]{1,0:T(8,128)(2,1)S(1)} %collective-permute-done.1.refs_1_), channel_id=1, source_target_pairs={{4,0},{5,1},{8,4},{9,5},{12,8},{13,9},{14,12},{15,13},{10,14},{11,... | collective-permute-start | bytes 3538952 | tf_op jit(solution)/shard_map/ppermute | solution.py:377
  37.3 10.1 %collective-permute-start.8 = (bf16[2,16,2048]{2,1,0:T(8,128)(2,1)S(1)}, bf16[2,16,2048]{2,1,0:T(8,128)(2,1)S(1)}, u32[]{:S(2)}, u32[]{:S(2)}) collective-permute-start(bf16[2,16,2048]{2,1,0:T(8,128)(2,1)S(1)} %pad_maximum_fusion), channel_id=1, source_target_pairs={{16,0},{0,16},{17,1},{1,17},{18,2},{2,18},{19,3},{3,19},{20,4},{4,... | collective-permute-start | bytes 393224 | tf_op jit(solution)/shard_map/ppermute | solution.py:381
  38.8 8.5 %collective-permute-start.9 = (bf16[1,16,2048]{2,1,0:T(8,128)(2,1)S(1)}, bf16[1,16,2048]{2,1,0:T(8,128)(2,1)S(1)}, u32[]{:S(2)}, u32[]{:S(2)}) collective-permute-start(bf16[1,16,2048]{2,1,0:T(8,128)(2,1)S(1)} %collective-permute-done.3.refs_0_), channel_id=1, source_target_pairs={{0,1},{1,0},{2,3},{3,2},{4,5},{5,4},{6,7},{7,6},{8,9},{9,8},{10,11... | collective-permute-start | bytes 196616 | tf_op jit(solution)/shard_map/ppermute | solution.py:377
  63.1 28.4 %collective-permute-start.10 = (bf16[144,4096]{1,0:T(8,128)(2,1)S(1)}, bf16[144,4096]{1,0:T(8,128)(2,1)S(1)}, u32[]{:S(2)}, u32[]{:S(2)}) collective-permute-start(bf16[144,4096]{1,0:T(8,128)(2,1)S(1)} %collective-permute-done.4.refs_0_), channel_id=1, source_target_pairs={{0,4},{1,5},{4,8},{5,9},{8,12},{9,13},{12,14},{13,15},{14,10},{15,... | collective-permute-start | bytes 3538952 | tf_op jit(solution)/shard_map/ppermute | solution.py:377
  64.9 6.5 %collective-permute-start.13 = (bf16[144,4096]{1,0:T(8,128)(2,1)S(1)}, bf16[144,4096]{1,0:T(8,128)(2,1)S(1)}, u32[]{:S(2)}, u32[]{:S(2)}) collective-permute-start(bf16[144,4096]{1,0:T(8,128)(2,1)S(1)} %collective-permute-done.5.refs_1_), channel_id=1, source_target_pairs={{0,1},{1,0},{2,3},{3,2},{4,5},{5,4},{6,7},{7,6},{8,9},{9,8},{10,11... | collective-permute-start | bytes 3538952 | tf_op jit(solution)/shard_map/ppermute | solution.py:377
  65.1 28.2 %collective-permute-start.11 = (bf16[144,4096]{1,0:T(8,128)(2,1)S(1)}, bf16[144,4096]{1,0:T(8,128)(2,1)S(1)}, u32[]{:S(2)}, u32[]{:S(2)}) collective-permute-start(bf16[144,4096]{1,0:T(8,128)(2,1)S(1)} %collective-permute-done.5.refs_1_), channel_id=1, source_target_pairs={{4,0},{5,1},{8,4},{9,5},{12,8},{13,9},{14,12},{15,13},{10,14},{11,... | collective-permute-start | bytes 3538952 | tf_op jit(solution)/shard_map/ppermute | solution.py:377
  65.4 10.3 %collective-permute-start.14 = (bf16[2,16,2048]{2,1,0:T(8,128)(2,1)S(1)}, bf16[2,16,2048]{2,1,0:T(8,128)(2,1)S(1)}, u32[]{:S(2)}, u32[]{:S(2)}) collective-permute-start(bf16[2,16,2048]{2,1,0:T(8,128)(2,1)S(1)} %pad_maximum_fusion.1), channel_id=1, source_target_pairs={{16,0},{0,16},{17,1},{1,17},{18,2},{2,18},{19,3},{3,19},{20,4},{4,... | collective-permute-start | bytes 393224 | tf_op jit(solution)/shard_map/ppermute | solution.py:381
  67.2 8.5 %collective-permute-start.15 = (bf16[2,16,2048]{2,1,0:T(8,128)(2,1)S(1)}, bf16[2,16,2048]{2,1,0:T(8,128)(2,1)S(1)}, u32[]{:S(2)}, u32[]{:S(2)}) collective-permute-start(bf16[2,16,2048]{2,1,0:T(8,128)(2,1)S(1)} %collective-permute-done.8.refs_2_), channel_id=1, source_target_pairs={{0,1},{1,0},{2,3},{3,2},{4,5},{5,4},{6,7},{7,6},{8,9},{9,8},{10,11... | collective-permute-start | bytes 393224 | tf_op jit(solution)/shard_map/ppermute | solution.py:377
  93.3 4.3 %collective-permute-start.18 = (bf16[144,4096]{1,0:T(8,128)(2,1)S(1)}, bf16[144,4096]{1,0:T(8,128)(2,1)S(1)}, u32[]{:S(2)}, u32[]{:S(2)}) collective-permute-start(bf16[144,4096]{1,0:T(8,128)(2,1)S(1)} %collective-permute-done.10.refs_0_), channel_id=1, source_target_pairs={{0,1},{1,0},{2,3},{3,2},{4,5},{5,4},{6,7},{7,6},{8,9},{9,8},{10,11... | collective-permute-start | bytes 3538952 | tf_op jit(solution)/shard_map/ppermute | solution.py:377
  93.4 8.4 %collective-permute-start.19 = (bf16[144,4096]{1,0:T(8,128)(2,1)S(1)}, bf16[144,4096]{1,0:T(8,128)(2,1)S(1)}, u32[]{:S(2)}, u32[]{:S(2)}) collective-permute-start(bf16[144,4096]{1,0:T(8,128)(2,1)S(1)} %collective-permute-done.11.refs_1_), channel_id=1, source_target_pairs={{0,1},{1,0},{2,3},{3,2},{4,5},{5,4},{6,7},{7,6},{8,9},{9,8},{10,11... | collective-permute-start | bytes 3538952 | tf_op jit(solution)/shard_map/ppermute | solution.py:377
  93.9 13.9 %collective-permute-start.16 = (bf16[64,4096]{1,0:T(8,128)(2,1)S(1)}, bf16[64,4096]{1,0:T(8,128)(2,1)S(1)}, u32[]{:S(2)}, u32[]{:S(2)}) collective-permute-start(bf16[64,4096]{1,0:T(8,128)(2,1)S(1)} %slice.31), channel_id=1, source_target_pairs={{0,4},{1,5},{4,8},{5,9},{8,12},{9,13},{12,14},{13,15},{14,10},{15,... | collective-permute-start | bytes 1572872 | tf_op jit(solution)/shard_map/ppermute | solution.py:377
  95.5 16.4 %collective-permute-start.17 = (bf16[80,4096]{1,0:T(8,128)(2,1)S(1)}, bf16[80,4096]{1,0:T(8,128)(2,1)S(1)}, u32[]{:S(2)}, u32[]{:S(2)}) collective-permute-start(bf16[80,4096]{1,0:T(8,128)(2,1)S(1)} %slice.32), channel_id=1, source_target_pairs={{4,0},{5,1},{8,4},{9,5},{12,8},{13,9},{14,12},{15,13},{10,14},{11,... | collective-permute-start | bytes 1966088 | tf_op jit(solution)/shard_map/ppermute | solution.py:377
  96.0 10.6 %collective-permute-start.20 = (bf16[2,16,2048]{2,1,0:T(8,128)(2,1)S(1)}, bf16[2,16,2048]{2,1,0:T(8,128)(2,1)S(1)}, u32[]{:S(2)}, u32[]{:S(2)}) collective-permute-start(bf16[2,16,2048]{2,1,0:T(8,128)(2,1)S(1)} %pad_maximum_fusion.2), channel_id=1, source_target_pairs={{16,0},{0,16},{17,1},{1,17},{18,2},{2,18},{19,3},{3,19},{20,4},{4,... | collective-permute-start | bytes 393224 | tf_op jit(solution)/shard_map/ppermute | solution.py:381
  97.6 9.1 %collective-permute-start.21 = (bf16[2,16,2048]{2,1,0:T(8,128)(2,1)S(1)}, bf16[2,16,2048]{2,1,0:T(8,128)(2,1)S(1)}, u32[]{:S(2)}, u32[]{:S(2)}) collective-permute-start(bf16[2,16,2048]{2,1,0:T(8,128)(2,1)S(1)} %collective-permute-done.14.refs_4_), channel_id=1, source_target_pairs={{0,1},{1,0},{2,3},{3,2},{4,5},{5,4},{6,7},{7,6},{8,9},{9,8},{10,11... | collective-permute-start | bytes 393224 | tf_op jit(solution)/shard_map/ppermute | solution.py:377
  111.9 7.1 %collective-permute-start.23 = (bf16[80,4096]{1,0:T(8,128)(2,1)S(1)}, bf16[80,4096]{1,0:T(8,128)(2,1)S(1)}, u32[]{:S(2)}, u32[]{:S(2)}) collective-permute-start(bf16[80,4096]{1,0:T(8,128)(2,1)S(1)} %collective-permute-done.17.refs_1_), channel_id=1, source_target_pairs={{0,1},{1,0},{2,3},{3,2},{4,5},{5,4},{6,7},{7,6},{8,9},{9,8},{10,11... | collective-permute-start | bytes 1966088 | tf_op jit(solution)/shard_map/ppermute | solution.py:377
  111.9 7.1 %collective-permute-start.22 = (bf16[64,4096]{1,0:T(8,128)(2,1)S(1)}, bf16[64,4096]{1,0:T(8,128)(2,1)S(1)}, u32[]{:S(2)}, u32[]{:S(2)}) collective-permute-start(bf16[64,4096]{1,0:T(8,128)(2,1)S(1)} %collective-permute-done.16.refs_0_), channel_id=1, source_target_pairs={{0,1},{1,0},{2,3},{3,2},{4,5},{5,4},{6,7},{7,6},{8,9},{9,8},{10,11... | collective-permute-start | bytes 1572872 | tf_op jit(solution)/shard_map/ppermute | solution.py:377
  113.9 7.5 %collective-permute-start.24 = (bf16[2,16,2048]{2,1,0:T(8,128)(2,1)S(1)}, bf16[2,16,2048]{2,1,0:T(8,128)(2,1)S(1)}, u32[]{:S(2)}, u32[]{:S(2)}) collective-permute-start(bf16[2,16,2048]{2,1,0:T(8,128)(2,1)S(1)} %collective-permute-done.20.refs_6_), channel_id=1, source_target_pairs={{0,1},{1,0},{2,3},{3,2},{4,5},{5,4},{6,7},{7,6},{8,9},{9,8},{10,11... | collective-permute-start | bytes 393224 | tf_op jit(solution)/shard_map/ppermute | solution.py:377
  116.7 4.7 %collective-permute-start.26 = (bf16[1,16,2048]{2,1,0:T(8,128)(2,1)S(1)}, bf16[1,16,2048]{2,1,0:T(8,128)(2,1)S(1)}, u32[]{:S(2)}, u32[]{:S(2)}) collective-permute-start(bf16[1,16,2048]{2,1,0:T(8,128)(2,1)S(1)} %collective-permute-done.25.refs_8_), channel_id=1, source_target_pairs={{0,1},{1,0},{2,3},{3,2},{4,5},{5,4},{6,7},{7,6},{8,9},{9,8},{10,11... | collective-permute-start | bytes 196616 | tf_op jit(solution)/shard_map/ppermute | solution.py:377
  (6 other events, 24.1 us)

commit v12 on v11

--- a/solution.py
+++ b/solution.py
@@ -414,8 +414,8 @@
             left, kept = chunk((own_f, own_b), (slot, slot + 2), kept, in_factor.T, left, 2 * r - 1)
             left, kept = chunk(swapped, (slot + 1, slot + 3), kept, in_factor.T, left, 2 * r)
         else:
-            pending = across(own_b[half:, :width][None])
-            crossed += [y for x in pending for y in (x, send(x, other_core))]
+            lasts = [across(x[half:, :width][None]) for x in (own_b, swapped[1])]
+            crossed += [y for pair in zip(*lasts) for y in pair]
             slot, at = devices - 2, 2 * (2 * far - 1)
             left, kept = chunk((own_f, own_b), (None, slot), kept, in_factor.T, left, at)
             left, kept = chunk(swapped, (None, slot + 1), kept, in_factor.T, left, at + 1)

time: 135 us -> 133 us (0.985)
  waiting for transfers between devices: 57.5 us -> 54.8 us
  starting transfers between devices: 19.3 us -> 20.8 us
    ppermute x5 -> x6, waiting for transfers between devices: 2.78 us -> 0.02 us  [across(): return [lax.ppermute(x, 'groups', way) for way in ways]]
    ppermute x5 -> x6, starting transfers between devices: 8.18 us -> 9.68 us  [across(): return [lax.ppermute(x, 'groups', way) for way in ways]]
    ppermute x22 -> x21, waiting for transfers between devices: 54.7 us -> 54.8 us  [send(): return lax.ppermute(x, 'examples', way)]
    ppermute x22 -> x21, starting transfers between devices: 11.2 us -> 11.2 us  [send(): return lax.ppermute(x, 'examples', way)]
  transfers between devices with their start and end apart: 27 -> 27, of which waited for: 9 -> 9; matrix products, arithmetic and copies ran while one was open for 0% -> 0% of each run, Pallas kernels for 30% -> 31%
where the time goes in v12:
time: 133 us
  waiting for transfers between devices  54.8 us (41%)
  Pallas kernels  44.8 us (34%)
  starting transfers between devices  20.8 us (16%)
  blocking collectives  10.3 us (8%)
    ppermute x21, waiting for transfers between devices, send(): return lax.ppermute(x, 'examples', way)  54.8 us
    pallas_call x9, Pallas kernels, chunk(): pl.pallas_call(functools.partial(chunk_body, slots), grid=(1,), in_specs=...  32.5 us
    ppermute x21, starting transfers between devices, send(): return lax.ppermute(x, 'examples', way)  11.2 us
    all_to_all x1, blocking collectives, local(): lax.all_to_all(partial, 'examples', split_axis=0, concat_axis=0, tiled=True)  10.3 us
    ppermute x6, starting transfers between devices, across(): return [lax.ppermute(x, 'groups', way) for way in ways]  9.68 us
    pallas_call x1, Pallas kernels, first_chunk(): pl.pallas_call(first_body, grid=(1,), in_specs=[vmem, hbm, hbm, vmem], ou...  7.6 us
  transfers between devices with their start and end apart: 27, of which 9 were waited for; matrix products, arithmetic and copies ran while one was open for 0% of the time, Pallas kernels for 31%

profile of v12, /device:TPU:0, one launch (start us, length us, event | category | flops | bytes accessed | tf_op | source)
XLA Modules:
  0.0 133.1 jit_solution(8494114072456025096)
XLA Ops:
  1.3 2.2 %prepare.1 = (bf16[144,4096]{1,0:T(8,128)(2,1)S(1)}, bf16[1,16,2048]{2,1,0:T(8,128)(2,1)S(1)}) custom-call(s32[1]{0:T(128)S(6)} %copy.85.lengths_ref, s32[1,16]{1,0:T(1,128)S(1)} %bitcast.33, bf16[128,4096]{1,0:T(8,128)(2,1)} %x_hbm.1, f32[1,4096]{1,0:T(1,128)} %bitcast.35, bf16[128,4096]{1,0:T(8,128)(2,1)} %grads_hbm.1, bf16[64,4096]{1,0:T(8,128)(2,1)} %bitcast.34, ...), custom_call_target="tpu_custom_call" | custom-call | flops 1000000 | bytes 100000 | tf_op jit(solution)/shard_map/prepare/pallas_call | solution.py:78
  4.1 2.6 %collective-permute-start.1 = (bf16[144,4096]{1,0:T(8,128)(2,1)S(1)}, bf16[144,4096]{1,0:T(8,128)(2,1)S(1)}, u32[]{:S(2)}, u32[]{:S(2)}) collective-permute-start(bf16[144,4096]{1,0:T(8,128)(2,1)S(1)} %get-tuple-element.75.x_ref), channel_id=1, source_target_pairs={{4,0},{5,1},{8,4},{9,5},{12,8},{13,9},{14,12},{15,13},{10,14},{11,... | collective-permute-start | bytes 3538952 | tf_op jit(solution)/shard_map/ppermute | solution.py:377
  6.8 1.9 %collective-permute-start.3 = (bf16[1,16,2048]{2,1,0:T(8,128)(2,1)S(1)}, bf16[1,16,2048]{2,1,0:T(8,128)(2,1)S(1)}, u32[]{:S(2)}, u32[]{:S(2)}) collective-permute-start(bf16[1,16,2048]{2,1,0:T(8,128)(2,1)S(1)} %get-tuple-element.81), channel_id=1, source_target_pairs={{16,0},{0,16},{17,1},{1,17},{18,2},{2,18},{19,3},{3,19},{20,4},{4,... | collective-permute-start | bytes 196616 | tf_op jit(solution)/shard_map/ppermute | solution.py:381
  8.7 7.6 %first_chunk.1 = (f32[2048,64]{1,0:T(8,128)S(1)}, bf16[4096,1024]{1,0:T(8,128)(2,1)S(1)}, bf16[4096,768]{1,0:T(8,128)(2,1)S(1)}, bf16[16,16,4096]{2,1,0:T(8,128)(2,1)S(1)}) custom-call(bf16[144,4096]{1,0:T(8,128)(2,1)S(1)} %get-tuple-element.75.x_ref, bf16[4096,896]{1,0:T(8,128)(2,1)} %gate_hbm.1, bf16[4096,896]{1,0:T(8,128)(2,1)} %up_hbm.1, ...), custom_call_target="tpu_custom_call" | custom-call | flops 1000000 | bytes 100000 | tf_op jit(solution)/shard_map/first_chunk/pallas_call | solution.py:162
  16.3 2.3 %chunk.9 = (f32[2048,64]{1,0:T(8,128)S(1)}, bf16[4096,1024]{1,0:T(8,128)(2,1)S(1)}, bf16[4096,768]{1,0:T(8,128)(2,1)S(1)}, bf16[16,16,4096]{2,1,0:T(8,128)(2,1)S(1)}) custom-call(bf16[144,4096]{1,0:T(8,128)(2,1)S(1)} %collective-permute-done.2.refs_0_, ...), custom_call_target="tpu_custom_call", output_to_operand_aliasing={{0}: (5, {}), {1}: (1, {}), {2}: (2, {}), {3}: (3, {})} | custom-call | flops 1000000 | bytes 100000 | tf_op jit(solution)/shard_map/chunk/pallas_call | solution.py:200
  18.6 14.7 %collective-permute-done.1.refs_1_ = bf16[144,4096]{1,0:T(8,128)(2,1)S(1)} collective-permute-done((bf16[144,4096]{1,0:T(8,128)(2,1)S(1)}, bf16[144,4096]{1,0:T(8,128)(2,1)S(1)}, u32[]{:S(2)}, u32[]{:S(2)}) %collective-permute-start.1) | collective-permute-done | bytes 1179680 | tf_op jit(solution)/shard_map/ppermute | solution.py:377
  35.5 1.7 %collective-permute-start.5 = (bf16[144,4096]{1,0:T(8,128)(2,1)S(1)}, bf16[144,4096]{1,0:T(8,128)(2,1)S(1)}, u32[]{:S(2)}, u32[]{:S(2)}) collective-permute-start(bf16[144,4096]{1,0:T(8,128)(2,1)S(1)} %collective-permute-done.1.refs_1_), channel_id=1, source_target_pairs={{4,0},{5,1},{8,4},{9,5},{12,8},{13,9},{14,12},{15,13},{10,14},{11,... | collective-permute-start | bytes 3538952 | tf_op jit(solution)/shard_map/ppermute | solution.py:377
  38.8 4.2 %chunk.10 = (f32[2048,64]{1,0:T(8,128)S(1)}, bf16[4096,1024]{1,0:T(8,128)(2,1)S(1)}, bf16[4096,768]{1,0:T(8,128)(2,1)S(1)}, bf16[16,16,4096]{2,1,0:T(8,128)(2,1)S(1)}) custom-call(bf16[144,4096]{1,0:T(8,128)(2,1)S(1)} %collective-permute-done.refs_0_, ...), custom_call_target="tpu_custom_call", output_to_operand_aliasing={{0}: (6, {}), {1}: (2, {}), {2}: (3, {}), {3}: (4, {})} | custom-call | flops 1000000 | bytes 100000 | tf_op jit(solution)/shard_map/chunk/pallas_call | solution.py:200
  43.1 4.3 %chunk.11 = (f32[2048,64]{1,0:T(8,128)S(1)}, bf16[4096,1024]{1,0:T(8,128)(2,1)S(1)}, bf16[4096,768]{1,0:T(8,128)(2,1)S(1)}, bf16[16,16,4096]{2,1,0:T(8,128)(2,1)S(1)}) custom-call(bf16[144,4096]{1,0:T(8,128)(2,1)S(1)} %collective-permute-done.6.refs_0_, ...), custom_call_target="tpu_custom_call", output_to_operand_aliasing={{0}: (6, {}), {1}: (2, {}), {2}: (3, {}), {3}: (4, {})} | custom-call | flops 1000000 | bytes 100000 | tf_op jit(solution)/shard_map/chunk/pallas_call | solution.py:200
  47.4 15.7 %collective-permute-done.4.refs_0_ = bf16[144,4096]{1,0:T(8,128)(2,1)S(1)} collective-permute-done((bf16[144,4096]{1,0:T(8,128)(2,1)S(1)}, bf16[144,4096]{1,0:T(8,128)(2,1)S(1)}, u32[]{:S(2)}, u32[]{:S(2)}) %collective-permute-start.4) | collective-permute-done | bytes 1179680 | tf_op jit(solution)/shard_map/ppermute | solution.py:377
  63.1 1.7 %collective-permute-start.10 = (bf16[144,4096]{1,0:T(8,128)(2,1)S(1)}, bf16[144,4096]{1,0:T(8,128)(2,1)S(1)}, u32[]{:S(2)}, u32[]{:S(2)}) collective-permute-start(bf16[144,4096]{1,0:T(8,128)(2,1)S(1)} %collective-permute-done.4.refs_0_), channel_id=1, source_target_pairs={{0,4},{1,5},{4,8},{5,9},{8,12},{9,13},{12,14},{13,15},{14,10},{15,... | collective-permute-start | bytes 3538952 | tf_op jit(solution)/shard_map/ppermute | solution.py:377
  65.4 1.7 %collective-permute-start.14 = (bf16[2,16,2048]{2,1,0:T(8,128)(2,1)S(1)}, bf16[2,16,2048]{2,1,0:T(8,128)(2,1)S(1)}, u32[]{:S(2)}, u32[]{:S(2)}) collective-permute-start(bf16[2,16,2048]{2,1,0:T(8,128)(2,1)S(1)} %pad_maximum_fusion.1), channel_id=1, source_target_pairs={{16,0},{0,16},{17,1},{1,17},{18,2},{2,18},{19,3},{3,19},{20,4},{4,... | collective-permute-start | bytes 393224 | tf_op jit(solution)/shard_map/ppermute | solution.py:381
  67.2 4.2 %chunk.12 = (f32[2048,64]{1,0:T(8,128)S(1)}, bf16[4096,1024]{1,0:T(8,128)(2,1)S(1)}, bf16[4096,768]{1,0:T(8,128)(2,1)S(1)}, bf16[16,16,4096]{2,1,0:T(8,128)(2,1)S(1)}) custom-call(bf16[144,4096]{1,0:T(8,128)(2,1)S(1)} %collective-permute-done.4.refs_0_, ...), custom_call_target="tpu_custom_call", output_to_operand_aliasing={{0}: (6, {}), {1}: (2, {}), {2}: (3, {}), {3}: (4, {})} | custom-call | flops 1000000 | bytes 100000 | tf_op jit(solution)/shard_map/chunk/pallas_call | solution.py:200
  71.4 4.3 %chunk.13 = (f32[2048,64]{1,0:T(8,128)S(1)}, bf16[4096,1024]{1,0:T(8,128)(2,1)S(1)}, bf16[4096,768]{1,0:T(8,128)(2,1)S(1)}, bf16[16,16,4096]{2,1,0:T(8,128)(2,1)S(1)}) custom-call(bf16[144,4096]{1,0:T(8,128)(2,1)S(1)} %collective-permute-done.12.refs_0_, ...), custom_call_target="tpu_custom_call", output_to_operand_aliasing={{0}: (6, {}), {1}: (2, {}), {2}: (3, {}), {3}: (4, {})} | custom-call | flops 1000000 | bytes 100000 | tf_op jit(solution)/shard_map/chunk/pallas_call | solution.py:200
  75.7 15.8 %collective-permute-done.10.refs_0_ = bf16[144,4096]{1,0:T(8,128)(2,1)S(1)} collective-permute-done((bf16[144,4096]{1,0:T(8,128)(2,1)S(1)}, bf16[144,4096]{1,0:T(8,128)(2,1)S(1)}, u32[]{:S(2)}, u32[]{:S(2)}) %collective-permute-start.10) | collective-permute-done | bytes 1179680 | tf_op jit(solution)/shard_map/ppermute | solution.py:377
  91.5 1.7 %collective-permute-done.11.refs_1_ = bf16[144,4096]{1,0:T(8,128)(2,1)S(1)} collective-permute-done((bf16[144,4096]{1,0:T(8,128)(2,1)S(1)}, bf16[144,4096]{1,0:T(8,128)(2,1)S(1)}, u32[]{:S(2)}, u32[]{:S(2)}) %collective-permute-start.11) | collective-permute-done | bytes 1179680 | tf_op jit(solution)/shard_map/ppermute | solution.py:377
  93.9 1.6 %collective-permute-start.16 = (bf16[64,4096]{1,0:T(8,128)(2,1)S(1)}, bf16[64,4096]{1,0:T(8,128)(2,1)S(1)}, u32[]{:S(2)}, u32[]{:S(2)}) collective-permute-start(bf16[64,4096]{1,0:T(8,128)(2,1)S(1)} %slice.34), channel_id=1, source_target_pairs={{0,4},{1,5},{4,8},{5,9},{8,12},{9,13},{12,14},{13,15},{14,10},{15,... | collective-permute-start | bytes 1572872 | tf_op jit(solution)/shard_map/ppermute | solution.py:377
  97.6 4.2 %chunk.14 = (f32[2048,64]{1,0:T(8,128)S(1)}, bf16[4096,1024]{1,0:T(8,128)(2,1)S(1)}, bf16[4096,768]{1,0:T(8,128)(2,1)S(1)}, bf16[16,16,4096]{2,1,0:T(8,128)(2,1)S(1)}) custom-call(bf16[144,4096]{1,0:T(8,128)(2,1)S(1)} %collective-permute-done.10.refs_0_, ...), custom_call_target="tpu_custom_call", output_to_operand_aliasing={{0}: (6, {}), {1}: (2, {}), {2}: (3, {}), {3}: (4, {})} | custom-call | flops 1000000 | bytes 100000 | tf_op jit(solution)/shard_map/chunk/pallas_call | solution.py:200
  101.8 4.2 %chunk.15 = (f32[2048,64]{1,0:T(8,128)S(1)}, bf16[4096,1024]{1,0:T(8,128)(2,1)S(1)}, bf16[4096,768]{1,0:T(8,128)(2,1)S(1)}, bf16[16,16,4096]{2,1,0:T(8,128)(2,1)S(1)}) custom-call(bf16[144,4096]{1,0:T(8,128)(2,1)S(1)} %collective-permute-done.18.refs_0_, ...), custom_call_target="tpu_custom_call", output_to_operand_aliasing={{0}: (6, {}), {1}: (2, {}), {2}: (3, {}), {3}: (4, {})} | custom-call | flops 1000000 | bytes 100000 | tf_op jit(solution)/shard_map/chunk/pallas_call | solution.py:200
  107.8 4.1 %collective-permute-done.17.refs_1_ = bf16[80,4096]{1,0:T(8,128)(2,1)S(1)} collective-permute-done((bf16[80,4096]{1,0:T(8,128)(2,1)S(1)}, bf16[80,4096]{1,0:T(8,128)(2,1)S(1)}, u32[]{:S(2)}, u32[]{:S(2)}) %collective-permute-start.17) | collective-permute-done | bytes 655392 | tf_op jit(solution)/shard_map/ppermute | solution.py:377
  115.5 2.3 %chunk.16 = (f32[2048,64]{1,0:T(8,128)S(1)}, bf16[4096,1024]{1,0:T(8,128)(2,1)S(1)}, bf16[4096,768]{1,0:T(8,128)(2,1)S(1)}, bf16[16,16,4096]{2,1,0:T(8,128)(2,1)S(1)}) custom-call(bf16[64,4096]{1,0:T(8,128)(2,1)S(1)} %collective-permute-done.16.refs_0_, ...), custom_call_target="tpu_custom_call", output_to_operand_aliasing={{0}: (6, {}), {1}: (2, {}), {2}: (3, {}), {3}: (4, {})} | custom-call | flops 1000000 | bytes 100000 | tf_op jit(solution)/shard_map/chunk/pallas_call | solution.py:200
  117.9 2.3 %chunk.17 = (f32[2048,64]{1,0:T(8,128)S(1)}, bf16[4096,1024]{1,0:T(8,128)(2,1)S(1)}, bf16[4096,768]{1,0:T(8,128)(2,1)S(1)}, bf16[16,16,4096]{2,1,0:T(8,128)(2,1)S(1)}) custom-call(bf16[64,4096]{1,0:T(8,128)(2,1)S(1)} %collective-permute-done.22.refs_0_, ...), custom_call_target="tpu_custom_call", output_to_operand_aliasing={{0}: (6, {}), {1}: (2, {}), {2}: (3, {}), {3}: (4, {})} | custom-call | flops 1000000 | bytes 100000 | tf_op jit(solution)/shard_map/chunk/pallas_call | solution.py:200
  120.3 2.0 %finish.1 = f32[16,256]{1,0:T(8,128)S(1)} custom-call(s32[16,16]{1,0:T(8,128)S(1)} %copy-done.1, f32[2048,64]{1,0:T(8,128)S(1)} %get-tuple-element.135.left_ref, f32[32,16,128]{2,1,0:T(8,128)S(1)} %sketches.1.flat_ref, bf16[16,16,4096]{2,1,0:T(8,128)(2,1)S(1)} %get-tuple-element.137.shares_ref, bf16[1,16,2048]{2,1,0:T(8,128)(2,1)S(1)} %collective-permute-done.3.refs_0_, ...), custom_call_target="tpu_custom_call" | custom-call | flops 1000000 | bytes 100000 | tf_op jit(solution)/shard_map/finish/pallas_call | solution.py:311
  122.3 10.3 %all_to_all.9 = f32[16,1,256]{2,1,0:T(1,128)S(1)} all-to-all(f32[16,1,256]{2,1,0:T(1,128)S(1)} %copy.48), channel_id=1, replica_groups=mesh['groups'=2,'examples'=16] {'examples'}, dimensions={0} | all-to-all | bytes 32768 | tf_op jit(solution)/shard_map/all_to_all | solution.py:427
  (64 shorter events, 14.5 us)
Async XLA Ops:
  3.6 12.7 %collective-permute-start.2 = (bf16[144,4096]{1,0:T(8,128)(2,1)S(1)}, bf16[144,4096]{1,0:T(8,128)(2,1)S(1)}, u32[]{:S(2)}, u32[]{:S(2)}) collective-permute-start(bf16[144,4096]{1,0:T(8,128)(2,1)S(1)} %get-tuple-element.75.x_ref), channel_id=1, source_target_pairs={{0,1},{1,0},{2,3},{3,2},{4,5},{5,4},{6,7},{7,6},{8,9},{9,8},{10,11... | collective-permute-start | bytes 3538952 | tf_op jit(solution)/shard_map/ppermute | solution.py:377
  4.1 29.2 %collective-permute-start.1 = (bf16[144,4096]{1,0:T(8,128)(2,1)S(1)}, bf16[144,4096]{1,0:T(8,128)(2,1)S(1)}, u32[]{:S(2)}, u32[]{:S(2)}) collective-permute-start(bf16[144,4096]{1,0:T(8,128)(2,1)S(1)} %get-tuple-element.75.x_ref), channel_id=1, source_target_pairs={{4,0},{5,1},{8,4},{9,5},{12,8},{13,9},{14,12},{15,13},{10,14},{11,... | collective-permute-start | bytes 3538952 | tf_op jit(solution)/shard_map/ppermute | solution.py:377
  6.7 28.0 %collective-permute-start = (bf16[144,4096]{1,0:T(8,128)(2,1)S(1)}, bf16[144,4096]{1,0:T(8,128)(2,1)S(1)}, u32[]{:S(2)}, u32[]{:S(2)}) collective-permute-start(bf16[144,4096]{1,0:T(8,128)(2,1)S(1)} %get-tuple-element.75.x_ref), channel_id=1, source_target_pairs={{0,4},{1,5},{4,8},{5,9},{8,12},{9,13},{12,14},{13,15},{14,10},{15,... | collective-permute-start | bytes 3538952 | tf_op jit(solution)/shard_map/ppermute | solution.py:377
  6.8 11.8 %collective-permute-start.3 = (bf16[1,16,2048]{2,1,0:T(8,128)(2,1)S(1)}, bf16[1,16,2048]{2,1,0:T(8,128)(2,1)S(1)}, u32[]{:S(2)}, u32[]{:S(2)}) collective-permute-start(bf16[1,16,2048]{2,1,0:T(8,128)(2,1)S(1)} %get-tuple-element.81), channel_id=1, source_target_pairs={{16,0},{0,16},{17,1},{1,17},{18,2},{2,18},{19,3},{3,19},{20,4},{4,... | collective-permute-start | bytes 196616 | tf_op jit(solution)/shard_map/ppermute | solution.py:381
  34.7 8.4 %collective-permute-start.7 = (bf16[144,4096]{1,0:T(8,128)(2,1)S(1)}, bf16[144,4096]{1,0:T(8,128)(2,1)S(1)}, u32[]{:S(2)}, u32[]{:S(2)}) collective-permute-start(bf16[144,4096]{1,0:T(8,128)(2,1)S(1)} %collective-permute-done.1.refs_1_), channel_id=1, source_target_pairs={{0,1},{1,0},{2,3},{3,2},{4,5},{5,4},{6,7},{7,6},{8,9},{9,8},{10,11... | collective-permute-start | bytes 3538952 | tf_op jit(solution)/shard_map/ppermute | solution.py:377
  35.2 27.9 %collective-permute-start.4 = (bf16[144,4096]{1,0:T(8,128)(2,1)S(1)}, bf16[144,4096]{1,0:T(8,128)(2,1)S(1)}, u32[]{:S(2)}, u32[]{:S(2)}) collective-permute-start(bf16[144,4096]{1,0:T(8,128)(2,1)S(1)} %collective-permute-done.refs_0_), channel_id=1, source_target_pairs={{0,4},{1,5},{4,8},{5,9},{8,12},{9,13},{12,14},{13,15},{14,10},{15,... | collective-permute-start | bytes 3538952 | tf_op jit(solution)/shard_map/ppermute | solution.py:377
  35.5 27.6 %collective-permute-start.5 = (bf16[144,4096]{1,0:T(8,128)(2,1)S(1)}, bf16[144,4096]{1,0:T(8,128)(2,1)S(1)}, u32[]{:S(2)}, u32[]{:S(2)}) collective-permute-start(bf16[144,4096]{1,0:T(8,128)(2,1)S(1)} %collective-permute-done.1.refs_1_), channel_id=1, source_target_pairs={{4,0},{5,1},{8,4},{9,5},{12,8},{13,9},{14,12},{15,13},{10,14},{11,... | collective-permute-start | bytes 3538952 | tf_op jit(solution)/shard_map/ppermute | solution.py:377
  37.3 10.1 %collective-permute-start.8 = (bf16[2,16,2048]{2,1,0:T(8,128)(2,1)S(1)}, bf16[2,16,2048]{2,1,0:T(8,128)(2,1)S(1)}, u32[]{:S(2)}, u32[]{:S(2)}) collective-permute-start(bf16[2,16,2048]{2,1,0:T(8,128)(2,1)S(1)} %pad_maximum_fusion), channel_id=1, source_target_pairs={{16,0},{0,16},{17,1},{1,17},{18,2},{2,18},{19,3},{3,19},{20,4},{4,... | collective-permute-start | bytes 393224 | tf_op jit(solution)/shard_map/ppermute | solution.py:381
  38.8 8.5 %collective-permute-start.9 = (bf16[1,16,2048]{2,1,0:T(8,128)(2,1)S(1)}, bf16[1,16,2048]{2,1,0:T(8,128)(2,1)S(1)}, u32[]{:S(2)}, u32[]{:S(2)}) collective-permute-start(bf16[1,16,2048]{2,1,0:T(8,128)(2,1)S(1)} %collective-permute-done.3.refs_0_), channel_id=1, source_target_pairs={{0,1},{1,0},{2,3},{3,2},{4,5},{5,4},{6,7},{7,6},{8,9},{9,8},{10,11... | collective-permute-start | bytes 196616 | tf_op jit(solution)/shard_map/ppermute | solution.py:377
  63.1 28.4 %collective-permute-start.10 = (bf16[144,4096]{1,0:T(8,128)(2,1)S(1)}, bf16[144,4096]{1,0:T(8,128)(2,1)S(1)}, u32[]{:S(2)}, u32[]{:S(2)}) collective-permute-start(bf16[144,4096]{1,0:T(8,128)(2,1)S(1)} %collective-permute-done.4.refs_0_), channel_id=1, source_target_pairs={{0,4},{1,5},{4,8},{5,9},{8,12},{9,13},{12,14},{13,15},{14,10},{15,... | collective-permute-start | bytes 3538952 | tf_op jit(solution)/shard_map/ppermute | solution.py:377
  64.9 6.5 %collective-permute-start.13 = (bf16[144,4096]{1,0:T(8,128)(2,1)S(1)}, bf16[144,4096]{1,0:T(8,128)(2,1)S(1)}, u32[]{:S(2)}, u32[]{:S(2)}) collective-permute-start(bf16[144,4096]{1,0:T(8,128)(2,1)S(1)} %collective-permute-done.5.refs_1_), channel_id=1, source_target_pairs={{0,1},{1,0},{2,3},{3,2},{4,5},{5,4},{6,7},{7,6},{8,9},{9,8},{10,11... | collective-permute-start | bytes 3538952 | tf_op jit(solution)/shard_map/ppermute | solution.py:377
  65.1 28.2 %collective-permute-start.11 = (bf16[144,4096]{1,0:T(8,128)(2,1)S(1)}, bf16[144,4096]{1,0:T(8,128)(2,1)S(1)}, u32[]{:S(2)}, u32[]{:S(2)}) collective-permute-start(bf16[144,4096]{1,0:T(8,128)(2,1)S(1)} %collective-permute-done.5.refs_1_), channel_id=1, source_target_pairs={{4,0},{5,1},{8,4},{9,5},{12,8},{13,9},{14,12},{15,13},{10,14},{11,... | collective-permute-start | bytes 3538952 | tf_op jit(solution)/shard_map/ppermute | solution.py:377
  65.4 10.3 %collective-permute-start.14 = (bf16[2,16,2048]{2,1,0:T(8,128)(2,1)S(1)}, bf16[2,16,2048]{2,1,0:T(8,128)(2,1)S(1)}, u32[]{:S(2)}, u32[]{:S(2)}) collective-permute-start(bf16[2,16,2048]{2,1,0:T(8,128)(2,1)S(1)} %pad_maximum_fusion.1), channel_id=1, source_target_pairs={{16,0},{0,16},{17,1},{1,17},{18,2},{2,18},{19,3},{3,19},{20,4},{4,... | collective-permute-start | bytes 393224 | tf_op jit(solution)/shard_map/ppermute | solution.py:381
  67.2 8.5 %collective-permute-start.15 = (bf16[2,16,2048]{2,1,0:T(8,128)(2,1)S(1)}, bf16[2,16,2048]{2,1,0:T(8,128)(2,1)S(1)}, u32[]{:S(2)}, u32[]{:S(2)}) collective-permute-start(bf16[2,16,2048]{2,1,0:T(8,128)(2,1)S(1)} %collective-permute-done.8.refs_2_), channel_id=1, source_target_pairs={{0,1},{1,0},{2,3},{3,2},{4,5},{5,4},{6,7},{7,6},{8,9},{9,8},{10,11... | collective-permute-start | bytes 393224 | tf_op jit(solution)/shard_map/ppermute | solution.py:377
  93.3 4.3 %collective-permute-start.18 = (bf16[144,4096]{1,0:T(8,128)(2,1)S(1)}, bf16[144,4096]{1,0:T(8,128)(2,1)S(1)}, u32[]{:S(2)}, u32[]{:S(2)}) collective-permute-start(bf16[144,4096]{1,0:T(8,128)(2,1)S(1)} %collective-permute-done.10.refs_0_), channel_id=1, source_target_pairs={{0,1},{1,0},{2,3},{3,2},{4,5},{5,4},{6,7},{7,6},{8,9},{9,8},{10,11... | collective-permute-start | bytes 3538952 | tf_op jit(solution)/shard_map/ppermute | solution.py:377
  93.4 8.4 %collective-permute-start.19 = (bf16[144,4096]{1,0:T(8,128)(2,1)S(1)}, bf16[144,4096]{1,0:T(8,128)(2,1)S(1)}, u32[]{:S(2)}, u32[]{:S(2)}) collective-permute-start(bf16[144,4096]{1,0:T(8,128)(2,1)S(1)} %collective-permute-done.11.refs_1_), channel_id=1, source_target_pairs={{0,1},{1,0},{2,3},{3,2},{4,5},{5,4},{6,7},{7,6},{8,9},{9,8},{10,11... | collective-permute-start | bytes 3538952 | tf_op jit(solution)/shard_map/ppermute | solution.py:377
  93.9 13.9 %collective-permute-start.16 = (bf16[64,4096]{1,0:T(8,128)(2,1)S(1)}, bf16[64,4096]{1,0:T(8,128)(2,1)S(1)}, u32[]{:S(2)}, u32[]{:S(2)}) collective-permute-start(bf16[64,4096]{1,0:T(8,128)(2,1)S(1)} %slice.34), channel_id=1, source_target_pairs={{0,4},{1,5},{4,8},{5,9},{8,12},{9,13},{12,14},{13,15},{14,10},{15,... | collective-permute-start | bytes 1572872 | tf_op jit(solution)/shard_map/ppermute | solution.py:377
  95.5 16.4 %collective-permute-start.17 = (bf16[80,4096]{1,0:T(8,128)(2,1)S(1)}, bf16[80,4096]{1,0:T(8,128)(2,1)S(1)}, u32[]{:S(2)}, u32[]{:S(2)}) collective-permute-start(bf16[80,4096]{1,0:T(8,128)(2,1)S(1)} %slice.35), channel_id=1, source_target_pairs={{4,0},{5,1},{8,4},{9,5},{12,8},{13,9},{14,12},{15,13},{10,14},{11,... | collective-permute-start | bytes 1966088 | tf_op jit(solution)/shard_map/ppermute | solution.py:377
  96.0 10.6 %collective-permute-start.20 = (bf16[2,16,2048]{2,1,0:T(8,128)(2,1)S(1)}, bf16[2,16,2048]{2,1,0:T(8,128)(2,1)S(1)}, u32[]{:S(2)}, u32[]{:S(2)}) collective-permute-start(bf16[2,16,2048]{2,1,0:T(8,128)(2,1)S(1)} %pad_maximum_fusion.2), channel_id=1, source_target_pairs={{16,0},{0,16},{17,1},{1,17},{18,2},{2,18},{19,3},{3,19},{20,4},{4,... | collective-permute-start | bytes 393224 | tf_op jit(solution)/shard_map/ppermute | solution.py:381
  97.6 9.1 %collective-permute-start.21 = (bf16[2,16,2048]{2,1,0:T(8,128)(2,1)S(1)}, bf16[2,16,2048]{2,1,0:T(8,128)(2,1)S(1)}, u32[]{:S(2)}, u32[]{:S(2)}) collective-permute-start(bf16[2,16,2048]{2,1,0:T(8,128)(2,1)S(1)} %collective-permute-done.14.refs_4_), channel_id=1, source_target_pairs={{0,1},{1,0},{2,3},{3,2},{4,5},{5,4},{6,7},{7,6},{8,9},{9,8},{10,11... | collective-permute-start | bytes 393224 | tf_op jit(solution)/shard_map/ppermute | solution.py:377
  111.9 5.9 %collective-permute-start.22 = (bf16[64,4096]{1,0:T(8,128)(2,1)S(1)}, bf16[64,4096]{1,0:T(8,128)(2,1)S(1)}, u32[]{:S(2)}, u32[]{:S(2)}) collective-permute-start(bf16[64,4096]{1,0:T(8,128)(2,1)S(1)} %collective-permute-done.16.refs_0_), channel_id=1, source_target_pairs={{0,1},{1,0},{2,3},{3,2},{4,5},{5,4},{6,7},{7,6},{8,9},{9,8},{10,11... | collective-permute-start | bytes 1572872 | tf_op jit(solution)/shard_map/ppermute | solution.py:377
  112.5 7.8 %collective-permute-start.25 = (bf16[1,16,2048]{2,1,0:T(8,128)(2,1)S(1)}, bf16[1,16,2048]{2,1,0:T(8,128)(2,1)S(1)}, u32[]{:S(2)}, u32[]{:S(2)}) collective-permute-start(bf16[1,16,2048]{2,1,0:T(8,128)(2,1)S(1)} %slice_bitcast_fusion.1), channel_id=1, source_target_pairs={{16,0},{0,16},{17,1},{1,17},{18,2},{2,18},{19,3},{3,19},{20,4},{4,... | collective-permute-start | bytes 196616 | tf_op jit(solution)/shard_map/ppermute | solution.py:381
  113.9 6.3 %collective-permute-start.24 = (bf16[2,16,2048]{2,1,0:T(8,128)(2,1)S(1)}, bf16[2,16,2048]{2,1,0:T(8,128)(2,1)S(1)}, u32[]{:S(2)}, u32[]{:S(2)}) collective-permute-start(bf16[2,16,2048]{2,1,0:T(8,128)(2,1)S(1)} %collective-permute-done.20.refs_6_), channel_id=1, source_target_pairs={{0,1},{1,0},{2,3},{3,2},{4,5},{5,4},{6,7},{7,6},{8,9},{9,8},{10,11... | collective-permute-start | bytes 393224 | tf_op jit(solution)/shard_map/ppermute | solution.py:377
  114.0 6.2 %collective-permute-start.26 = (bf16[1,16,2048]{2,1,0:T(8,128)(2,1)S(1)}, bf16[1,16,2048]{2,1,0:T(8,128)(2,1)S(1)}, u32[]{:S(2)}, u32[]{:S(2)}) collective-permute-start(bf16[1,16,2048]{2,1,0:T(8,128)(2,1)S(1)} %slice_bitcast_fusion), channel_id=1, source_target_pairs={{16,0},{0,16},{17,1},{1,17},{18,2},{2,18},{19,3},{3,19},{20,4},{4,... | collective-permute-start | bytes 196616 | tf_op jit(solution)/shard_map/ppermute | solution.py:381
  (6 other events, 21.9 us)
